TPU v7x, 32 devices: a whole 2x2x4 slice. The times are simulated.
32 devices in a mesh: req: 2 (over y), ctx: 4 (over x, core), tp: 4 (over z).
Axes of the slice: x: 2, y: 2, z: 4, core: 2. Of those that a mesh axis runs over, the one named last changes fastest.
Arguments:
- hidden_in: bfloat16 [4096, 6144], P(('req', 'ctx', 'tp')), parts along dimension 0, may hold values from -5 to 5
- queries: bfloat16 [4096, 4096], P(('req', 'ctx', 'tp')), parts along dimension 0, may hold values from -40 to 40
- keys: bfloat16 [4096, 1024], P(('req', 'ctx', 'tp')), parts along dimension 0, may hold values from -8 to 8
- values: bfloat16 [4096, 1024], P(('req', 'ctx', 'tp')), parts along dimension 0, may hold values from -6 to 6
- block_order: int32 [8], P('req'), parts along dimension 0, may hold values from 0 to 3, each once
- routes: int32 [4096, 2], P(('req', 'ctx')), parts along dimension 0, may hold values from 0 to 7, as said below
- out_weight: bfloat16 [4096, 6144], P('tp'), may hold values from -0.09375 to 0.09375
- norm_gain: float32 [6144], replicated, may hold values from 0.1 to 1.9
- router_weight: bfloat16 [6144, 8], replicated, may hold values from -0.078125 to 0.078125
- gate_weight: bfloat16 [6144, 8192], P(None, 'tp'), may hold values from -0.078125 to 0.078125
- up_weight: bfloat16 [6144, 8192], P(None, 'tp'), may hold values from -0.078125 to 0.078125
- down_weight: bfloat16 [8192, 6144], P('tp'), may hold values from -0.0625 to 0.0625
Outputs:
- attended: bfloat16 [4096, 6144], P(('req', 'ctx', 'tp')), parts along dimension 0
- expert_out: bfloat16 [4096, 6144], P(('req', 'ctx', 'tp')), parts along dimension 0
There are 2 independent parts, one for each index of `req`. A program takes and returns all parts, laid end to end along the dimension named above; an argument that names none is the same for every part. Nothing has to cross between parts.
Inputs may be any that keep to these rules, and one draw needn't show every extreme that they name: `routes`: each row names two different experts. In each block of 512 rows at most 192 rows name expert 0, and exactly 192 in at least one block.
All inputs are finite; a program needn't handle non-finite values.
Results may differ from a plain program's by a relative error of at most 0.023.
Values may be sent and summed in bfloat16 or wider, within the bound.
No kernel may reach another device: no remote copies, remote signals or barrier semaphores. Data moves between devices by JAX's collectives and lax.ppermute only.
A program may use at most 256 MiB of HBM per device.

v0:
```python
import functools
import math

import jax
import jax.numpy as jnp
from jax import lax
from jax.experimental import pallas as pl
from jax.experimental.pallas import tpu as pltpu
from jax.sharding import PartitionSpec as P

HEADS = 32
KV_HEADS = 8
HD = 128
FACTOR = math.log2(math.e) / math.sqrt(HD)
LINE = 4
SUM_ROWS = 16
TILE = 256
VMEM_SMALL = 12 * 1024 * 1024
VMEM_HELD = 20 * 1024 * 1024
VMEM_LARGE = 40 * 1024 * 1024


def attention_kernel(slots, together, held, pairs, sharing, block_rows, *refs):
    (order, mine), refs = refs[:2], refs[2:]
    query_refs, refs = refs[:slots], refs[slots:]
    place_ref, key_place_ref, refs = refs[0], refs[1], refs[2:]
    pair_refs, refs = refs[: len(held)], refs[len(held) :]
    out_ref, query_ref, key_ref, value_ref, top_ref, total_ref = refs
    half = out_ref.shape[1]
    me = mine[0]
    my_block = order[me]
    blocks = [(ref, index, offset) for ref, group in zip(pair_refs, held) for index, offset in enumerate(group)]

    @pl.when(pl.program_id(0) == 0)
    def _():
        value_ref[:, :, HD:, :] = jnp.ones((len(blocks), pairs, SUM_ROWS, block_rows), jnp.bfloat16)

    for at, (ref, index, offset) in enumerate(blocks):

        @pl.when((pl.program_id(0) == 0) & (order[me ^ offset] <= my_block))
        def _():
            for p in range(pairs):
                rows = slice(index * block_rows, (index + 1) * block_rows)
                key_ref[at, p] = ref[rows, p * HD : (p + 1) * HD]
                value_ref[at, p, :HD, :] = ref[rows, (pairs + p) * HD : (pairs + p + 1) * HD].T

    for at in range(slots):

        @pl.when(pl.program_id(0) == at // together)
        def _():
            for p in range(pairs):
                for g in range(sharing):
                    column = (p * sharing + g) * HD
                    row = (at % together * sharing + g) * half
                    query_ref[p, row : row + half, :] = query_refs[at][:, column : column + HD]

    def scores_of(p, at):
        return lax.dot_general(
            key_ref[at, p], query_ref[p], (((1,), (1,)), ((), ())), preferred_element_type=jnp.float32
        )

    def mixed_of(p, at, weights):
        return jnp.dot(value_ref[at, p], weights, preferred_element_type=jnp.float32)

    place = jnp.concatenate([place_ref[i] for i in range(together) for _ in range(sharing)], axis=1)
    visible = key_place_ref[...] <= place
    for p in range(pairs):
        scores = jnp.where(visible, scores_of(p, 0), -1e30)
        top = jnp.max(scores, axis=0, keepdims=True)
        weights = jnp.exp2((scores - top) * FACTOR).astype(jnp.bfloat16)
        top_ref[p, 0:1, :] = top
        total_ref[p] = mixed_of(p, 0, weights)

    @pl.loop(1, len(blocks))
    def _(at):
        offset = blocks[1][2] if len(blocks) > 1 else 0
        for other in range(2, len(blocks)):
            offset = jnp.where(at == other, blocks[other][2], offset)

        @pl.when(order[me ^ offset] < my_block)
        def _():
            for p in range(pairs):
                top = top_ref[p, 0:1, :]
                scores = scores_of(p, at)
                raised = jnp.maximum(top, jnp.max(scores, axis=0, keepdims=True))
                weights = jnp.exp2((scores - raised) * FACTOR).astype(jnp.bfloat16)
                top_ref[p, 0:1, :] = raised
                total_ref[p] = total_ref[p] * jnp.exp2((top - raised) * FACTOR) + mixed_of(p, at, weights)

    for p in range(pairs):
        mixed = (total_ref[p, :HD, :] / total_ref[p, HD : HD + 1, :]).T.astype(jnp.bfloat16)
        for i in range(together):
            for g in range(sharing):
                column = (p * sharing + g) * HD
                row = (i * sharing + g) * half
                out_ref[i, :, column : column + HD] = mixed[row : row + half]


def attend(order, mine, queries, places, key_places, pair_list, held, pairs, sharing, block_rows):
    slots = len(queries)
    half, width = queries[0].shape
    together = 2 if slots <= LINE else 1
    tall = together * sharing * half
    blocks = sum(len(group) for group in held)
    count = blocks * block_rows
    kernel = functools.partial(attention_kernel, slots, together, held, pairs, sharing, block_rows)
    whole = [pl.BlockSpec(memory_space=pltpu.VMEM) for _ in pair_list]
    return pl.pallas_call(
        kernel,
        grid_spec=pltpu.PrefetchScalarGridSpec(
            num_scalar_prefetch=2,
            grid=(slots // together,),
            in_specs=[pl.BlockSpec((half, width), lambda s, *_: (0, 0))] * slots
            + [
                pl.BlockSpec((together, 1, half), lambda s, *_: (s, 0, 0)),
                pl.BlockSpec((block_rows, 1), lambda s, *_: (0, 0)),
            ]
            + whole,
            out_specs=pl.BlockSpec((together, half, width), lambda s, *_: (s, 0, 0)),
            scratch_shapes=[
                pltpu.VMEM((pairs, tall, HD), jnp.bfloat16),
                pltpu.VMEM((blocks, pairs, block_rows, HD), jnp.bfloat16),
                pltpu.VMEM((blocks, pairs, HD + SUM_ROWS, block_rows), jnp.bfloat16),
                pltpu.VMEM((pairs, 8, tall), jnp.float32),
                pltpu.VMEM((pairs, HD + SUM_ROWS, tall), jnp.float32),
            ],
        ),
        out_shape=jax.ShapeDtypeStruct((slots, half, width), jnp.bfloat16),
        compiler_params=pltpu.CompilerParams(vmem_limit_bytes=12 * 1024 * 1024),
        cost_estimate=pl.CostEstimate(
            flops=40 * slots * half * width * count,
            bytes_accessed=2 * (2 * slots * half * width + count * 2 * pairs * HD),
            transcendentals=slots * half * width // HD * count,
        ),
    )(order, mine, *queries, places, key_places, *pair_list)


def hidden_kernel(plan, *refs):
    mine, refs = refs[0], refs[1:]
    sources = []
    for count in plan:
        sources.append(refs[:count])
        refs = refs[count:]
    gate_weight, up_weight, out, chosen = refs

    def place(s, source):
        rows, width = source[0].shape
        for c, ref in enumerate(source):
            chosen[s * rows : (s + 1) * rows, c * width : (c + 1) * width] = ref[...]

    @pl.when(pl.program_id(0) == 0)
    def _():
        place(0, sources[0])
        for s in range(1, (len(plan) + 1) // 2):
            right, left = sources[s], sources[len(plan) - s]

            @pl.when(mine[0] >= s)
            def _():
                place(s, right)

            @pl.when(mine[0] < s)
            def _():
                place(s, left)

    gate = jnp.dot(chosen[...], gate_weight[...], preferred_element_type=jnp.float32)
    upward = jnp.dot(chosen[...], up_weight[...], preferred_element_type=jnp.float32)
    out[...] = (gate / (1.0 + jnp.exp(-gate)) * upward).astype(jnp.bfloat16)


def hidden_units(mine, sources, gate_weight, up_weight):
    flat = [piece for source in sources for piece in source]
    rows = flat[0].shape[0] * ((len(sources) + 1) // 2)
    depth, width = gate_weight.shape
    tile = min(TILE, width)
    weight = pl.BlockSpec((depth, tile), lambda n, *_: (0, n))
    return pl.pallas_call(
        functools.partial(hidden_kernel, [len(source) for source in sources]),
        grid_spec=pltpu.PrefetchScalarGridSpec(
            num_scalar_prefetch=1,
            grid=(width // tile,),
            in_specs=[pl.BlockSpec(memory_space=pltpu.VMEM)] * len(flat) + [weight, weight],
            out_specs=pl.BlockSpec((rows, tile), lambda n, *_: (0, n)),
            scratch_shapes=[pltpu.VMEM((rows, depth), jnp.bfloat16)],
        ),
        out_shape=jax.ShapeDtypeStruct((rows, width), jnp.bfloat16),
        compiler_params=pltpu.CompilerParams(vmem_limit_bytes=VMEM_LARGE),
        cost_estimate=pl.CostEstimate(
            flops=4 * rows * depth * width, bytes_accessed=4 * depth * width, transcendentals=rows * width
        ),
    )(mine, *flat, gate_weight, up_weight)


def product_kernel(left_ref, weight, out_ref):
    out_ref[...] = jnp.dot(left_ref[...], weight[...], preferred_element_type=jnp.float32).astype(jnp.bfloat16)


def resident_product_kernel(cut, left_ref, weight, out_ref):
    tile = out_ref.shape[1]
    columns = pl.ds(pl.multiple_of((cut * pl.num_programs(0) + pl.program_id(0)) * tile, tile), tile)
    out_ref[...] = jnp.dot(left_ref[...], weight[:, columns], preferred_element_type=jnp.float32).astype(
        jnp.bfloat16
    )


def product(left, weight, cut, pieces, resident=False):
    rows, depth = left.shape
    width = weight.shape[1] // pieces
    tile = 2 * TILE
    in_place = pl.BlockSpec(memory_space=pltpu.VMEM)
    streamed = pl.BlockSpec((depth, tile), lambda n: (0, cut * (width // tile) + n))
    return pl.pallas_call(
        functools.partial(resident_product_kernel, cut) if resident else product_kernel,
        grid=(width // tile,),
        in_specs=[in_place, in_place if resident else streamed],
        out_specs=pl.BlockSpec((rows, tile), lambda n: (0, n)),
        out_shape=jax.ShapeDtypeStruct((rows, width), jnp.bfloat16),
        compiler_params=pltpu.CompilerParams(vmem_limit_bytes=VMEM_HELD if resident else VMEM_SMALL),
        cost_estimate=pl.CostEstimate(
            flops=2 * rows * depth * width, bytes_accessed=2 * depth * width, transcendentals=0
        ),
    )(left, weight)


def pack_pairs_kernel(shards, mine, keys_ref, values_ref, *outs):
    width = keys_ref.shape[1] // shards
    for s in range(shards):
        columns = pl.ds(pl.multiple_of(lax.rem(mine[0] + s, shards) * width, width), width)
        outs[s][:, :width] = keys_ref[:, columns]
        outs[s][:, width:] = values_ref[:, columns]


def pack_pairs(mine, keys, values, shards):
    rows, width = keys.shape
    spec = pl.BlockSpec((rows, width), lambda k, *_: (0, 0))
    out = (rows, 2 * width // shards)
    return pl.pallas_call(
        functools.partial(pack_pairs_kernel, shards),
        grid_spec=pltpu.PrefetchScalarGridSpec(
            num_scalar_prefetch=1,
            grid=(1,),
            in_specs=[spec, spec],
            out_specs=[pl.BlockSpec(out, lambda k, *_: (0, 0))] * shards,
        ),
        out_shape=[jax.ShapeDtypeStruct(out, keys.dtype)] * shards,
    )(mine, keys, values)


def pack_queries_kernel(shards, halves, mine, picked_ref, query_ref, *outs):
    rows = query_ref.shape[0]
    half = rows // halves
    width = query_ref.shape[1] // shards
    packed, (order_ref, places_ref, count_ref) = outs[: halves * shards], outs[halves * shards :]
    me = mine[0]
    across = lax.broadcasted_iota(jnp.int32, (rows, rows), 1)
    down = lax.broadcasted_iota(jnp.int32, (rows, rows), 0)
    up_to = jnp.where(down <= across, 1.0, 0.0).astype(jnp.bfloat16)
    picked = picked_ref[...]
    seen = jnp.dot(picked.astype(jnp.bfloat16), up_to, preferred_element_type=jnp.float32).astype(jnp.int32)
    count = seen[:, rows - 1 : rows]
    row_ids = lax.broadcasted_iota(jnp.int32, seen.shape, 1)
    slot = jnp.where(picked > 0, seen - 1, count + row_ids - seen)
    count_ref[...] = jnp.broadcast_to(jnp.max(count, axis=0, keepdims=True), count_ref.shape).astype(jnp.float32)
    ids = row_ids.astype(jnp.bfloat16)
    for s in range(shards):
        shard = lax.rem(me - s + shards, shards)
        mine_slot = slot[0:1]
        for other in range(1, shards):
            mine_slot = jnp.where(shard == other, slot[other : other + 1], mine_slot)
        at_slot = jnp.where(mine_slot == down, 1.0, 0.0).astype(jnp.bfloat16)
        rows_at = lax.dot_general(ids, at_slot, (((1,), (1,)), ((), ())), preferred_element_type=jnp.float32)
        places_ref[s] = rows_at[0:1].astype(jnp.int32) + shard * rows
        if s == 0:
            order_ref[...] = at_slot
    for s in range(shards):
        columns = pl.ds(pl.multiple_of(lax.rem(me + s, shards) * width, width), width)
        ordered = jnp.dot(order_ref[...], query_ref[:, columns], preferred_element_type=jnp.float32)
        ordered = ordered.astype(jnp.bfloat16)
        for h in range(halves):
            packed[h * shards + s][...] = ordered[h * half : (h + 1) * half]


def pack_queries(mine, picked, queries, shards, halves):
    rows, width = queries.shape
    packed = (rows // halves, width // shards)
    shapes = [jax.ShapeDtypeStruct(packed, jnp.bfloat16)] * (halves * shards) + [
        jax.ShapeDtypeStruct((rows, rows), jnp.bfloat16),
        jax.ShapeDtypeStruct((shards, 1, rows), jnp.int32),
        jax.ShapeDtypeStruct((8, 128), jnp.float32),
    ]

    def whole(shape):
        return pl.BlockSpec(shape, lambda k, *_: (0,) * len(shape))

    got = pl.pallas_call(
        functools.partial(pack_queries_kernel, shards, halves),
        grid_spec=pltpu.PrefetchScalarGridSpec(
            num_scalar_prefetch=1,
            grid=(1,),
            in_specs=[whole(picked.shape), whole(queries.shape)],
            out_specs=[whole(shape.shape) for shape in shapes],
        ),
        out_shape=shapes,
    )(mine, picked, queries)
    return [got[h * shards : (h + 1) * shards] for h in range(halves)], *got[halves * shards :]


def on_device(
    hidden_in,
    queries,
    keys,
    values,
    block_order,
    routes,
    out_weight,
    norm_gain,
    router_weight,
    gate_weight,
    up_weight,
    down_weight,
):
    shards = lax.axis_size("tp")
    blocks = lax.axis_size("ctx")
    me = lax.axis_index("tp")
    rows, model = hidden_in.shape
    block_rows = rows * shards
    per_device = HEADS // shards
    grouping = HEADS // KV_HEADS
    repeat_by = max(1, grouping // per_device)
    pairs = max(1, per_device // grouping)
    sharing = per_device // pairs
    half = rows // 2 if rows % 32 == 0 else rows
    halves = rows // half
    line = shards <= LINE
    pieces = 2 if line else 1
    cuts = [slice(c * (model // pieces), (c + 1) * (model // pieces)) for c in range(pieces)]
    shard_of = lax.rem(me - jnp.arange(shards, dtype=jnp.int32) + shards, shards)

    def shift(parts):
        moves = [[(i, (i + s) % shards) for i in range(shards)] for s in range(shards)]
        return [parts[0]] + [lax.ppermute(parts[s], "tp", moves[s]) for s in range(1, shards)]

    def exchange(source):
        got = lax.all_to_all(source, "tp", split_axis=1, concat_axis=0, tiled=True)
        got = got.reshape(shards, rows, source.shape[2])
        return [lax.dynamic_index_in_dim(got, shard_of[s], 0, keepdims=False) for s in range(shards)]

    def rights(count):
        return [(i, i + 1) for i in range(count)]

    def lefts(count):
        return [(i, i - 1) for i in range(shards - count, shards)]

    def reduce_line(pieces_terms):
        if not line:
            by_shard = [jnp.take(jnp.stack(terms), shard_of, axis=0).reshape(-1, terms[0].shape[1]) for terms in pieces_terms]
            return [
                lax.psum_scatter(term, "tp", scatter_dimension=0, tiled=True).astype(jnp.float32) for term in by_shard
            ], None
        got = [None] * len(pieces_terms)
        marks = []
        for s in range(1, shards):
            for c, terms in enumerate(pieces_terms):
                if got[c] is None:
                    sent = (terms[s], terms[shards - s])
                else:
                    arrived = got[c]
                    sent = (terms[s] + arrived[0], terms[shards - s] + arrived[1])
                right = lax.ppermute(sent[0], "tp", rights(s))
                left = lax.ppermute(sent[1], "tp", lefts(s))
                got[c] = lax.optimization_barrier((right, left))
            marks.append(got[0])
        return [
            terms[0].astype(jnp.float32) + right.astype(jnp.float32) + left.astype(jnp.float32)
            for terms, (right, left) in zip(pieces_terms, got)
        ], marks

    def gather_line(source, terms=None):
        if not line:
            got = lax.all_gather(source, "tp", axis=0)
            return [[jnp.take(got, shard_of, axis=0).reshape(shards * half, -1)]], None
        first_right = lax.ppermute(source, "tp", rights(shards - 1))
        first_left = lax.ppermute(source, "tp", lefts(shards - 1))
        first_right, first_left = lax.optimization_barrier((first_right, first_left))
        got = [(first_right[:, cut], first_left[:, cut]) for cut in cuts]
        from_left, from_right = [], []
        for s in range(2, shards):
            if terms is None:
                sent = got
                to_right = [(i, i + 1) for i in range(s - 1, shards - 1)]
                to_left = [(i, i - 1) for i in range(1, shards - s + 1)]
            else:
                sent = [
                    (
                        jnp.where(me >= s - 1, right, right + term[s - 1]),
                        jnp.where(me <= shards - s, left, left + term[shards - s + 1]),
                    )
                    for (right, left), term in zip(got, terms)
                ]
                to_right, to_left = rights(shards - 1), lefts(shards - 1)
            from_left.append([right for right, _ in sent])
            from_right.append([left for _, left in sent])
            got = [
                lax.optimization_barrier((lax.ppermute(right, "tp", to_right), lax.ppermute(left, "tp", to_left)))
                for right, left in sent
            ]
        from_left.append([right for right, _ in got])
        from_right.append([left for _, left in got])
        total = None
        if terms is not None:
            right = jnp.concatenate([right + term[shards - 1] for (right, _), term in zip(got, terms)], axis=1)
            left = jnp.concatenate([left + term[1] for (_, left), term in zip(got, terms)], axis=1)
            right = lax.ppermute(right, "tp", rights(shards - 1)).astype(jnp.float32)
            left = lax.ppermute(left, "tp", lefts(shards - 1)).astype(jnp.float32)
            total = jnp.concatenate([term[0] for term in terms], axis=1).astype(jnp.float32) + right + left
        return [[source]] + from_left + from_right, total

    key_places = (shard_of[:, None] * rows + jnp.arange(rows, dtype=jnp.int32)[None, :]).reshape(block_rows, 1)
    picked = ((routes[:, 0] == 0) | (routes[:, 1] == 0)).reshape(shards, rows)
    if line:
        sent_pairs = pack_pairs(me[None], keys, values, shards)
        own_pairs = jnp.concatenate(shift(sent_pairs), axis=0)
        picked, _ = lax.optimization_barrier((picked.astype(jnp.int32), sent_pairs))
        packed, order, places, fullest = pack_queries(me[None], picked, queries, shards, halves)
        asked = [shift(packed[h]) for h in range(halves)]
    else:

        def spread(source):
            widened = jnp.repeat(source.reshape(rows, KV_HEADS, HD), repeat_by, axis=1)
            return widened.reshape(rows, shards, pairs * HD)

        own_pairs = exchange(jnp.concatenate([spread(keys), spread(values)], axis=2))
        own_pairs = jnp.concatenate(own_pairs, axis=0)
        row_ids = jnp.arange(rows, dtype=jnp.int32)
        seen = jnp.cumsum(picked.astype(jnp.int32), axis=1)
        slot = jnp.where(picked, seen - 1, seen[:, -1:] + row_ids[None, :] - seen)
        at_slot = slot[:, None, :] == row_ids[None, :, None]
        row_of_slot = jnp.sum(jnp.where(at_slot, row_ids[None, None, :], 0), axis=2)
        places = row_of_slot + jnp.arange(shards, dtype=jnp.int32)[:, None] * rows
        places = jnp.take(places, shard_of, axis=0)[:, None, :]
        order = lax.dynamic_index_in_dim(at_slot, me, 0, keepdims=False).astype(jnp.bfloat16)
        ordered = jnp.dot(order, queries, preferred_element_type=jnp.float32).astype(jnp.bfloat16)
        asked = [exchange(ordered.reshape(rows, shards, per_device * HD))]

    pair_list, held = [own_pairs], [[0]]
    offset = blocks // 2
    while offset >= 1:
        pair_list += [lax.ppermute(part, "ctx", [(i, i ^ offset) for i in range(blocks)]) for part in pair_list]
        held += [[other ^ offset for other in group] for group in held]
        offset //= 2

    def reorder(source):
        return jnp.dot(order, source, preferred_element_type=jnp.float32).astype(jnp.bfloat16)

    def restore(parts):
        whole = jnp.concatenate(parts, axis=0) if len(parts) > 1 else parts[0]
        return lax.dot_general(
            order, whole, (((0,), (0,)), ((), ())), preferred_element_type=jnp.float32
        ).astype(jnp.bfloat16)

    mine = lax.axis_index("ctx").astype(jnp.int32)[None]
    expert_ids = jnp.arange(router_weight.shape[1], dtype=jnp.int32)
    slots = [s for s in range(1, shards, 2)] + [s for s in range(2, shards, 2)] + [0]

    def project(which):
        heads = attend(
            block_order,
            mine,
            [asked[which][s] for s in slots],
            jnp.stack([places[s, :, which * half : (which + 1) * half] for s in slots]),
            key_places,
            pair_list,
            held,
            pairs,
            sharing,
            block_rows,
        ).reshape(shards * half, per_device * HD)
        terms = []
        for c in range(pieces):
            term = product(heads, out_weight, c, pieces, True)
            terms.append([term[slots.index(s) * half : (slots.index(s) + 1) * half] for s in range(shards)])
        return terms

    def finish(which, head_sums):
        base = hidden[which * half : (which + 1) * half].astype(jnp.float32)
        return jnp.concatenate(
            [(base[:, cut] + head_sum).astype(jnp.bfloat16) for cut, head_sum in zip(cuts, head_sums)], axis=1
        )

    def normalise(attended):
        widened = attended.astype(jnp.float32)
        return (
            widened * lax.rsqrt(jnp.mean(widened * widened, axis=1, keepdims=True) + 1e-05) * norm_gain
        ).astype(jnp.bfloat16)

    def activate(normed, terms=None):
        sources, total = gather_line(normed, terms)
        return hidden_units(me[None], sources, gate_weight, up_weight), total

    def share_of(which, normed):
        logits = jnp.dot(normed, router_weight, preferred_element_type=jnp.float32)
        named = my_routes[which * half : (which + 1) * half]
        first = jnp.sum(jnp.where(named[:, 0:1] == expert_ids[None, :], logits, 0.0), axis=1)
        second = jnp.sum(jnp.where(named[:, 1:2] == expert_ids[None, :], logits, 0.0), axis=1)
        share = jnp.where(named[:, 0] == 0, 1.0 / (1.0 + jnp.exp(second - first)), 0.0)
        return share + jnp.where(named[:, 1] == 0, 1.0 / (1.0 + jnp.exp(first - second)), 0.0)

    def deliver(which, acts, normed):
        terms = [product(acts, down_weight, c, pieces).reshape(shards, half, -1) for c in range(pieces)]
        sums, marks = reduce_line([[term[s] for s in range(shards)] for term in terms])
        if line:
            normed, _ = lax.optimization_barrier((normed, marks[0]))
        share = share_of(which, normed)
        return jnp.concatenate([(total * share[:, None]).astype(jnp.bfloat16) for total in sums], axis=1)

    def late_expert(source):
        normed = normalise(source)
        return deliver(1, activate(normed)[0], normed)

    terms = project(0)
    if halves > 1:
        terms, asked[1] = lax.optimization_barrier((terms, asked[1]))
    totals, marks = reduce_line(terms)
    if line:
        hidden_in, order, _ = lax.optimization_barrier((hidden_in, order, marks[0]))
    hidden = reorder(hidden_in)
    my_routes = lax.dynamic_slice_in_dim(routes, me * rows, rows, 0).astype(jnp.bfloat16)
    my_routes = reorder(my_routes).astype(jnp.int32)
    first_half = finish(0, totals)
    normed = normalise(first_half)
    if halves == 1:
        return (restore([first_half]), restore([deliver(0, activate(normed)[0], normed)]))
    asked[1], _ = lax.optimization_barrier((asked[1], normed))
    acts, second_sum = activate(normed, project(1))
    second_half = (hidden[half:].astype(jnp.float32) + second_sum).astype(jnp.bfloat16)
    acts, second_half = lax.optimization_barrier((acts, second_half))
    part = deliver(0, acts, normed)
    part, late, fullest = lax.optimization_barrier((part, second_half, fullest))
    late = lax.cond(fullest[0, 0] > half, late_expert, jnp.zeros_like, late)
    return (restore([first_half, second_half]), restore([part, late]))


def solution(mesh):
    return jax.shard_map(
        on_device,
        mesh=mesh,
        in_specs=(
            P(("req", "ctx", "tp"), None),
            P(("req", "ctx", "tp"), None),
            P(("req", "ctx", "tp"), None),
            P(("req", "ctx", "tp"), None),
            P("req"),
            P(("req", "ctx"), None),
            P("tp", None),
            P(),
            P(),
            P(None, "tp"),
            P(None, "tp"),
            P("tp", None),
        ),
        out_specs=(P(("req", "ctx", "tp"), None), P(("req", "ctx", "tp"), None)),
        check_vma=False,
    )
```

profile of v0, /device:TPU:0, one launch (start us, length us, event | category | flops | bytes accessed | tf_op | source)
XLA Modules:
  0.0 288.0 jit_solution(6451648681665682946)
XLA Ops:
  2.7 3.0 %collective-permute-start.25 = (bf16[128,512]{1,0:T(8,128)(2,1)}, bf16[128,512]{1,0:T(8,128)(2,1)S(1)}, u32[]{:S(2)}, u32[]{:S(2)}) collective-permute-start(bf16[128,512]{1,0:T(8,128)(2,1)} %get-tuple-element.132), channel_id=1, source_target_pairs={{0,1},{1,2},{2,3},{3,0},{4,5},{5,6},{6,7},{7,4},{8,9},{9,10},{10,1... | collective-permute-start | bytes 393224 | tf_op jit(solution)/shard_map/ppermute | solution.py:340
  12.4 4.8 %collective-permute-done.26 = bf16[128,512]{1,0:T(8,128)(2,1)S(1)} collective-permute-done((bf16[128,512]{1,0:T(8,128)(2,1)}, bf16[128,512]{1,0:T(8,128)(2,1)S(1)}, u32[]{:S(2)}, u32[]{:S(2)}) %collective-permute-start.26) | collective-permute-done | bytes 131104 | tf_op jit(solution)/shard_map/ppermute | solution.py:340
  22.1 3.3 %collective-permute-start.22 = (bf16[64,1024]{1,0:T(8,128)(2,1)}, bf16[64,1024]{1,0:T(8,128)(2,1)S(1)}, u32[]{:S(2)}, u32[]{:S(2)}) collective-permute-start(bf16[64,1024]{1,0:T(8,128)(2,1)} %get-tuple-element.137), channel_id=1, source_target_pairs={{0,1},{1,2},{2,3},{3,0},{4,5},{5,6},{6,7},{7,4},{8,9},{9,10},{10,1... | collective-permute-start | bytes 393224 | tf_op jit(solution)/shard_map/ppermute | solution.py:340
  27.0 4.0 %collective-permute-done.28.refs_9_ = bf16[512,512]{1,0:T(8,128)(2,1)S(1)} collective-permute-done((bf16[512,512]{1,0:T(8,128)(2,1)S(1)}, bf16[512,512]{1,0:T(8,128)(2,1)S(1)}, u32[]{:S(2)}, u32[]{:S(2)}) %collective-permute-start.28) | collective-permute-done | bytes 524320 | tf_op jit(solution)/shard_map/ppermute | solution.py:447
  34.0 3.3 %collective-permute-start.31 = (bf16[64,1024]{1,0:T(8,128)(2,1)}, bf16[64,1024]{1,0:T(8,128)(2,1)S(1)}, u32[]{:S(2)}, u32[]{:S(2)}) collective-permute-start(bf16[64,1024]{1,0:T(8,128)(2,1)} %get-tuple-element.143), channel_id=1, source_target_pairs={{0,1},{1,2},{2,3},{3,0},{4,5},{5,6},{6,7},{7,4},{8,9},{9,10},{10,1... | collective-permute-start | bytes 393224 | tf_op jit(solution)/shard_map/ppermute | solution.py:340
  41.6 9.4 %shard_map.133 = bf16[4,64,1024]{2,1,0:T(8,128)(2,1)S(1)} custom-call(s32[4]{0:T(128)S(1)} %copy-done.15, s32[1]{0:T(128)} %bitcast.8.refs_1_, bf16[64,1024]{1,0:T(8,128)(2,1)S(1)} %copy-done.14, bf16[64,1024]{1,0:T(8,128)(2,1)} %collective-permute-done.23.refs_3_, bf16[64,1024]{1,0:T(8,128)(2,1)} %collective-permute-done.24.refs_4_, ...), custom_call_target="tpu_custom_call" | custom-call | flops 21474836480 | bytes 3145728 | tf_op jit(solution)/shard_map/pallas_call | solution.py:108
  51.1 4.6 %copy-done.2 = bf16[1024,6144]{1,0:T(8,128)(2,1)S(1)} copy-done((bf16[1024,6144]{1,0:T(8,128)(2,1)S(1)}, bf16[1024,6144]{1,0:T(8,128)(2,1)}, u32[]{:S(2)}) %copy-start.2) | copy-done | bytes 12582936
  64.1 2.8 collective-permute-start.34
  70.5 4.5 %collective-permute-done.34 = bf16[64,3072]{1,0:T(8,128)(2,1)} collective-permute-done((bf16[64,3072]{1,0:T(8,128)(2,1)}, bf16[64,3072]{1,0:T(8,128)(2,1)}, u32[]{:S(2)}, u32[]{:S(2)}) %collective-permute-start.34) | collective-permute-done | bytes 393248 | tf_op jit(solution)/shard_map/ppermute | solution.py:368
  77.0 5.0 %collective-permute-start.36 = (bf16[64,3072]{1,0:T(8,128)(2,1)S(1)}, bf16[64,3072]{1,0:T(8,128)(2,1)S(1)}, u32[]{:S(2)}, u32[]{:S(2)}) collective-permute-start(bf16[64,3072]{1,0:T(8,128)(2,1)S(1)} %get-tuple-element.268), channel_id=1, source_target_pairs={{0,1},{1,2},{4,5},{5,6},{8,9},{9,10},{12,13},{13,14},{16,17},{17,1... | collective-permute-start | bytes 1179656 | tf_op jit(solution)/shard_map/ppermute | solution.py:368
  84.2 4.9 %collective-permute-start.42 = (bf16[64,3072]{1,0:T(8,128)(2,1)S(1)}, bf16[64,3072]{1,0:T(8,128)(2,1)S(1)}, u32[]{:S(2)}, u32[]{:S(2)}) collective-permute-start(bf16[64,3072]{1,0:T(8,128)(2,1)S(1)} %get-tuple-element.270), channel_id=1, source_target_pairs={{0,1},{1,2},{4,5},{5,6},{8,9},{9,10},{12,13},{13,14},{16,17},{17,1... | collective-permute-start | bytes 1179656 | tf_op jit(solution)/shard_map/ppermute | solution.py:368
  95.2 5.0 %collective-permute-start.38 = (bf16[64,3072]{1,0:T(8,128)(2,1)S(1)}, bf16[64,3072]{1,0:T(8,128)(2,1)S(1)}, u32[]{:S(2)}, u32[]{:S(2)}) collective-permute-start(bf16[64,3072]{1,0:T(8,128)(2,1)S(1)} %add.267), channel_id=1, source_target_pairs={{0,1},{1,2},{2,3},{4,5},{5,6},{6,7},{8,9},{9,10},{10,11},{12,13},{... | collective-permute-start | bytes 1179656 | tf_op jit(solution)/shard_map/ppermute | solution.py:368
  102.0 4.9 %collective-permute-start.44 = (bf16[64,3072]{1,0:T(8,128)(2,1)S(1)}, bf16[64,3072]{1,0:T(8,128)(2,1)S(1)}, u32[]{:S(2)}, u32[]{:S(2)}) collective-permute-start(bf16[64,3072]{1,0:T(8,128)(2,1)S(1)} %add.274), channel_id=1, source_target_pairs={{0,1},{1,2},{2,3},{4,5},{5,6},{6,7},{8,9},{9,10},{10,11},{12,13},{... | collective-permute-start | bytes 1179656 | tf_op jit(solution)/shard_map/ppermute | solution.py:368
  108.5 6.6 %collective-permute-done.45 = bf16[64,3072]{1,0:T(8,128)(2,1)S(1)} collective-permute-done((bf16[64,3072]{1,0:T(8,128)(2,1)S(1)}, bf16[64,3072]{1,0:T(8,128)(2,1)S(1)}, u32[]{:S(2)}, u32[]{:S(2)}) %collective-permute-start.45) | collective-permute-done | bytes 393248 | tf_op jit(solution)/shard_map/ppermute | solution.py:369
  119.6 5.6 %collective-permute-start.46 = (bf16[64,6144]{1,0:T(8,128)(2,1)S(1)}, bf16[64,6144]{1,0:T(8,128)(2,1)S(1)}, u32[]{:S(2)}, u32[]{:S(2)}) collective-permute-start(bf16[64,6144]{1,0:T(8,128)(2,1)S(1)} %fusion.7.refs_1_), channel_id=1, source_target_pairs={{0,1},{1,2},{2,3},{4,5},{5,6},{6,7},{8,9},{9,10},{10,11},{12,13},{... | collective-permute-start | bytes 2359304 | tf_op jit(solution)/shard_map/ppermute | solution.py:381
  125.3 9.3 %shard_map.136 = bf16[4,64,1024]{2,1,0:T(8,128)(2,1)S(1)} custom-call(s32[4]{0:T(128)S(1)} %copy-done.15, s32[1]{0:T(128)} %bitcast.8.refs_1_, bf16[64,1024]{1,0:T(8,128)(2,1)S(1)} %collective-permute-done.31.refs_2_, bf16[64,1024]{1,0:T(8,128)(2,1)S(1)} %copy-done.11, bf16[64,1024]{1,0:T(8,128)(2,1)S(1)} %copy-done.9, bf16[64,1024]{1,0:T(8,128)(2,1)S(1)} %copy-done.7, ...), custom_call_target="tpu_custom_call" | custom-call | flops 21474836480 | bytes 3145728 | tf_op jit(solution)/shard_map/pallas_call | solution.py:108
  145.3 5.8 %collective-permute-start.48 = (bf16[64,3072]{1,0:T(8,128)(2,1)}, bf16[64,3072]{1,0:T(8,128)(2,1)}, u32[]{:S(2)}, u32[]{:S(2)}) collective-permute-start(bf16[64,3072]{1,0:T(8,128)(2,1)} %get-tuple-element.254.refs_2_), channel_id=1, source_target_pairs={{0,1},{1,2},{2,3},{4,5},{5,6},{6,7},{8,9},{9,10},{10,11},{12,13},{... | collective-permute-start | bytes 1179656 | tf_op jit(solution)/shard_map/ppermute | solution.py:403
  151.1 3.2 %collective-permute-start.50 = (bf16[64,3072]{1,0:T(8,128)(2,1)}, bf16[64,3072]{1,0:T(8,128)(2,1)S(1)}, u32[]{:S(2)}, u32[]{:S(2)}) collective-permute-start(bf16[64,3072]{1,0:T(8,128)(2,1)} %get-tuple-element.255.refs_3_), channel_id=1, source_target_pairs={{0,1},{1,2},{2,3},{4,5},{5,6},{6,7},{8,9},{9,10},{10,11},{12,13},{... | collective-permute-start | bytes 1179656 | tf_op jit(solution)/shard_map/ppermute | solution.py:403
  162.6 5.0 %collective-permute-start.52 = (bf16[64,3072]{1,0:T(8,128)(2,1)S(1)}, bf16[64,3072]{1,0:T(8,128)(2,1)S(1)}, u32[]{:S(2)}, u32[]{:S(2)}) collective-permute-start(bf16[64,3072]{1,0:T(8,128)(2,1)S(1)} %get-tuple-element.250.refs_4_), channel_id=1, source_target_pairs={{0,1},{1,2},{2,3},{4,5},{5,6},{6,7},{8,9},{9,10},{10,11},{12,13},{... | collective-permute-start | bytes 1179656 | tf_op jit(solution)/shard_map/ppermute | solution.py:403
  170.4 4.6 %collective-permute-start.54 = (bf16[64,3072]{1,0:T(8,128)(2,1)S(1)}, bf16[64,3072]{1,0:T(8,128)(2,1)S(1)}, u32[]{:S(2)}, u32[]{:S(2)}) collective-permute-start(bf16[64,3072]{1,0:T(8,128)(2,1)S(1)} %get-tuple-element.248.refs_5_), channel_id=1, source_target_pairs={{0,1},{1,2},{2,3},{4,5},{5,6},{6,7},{8,9},{9,10},{10,11},{12,13},{... | collective-permute-start | bytes 1179656 | tf_op jit(solution)/shard_map/ppermute | solution.py:403
  177.5 7.0 %collective-permute-done.55.refs_13_ = bf16[64,3072]{1,0:T(8,128)(2,1)S(1)} collective-permute-done((bf16[64,3072]{1,0:T(8,128)(2,1)S(1)}, bf16[64,3072]{1,0:T(8,128)(2,1)S(1)}, u32[]{:S(2)}, u32[]{:S(2)}) %collective-permute-start.55) | collective-permute-done | bytes 393248 | tf_op jit(solution)/shard_map/ppermute | solution.py:403
  184.8 4.6 %collective-permute-start.56 = (bf16[64,6144]{1,0:T(8,128)(2,1)S(1)}, bf16[64,6144]{1,0:T(8,128)(2,1)S(1)}, u32[]{:S(2)}, u32[]{:S(2)}) collective-permute-start(bf16[64,6144]{1,0:T(8,128)(2,1)S(1)} %pad_maximum_fusion.2), channel_id=1, source_target_pairs={{0,1},{1,2},{2,3},{4,5},{5,6},{6,7},{8,9},{9,10},{10,11},{12,13},{... | collective-permute-start | bytes 2359304 | tf_op jit(solution)/shard_map/ppermute | solution.py:412
  190.9 21.4 %shard_map.139.left_ref = bf16[256,2048]{1,0:T(8,128)(2,1)S(1)} custom-call(s32[1]{0:T(128)} %bitcast.6.mine.refs_0_, bf16[64,6144]{1,0:T(8,128)(2,1)S(1)} %copy-done.4, bf16[64,3072]{1,0:T(8,128)(2,1)} %get-tuple-element.254.refs_2_, bf16[64,3072]{1,0:T(8,128)(2,1)S(1)} %copy-done.5, bf16[64,3072]{1,0:T(8,128)(2,1)S(1)} %get-tuple-element.250.refs_4_, ...), custom_call_target="tpu_custom_call" | custom-call | flops 12884901888 | bytes 50331648 | tf_op jit(solution)/shard_map/pallas_call | solution.py:176
  212.7 8.0 %shard_map.141 = bf16[256,3072]{1,0:T(8,128)(2,1)S(1)} custom-call(bf16[256,2048]{1,0:T(8,128)(2,1)S(1)} %shard_map.139.left_ref, bf16[2048,6144]{1,0:T(8,128)(2,1)} %weight.11), custom_call_target="tpu_custom_call" | custom-call | flops 3221225472 | bytes 12582912 | tf_op jit(solution)/shard_map/pallas_call | solution.py:211
  220.7 8.0 %shard_map.140 = bf16[256,3072]{1,0:T(8,128)(2,1)S(1)} custom-call(bf16[256,2048]{1,0:T(8,128)(2,1)S(1)} %shard_map.139.left_ref, bf16[2048,6144]{1,0:T(8,128)(2,1)} %weight.11), custom_call_target="tpu_custom_call" | custom-call | flops 3221225472 | bytes 12582912 | tf_op jit(solution)/shard_map/pallas_call | solution.py:211
  229.5 4.6 %collective-permute-start.58 = (bf16[64,3072]{1,0:T(8,128)(2,1)S(1)}, bf16[64,3072]{1,0:T(8,128)(2,1)S(1)}, u32[]{:S(2)}, u32[]{:S(2)}) collective-permute-start(bf16[64,3072]{1,0:T(8,128)(2,1)S(1)} %get-tuple-element.234), channel_id=1, source_target_pairs={{0,1},{4,5},{8,9},{12,13},{16,17},{20,21},{24,25},{28,29}} | collective-permute-start | bytes 1179656 | tf_op jit(solution)/shard_map/ppermute | solution.py:368
  236.1 7.4 %collective-permute-done.58 = bf16[64,3072]{1,0:T(8,128)(2,1)S(1)} collective-permute-done((bf16[64,3072]{1,0:T(8,128)(2,1)S(1)}, bf16[64,3072]{1,0:T(8,128)(2,1)S(1)}, u32[]{:S(2)}, u32[]{:S(2)}) %collective-permute-start.58) | collective-permute-done | bytes 393248 | tf_op jit(solution)/shard_map/ppermute | solution.py:368
  244.3 5.0 %collective-permute-start.60 = (bf16[64,3072]{1,0:T(8,128)(2,1)S(1)}, bf16[64,3072]{1,0:T(8,128)(2,1)S(1)}, u32[]{:S(2)}, u32[]{:S(2)}) collective-permute-start(bf16[64,3072]{1,0:T(8,128)(2,1)S(1)} %get-tuple-element.232), channel_id=1, source_target_pairs={{0,1},{1,2},{4,5},{5,6},{8,9},{9,10},{12,13},{13,14},{16,17},{17,1... | collective-permute-start | bytes 1179656 | tf_op jit(solution)/shard_map/ppermute | solution.py:368
  252.8 5.0 %collective-permute-start.66 = (bf16[64,3072]{1,0:T(8,128)(2,1)S(1)}, bf16[64,3072]{1,0:T(8,128)(2,1)S(1)}, u32[]{:S(2)}, u32[]{:S(2)}) collective-permute-start(bf16[64,3072]{1,0:T(8,128)(2,1)S(1)} %get-tuple-element.238), channel_id=1, source_target_pairs={{0,1},{1,2},{4,5},{5,6},{8,9},{9,10},{12,13},{13,14},{16,17},{17,1... | collective-permute-start | bytes 1179656 | tf_op jit(solution)/shard_map/ppermute | solution.py:368
  262.0 5.0 %collective-permute-start.62 = (bf16[64,3072]{1,0:T(8,128)(2,1)S(1)}, bf16[64,3072]{1,0:T(8,128)(2,1)S(1)}, u32[]{:S(2)}, u32[]{:S(2)}) collective-permute-start(bf16[64,3072]{1,0:T(8,128)(2,1)S(1)} %get-tuple-element.230), channel_id=1, source_target_pairs={{0,1},{1,2},{2,3},{4,5},{5,6},{6,7},{8,9},{9,10},{10,11},{12,13},{... | collective-permute-start | bytes 1179656 | tf_op jit(solution)/shard_map/ppermute | solution.py:368
  270.3 5.2 %collective-permute-start.68 = (bf16[64,3072]{1,0:T(8,128)(2,1)S(1)}, bf16[64,3072]{1,0:T(8,128)(2,1)S(1)}, u32[]{:S(2)}, u32[]{:S(2)}) collective-permute-start(bf16[64,3072]{1,0:T(8,128)(2,1)S(1)} %get-tuple-element.236), channel_id=1, source_target_pairs={{0,1},{1,2},{2,3},{4,5},{5,6},{6,7},{8,9},{9,10},{10,11},{12,13},{... | collective-permute-start | bytes 1179656 | tf_op jit(solution)/shard_map/ppermute | solution.py:368
  279.2 3.9 %collective-permute-done.68 = bf16[64,3072]{1,0:T(8,128)(2,1)S(1)} collective-permute-done((bf16[64,3072]{1,0:T(8,128)(2,1)S(1)}, bf16[64,3072]{1,0:T(8,128)(2,1)S(1)}, u32[]{:S(2)}, u32[]{:S(2)}) %collective-permute-start.68) | collective-permute-done | bytes 393248 | tf_op jit(solution)/shard_map/ppermute | solution.py:368
  (206 shorter events, 100.9 us)
Async XLA Ops:
  17.2 13.8 %collective-permute-start.28 = (bf16[512,512]{1,0:T(8,128)(2,1)S(1)}, bf16[512,512]{1,0:T(8,128)(2,1)S(1)}, u32[]{:S(2)}, u32[]{:S(2)}) collective-permute-start(bf16[512,512]{1,0:T(8,128)(2,1)S(1)} %constant_dynamic-update-slice_fusion.refs_8_), channel_id=1, source_target_pairs={{0,8},{4,12},{8,0},{12,4},{1,9},{5,13},{9,1},{13,5},{2,10},{6,14},... | collective-permute-start | bytes 1572872 | tf_op jit(solution)/shard_map/ppermute | solution.py:447
  34.0 28.8 %collective-permute-start.31 = (bf16[64,1024]{1,0:T(8,128)(2,1)}, bf16[64,1024]{1,0:T(8,128)(2,1)S(1)}, u32[]{:S(2)}, u32[]{:S(2)}) collective-permute-start(bf16[64,1024]{1,0:T(8,128)(2,1)} %get-tuple-element.143), channel_id=1, source_target_pairs={{0,1},{1,2},{2,3},{3,0},{4,5},{5,6},{6,7},{7,4},{8,9},{9,10},{10,1... | collective-permute-start | bytes 393224 | tf_op jit(solution)/shard_map/ppermute | solution.py:340
  37.3 25.5 %collective-permute-start.32 = (bf16[64,1024]{1,0:T(8,128)(2,1)}, bf16[64,1024]{1,0:T(8,128)(2,1)S(1)}, u32[]{:S(2)}, u32[]{:S(2)}) collective-permute-start(bf16[64,1024]{1,0:T(8,128)(2,1)} %get-tuple-element.144), channel_id=1, source_target_pairs={{0,2},{1,3},{2,0},{3,1},{4,6},{5,7},{6,4},{7,5},{8,10},{9,11},{10,... | collective-permute-start | bytes 393224 | tf_op jit(solution)/shard_map/ppermute | solution.py:340
  37.9 25.5 %collective-permute-start.33 = (bf16[64,1024]{1,0:T(8,128)(2,1)}, bf16[64,1024]{1,0:T(8,128)(2,1)S(1)}, u32[]{:S(2)}, u32[]{:S(2)}) collective-permute-start(bf16[64,1024]{1,0:T(8,128)(2,1)} %get-tuple-element.145), channel_id=1, source_target_pairs={{0,3},{1,0},{2,1},{3,2},{4,7},{5,4},{6,5},{7,6},{8,11},{9,8},{10,9... | collective-permute-start | bytes 393224 | tf_op jit(solution)/shard_map/ppermute | solution.py:340
  68.4 13.6 %collective-permute-start.41 = (bf16[64,3072]{1,0:T(8,128)(2,1)}, bf16[64,3072]{1,0:T(8,128)(2,1)S(1)}, u32[]{:S(2)}, u32[]{:S(2)}) collective-permute-start(bf16[64,3072]{1,0:T(8,128)(2,1)} %get-tuple-element.159), channel_id=1, source_target_pairs={{3,2},{7,6},{11,10},{15,14},{19,18},{23,22},{27,26},{31,30}} | collective-permute-start | bytes 1179656 | tf_op jit(solution)/shard_map/ppermute | solution.py:369
  69.2 14.2 %collective-permute-start.40 = (bf16[64,3072]{1,0:T(8,128)(2,1)}, bf16[64,3072]{1,0:T(8,128)(2,1)S(1)}, u32[]{:S(2)}, u32[]{:S(2)}) collective-permute-start(bf16[64,3072]{1,0:T(8,128)(2,1)} %get-tuple-element.161), channel_id=1, source_target_pairs={{0,1},{4,5},{8,9},{12,13},{16,17},{20,21},{24,25},{28,29}} | collective-permute-start | bytes 1179656 | tf_op jit(solution)/shard_map/ppermute | solution.py:368
  77.0 14.7 %collective-permute-start.36 = (bf16[64,3072]{1,0:T(8,128)(2,1)S(1)}, bf16[64,3072]{1,0:T(8,128)(2,1)S(1)}, u32[]{:S(2)}, u32[]{:S(2)}) collective-permute-start(bf16[64,3072]{1,0:T(8,128)(2,1)S(1)} %get-tuple-element.268), channel_id=1, source_target_pairs={{0,1},{1,2},{4,5},{5,6},{8,9},{9,10},{12,13},{13,14},{16,17},{17,1... | collective-permute-start | bytes 1179656 | tf_op jit(solution)/shard_map/ppermute | solution.py:368
  83.5 16.8 %collective-permute-start.43 = (bf16[64,3072]{1,0:T(8,128)(2,1)S(1)}, bf16[64,3072]{1,0:T(8,128)(2,1)S(1)}, u32[]{:S(2)}, u32[]{:S(2)}) collective-permute-start(bf16[64,3072]{1,0:T(8,128)(2,1)S(1)} %get-tuple-element.269), channel_id=1, source_target_pairs={{2,1},{3,2},{6,5},{7,6},{10,9},{11,10},{14,13},{15,14},{18,17},{19... | collective-permute-start | bytes 1179656 | tf_op jit(solution)/shard_map/ppermute | solution.py:369
  84.2 16.1 %collective-permute-start.42 = (bf16[64,3072]{1,0:T(8,128)(2,1)S(1)}, bf16[64,3072]{1,0:T(8,128)(2,1)S(1)}, u32[]{:S(2)}, u32[]{:S(2)}) collective-permute-start(bf16[64,3072]{1,0:T(8,128)(2,1)S(1)} %get-tuple-element.270), channel_id=1, source_target_pairs={{0,1},{1,2},{4,5},{5,6},{8,9},{9,10},{12,13},{13,14},{16,17},{17,1... | collective-permute-start | bytes 1179656 | tf_op jit(solution)/shard_map/ppermute | solution.py:368
  100.5 14.7 %collective-permute-start.45 = (bf16[64,3072]{1,0:T(8,128)(2,1)S(1)}, bf16[64,3072]{1,0:T(8,128)(2,1)S(1)}, u32[]{:S(2)}, u32[]{:S(2)}) collective-permute-start(bf16[64,3072]{1,0:T(8,128)(2,1)S(1)} %add.275), channel_id=1, source_target_pairs={{1,0},{2,1},{3,2},{5,4},{6,5},{7,6},{9,8},{10,9},{11,10},{13,12},{... | collective-permute-start | bytes 1179656 | tf_op jit(solution)/shard_map/ppermute | solution.py:369
  102.0 15.0 %collective-permute-start.44 = (bf16[64,3072]{1,0:T(8,128)(2,1)S(1)}, bf16[64,3072]{1,0:T(8,128)(2,1)S(1)}, u32[]{:S(2)}, u32[]{:S(2)}) collective-permute-start(bf16[64,3072]{1,0:T(8,128)(2,1)S(1)} %add.274), channel_id=1, source_target_pairs={{0,1},{1,2},{2,3},{4,5},{5,6},{6,7},{8,9},{9,10},{10,11},{12,13},{... | collective-permute-start | bytes 1179656 | tf_op jit(solution)/shard_map/ppermute | solution.py:368
  118.1 22.9 %collective-permute-start.47 = (bf16[64,6144]{1,0:T(8,128)(2,1)S(1)}, bf16[64,6144]{1,0:T(8,128)(2,1)S(1)}, u32[]{:S(2)}, u32[]{:S(2)}) collective-permute-start(bf16[64,6144]{1,0:T(8,128)(2,1)S(1)} %fusion.7.refs_1_), channel_id=1, source_target_pairs={{1,0},{2,1},{3,2},{5,4},{6,5},{7,6},{9,8},{10,9},{11,10},{13,12},{... | collective-permute-start | bytes 2359304 | tf_op jit(solution)/shard_map/ppermute | solution.py:382
  119.6 23.3 %collective-permute-start.46 = (bf16[64,6144]{1,0:T(8,128)(2,1)S(1)}, bf16[64,6144]{1,0:T(8,128)(2,1)S(1)}, u32[]{:S(2)}, u32[]{:S(2)}) collective-permute-start(bf16[64,6144]{1,0:T(8,128)(2,1)S(1)} %fusion.7.refs_1_), channel_id=1, source_target_pairs={{0,1},{1,2},{2,3},{4,5},{5,6},{6,7},{8,9},{9,10},{10,11},{12,13},{... | collective-permute-start | bytes 2359304 | tf_op jit(solution)/shard_map/ppermute | solution.py:381
  144.0 13.9 %collective-permute-start.49 = (bf16[64,3072]{1,0:T(8,128)(2,1)S(1)}, bf16[64,3072]{1,0:T(8,128)(2,1)}, u32[]{:S(2)}, u32[]{:S(2)}) collective-permute-start(bf16[64,3072]{1,0:T(8,128)(2,1)S(1)} %get-tuple-element.253.refs_8_), channel_id=1, source_target_pairs={{1,0},{2,1},{3,2},{5,4},{6,5},{7,6},{9,8},{10,9},{11,10},{13,12},{... | collective-permute-start | bytes 1179656 | tf_op jit(solution)/shard_map/ppermute | solution.py:403
  145.3 14.8 %collective-permute-start.48 = (bf16[64,3072]{1,0:T(8,128)(2,1)}, bf16[64,3072]{1,0:T(8,128)(2,1)}, u32[]{:S(2)}, u32[]{:S(2)}) collective-permute-start(bf16[64,3072]{1,0:T(8,128)(2,1)} %get-tuple-element.254.refs_2_), channel_id=1, source_target_pairs={{0,1},{1,2},{2,3},{4,5},{5,6},{6,7},{8,9},{9,10},{10,11},{12,13},{... | collective-permute-start | bytes 1179656 | tf_op jit(solution)/shard_map/ppermute | solution.py:403
  151.1 17.5 %collective-permute-start.50 = (bf16[64,3072]{1,0:T(8,128)(2,1)}, bf16[64,3072]{1,0:T(8,128)(2,1)S(1)}, u32[]{:S(2)}, u32[]{:S(2)}) collective-permute-start(bf16[64,3072]{1,0:T(8,128)(2,1)} %get-tuple-element.255.refs_3_), channel_id=1, source_target_pairs={{0,1},{1,2},{2,3},{4,5},{5,6},{6,7},{8,9},{9,10},{10,11},{12,13},{... | collective-permute-start | bytes 1179656 | tf_op jit(solution)/shard_map/ppermute | solution.py:403
  154.3 14.7 %collective-permute-start.51 = (bf16[64,3072]{1,0:T(8,128)(2,1)}, bf16[64,3072]{1,0:T(8,128)(2,1)S(1)}, u32[]{:S(2)}, u32[]{:S(2)}) collective-permute-start(bf16[64,3072]{1,0:T(8,128)(2,1)} %get-tuple-element.256.refs_9_), channel_id=1, source_target_pairs={{1,0},{2,1},{3,2},{5,4},{6,5},{7,6},{9,8},{10,9},{11,10},{13,12},{... | collective-permute-start | bytes 1179656 | tf_op jit(solution)/shard_map/ppermute | solution.py:403
  161.3 16.2 %collective-permute-start.53 = (bf16[64,3072]{1,0:T(8,128)(2,1)S(1)}, bf16[64,3072]{1,0:T(8,128)(2,1)S(1)}, u32[]{:S(2)}, u32[]{:S(2)}) collective-permute-start(bf16[64,3072]{1,0:T(8,128)(2,1)S(1)} %get-tuple-element.249.refs_10_), channel_id=1, source_target_pairs={{1,0},{2,1},{3,2},{5,4},{6,5},{7,6},{9,8},{10,9},{11,10},{13,12},{... | collective-permute-start | bytes 1179656 | tf_op jit(solution)/shard_map/ppermute | solution.py:403
  162.6 14.9 %collective-permute-start.52 = (bf16[64,3072]{1,0:T(8,128)(2,1)S(1)}, bf16[64,3072]{1,0:T(8,128)(2,1)S(1)}, u32[]{:S(2)}, u32[]{:S(2)}) collective-permute-start(bf16[64,3072]{1,0:T(8,128)(2,1)S(1)} %get-tuple-element.250.refs_4_), channel_id=1, source_target_pairs={{0,1},{1,2},{2,3},{4,5},{5,6},{6,7},{8,9},{9,10},{10,11},{12,13},{... | collective-permute-start | bytes 1179656 | tf_op jit(solution)/shard_map/ppermute | solution.py:403
  169.1 15.3 %collective-permute-start.55 = (bf16[64,3072]{1,0:T(8,128)(2,1)S(1)}, bf16[64,3072]{1,0:T(8,128)(2,1)S(1)}, u32[]{:S(2)}, u32[]{:S(2)}) collective-permute-start(bf16[64,3072]{1,0:T(8,128)(2,1)S(1)} %get-tuple-element.247.refs_11_), channel_id=1, source_target_pairs={{1,0},{2,1},{3,2},{5,4},{6,5},{7,6},{9,8},{10,9},{11,10},{13,12},{... | collective-permute-start | bytes 1179656 | tf_op jit(solution)/shard_map/ppermute | solution.py:403
  170.4 14.1 %collective-permute-start.54 = (bf16[64,3072]{1,0:T(8,128)(2,1)S(1)}, bf16[64,3072]{1,0:T(8,128)(2,1)S(1)}, u32[]{:S(2)}, u32[]{:S(2)}) collective-permute-start(bf16[64,3072]{1,0:T(8,128)(2,1)S(1)} %get-tuple-element.248.refs_5_), channel_id=1, source_target_pairs={{0,1},{1,2},{2,3},{4,5},{5,6},{6,7},{8,9},{9,10},{10,11},{12,13},{... | collective-permute-start | bytes 1179656 | tf_op jit(solution)/shard_map/ppermute | solution.py:403
  184.8 27.5 %collective-permute-start.56 = (bf16[64,6144]{1,0:T(8,128)(2,1)S(1)}, bf16[64,6144]{1,0:T(8,128)(2,1)S(1)}, u32[]{:S(2)}, u32[]{:S(2)}) collective-permute-start(bf16[64,6144]{1,0:T(8,128)(2,1)S(1)} %pad_maximum_fusion.2), channel_id=1, source_target_pairs={{0,1},{1,2},{2,3},{4,5},{5,6},{6,7},{8,9},{9,10},{10,11},{12,13},{... | collective-permute-start | bytes 2359304 | tf_op jit(solution)/shard_map/ppermute | solution.py:412
  189.4 22.9 %collective-permute-start.57 = (bf16[64,6144]{1,0:T(8,128)(2,1)S(1)}, bf16[64,6144]{1,0:T(8,128)(2,1)S(1)}, u32[]{:S(2)}, u32[]{:S(2)}) collective-permute-start(bf16[64,6144]{1,0:T(8,128)(2,1)S(1)} %pad_maximum_fusion.3), channel_id=1, source_target_pairs={{1,0},{2,1},{3,2},{5,4},{6,5},{7,6},{9,8},{10,9},{11,10},{13,12},{... | collective-permute-start | bytes 2359304 | tf_op jit(solution)/shard_map/ppermute | solution.py:413
  229.5 14.1 %collective-permute-start.58 = (bf16[64,3072]{1,0:T(8,128)(2,1)S(1)}, bf16[64,3072]{1,0:T(8,128)(2,1)S(1)}, u32[]{:S(2)}, u32[]{:S(2)}) collective-permute-start(bf16[64,3072]{1,0:T(8,128)(2,1)S(1)} %get-tuple-element.234), channel_id=1, source_target_pairs={{0,1},{4,5},{8,9},{12,13},{16,17},{20,21},{24,25},{28,29}} | collective-permute-start | bytes 1179656 | tf_op jit(solution)/shard_map/ppermute | solution.py:368
  234.1 15.3 %collective-permute-start.65 = (bf16[64,3072]{1,0:T(8,128)(2,1)S(1)}, bf16[64,3072]{1,0:T(8,128)(2,1)S(1)}, u32[]{:S(2)}, u32[]{:S(2)}) collective-permute-start(bf16[64,3072]{1,0:T(8,128)(2,1)S(1)} %get-tuple-element.239), channel_id=1, source_target_pairs={{3,2},{7,6},{11,10},{15,14},{19,18},{23,22},{27,26},{31,30}} | collective-permute-start | bytes 1179656 | tf_op jit(solution)/shard_map/ppermute | solution.py:369
  234.8 17.2 %collective-permute-start.64 = (bf16[64,3072]{1,0:T(8,128)(2,1)S(1)}, bf16[64,3072]{1,0:T(8,128)(2,1)S(1)}, u32[]{:S(2)}, u32[]{:S(2)}) collective-permute-start(bf16[64,3072]{1,0:T(8,128)(2,1)S(1)} %get-tuple-element.240), channel_id=1, source_target_pairs={{0,1},{4,5},{8,9},{12,13},{16,17},{20,21},{24,25},{28,29}} | collective-permute-start | bytes 1179656 | tf_op jit(solution)/shard_map/ppermute | solution.py:368
  243.6 14.2 %collective-permute-start.61 = (bf16[64,3072]{1,0:T(8,128)(2,1)S(1)}, bf16[64,3072]{1,0:T(8,128)(2,1)S(1)}, u32[]{:S(2)}, u32[]{:S(2)}) collective-permute-start(bf16[64,3072]{1,0:T(8,128)(2,1)S(1)} %get-tuple-element.231), channel_id=1, source_target_pairs={{2,1},{3,2},{6,5},{7,6},{10,9},{11,10},{14,13},{15,14},{18,17},{19... | collective-permute-start | bytes 1179656 | tf_op jit(solution)/shard_map/ppermute | solution.py:369
  244.3 16.1 %collective-permute-start.60 = (bf16[64,3072]{1,0:T(8,128)(2,1)S(1)}, bf16[64,3072]{1,0:T(8,128)(2,1)S(1)}, u32[]{:S(2)}, u32[]{:S(2)}) collective-permute-start(bf16[64,3072]{1,0:T(8,128)(2,1)S(1)} %get-tuple-element.232), channel_id=1, source_target_pairs={{0,1},{1,2},{4,5},{5,6},{8,9},{9,10},{12,13},{13,14},{16,17},{17,1... | collective-permute-start | bytes 1179656 | tf_op jit(solution)/shard_map/ppermute | solution.py:368
  252.1 14.9 %collective-permute-start.67 = (bf16[64,3072]{1,0:T(8,128)(2,1)S(1)}, bf16[64,3072]{1,0:T(8,128)(2,1)S(1)}, u32[]{:S(2)}, u32[]{:S(2)}) collective-permute-start(bf16[64,3072]{1,0:T(8,128)(2,1)S(1)} %get-tuple-element.237), channel_id=1, source_target_pairs={{2,1},{3,2},{6,5},{7,6},{10,9},{11,10},{14,13},{15,14},{18,17},{19... | collective-permute-start | bytes 1179656 | tf_op jit(solution)/shard_map/ppermute | solution.py:369
  252.8 16.1 %collective-permute-start.66 = (bf16[64,3072]{1,0:T(8,128)(2,1)S(1)}, bf16[64,3072]{1,0:T(8,128)(2,1)S(1)}, u32[]{:S(2)}, u32[]{:S(2)}) collective-permute-start(bf16[64,3072]{1,0:T(8,128)(2,1)S(1)} %get-tuple-element.238), channel_id=1, source_target_pairs={{0,1},{1,2},{4,5},{5,6},{8,9},{9,10},{12,13},{13,14},{16,17},{17,1... | collective-permute-start | bytes 1179656 | tf_op jit(solution)/shard_map/ppermute | solution.py:368
  260.5 17.1 %collective-permute-start.63 = (bf16[64,3072]{1,0:T(8,128)(2,1)S(1)}, bf16[64,3072]{1,0:T(8,128)(2,1)S(1)}, u32[]{:S(2)}, u32[]{:S(2)}) collective-permute-start(bf16[64,3072]{1,0:T(8,128)(2,1)S(1)} %get-tuple-element.229), channel_id=1, source_target_pairs={{1,0},{2,1},{3,2},{5,4},{6,5},{7,6},{9,8},{10,9},{11,10},{13,12},{... | collective-permute-start | bytes 1179656 | tf_op jit(solution)/shard_map/ppermute | solution.py:369
  262.0 15.6 %collective-permute-start.62 = (bf16[64,3072]{1,0:T(8,128)(2,1)S(1)}, bf16[64,3072]{1,0:T(8,128)(2,1)S(1)}, u32[]{:S(2)}, u32[]{:S(2)}) collective-permute-start(bf16[64,3072]{1,0:T(8,128)(2,1)S(1)} %get-tuple-element.230), channel_id=1, source_target_pairs={{0,1},{1,2},{2,3},{4,5},{5,6},{6,7},{8,9},{9,10},{10,11},{12,13},{... | collective-permute-start | bytes 1179656 | tf_op jit(solution)/shard_map/ppermute | solution.py:368
  (56 other events, 708.9 us)
where the time goes:
time: 286 us; the launch traced here: 288 us
  starting transfers between devices  118 us (41%)
  Pallas kernels  71.7 us (25%)
  waiting for transfers between devices  66.5 us (23%)
  local copies, waits for them, and re-layouts  14.7 us (5%)
  other arithmetic  10 us (3%)
  matrix products  4.49 us (2%)
    ppermute x12, starting transfers between devices, reduce_line(): right = lax.ppermute(sent[0], 'tp', rights(s))  50.1 us
    ppermute x12, waiting for transfers between devices, reduce_line(): right = lax.ppermute(sent[0], 'tp', rights(s))  29.6 us
    pallas_call x6, Pallas kernels, product(): pl.pallas_call(functools.partial(resident_product_kernel, cut) if residen...  26.9 us
    pallas_call x1, Pallas kernels, hidden_units(): pl.pallas_call(functools.partial(hidden_kernel, [len(source) for source i...  21.4 us
    pallas_call x2, Pallas kernels, attend(): pl.pallas_call(kernel, grid_spec=pltpu.PrefetchScalarGridSpec(num_scalar_...  18.7 us
    ppermute x4, starting transfers between devices, gather_line(): lax.ppermute(right, 'tp', to_right)  18.6 us
    ppermute x9, starting transfers between devices, shift(): lax.ppermute(parts[s], 'tp', moves[s])  17.7 us
    ppermute x4, waiting for transfers between devices, gather_line(): lax.ppermute(left, 'tp', to_left)  12 us
  transfers between devices with their start and end apart: 48, of which 23 were waited for; matrix products, arithmetic and copies ran while one was open for 5% of the time, Pallas kernels for 19%

commit v1 on v0

--- a/solution.py
+++ b/solution.py
@@ -20,24 +20,29 @@
 VMEM_LARGE = 40 * 1024 * 1024
 
 
-def attention_kernel(slots, together, held, pairs, sharing, block_rows, *refs):
+def attention_kernel(slots, together, held, pairs, sharing, block_rows, plan, *refs):
+    pieces, grouped = plan
     (order, mine), refs = refs[:2], refs[2:]
     query_refs, refs = refs[:slots], refs[slots:]
     place_ref, key_place_ref, refs = refs[0], refs[1], refs[2:]
-    pair_refs, refs = refs[: len(held)], refs[len(held) :]
-    out_ref, query_ref, key_ref, value_ref, top_ref, total_ref = refs
-    half = out_ref.shape[1]
+    pair_refs, weight, refs = refs[: len(held)], refs[len(held)], refs[len(held) + 1 :]
+    outs, refs = refs[: pieces * (slots if grouped else 1)], refs[pieces * (slots if grouped else 1) :]
+    query_ref, key_ref, value_ref, top_ref, total_ref, head_ref, weight_ref, arrived = refs
+    half = query_refs[0].shape[0]
+    step = pl.program_id(0)
     me = mine[0]
     my_block = order[me]
     blocks = [(ref, index, offset) for ref, group in zip(pair_refs, held) for index, offset in enumerate(group)]
-
-    @pl.when(pl.program_id(0) == 0)
+    weight_copy = pltpu.make_async_copy(weight, weight_ref, arrived)
+
+    @pl.when(step == 0)
     def _():
+        weight_copy.start()
         value_ref[:, :, HD:, :] = jnp.ones((len(blocks), pairs, SUM_ROWS, block_rows), jnp.bfloat16)
 
     for at, (ref, index, offset) in enumerate(blocks):
 
-        @pl.when((pl.program_id(0) == 0) & (order[me ^ offset] <= my_block))
+        @pl.when((step == 0) & (order[me ^ offset] <= my_block))
         def _():
             for p in range(pairs):
                 rows = slice(index * block_rows, (index + 1) * block_rows)
@@ -46,7 +51,7 @@
 
     for at in range(slots):
 
-        @pl.when(pl.program_id(0) == at // together)
+        @pl.when(step == at // together)
         def _():
             for p in range(pairs):
                 for g in range(sharing):
@@ -93,62 +98,106 @@
             for g in range(sharing):
                 column = (p * sharing + g) * HD
                 row = (i * sharing + g) * half
-                out_ref[i, :, column : column + HD] = mixed[row : row + half]
-
-
-def attend(order, mine, queries, places, key_places, pair_list, held, pairs, sharing, block_rows):
+                at = pl.multiple_of((step * together + i) * half, half)
+                head_ref[pl.ds(at, half), column : column + HD] = mixed[row : row + half]
+
+    @pl.when(step == pl.num_programs(0) - 1)
+    def _():
+        weight_copy.wait()
+        width = weight.shape[1] // pieces
+        tile = 2 * TILE
+        for c in range(pieces):
+
+            @pl.loop(0, width // tile)
+            def _(n):
+                columns = pl.ds(pl.multiple_of(c * width + n * tile, tile), tile)
+                value = jnp.dot(head_ref[...], weight_ref[:, columns], preferred_element_type=jnp.float32)
+                share_out(outs[c * len(outs) // pieces :], pl.ds(pl.multiple_of(n * tile, tile), tile), value)
+
+
+def share_out(outs, columns, value):
+    rows = outs[0].shape[0]
+    for g in range(value.shape[0] // rows):
+        outs[g][:, columns] = value[g * rows : (g + 1) * rows].astype(jnp.bfloat16)
+
+
+def piece_shapes(rows, width, slots, pieces, grouped):
+    return [jax.ShapeDtypeStruct((rows // slots if grouped else rows, width // pieces), jnp.bfloat16)] * (
+        pieces * (slots if grouped else 1)
+    )
+
+
+def by_piece(outs, slots, pieces, grouped):
+    if grouped:
+        return [outs[c * slots : (c + 1) * slots] for c in range(pieces)]
+    return [[out[s * (out.shape[0] // slots) : (s + 1) * (out.shape[0] // slots)] for s in range(slots)] for out in outs]
+
+
+def attend(order, mine, queries, places, key_places, pair_list, held, pairs, sharing, block_rows, weight, pieces, grouped):
     slots = len(queries)
     half, width = queries[0].shape
     together = 2 if slots <= LINE else 1
     tall = together * sharing * half
     blocks = sum(len(group) for group in held)
     count = blocks * block_rows
-    kernel = functools.partial(attention_kernel, slots, together, held, pairs, sharing, block_rows)
-    whole = [pl.BlockSpec(memory_space=pltpu.VMEM) for _ in pair_list]
-    return pl.pallas_call(
+    shapes = piece_shapes(slots * half, weight.shape[1], slots, pieces, grouped)
+    kernel = functools.partial(
+        attention_kernel, slots, together, held, pairs, sharing, block_rows, (pieces, grouped)
+    )
+    in_place = pl.BlockSpec(memory_space=pltpu.VMEM)
+    outs = pl.pallas_call(
         kernel,
         grid_spec=pltpu.PrefetchScalarGridSpec(
             num_scalar_prefetch=2,
             grid=(slots // together,),
-            in_specs=[pl.BlockSpec((half, width), lambda s, *_: (0, 0))] * slots
+            in_specs=[in_place] * slots
             + [
                 pl.BlockSpec((together, 1, half), lambda s, *_: (s, 0, 0)),
                 pl.BlockSpec((block_rows, 1), lambda s, *_: (0, 0)),
             ]
-            + whole,
-            out_specs=pl.BlockSpec((together, half, width), lambda s, *_: (s, 0, 0)),
+            + [in_place] * len(pair_list)
+            + [pl.BlockSpec(memory_space=pl.ANY)],
+            out_specs=[in_place] * len(shapes),
             scratch_shapes=[
                 pltpu.VMEM((pairs, tall, HD), jnp.bfloat16),
                 pltpu.VMEM((blocks, pairs, block_rows, HD), jnp.bfloat16),
                 pltpu.VMEM((blocks, pairs, HD + SUM_ROWS, block_rows), jnp.bfloat16),
                 pltpu.VMEM((pairs, 8, tall), jnp.float32),
                 pltpu.VMEM((pairs, HD + SUM_ROWS, tall), jnp.float32),
+                pltpu.VMEM((slots * half, width), jnp.bfloat16),
+                pltpu.VMEM(weight.shape, weight.dtype),
+                pltpu.SemaphoreType.DMA,
             ],
         ),
-        out_shape=jax.ShapeDtypeStruct((slots, half, width), jnp.bfloat16),
-        compiler_params=pltpu.CompilerParams(vmem_limit_bytes=12 * 1024 * 1024),
+        out_shape=shapes,
+        compiler_params=pltpu.CompilerParams(vmem_limit_bytes=VMEM_LARGE),
         cost_estimate=pl.CostEstimate(
             flops=40 * slots * half * width * count,
-            bytes_accessed=2 * (2 * slots * half * width + count * 2 * pairs * HD),
+            bytes_accessed=2 * (2 * slots * half * width + count * 2 * pairs * HD + weight.size),
             transcendentals=slots * half * width // HD * count,
         ),
-    )(order, mine, *queries, places, key_places, *pair_list)
-
-
-def hidden_kernel(plan, *refs):
+    )(order, mine, *queries, places, key_places, *pair_list, weight)
+    return by_piece(outs, slots, pieces, grouped)
+
+
+def expert_kernel(plan, pieces, *refs):
     mine, refs = refs[0], refs[1:]
     sources = []
     for count in plan:
         sources.append(refs[:count])
         refs = refs[count:]
-    gate_weight, up_weight, out, chosen = refs
+    gate_weight, up_weight, down_weight, refs = refs[0], refs[1], refs[2], refs[3:]
+    outs, (chosen, acts) = refs[:-2], refs[-2:]
+    step = pl.program_id(0)
+    tile = gate_weight.shape[1]
+    first = acts.shape[1] // tile
 
     def place(s, source):
         rows, width = source[0].shape
         for c, ref in enumerate(source):
             chosen[s * rows : (s + 1) * rows, c * width : (c + 1) * width] = ref[...]
 
-    @pl.when(pl.program_id(0) == 0)
+    @pl.when(step == 0)
     def _():
         place(0, sources[0])
         for s in range(1, (len(plan) + 1) // 2):
@@ -162,63 +211,52 @@
             def _():
                 place(s, left)
 
-    gate = jnp.dot(chosen[...], gate_weight[...], preferred_element_type=jnp.float32)
-    upward = jnp.dot(chosen[...], up_weight[...], preferred_element_type=jnp.float32)
-    out[...] = (gate / (1.0 + jnp.exp(-gate)) * upward).astype(jnp.bfloat16)
-
-
-def hidden_units(mine, sources, gate_weight, up_weight):
+    @pl.when(step < first)
+    def _():
+        gate = jnp.dot(chosen[...], gate_weight[...], preferred_element_type=jnp.float32)
+        upward = jnp.dot(chosen[...], up_weight[...], preferred_element_type=jnp.float32)
+        columns = pl.ds(pl.multiple_of(step * tile, tile), tile)
+        acts[:, columns] = (gate / (1.0 + jnp.exp(-gate)) * upward).astype(jnp.bfloat16)
+
+    @pl.when(step >= first)
+    def _():
+        value = jnp.dot(acts[...], down_weight[...], preferred_element_type=jnp.float32)
+        strip = down_weight.shape[1]
+        strips = outs[0].shape[1] // strip
+        for c in range(pieces):
+
+            @pl.when((step - first) // strips == c)
+            def _():
+                columns = pl.ds(pl.multiple_of((step - first - c * strips) * strip, strip), strip)
+                share_out(outs[c * len(outs) // pieces :], columns, value)
+
+
+def expert_rows(mine, sources, gate_weight, up_weight, down_weight, slots, pieces, grouped):
     flat = [piece for source in sources for piece in source]
     rows = flat[0].shape[0] * ((len(sources) + 1) // 2)
     depth, width = gate_weight.shape
-    tile = min(TILE, width)
-    weight = pl.BlockSpec((depth, tile), lambda n, *_: (0, n))
-    return pl.pallas_call(
-        functools.partial(hidden_kernel, [len(source) for source in sources]),
+    tile, strip = min(TILE, width), 2 * TILE
+    first = width // tile
+    shapes = piece_shapes(rows, depth, slots, pieces, grouped)
+    in_place = pl.BlockSpec(memory_space=pltpu.VMEM)
+    weight = pl.BlockSpec((depth, tile), lambda n, *_: (0, jnp.minimum(n, first - 1)))
+    outs = pl.pallas_call(
+        functools.partial(expert_kernel, [len(source) for source in sources], pieces),
         grid_spec=pltpu.PrefetchScalarGridSpec(
             num_scalar_prefetch=1,
-            grid=(width // tile,),
-            in_specs=[pl.BlockSpec(memory_space=pltpu.VMEM)] * len(flat) + [weight, weight],
-            out_specs=pl.BlockSpec((rows, tile), lambda n, *_: (0, n)),
-            scratch_shapes=[pltpu.VMEM((rows, depth), jnp.bfloat16)],
+            grid=(first + depth // strip,),
+            in_specs=[in_place] * len(flat)
+            + [weight, weight, pl.BlockSpec((width, strip), lambda n, *_: (0, jnp.maximum(n - first, 0)))],
+            out_specs=[in_place] * len(shapes),
+            scratch_shapes=[pltpu.VMEM((rows, depth), jnp.bfloat16), pltpu.VMEM((rows, width), jnp.bfloat16)],
         ),
-        out_shape=jax.ShapeDtypeStruct((rows, width), jnp.bfloat16),
+        out_shape=shapes,
         compiler_params=pltpu.CompilerParams(vmem_limit_bytes=VMEM_LARGE),
         cost_estimate=pl.CostEstimate(
-            flops=4 * rows * depth * width, bytes_accessed=4 * depth * width, transcendentals=rows * width
+            flops=6 * rows * depth * width, bytes_accessed=6 * depth * width, transcendentals=rows * width
         ),
-    )(mine, *flat, gate_weight, up_weight)
-
-
-def product_kernel(left_ref, weight, out_ref):
-    out_ref[...] = jnp.dot(left_ref[...], weight[...], preferred_element_type=jnp.float32).astype(jnp.bfloat16)
-
-
-def resident_product_kernel(cut, left_ref, weight, out_ref):
-    tile = out_ref.shape[1]
-    columns = pl.ds(pl.multiple_of((cut * pl.num_programs(0) + pl.program_id(0)) * tile, tile), tile)
-    out_ref[...] = jnp.dot(left_ref[...], weight[:, columns], preferred_element_type=jnp.float32).astype(
-        jnp.bfloat16
-    )
-
-
-def product(left, weight, cut, pieces, resident=False):
-    rows, depth = left.shape
-    width = weight.shape[1] // pieces
-    tile = 2 * TILE
-    in_place = pl.BlockSpec(memory_space=pltpu.VMEM)
-    streamed = pl.BlockSpec((depth, tile), lambda n: (0, cut * (width // tile) + n))
-    return pl.pallas_call(
-        functools.partial(resident_product_kernel, cut) if resident else product_kernel,
-        grid=(width // tile,),
-        in_specs=[in_place, in_place if resident else streamed],
-        out_specs=pl.BlockSpec((rows, tile), lambda n: (0, n)),
-        out_shape=jax.ShapeDtypeStruct((rows, width), jnp.bfloat16),
-        compiler_params=pltpu.CompilerParams(vmem_limit_bytes=VMEM_HELD if resident else VMEM_SMALL),
-        cost_estimate=pl.CostEstimate(
-            flops=2 * rows * depth * width, bytes_accessed=2 * depth * width, transcendentals=0
-        ),
-    )(left, weight)
+    )(mine, *flat, gate_weight, up_weight, down_weight)
+    return by_piece(outs, slots, pieces, grouped)
 
 
 def pack_pairs_kernel(shards, mine, keys_ref, values_ref, *outs):
@@ -245,11 +283,13 @@
     )(mine, keys, values)
 
 
-def pack_queries_kernel(shards, halves, mine, picked_ref, query_ref, *outs):
+def pack_queries_kernel(slots, halves, mine, picked_ref, query_ref, *outs):
+    shards = len(slots)
     rows = query_ref.shape[0]
     half = rows // halves
     width = query_ref.shape[1] // shards
-    packed, (order_ref, places_ref, count_ref) = outs[: halves * shards], outs[halves * shards :]
+    packed, outs = outs[: halves * shards], outs[halves * shards :]
+    place_refs, (order_ref, count_ref) = outs[:halves], outs[halves:]
     me = mine[0]
     across = lax.broadcasted_iota(jnp.int32, (rows, rows), 1)
     down = lax.broadcasted_iota(jnp.int32, (rows, rows), 0)
@@ -268,7 +308,9 @@
             mine_slot = jnp.where(shard == other, slot[other : other + 1], mine_slot)
         at_slot = jnp.where(mine_slot == down, 1.0, 0.0).astype(jnp.bfloat16)
         rows_at = lax.dot_general(ids, at_slot, (((1,), (1,)), ((), ())), preferred_element_type=jnp.float32)
-        places_ref[s] = rows_at[0:1].astype(jnp.int32) + shard * rows
+        for h in range(halves):
+            here = rows_at[0:1, h * half : (h + 1) * half]
+            place_refs[h][slots.index(s)] = here.astype(jnp.int32) + shard * rows
         if s == 0:
             order_ref[...] = at_slot
     for s in range(shards):
@@ -279,20 +321,19 @@
             packed[h * shards + s][...] = ordered[h * half : (h + 1) * half]
 
 
-def pack_queries(mine, picked, queries, shards, halves):
+def pack_queries(mine, picked, queries, slots, halves):
+    shards = len(slots)
     rows, width = queries.shape
     packed = (rows // halves, width // shards)
-    shapes = [jax.ShapeDtypeStruct(packed, jnp.bfloat16)] * (halves * shards) + [
-        jax.ShapeDtypeStruct((rows, rows), jnp.bfloat16),
-        jax.ShapeDtypeStruct((shards, 1, rows), jnp.int32),
-        jax.ShapeDtypeStruct((8, 128), jnp.float32),
-    ]
+    shapes = [jax.ShapeDtypeStruct(packed, jnp.bfloat16)] * (halves * shards)
+    shapes += [jax.ShapeDtypeStruct((shards, 1, rows // halves), jnp.int32)] * halves
+    shapes += [jax.ShapeDtypeStruct((rows, rows), jnp.bfloat16), jax.ShapeDtypeStruct((8, 128), jnp.float32)]
 
     def whole(shape):
         return pl.BlockSpec(shape, lambda k, *_: (0,) * len(shape))
 
     got = pl.pallas_call(
-        functools.partial(pack_queries_kernel, shards, halves),
+        functools.partial(pack_queries_kernel, slots, halves),
         grid_spec=pltpu.PrefetchScalarGridSpec(
             num_scalar_prefetch=1,
             grid=(1,),
@@ -301,7 +342,8 @@
         ),
         out_shape=shapes,
     )(mine, picked, queries)
-    return [got[h * shards : (h + 1) * shards] for h in range(halves)], *got[halves * shards :]
+    packed, got = got[: halves * shards], got[halves * shards :]
+    return [packed[h * shards : (h + 1) * shards] for h in range(halves)], got[:halves], *got[halves:]
 
 
 def on_device(
@@ -333,6 +375,7 @@
     line = shards <= LINE
     pieces = 2 if line else 1
     cuts = [slice(c * (model // pieces), (c + 1) * (model // pieces)) for c in range(pieces)]
+    slots = [s for s in range(1, shards, 2)] + [s for s in range(2, shards, 2)] + [0]
     shard_of = lax.rem(me - jnp.arange(shards, dtype=jnp.int32) + shards, shards)
 
     def shift(parts):
@@ -420,8 +463,8 @@
         sent_pairs = pack_pairs(me[None], keys, values, shards)
         own_pairs = jnp.concatenate(shift(sent_pairs), axis=0)
         picked, _ = lax.optimization_barrier((picked.astype(jnp.int32), sent_pairs))
-        packed, order, places, fullest = pack_queries(me[None], picked, queries, shards, halves)
-        asked = [shift(packed[h]) for h in range(halves)]
+        packed, places, order, fullest = pack_queries(me[None], picked, queries, slots, halves)
+        asked = [shift(packed[0])]
     else:
 
         def spread(source):
@@ -436,7 +479,7 @@
         at_slot = slot[:, None, :] == row_ids[None, :, None]
         row_of_slot = jnp.sum(jnp.where(at_slot, row_ids[None, None, :], 0), axis=2)
         places = row_of_slot + jnp.arange(shards, dtype=jnp.int32)[:, None] * rows
-        places = jnp.take(places, shard_of, axis=0)[:, None, :]
+        places = [jnp.stack([jnp.take(places, shard_of[s], axis=0) for s in slots])[:, None, :]]
         order = lax.dynamic_index_in_dim(at_slot, me, 0, keepdims=False).astype(jnp.bfloat16)
         ordered = jnp.dot(order, queries, preferred_element_type=jnp.float32).astype(jnp.bfloat16)
         asked = [exchange(ordered.reshape(rows, shards, per_device * HD))]
@@ -459,26 +502,24 @@
 
     mine = lax.axis_index("ctx").astype(jnp.int32)[None]
     expert_ids = jnp.arange(router_weight.shape[1], dtype=jnp.int32)
-    slots = [s for s in range(1, shards, 2)] + [s for s in range(2, shards, 2)] + [0]
 
     def project(which):
-        heads = attend(
+        terms = attend(
             block_order,
-            mine,
+            lax.axis_index("ctx").astype(jnp.int32)[None],
             [asked[which][s] for s in slots],
-            jnp.stack([places[s, :, which * half : (which + 1) * half] for s in slots]),
+            places[which],
             key_places,
             pair_list,
             held,
             pairs,
             sharing,
             block_rows,
-        ).reshape(shards * half, per_device * HD)
-        terms = []
-        for c in range(pieces):
-            term = product(heads, out_weight, c, pieces, True)
-            terms.append([term[slots.index(s) * half : (slots.index(s) + 1) * half] for s in range(shards)])
-        return terms
+            out_weight,
+            pieces,
+            line,
+        )
+        return [[term[slots.index(s)] for s in range(shards)] for term in terms]
 
     def finish(which, head_sums):
         base = hidden[which * half : (which + 1) * half].astype(jnp.float32)
@@ -491,10 +532,6 @@
         return (
             widened * lax.rsqrt(jnp.mean(widened * widened, axis=1, keepdims=True) + 1e-05) * norm_gain
         ).astype(jnp.bfloat16)
-
-    def activate(normed, terms=None):
-        sources, total = gather_line(normed, terms)
-        return hidden_units(me[None], sources, gate_weight, up_weight), total
 
     def share_of(which, normed):
         logits = jnp.dot(normed, router_weight, preferred_element_type=jnp.float32)
@@ -504,20 +541,24 @@
         share = jnp.where(named[:, 0] == 0, 1.0 / (1.0 + jnp.exp(second - first)), 0.0)
         return share + jnp.where(named[:, 1] == 0, 1.0 / (1.0 + jnp.exp(first - second)), 0.0)
 
-    def deliver(which, acts, normed):
-        terms = [product(acts, down_weight, c, pieces).reshape(shards, half, -1) for c in range(pieces)]
-        sums, marks = reduce_line([[term[s] for s in range(shards)] for term in terms])
+    def expert(which, normed, sources, beside=None):
+        terms = expert_rows(me[None], sources, gate_weight, up_weight, down_weight, shards, pieces, line)
+        if beside is not None:
+            terms, beside = lax.optimization_barrier((terms, beside))
+        sums, marks = reduce_line(terms)
         if line:
             normed, _ = lax.optimization_barrier((normed, marks[0]))
         share = share_of(which, normed)
-        return jnp.concatenate([(total * share[:, None]).astype(jnp.bfloat16) for total in sums], axis=1)
+        parts = [(total * share[:, None]).astype(jnp.bfloat16) for total in sums]
+        return jnp.concatenate(parts, axis=1), beside
 
     def late_expert(source):
         normed = normalise(source)
-        return deliver(1, activate(normed)[0], normed)
+        return expert(1, normed, gather_line(normed)[0])[0]
 
     terms = project(0)
     if halves > 1:
+        asked.append(shift(packed[1]))
         terms, asked[1] = lax.optimization_barrier((terms, asked[1]))
     totals, marks = reduce_line(terms)
     if line:
@@ -528,12 +569,11 @@
     first_half = finish(0, totals)
     normed = normalise(first_half)
     if halves == 1:
-        return (restore([first_half]), restore([deliver(0, activate(normed)[0], normed)]))
+        return (restore([first_half]), restore([expert(0, normed, gather_line(normed)[0])[0]]))
     asked[1], _ = lax.optimization_barrier((asked[1], normed))
-    acts, second_sum = activate(normed, project(1))
+    sources, second_sum = gather_line(normed, project(1))
     second_half = (hidden[half:].astype(jnp.float32) + second_sum).astype(jnp.bfloat16)
-    acts, second_half = lax.optimization_barrier((acts, second_half))
-    part = deliver(0, acts, normed)
+    part, second_half = expert(0, normed, sources, second_half)
     part, late, fullest = lax.optimization_barrier((part, second_half, fullest))
     late = lax.cond(fullest[0, 0] > half, late_expert, jnp.zeros_like, late)
     return (restore([first_half, second_half]), restore([part, late]))

time: 286 us -> 305 us (1.066); the launches traced: 288 us -> 303 us
  waiting for transfers between devices: 66.5 us -> 78.4 us
  starting transfers between devices: 118 us -> 111 us
  other arithmetic: 10 us -> 14.8 us
  Pallas kernels: 71.7 us -> 75.9 us
    pallas_call x2, Pallas kernels: 18.7 us -> 33.9 us  [attend(): pl.pallas_call(kernel, grid_spec=pltpu.PrefetchScalarGridSpec(num_scalar_...]
    ppermute x9, waiting for transfers between devices: 6.59 us -> 18.9 us  [shift(): lax.ppermute(parts[s], 'tp', moves[s])]
    pallas_call x8 -> x2, Pallas kernels: 51.1 us -> 40 us  [the longest x1 37.3 us: expert_rows(): pl.pallas_call(functools.partial(expert_kernel, [len(source) for source i...]
    ppermute x3, waiting for transfers between devices: 4 us -> 12.3 us  [on_device(): lax.ppermute(part, 'ctx', [(i, i ^ offset) for i in range(blocks)])]
    add x10 -> x12, other arithmetic: 4.08 us -> 10.1 us  [reduce_line(): sent = (terms[s] + arrived[0], terms[shards - s] + arrived[1])]
    ppermute x12, waiting for transfers between devices: 29.6 us -> 25 us  [reduce_line(): right = lax.ppermute(sent[0], 'tp', rights(s))]
    ppermute x12, waiting for transfers between devices: 8.3 us -> 3.97 us  [reduce_line(): left = lax.ppermute(sent[1], 'tp', lefts(s))]
    unnamed x83 -> x119, local copies, waits for them, and re-layouts: 10.1 us -> 13.4 us
  transfers between devices with their start and end apart: 48 -> 48, of which waited for: 23 -> 20; matrix products, arithmetic and copies ran while one was open for 5% -> 6% of each run, Pallas kernels for 19% -> 24%
where the time goes in v1:
time: 305 us; the launch traced here: 303 us
  starting transfers between devices  111 us (36%)
  waiting for transfers between devices  78.4 us (26%)
  Pallas kernels  75.9 us (25%)
  local copies, waits for them, and re-layouts  15.5 us (5%)
  other arithmetic  14.8 us (5%)
  matrix products  5.29 us (2%)
    ppermute x12, starting transfers between devices, reduce_line(): right = lax.ppermute(sent[0], 'tp', rights(s))  48.5 us
    pallas_call x1, Pallas kernels, expert_rows(): pl.pallas_call(functools.partial(expert_kernel, [len(source) for source i...  37.3 us
    pallas_call x2, Pallas kernels, attend(): pl.pallas_call(kernel, grid_spec=pltpu.PrefetchScalarGridSpec(num_scalar_...  33.9 us
    ppermute x12, waiting for transfers between devices, reduce_line(): right = lax.ppermute(sent[0], 'tp', rights(s))  25 us
    ppermute x9, waiting for transfers between devices, shift(): lax.ppermute(parts[s], 'tp', moves[s])  18.9 us
    ppermute x4, starting transfers between devices, gather_line(): lax.ppermute(right, 'tp', to_right)  18.1 us
    ppermute x9, starting transfers between devices, shift(): lax.ppermute(parts[s], 'tp', moves[s])  14.4 us
    unnamed x119, local copies, waits for them, and re-layouts  13.4 us
  transfers between devices with their start and end apart: 48, of which 20 were waited for; matrix products, arithmetic and copies ran while one was open for 6% of the time, Pallas kernels for 24%

profile of v1, /device:TPU:0, one launch (start us, length us, event | category | flops | bytes accessed | tf_op | source)
XLA Modules:
  0.0 303.2 jit_solution(18325015068573912835)
XLA Ops:
  2.7 3.0 collective-permute-start.25
  12.4 4.8 %collective-permute-done.26 = bf16[128,512]{1,0:T(8,128)(2,1)S(1)} collective-permute-done((bf16[128,512]{1,0:T(8,128)(2,1)}, bf16[128,512]{1,0:T(8,128)(2,1)S(1)}, u32[]{:S(2)}, u32[]{:S(2)}) %collective-permute-start.26) | collective-permute-done | bytes 131104 | tf_op jit(solution)/shard_map/ppermute | solution.py:383
  18.7 12.3 %collective-permute-done.28.refs_9_ = bf16[512,512]{1,0:T(8,128)(2,1)S(1)} collective-permute-done((bf16[512,512]{1,0:T(8,128)(2,1)S(1)}, bf16[512,512]{1,0:T(8,128)(2,1)S(1)}, u32[]{:S(2)}, u32[]{:S(2)}) %collective-permute-start.28) | collective-permute-done | bytes 524320 | tf_op jit(solution)/shard_map/ppermute | solution.py:490
  31.7 2.7 shard_map.132
  34.4 3.4 %collective-permute-start.22 = (bf16[64,1024]{1,0:T(8,128)(2,1)}, bf16[64,1024]{1,0:T(8,128)(2,1)S(1)}, u32[]{:S(2)}, u32[]{:S(2)}) collective-permute-start(bf16[64,1024]{1,0:T(8,128)(2,1)} %get-tuple-element.177), channel_id=1, source_target_pairs={{0,1},{1,2},{2,3},{3,0},{4,5},{5,6},{6,7},{7,4},{8,9},{9,10},{10,1... | collective-permute-start | bytes 393224 | tf_op jit(solution)/shard_map/ppermute | solution.py:383
  46.7 9.6 %collective-permute-done.24.refs_4_ = bf16[64,1024]{1,0:T(8,128)(2,1)S(1)} collective-permute-done((bf16[64,1024]{1,0:T(8,128)(2,1)}, bf16[64,1024]{1,0:T(8,128)(2,1)S(1)}, u32[]{:S(2)}, u32[]{:S(2)}) %collective-permute-start.24) | collective-permute-done | bytes 131104 | tf_op jit(solution)/shard_map/ppermute | solution.py:383
  66.2 16.9 %shard_map.133 = (bf16[64,3072]{1,0:T(8,128)(2,1)S(1)}, bf16[64,3072]{1,0:T(8,128)(2,1)S(1)}, bf16[64,3072]{1,0:T(8,128)(2,1)S(1)}, bf16[64,3072]{1,0:T(8,128)(2...) custom-call(s32[4]{0:T(128)S(1)} %copy-done.45, ...), custom_call_target="tpu_custom_call" | custom-call | flops 21474836480 | bytes 15728640 | tf_op jit(solution)/shard_map/pallas_call | solution.py:148
  83.2 4.0 %collective-permute-start.40 = (bf16[64,3072]{1,0:T(8,128)(2,1)S(1)}, bf16[64,3072]{1,0:T(8,128)(2,1)S(1)}, u32[]{:S(2)}, u32[]{:S(2)}) collective-permute-start(bf16[64,3072]{1,0:T(8,128)(2,1)S(1)} %get-tuple-element.209), channel_id=1, source_target_pairs={{0,1},{4,5},{8,9},{12,13},{16,17},{20,21},{24,25},{28,29}} | collective-permute-start | bytes 1179656 | tf_op jit(solution)/shard_map/ppermute | solution.py:411
  89.8 6.8 %collective-permute-done.40 = bf16[64,3072]{1,0:T(8,128)(2,1)S(1)} collective-permute-done((bf16[64,3072]{1,0:T(8,128)(2,1)S(1)}, bf16[64,3072]{1,0:T(8,128)(2,1)S(1)}, u32[]{:S(2)}, u32[]{:S(2)}) %collective-permute-start.40) | collective-permute-done | bytes 393248 | tf_op jit(solution)/shard_map/ppermute | solution.py:411
  97.6 5.1 %collective-permute-start.42 = (bf16[64,3072]{1,0:T(8,128)(2,1)}, bf16[64,3072]{1,0:T(8,128)(2,1)}, u32[]{:S(2)}, u32[]{:S(2)}) collective-permute-start(bf16[64,3072]{1,0:T(8,128)(2,1)} %get-tuple-element.310), channel_id=1, source_target_pairs={{0,1},{1,2},{4,5},{5,6},{8,9},{9,10},{12,13},{13,14},{16,17},{17,1... | collective-permute-start | bytes 1179656 | tf_op jit(solution)/shard_map/ppermute | solution.py:411
  106.1 5.1 %collective-permute-start.36 = (bf16[64,3072]{1,0:T(8,128)(2,1)}, bf16[64,3072]{1,0:T(8,128)(2,1)}, u32[]{:S(2)}, u32[]{:S(2)}) collective-permute-start(bf16[64,3072]{1,0:T(8,128)(2,1)} %get-tuple-element.308), channel_id=1, source_target_pairs={{0,1},{1,2},{4,5},{5,6},{8,9},{9,10},{12,13},{13,14},{16,17},{17,1... | collective-permute-start | bytes 1179656 | tf_op jit(solution)/shard_map/ppermute | solution.py:411
  117.8 4.6 %collective-permute-start.44 = (bf16[64,3072]{1,0:T(8,128)(2,1)S(1)}, bf16[64,3072]{1,0:T(8,128)(2,1)S(1)}, u32[]{:S(2)}, u32[]{:S(2)}) collective-permute-start(bf16[64,3072]{1,0:T(8,128)(2,1)S(1)} %add.274), channel_id=1, source_target_pairs={{0,1},{1,2},{2,3},{4,5},{5,6},{6,7},{8,9},{9,10},{10,11},{12,13},{... | collective-permute-start | bytes 1179656 | tf_op jit(solution)/shard_map/ppermute | solution.py:411
  125.9 4.6 %collective-permute-start.38 = (bf16[64,3072]{1,0:T(8,128)(2,1)S(1)}, bf16[64,3072]{1,0:T(8,128)(2,1)S(1)}, u32[]{:S(2)}, u32[]{:S(2)}) collective-permute-start(bf16[64,3072]{1,0:T(8,128)(2,1)S(1)} %add.267), channel_id=1, source_target_pairs={{0,1},{1,2},{2,3},{4,5},{5,6},{6,7},{8,9},{9,10},{10,11},{12,13},{... | collective-permute-start | bytes 1179656 | tf_op jit(solution)/shard_map/ppermute | solution.py:411
  133.2 6.7 %collective-permute-done.38 = bf16[64,3072]{1,0:T(8,128)(2,1)S(1)} collective-permute-done((bf16[64,3072]{1,0:T(8,128)(2,1)S(1)}, bf16[64,3072]{1,0:T(8,128)(2,1)S(1)}, u32[]{:S(2)}, u32[]{:S(2)}) %collective-permute-start.38) | collective-permute-done | bytes 393248 | tf_op jit(solution)/shard_map/ppermute | solution.py:411
  140.9 4.6 %collective-permute-start.46 = (bf16[64,6144]{1,0:T(8,128)(2,1)S(1)}, bf16[64,6144]{1,0:T(8,128)(2,1)S(1)}, u32[]{:S(2)}, u32[]{:S(2)}) collective-permute-start(bf16[64,6144]{1,0:T(8,128)(2,1)S(1)} %fusion.7.refs_1_), channel_id=1, source_target_pairs={{0,1},{1,2},{2,3},{4,5},{5,6},{6,7},{8,9},{9,10},{10,11},{12,13},{... | collective-permute-start | bytes 2359304 | tf_op jit(solution)/shard_map/ppermute | solution.py:424
  147.1 16.9 %shard_map.134 = (bf16[64,3072]{1,0:T(8,128)(2,1)S(1)}, bf16[64,3072]{1,0:T(8,128)(2,1)S(1)}, bf16[64,3072]{1,0:T(8,128)(2,1)S(1)}, bf16[64,3072]{1,0:T(8,128)(2...) custom-call(s32[4]{0:T(128)S(1)} %copy-done.45, ...), custom_call_target="tpu_custom_call" | custom-call | flops 21474836480 | bytes 15728640 | tf_op jit(solution)/shard_map/pallas_call | solution.py:148
  164.1 2.8 collective-permute-done.47
  168.4 5.3 %collective-permute-start.48 = (bf16[64,3072]{1,0:T(8,128)(2,1)S(1)}, bf16[64,3072]{1,0:T(8,128)(2,1)}, u32[]{:S(2)}, u32[]{:S(2)}) collective-permute-start(bf16[64,3072]{1,0:T(8,128)(2,1)S(1)} %get-tuple-element.298.refs_2_), channel_id=1, source_target_pairs={{0,1},{1,2},{2,3},{4,5},{5,6},{6,7},{8,9},{9,10},{10,11},{12,13},{... | collective-permute-start | bytes 1179656 | tf_op jit(solution)/shard_map/ppermute | solution.py:446
  175.1 4.6 %collective-permute-start.50 = (bf16[64,3072]{1,0:T(8,128)(2,1)S(1)}, bf16[64,3072]{1,0:T(8,128)(2,1)S(1)}, u32[]{:S(2)}, u32[]{:S(2)}) collective-permute-start(bf16[64,3072]{1,0:T(8,128)(2,1)S(1)} %get-tuple-element.297.refs_3_), channel_id=1, source_target_pairs={{0,1},{1,2},{2,3},{4,5},{5,6},{6,7},{8,9},{9,10},{10,11},{12,13},{... | collective-permute-start | bytes 1179656 | tf_op jit(solution)/shard_map/ppermute | solution.py:446
  182.1 3.6 %collective-permute-start.52 = (bf16[64,3072]{1,0:T(8,128)(2,1)S(1)}, bf16[64,3072]{1,0:T(8,128)(2,1)S(1)}, u32[]{:S(2)}, u32[]{:S(2)}) collective-permute-start(bf16[64,3072]{1,0:T(8,128)(2,1)S(1)} %get-tuple-element.306.refs_4_), channel_id=1, source_target_pairs={{0,1},{1,2},{2,3},{4,5},{5,6},{6,7},{8,9},{9,10},{10,11},{12,13},{... | collective-permute-start | bytes 1179656 | tf_op jit(solution)/shard_map/ppermute | solution.py:446
  187.2 4.6 %collective-permute-start.54 = (bf16[64,3072]{1,0:T(8,128)(2,1)S(1)}, bf16[64,3072]{1,0:T(8,128)(2,1)S(1)}, u32[]{:S(2)}, u32[]{:S(2)}) collective-permute-start(bf16[64,3072]{1,0:T(8,128)(2,1)S(1)} %get-tuple-element.304.refs_5_), channel_id=1, source_target_pairs={{0,1},{1,2},{2,3},{4,5},{5,6},{6,7},{8,9},{9,10},{10,11},{12,13},{... | collective-permute-start | bytes 1179656 | tf_op jit(solution)/shard_map/ppermute | solution.py:446
  194.9 4.2 %collective-permute-done.53.refs_12_ = bf16[64,3072]{1,0:T(8,128)(2,1)S(1)} collective-permute-done((bf16[64,3072]{1,0:T(8,128)(2,1)S(1)}, bf16[64,3072]{1,0:T(8,128)(2,1)S(1)}, u32[]{:S(2)}, u32[]{:S(2)}) %collective-permute-start.53) | collective-permute-done | bytes 393248 | tf_op jit(solution)/shard_map/ppermute | solution.py:446
  199.3 4.1 %collective-permute-done.54.refs_7_ = bf16[64,3072]{1,0:T(8,128)(2,1)S(1)} collective-permute-done((bf16[64,3072]{1,0:T(8,128)(2,1)S(1)}, bf16[64,3072]{1,0:T(8,128)(2,1)S(1)}, u32[]{:S(2)}, u32[]{:S(2)}) %collective-permute-start.54) | collective-permute-done | bytes 393248 | tf_op jit(solution)/shard_map/ppermute | solution.py:446
  203.4 4.2 %collective-permute-done.55.refs_13_ = bf16[64,3072]{1,0:T(8,128)(2,1)S(1)} collective-permute-done((bf16[64,3072]{1,0:T(8,128)(2,1)S(1)}, bf16[64,3072]{1,0:T(8,128)(2,1)S(1)}, u32[]{:S(2)}, u32[]{:S(2)}) %collective-permute-start.55) | collective-permute-done | bytes 393248 | tf_op jit(solution)/shard_map/ppermute | solution.py:446
  207.7 3.2 %collective-permute-start.56 = (bf16[64,6144]{1,0:T(8,128)(2,1)S(1)}, bf16[64,6144]{1,0:T(8,128)(2,1)S(1)}, u32[]{:S(2)}, u32[]{:S(2)}) collective-permute-start(bf16[64,6144]{1,0:T(8,128)(2,1)S(1)} %pad_maximum_fusion.2), channel_id=1, source_target_pairs={{0,1},{1,2},{2,3},{4,5},{5,6},{6,7},{8,9},{9,10},{10,11},{12,13},{... | collective-permute-start | bytes 2359304 | tf_op jit(solution)/shard_map/ppermute | solution.py:455
  212.7 37.3 %shard_map.135 = (bf16[64,3072]{1,0:T(8,128)(2,1)S(1)}, bf16[64,3072]{1,0:T(8,128)(2,1)S(1)}, bf16[64,3072]{1,0:T(8,128)(2,1)S(1)}, bf16[64,3072]{1,0:T(8,128)(2...) custom-call(s32[1]{0:T(128)} %bitcast.6.mine.refs_0_, ...), custom_call_target="tpu_custom_call" | custom-call | flops 19327352832 | bytes 75497472 | tf_op jit(solution)/shard_map/pallas_call | solution.py:243
  251.0 4.6 %collective-permute-start.64 = (bf16[64,3072]{1,0:T(8,128)(2,1)}, bf16[64,3072]{1,0:T(8,128)(2,1)S(1)}, u32[]{:S(2)}, u32[]{:S(2)}) collective-permute-start(bf16[64,3072]{1,0:T(8,128)(2,1)} %get-tuple-element.266), channel_id=1, source_target_pairs={{0,1},{4,5},{8,9},{12,13},{16,17},{20,21},{24,25},{28,29}} | collective-permute-start | bytes 1179656 | tf_op jit(solution)/shard_map/ppermute | solution.py:411
  258.3 7.0 %collective-permute-done.64 = bf16[64,3072]{1,0:T(8,128)(2,1)S(1)} collective-permute-done((bf16[64,3072]{1,0:T(8,128)(2,1)}, bf16[64,3072]{1,0:T(8,128)(2,1)S(1)}, u32[]{:S(2)}, u32[]{:S(2)}) %collective-permute-start.64) | collective-permute-done | bytes 393248 | tf_op jit(solution)/shard_map/ppermute | solution.py:411
  266.4 4.3 %collective-permute-start.66 = (bf16[64,3072]{1,0:T(8,128)(2,1)S(1)}, bf16[64,3072]{1,0:T(8,128)(2,1)S(1)}, u32[]{:S(2)}, u32[]{:S(2)}) collective-permute-start(bf16[64,3072]{1,0:T(8,128)(2,1)S(1)} %get-tuple-element.302), channel_id=1, source_target_pairs={{0,1},{1,2},{4,5},{5,6},{8,9},{9,10},{12,13},{13,14},{16,17},{17,1... | collective-permute-start | bytes 1179656 | tf_op jit(solution)/shard_map/ppermute | solution.py:411
  273.4 4.4 %collective-permute-start.60 = (bf16[64,3072]{1,0:T(8,128)(2,1)S(1)}, bf16[64,3072]{1,0:T(8,128)(2,1)S(1)}, u32[]{:S(2)}, u32[]{:S(2)}) collective-permute-start(bf16[64,3072]{1,0:T(8,128)(2,1)S(1)} %get-tuple-element.300), channel_id=1, source_target_pairs={{0,1},{1,2},{4,5},{5,6},{8,9},{9,10},{12,13},{13,14},{16,17},{17,1... | collective-permute-start | bytes 1179656 | tf_op jit(solution)/shard_map/ppermute | solution.py:411
  282.3 4.6 %collective-permute-start.68 = (bf16[64,3072]{1,0:T(8,128)(2,1)S(1)}, bf16[64,3072]{1,0:T(8,128)(2,1)S(1)}, u32[]{:S(2)}, u32[]{:S(2)}) collective-permute-start(bf16[64,3072]{1,0:T(8,128)(2,1)S(1)} %add.307), channel_id=1, source_target_pairs={{0,1},{1,2},{2,3},{4,5},{5,6},{6,7},{8,9},{9,10},{10,11},{12,13},{... | collective-permute-start | bytes 1179656 | tf_op jit(solution)/shard_map/ppermute | solution.py:411
  288.4 4.7 %collective-permute-start.62 = (bf16[64,3072]{1,0:T(8,128)(2,1)S(1)}, bf16[64,3072]{1,0:T(8,128)(2,1)S(1)}, u32[]{:S(2)}, u32[]{:S(2)}) collective-permute-start(bf16[64,3072]{1,0:T(8,128)(2,1)S(1)} %add.297), channel_id=1, source_target_pairs={{0,1},{1,2},{2,3},{4,5},{5,6},{6,7},{8,9},{9,10},{10,11},{12,13},{... | collective-permute-start | bytes 1179656 | tf_op jit(solution)/shard_map/ppermute | solution.py:411
  (234 shorter events, 86.3 us)
Async XLA Ops:
  17.2 13.8 %collective-permute-start.28 = (bf16[512,512]{1,0:T(8,128)(2,1)S(1)}, bf16[512,512]{1,0:T(8,128)(2,1)S(1)}, u32[]{:S(2)}, u32[]{:S(2)}) collective-permute-start(bf16[512,512]{1,0:T(8,128)(2,1)S(1)} %constant_dynamic-update-slice_fusion.refs_8_), channel_id=1, source_target_pairs={{0,8},{4,12},{8,0},{12,4},{1,9},{5,13},{9,1},{13,5},{2,10},{6,14},... | collective-permute-start | bytes 1572872 | tf_op jit(solution)/shard_map/ppermute | solution.py:490
  18.7 38.2 %collective-permute-start.29 = (bf16[512,512]{1,0:T(8,128)(2,1)S(1)}, bf16[512,512]{1,0:T(8,128)(2,1)S(1)}, u32[]{:S(2)}, u32[]{:S(2)}) collective-permute-start(bf16[512,512]{1,0:T(8,128)(2,1)S(1)} %constant_dynamic-update-slice_fusion.refs_8_), channel_id=1, source_target_pairs={{0,4},{4,0},{8,12},{12,8},{1,5},{5,1},{9,13},{13,9},{2,6},{6,2},{1... | collective-permute-start | bytes 1572872 | tf_op jit(solution)/shard_map/ppermute | solution.py:490
  31.0 26.8 %collective-permute-start.30 = (bf16[512,512]{1,0:T(8,128)(2,1)S(1)}, bf16[512,512]{1,0:T(8,128)(2,1)}, u32[]{:S(2)}, u32[]{:S(2)}) collective-permute-start(bf16[512,512]{1,0:T(8,128)(2,1)S(1)} %collective-permute-done.28.refs_9_), channel_id=1, source_target_pairs={{0,4},{4,0},{8,12},{12,8},{1,5},{5,1},{9,13},{13,9},{2,6},{6,2},{1... | collective-permute-start | bytes 1572872 | tf_op jit(solution)/shard_map/ppermute | solution.py:490
  38.2 18.1 %collective-permute-start.24 = (bf16[64,1024]{1,0:T(8,128)(2,1)}, bf16[64,1024]{1,0:T(8,128)(2,1)S(1)}, u32[]{:S(2)}, u32[]{:S(2)}) collective-permute-start(bf16[64,1024]{1,0:T(8,128)(2,1)} %get-tuple-element.179), channel_id=1, source_target_pairs={{0,2},{1,3},{2,0},{3,1},{4,6},{5,7},{6,4},{7,5},{8,10},{9,11},{10,... | collective-permute-start | bytes 393224 | tf_op jit(solution)/shard_map/ppermute | solution.py:383
  43.3 39.8 %collective-permute-start.31 = (bf16[64,1024]{1,0:T(8,128)(2,1)}, bf16[64,1024]{1,0:T(8,128)(2,1)S(1)}, u32[]{:S(2)}, u32[]{:S(2)}) collective-permute-start(bf16[64,1024]{1,0:T(8,128)(2,1)} %get-tuple-element.191), channel_id=1, source_target_pairs={{0,1},{1,2},{2,3},{3,0},{4,5},{5,6},{6,7},{7,4},{8,9},{9,10},{10,1... | collective-permute-start | bytes 393224 | tf_op jit(solution)/shard_map/ppermute | solution.py:383
  45.7 37.4 %collective-permute-start.32 = (bf16[64,1024]{1,0:T(8,128)(2,1)}, bf16[64,1024]{1,0:T(8,128)(2,1)S(1)}, u32[]{:S(2)}, u32[]{:S(2)}) collective-permute-start(bf16[64,1024]{1,0:T(8,128)(2,1)} %get-tuple-element.192), channel_id=1, source_target_pairs={{0,2},{1,3},{2,0},{3,1},{4,6},{5,7},{6,4},{7,5},{8,10},{9,11},{10,... | collective-permute-start | bytes 393224 | tf_op jit(solution)/shard_map/ppermute | solution.py:383
  57.0 26.2 %collective-permute-start.33 = (bf16[64,1024]{1,0:T(8,128)(2,1)}, bf16[64,1024]{1,0:T(8,128)(2,1)S(1)}, u32[]{:S(2)}, u32[]{:S(2)}) collective-permute-start(bf16[64,1024]{1,0:T(8,128)(2,1)} %get-tuple-element.193), channel_id=1, source_target_pairs={{0,3},{1,0},{2,1},{3,2},{4,7},{5,4},{6,5},{7,6},{8,11},{9,8},{10,9... | collective-permute-start | bytes 393224 | tf_op jit(solution)/shard_map/ppermute | solution.py:383
  83.2 13.5 %collective-permute-start.40 = (bf16[64,3072]{1,0:T(8,128)(2,1)S(1)}, bf16[64,3072]{1,0:T(8,128)(2,1)S(1)}, u32[]{:S(2)}, u32[]{:S(2)}) collective-permute-start(bf16[64,3072]{1,0:T(8,128)(2,1)S(1)} %get-tuple-element.209), channel_id=1, source_target_pairs={{0,1},{4,5},{8,9},{12,13},{16,17},{20,21},{24,25},{28,29}} | collective-permute-start | bytes 1179656 | tf_op jit(solution)/shard_map/ppermute | solution.py:411
  87.8 17.3 %collective-permute-start.34 = (bf16[64,3072]{1,0:T(8,128)(2,1)S(1)}, bf16[64,3072]{1,0:T(8,128)(2,1)S(1)}, u32[]{:S(2)}, u32[]{:S(2)}) collective-permute-start(bf16[64,3072]{1,0:T(8,128)(2,1)S(1)} %get-tuple-element.194), channel_id=1, source_target_pairs={{0,1},{4,5},{8,9},{12,13},{16,17},{20,21},{24,25},{28,29}} | collective-permute-start | bytes 1179656 | tf_op jit(solution)/shard_map/ppermute | solution.py:411
  89.1 15.9 %collective-permute-start.35 = (bf16[64,3072]{1,0:T(8,128)(2,1)S(1)}, bf16[64,3072]{1,0:T(8,128)(2,1)S(1)}, u32[]{:S(2)}, u32[]{:S(2)}) collective-permute-start(bf16[64,3072]{1,0:T(8,128)(2,1)S(1)} %get-tuple-element.195), channel_id=1, source_target_pairs={{3,2},{7,6},{11,10},{15,14},{19,18},{23,22},{27,26},{31,30}} | collective-permute-start | bytes 1179656 | tf_op jit(solution)/shard_map/ppermute | solution.py:412
  97.6 16.4 %collective-permute-start.42 = (bf16[64,3072]{1,0:T(8,128)(2,1)}, bf16[64,3072]{1,0:T(8,128)(2,1)}, u32[]{:S(2)}, u32[]{:S(2)}) collective-permute-start(bf16[64,3072]{1,0:T(8,128)(2,1)} %get-tuple-element.310), channel_id=1, source_target_pairs={{0,1},{1,2},{4,5},{5,6},{8,9},{9,10},{12,13},{13,14},{16,17},{17,1... | collective-permute-start | bytes 1179656 | tf_op jit(solution)/shard_map/ppermute | solution.py:411
  106.1 16.3 %collective-permute-start.36 = (bf16[64,3072]{1,0:T(8,128)(2,1)}, bf16[64,3072]{1,0:T(8,128)(2,1)}, u32[]{:S(2)}, u32[]{:S(2)}) collective-permute-start(bf16[64,3072]{1,0:T(8,128)(2,1)} %get-tuple-element.308), channel_id=1, source_target_pairs={{0,1},{1,2},{4,5},{5,6},{8,9},{9,10},{12,13},{13,14},{16,17},{17,1... | collective-permute-start | bytes 1179656 | tf_op jit(solution)/shard_map/ppermute | solution.py:411
  115.4 15.2 %collective-permute-start.45 = (bf16[64,3072]{1,0:T(8,128)(2,1)S(1)}, bf16[64,3072]{1,0:T(8,128)(2,1)S(1)}, u32[]{:S(2)}, u32[]{:S(2)}) collective-permute-start(bf16[64,3072]{1,0:T(8,128)(2,1)S(1)} %add.275), channel_id=1, source_target_pairs={{1,0},{2,1},{3,2},{5,4},{6,5},{7,6},{9,8},{10,9},{11,10},{13,12},{... | collective-permute-start | bytes 1179656 | tf_op jit(solution)/shard_map/ppermute | solution.py:412
  117.8 12.8 %collective-permute-start.44 = (bf16[64,3072]{1,0:T(8,128)(2,1)S(1)}, bf16[64,3072]{1,0:T(8,128)(2,1)S(1)}, u32[]{:S(2)}, u32[]{:S(2)}) collective-permute-start(bf16[64,3072]{1,0:T(8,128)(2,1)S(1)} %add.274), channel_id=1, source_target_pairs={{0,1},{1,2},{2,3},{4,5},{5,6},{6,7},{8,9},{9,10},{10,11},{12,13},{... | collective-permute-start | bytes 1179656 | tf_op jit(solution)/shard_map/ppermute | solution.py:411
  125.9 14.0 %collective-permute-start.38 = (bf16[64,3072]{1,0:T(8,128)(2,1)S(1)}, bf16[64,3072]{1,0:T(8,128)(2,1)S(1)}, u32[]{:S(2)}, u32[]{:S(2)}) collective-permute-start(bf16[64,3072]{1,0:T(8,128)(2,1)S(1)} %add.267), channel_id=1, source_target_pairs={{0,1},{1,2},{2,3},{4,5},{5,6},{6,7},{8,9},{9,10},{10,11},{12,13},{... | collective-permute-start | bytes 1179656 | tf_op jit(solution)/shard_map/ppermute | solution.py:411
  140.9 23.2 %collective-permute-start.46 = (bf16[64,6144]{1,0:T(8,128)(2,1)S(1)}, bf16[64,6144]{1,0:T(8,128)(2,1)S(1)}, u32[]{:S(2)}, u32[]{:S(2)}) collective-permute-start(bf16[64,6144]{1,0:T(8,128)(2,1)S(1)} %fusion.7.refs_1_), channel_id=1, source_target_pairs={{0,1},{1,2},{2,3},{4,5},{5,6},{6,7},{8,9},{9,10},{10,11},{12,13},{... | collective-permute-start | bytes 2359304 | tf_op jit(solution)/shard_map/ppermute | solution.py:424
  145.5 21.3 %collective-permute-start.47 = (bf16[64,6144]{1,0:T(8,128)(2,1)S(1)}, bf16[64,6144]{1,0:T(8,128)(2,1)S(1)}, u32[]{:S(2)}, u32[]{:S(2)}) collective-permute-start(bf16[64,6144]{1,0:T(8,128)(2,1)S(1)} %fusion.7.refs_1_), channel_id=1, source_target_pairs={{1,0},{2,1},{3,2},{5,4},{6,5},{7,6},{9,8},{10,9},{11,10},{13,12},{... | collective-permute-start | bytes 2359304 | tf_op jit(solution)/shard_map/ppermute | solution.py:425
  166.9 13.8 %collective-permute-start.49 = (bf16[64,3072]{1,0:T(8,128)(2,1)S(1)}, bf16[64,3072]{1,0:T(8,128)(2,1)}, u32[]{:S(2)}, u32[]{:S(2)}) collective-permute-start(bf16[64,3072]{1,0:T(8,128)(2,1)S(1)} %get-tuple-element.296.refs_8_), channel_id=1, source_target_pairs={{1,0},{2,1},{3,2},{5,4},{6,5},{7,6},{9,8},{10,9},{11,10},{13,12},{... | collective-permute-start | bytes 1179656 | tf_op jit(solution)/shard_map/ppermute | solution.py:446
  168.4 12.3 %collective-permute-start.48 = (bf16[64,3072]{1,0:T(8,128)(2,1)S(1)}, bf16[64,3072]{1,0:T(8,128)(2,1)}, u32[]{:S(2)}, u32[]{:S(2)}) collective-permute-start(bf16[64,3072]{1,0:T(8,128)(2,1)S(1)} %get-tuple-element.298.refs_2_), channel_id=1, source_target_pairs={{0,1},{1,2},{2,3},{4,5},{5,6},{6,7},{8,9},{9,10},{10,11},{12,13},{... | collective-permute-start | bytes 1179656 | tf_op jit(solution)/shard_map/ppermute | solution.py:446
  173.7 13.4 %collective-permute-start.51 = (bf16[64,3072]{1,0:T(8,128)(2,1)S(1)}, bf16[64,3072]{1,0:T(8,128)(2,1)S(1)}, u32[]{:S(2)}, u32[]{:S(2)}) collective-permute-start(bf16[64,3072]{1,0:T(8,128)(2,1)S(1)} %get-tuple-element.295.refs_9_), channel_id=1, source_target_pairs={{1,0},{2,1},{3,2},{5,4},{6,5},{7,6},{9,8},{10,9},{11,10},{13,12},{... | collective-permute-start | bytes 1179656 | tf_op jit(solution)/shard_map/ppermute | solution.py:446
  182.1 12.9 %collective-permute-start.52 = (bf16[64,3072]{1,0:T(8,128)(2,1)S(1)}, bf16[64,3072]{1,0:T(8,128)(2,1)S(1)}, u32[]{:S(2)}, u32[]{:S(2)}) collective-permute-start(bf16[64,3072]{1,0:T(8,128)(2,1)S(1)} %get-tuple-element.306.refs_4_), channel_id=1, source_target_pairs={{0,1},{1,2},{2,3},{4,5},{5,6},{6,7},{8,9},{9,10},{10,11},{12,13},{... | collective-permute-start | bytes 1179656 | tf_op jit(solution)/shard_map/ppermute | solution.py:446
  185.7 13.4 %collective-permute-start.53 = (bf16[64,3072]{1,0:T(8,128)(2,1)S(1)}, bf16[64,3072]{1,0:T(8,128)(2,1)S(1)}, u32[]{:S(2)}, u32[]{:S(2)}) collective-permute-start(bf16[64,3072]{1,0:T(8,128)(2,1)S(1)} %get-tuple-element.305.refs_10_), channel_id=1, source_target_pairs={{1,0},{2,1},{3,2},{5,4},{6,5},{7,6},{9,8},{10,9},{11,10},{13,12},{... | collective-permute-start | bytes 1179656 | tf_op jit(solution)/shard_map/ppermute | solution.py:446
  187.2 16.2 %collective-permute-start.54 = (bf16[64,3072]{1,0:T(8,128)(2,1)S(1)}, bf16[64,3072]{1,0:T(8,128)(2,1)S(1)}, u32[]{:S(2)}, u32[]{:S(2)}) collective-permute-start(bf16[64,3072]{1,0:T(8,128)(2,1)S(1)} %get-tuple-element.304.refs_5_), channel_id=1, source_target_pairs={{0,1},{1,2},{2,3},{4,5},{5,6},{6,7},{8,9},{9,10},{10,11},{12,13},{... | collective-permute-start | bytes 1179656 | tf_op jit(solution)/shard_map/ppermute | solution.py:446
  191.7 15.9 %collective-permute-start.55 = (bf16[64,3072]{1,0:T(8,128)(2,1)S(1)}, bf16[64,3072]{1,0:T(8,128)(2,1)S(1)}, u32[]{:S(2)}, u32[]{:S(2)}) collective-permute-start(bf16[64,3072]{1,0:T(8,128)(2,1)S(1)} %get-tuple-element.303.refs_11_), channel_id=1, source_target_pairs={{1,0},{2,1},{3,2},{5,4},{6,5},{7,6},{9,8},{10,9},{11,10},{13,12},{... | collective-permute-start | bytes 1179656 | tf_op jit(solution)/shard_map/ppermute | solution.py:446
  207.7 42.3 %collective-permute-start.56 = (bf16[64,6144]{1,0:T(8,128)(2,1)S(1)}, bf16[64,6144]{1,0:T(8,128)(2,1)S(1)}, u32[]{:S(2)}, u32[]{:S(2)}) collective-permute-start(bf16[64,6144]{1,0:T(8,128)(2,1)S(1)} %pad_maximum_fusion.2), channel_id=1, source_target_pairs={{0,1},{1,2},{2,3},{4,5},{5,6},{6,7},{8,9},{9,10},{10,11},{12,13},{... | collective-permute-start | bytes 2359304 | tf_op jit(solution)/shard_map/ppermute | solution.py:455
  211.3 38.8 %collective-permute-start.57 = (bf16[64,6144]{1,0:T(8,128)(2,1)S(1)}, bf16[64,6144]{1,0:T(8,128)(2,1)S(1)}, u32[]{:S(2)}, u32[]{:S(2)}) collective-permute-start(bf16[64,6144]{1,0:T(8,128)(2,1)S(1)} %pad_maximum_fusion.3), channel_id=1, source_target_pairs={{1,0},{2,1},{3,2},{5,4},{6,5},{7,6},{9,8},{10,9},{11,10},{13,12},{... | collective-permute-start | bytes 2359304 | tf_op jit(solution)/shard_map/ppermute | solution.py:456
  251.0 14.3 %collective-permute-start.64 = (bf16[64,3072]{1,0:T(8,128)(2,1)}, bf16[64,3072]{1,0:T(8,128)(2,1)S(1)}, u32[]{:S(2)}, u32[]{:S(2)}) collective-permute-start(bf16[64,3072]{1,0:T(8,128)(2,1)} %get-tuple-element.266), channel_id=1, source_target_pairs={{0,1},{4,5},{8,9},{12,13},{16,17},{20,21},{24,25},{28,29}} | collective-permute-start | bytes 1179656 | tf_op jit(solution)/shard_map/ppermute | solution.py:411
  256.3 17.0 %collective-permute-start.58 = (bf16[64,3072]{1,0:T(8,128)(2,1)S(1)}, bf16[64,3072]{1,0:T(8,128)(2,1)S(1)}, u32[]{:S(2)}, u32[]{:S(2)}) collective-permute-start(bf16[64,3072]{1,0:T(8,128)(2,1)S(1)} %get-tuple-element.255), channel_id=1, source_target_pairs={{0,1},{4,5},{8,9},{12,13},{16,17},{20,21},{24,25},{28,29}} | collective-permute-start | bytes 1179656 | tf_op jit(solution)/shard_map/ppermute | solution.py:411
  257.6 15.7 %collective-permute-start.59 = (bf16[64,3072]{1,0:T(8,128)(2,1)S(1)}, bf16[64,3072]{1,0:T(8,128)(2,1)S(1)}, u32[]{:S(2)}, u32[]{:S(2)}) collective-permute-start(bf16[64,3072]{1,0:T(8,128)(2,1)S(1)} %get-tuple-element.253), channel_id=1, source_target_pairs={{3,2},{7,6},{11,10},{15,14},{19,18},{23,22},{27,26},{31,30}} | collective-permute-start | bytes 1179656 | tf_op jit(solution)/shard_map/ppermute | solution.py:412
  273.4 13.5 %collective-permute-start.60 = (bf16[64,3072]{1,0:T(8,128)(2,1)S(1)}, bf16[64,3072]{1,0:T(8,128)(2,1)S(1)}, u32[]{:S(2)}, u32[]{:S(2)}) collective-permute-start(bf16[64,3072]{1,0:T(8,128)(2,1)S(1)} %get-tuple-element.300), channel_id=1, source_target_pairs={{0,1},{1,2},{4,5},{5,6},{8,9},{9,10},{12,13},{13,14},{16,17},{17,1... | collective-permute-start | bytes 1179656 | tf_op jit(solution)/shard_map/ppermute | solution.py:411
  279.8 15.5 %collective-permute-start.69 = (bf16[64,3072]{1,0:T(8,128)(2,1)S(1)}, bf16[64,3072]{1,0:T(8,128)(2,1)S(1)}, u32[]{:S(2)}, u32[]{:S(2)}) collective-permute-start(bf16[64,3072]{1,0:T(8,128)(2,1)S(1)} %add.308), channel_id=1, source_target_pairs={{1,0},{2,1},{3,2},{5,4},{6,5},{7,6},{9,8},{10,9},{11,10},{13,12},{... | collective-permute-start | bytes 1179656 | tf_op jit(solution)/shard_map/ppermute | solution.py:412
  282.3 13.0 %collective-permute-start.68 = (bf16[64,3072]{1,0:T(8,128)(2,1)S(1)}, bf16[64,3072]{1,0:T(8,128)(2,1)S(1)}, u32[]{:S(2)}, u32[]{:S(2)}) collective-permute-start(bf16[64,3072]{1,0:T(8,128)(2,1)S(1)} %add.307), channel_id=1, source_target_pairs={{0,1},{1,2},{2,3},{4,5},{5,6},{6,7},{8,9},{9,10},{10,11},{12,13},{... | collective-permute-start | bytes 1179656 | tf_op jit(solution)/shard_map/ppermute | solution.py:411
  (74 other events, 882.3 us)

commit v2 on v1

--- a/solution.py
+++ b/solution.py
@@ -24,7 +24,7 @@
     pieces, grouped = plan
     (order, mine), refs = refs[:2], refs[2:]
     query_refs, refs = refs[:slots], refs[slots:]
-    place_ref, key_place_ref, refs = refs[0], refs[1], refs[2:]
+    place_ref, refs = refs[0], refs[1:]
     pair_refs, weight, refs = refs[: len(held)], refs[len(held)], refs[len(held) + 1 :]
     outs, refs = refs[: pieces * (slots if grouped else 1)], refs[pieces * (slots if grouped else 1) :]
     query_ref, key_ref, value_ref, top_ref, total_ref, head_ref, weight_ref, arrived = refs
@@ -68,7 +68,11 @@
         return jnp.dot(value_ref[at, p], weights, preferred_element_type=jnp.float32)
 
     place = jnp.concatenate([place_ref[i] for i in range(together) for _ in range(sharing)], axis=1)
-    visible = key_place_ref[...] <= place
+    rows = block_rows // slots
+    down = lax.broadcasted_iota(jnp.int32, (rows, place.shape[1]), 0)
+    visible = jnp.concatenate(
+        [down <= place - lax.rem(mine[1] - s + slots, slots) * rows for s in range(slots)], axis=0
+    )
     for p in range(pairs):
         scores = jnp.where(visible, scores_of(p, 0), -1e30)
         top = jnp.max(scores, axis=0, keepdims=True)
@@ -133,7 +137,7 @@
     return [[out[s * (out.shape[0] // slots) : (s + 1) * (out.shape[0] // slots)] for s in range(slots)] for out in outs]
 
 
-def attend(order, mine, queries, places, key_places, pair_list, held, pairs, sharing, block_rows, weight, pieces, grouped):
+def attend(order, mine, queries, places, pair_list, held, pairs, sharing, block_rows, weight, pieces, grouped):
     slots = len(queries)
     half, width = queries[0].shape
     together = 2 if slots <= LINE else 1
@@ -144,20 +148,16 @@
     kernel = functools.partial(
         attention_kernel, slots, together, held, pairs, sharing, block_rows, (pieces, grouped)
     )
-    in_place = pl.BlockSpec(memory_space=pltpu.VMEM)
     outs = pl.pallas_call(
         kernel,
         grid_spec=pltpu.PrefetchScalarGridSpec(
             num_scalar_prefetch=2,
             grid=(slots // together,),
-            in_specs=[in_place] * slots
-            + [
-                pl.BlockSpec((together, 1, half), lambda s, *_: (s, 0, 0)),
-                pl.BlockSpec((block_rows, 1), lambda s, *_: (0, 0)),
-            ]
-            + [in_place] * len(pair_list)
+            in_specs=[pl.BlockSpec((half, width), lambda s, *_: (0, 0))] * slots
+            + [pl.BlockSpec((together, 1, half), lambda s, *_: (s, 0, 0))]
+            + [pl.BlockSpec(pair.shape, lambda s, *_: (0, 0)) for pair in pair_list]
             + [pl.BlockSpec(memory_space=pl.ANY)],
-            out_specs=[in_place] * len(shapes),
+            out_specs=[pl.BlockSpec(shape.shape, lambda s, *_: (0, 0)) for shape in shapes],
             scratch_shapes=[
                 pltpu.VMEM((pairs, tall, HD), jnp.bfloat16),
                 pltpu.VMEM((blocks, pairs, block_rows, HD), jnp.bfloat16),
@@ -176,7 +176,7 @@
             bytes_accessed=2 * (2 * slots * half * width + count * 2 * pairs * HD + weight.size),
             transcendentals=slots * half * width // HD * count,
         ),
-    )(order, mine, *queries, places, key_places, *pair_list, weight)
+    )(order, mine, *queries, places, *pair_list, weight)
     return by_piece(outs, slots, pieces, grouped)
 
 
@@ -186,7 +186,7 @@
     for count in plan:
         sources.append(refs[:count])
         refs = refs[count:]
-    gate_weight, up_weight, down_weight, refs = refs[0], refs[1], refs[2], refs[3:]
+    gate_weight, up_weight, down_weights, refs = refs[0], refs[1], refs[2:4], refs[4:]
     outs, (chosen, acts) = refs[:-2], refs[-2:]
     step = pl.program_id(0)
     tile = gate_weight.shape[1]
@@ -220,15 +220,16 @@
 
     @pl.when(step >= first)
     def _():
-        value = jnp.dot(acts[...], down_weight[...], preferred_element_type=jnp.float32)
-        strip = down_weight.shape[1]
-        strips = outs[0].shape[1] // strip
-        for c in range(pieces):
-
-            @pl.when((step - first) // strips == c)
-            def _():
-                columns = pl.ds(pl.multiple_of((step - first - c * strips) * strip, strip), strip)
-                share_out(outs[c * len(outs) // pieces :], columns, value)
+        strip = down_weights[0].shape[1]
+        pairs = outs[0].shape[1] // (2 * strip)
+        for j, down_weight in enumerate(down_weights):
+            value = jnp.dot(acts[...], down_weight[...], preferred_element_type=jnp.float32)
+            for c in range(pieces):
+
+                @pl.when((step - first) // pairs == c)
+                def _():
+                    at = (2 * (step - first - c * pairs) + j) * strip
+                    share_out(outs[c * len(outs) // pieces :], pl.ds(pl.multiple_of(at, strip), strip), value)
 
 
 def expert_rows(mine, sources, gate_weight, up_weight, down_weight, slots, pieces, grouped):
@@ -244,9 +245,13 @@
         functools.partial(expert_kernel, [len(source) for source in sources], pieces),
         grid_spec=pltpu.PrefetchScalarGridSpec(
             num_scalar_prefetch=1,
-            grid=(first + depth // strip,),
+            grid=(first + depth // (2 * strip),),
             in_specs=[in_place] * len(flat)
-            + [weight, weight, pl.BlockSpec((width, strip), lambda n, *_: (0, jnp.maximum(n - first, 0)))],
+            + [weight, weight]
+            + [
+                pl.BlockSpec((width, strip), functools.partial(lambda j, n, *_: (0, 2 * jnp.maximum(n - first, 0) + j), j))
+                for j in range(2)
+            ],
             out_specs=[in_place] * len(shapes),
             scratch_shapes=[pltpu.VMEM((rows, depth), jnp.bfloat16), pltpu.VMEM((rows, width), jnp.bfloat16)],
         ),
@@ -255,7 +260,7 @@
         cost_estimate=pl.CostEstimate(
             flops=6 * rows * depth * width, bytes_accessed=6 * depth * width, transcendentals=rows * width
         ),
-    )(mine, *flat, gate_weight, up_weight, down_weight)
+    )(mine, *flat, gate_weight, up_weight, down_weight, down_weight)
     return by_piece(outs, slots, pieces, grouped)
 
 
@@ -457,7 +462,6 @@
             total = jnp.concatenate([term[0] for term in terms], axis=1).astype(jnp.float32) + right + left
         return [[source]] + from_left + from_right, total
 
-    key_places = (shard_of[:, None] * rows + jnp.arange(rows, dtype=jnp.int32)[None, :]).reshape(block_rows, 1)
     picked = ((routes[:, 0] == 0) | (routes[:, 1] == 0)).reshape(shards, rows)
     if line:
         sent_pairs = pack_pairs(me[None], keys, values, shards)
@@ -489,6 +493,8 @@
     while offset >= 1:
         pair_list += [lax.ppermute(part, "ctx", [(i, i ^ offset) for i in range(blocks)]) for part in pair_list]
         held += [[other ^ offset for other in group] for group in held]
+        if line and len(pair_list) == 2:
+            pair_list[1], asked[0] = lax.optimization_barrier((pair_list[1], asked[0]))
         offset //= 2
 
     def reorder(source):
@@ -506,10 +512,9 @@
     def project(which):
         terms = attend(
             block_order,
-            lax.axis_index("ctx").astype(jnp.int32)[None],
+            jnp.stack([lax.axis_index("ctx"), me]).astype(jnp.int32),
             [asked[which][s] for s in slots],
             places[which],
-            key_places,
             pair_list,
             held,
             pairs,
@@ -546,6 +551,8 @@
         if beside is not None:
             terms, beside = lax.optimization_barrier((terms, beside))
         sums, marks = reduce_line(terms)
+        if beside is not None:
+            beside = (beside[0], lax.optimization_barrier((beside[1], marks[0]))[0][0, 0] > half)
         if line:
             normed, _ = lax.optimization_barrier((normed, marks[0]))
         share = share_of(which, normed)
@@ -573,9 +580,9 @@
     asked[1], _ = lax.optimization_barrier((asked[1], normed))
     sources, second_sum = gather_line(normed, project(1))
     second_half = (hidden[half:].astype(jnp.float32) + second_sum).astype(jnp.bfloat16)
-    part, second_half = expert(0, normed, sources, second_half)
-    part, late, fullest = lax.optimization_barrier((part, second_half, fullest))
-    late = lax.cond(fullest[0, 0] > half, late_expert, jnp.zeros_like, late)
+    part, (second_half, crowded) = expert(0, normed, sources, (second_half, fullest))
+    part, late, crowded = lax.optimization_barrier((part, second_half, crowded))
+    late = lax.cond(crowded, late_expert, jnp.zeros_like, late)
     return (restore([first_half, second_half]), restore([part, late]))
 
 

time: 305 us -> 294 us (0.964); the launches traced: 303 us -> 289 us
  Pallas kernels: 75.9 us -> 64.2 us
  waiting for transfers between devices: 78.4 us -> 69.9 us
  starting transfers between devices: 111 us -> 117 us
    ppermute x3, waiting for transfers between devices: 12.3 us -> 0.01 us  [on_device(): lax.ppermute(part, 'ctx', [(i, i ^ offset) for i in range(blocks)])]
    pallas_call x2, Pallas kernels: 33.9 us -> 24.7 us  [attend(): pl.pallas_call(kernel, grid_spec=pltpu.PrefetchScalarGridSpec(num_scalar_...]
    ppermute x4, waiting for transfers between devices: 9.48 us -> 2.16 us  [gather_line(): lax.ppermute(left, 'tp', to_left)]
    ppermute x4, waiting for transfers between devices: 6.03 us -> 12.7 us  [gather_line(): lax.ppermute(right, 'tp', to_right)]
    ppermute x9, waiting for transfers between devices: 18.9 us -> 13.5 us  [shift(): lax.ppermute(parts[s], 'tp', moves[s])]
    ppermute x12, waiting for transfers between devices: 3.97 us -> 7.41 us  [reduce_line(): left = lax.ppermute(sent[1], 'tp', lefts(s))]
    ppermute x9, starting transfers between devices: 14.4 us -> 17.7 us  [shift(): lax.ppermute(parts[s], 'tp', moves[s])]
    ppermute x12, waiting for transfers between devices: 25 us -> 28.3 us  [reduce_line(): right = lax.ppermute(sent[0], 'tp', rights(s))]
  transfers between devices with their start and end apart: 48 -> 48, of which waited for: 20 -> 21; matrix products, arithmetic and copies ran while one was open for 6% -> 6% of each run, Pallas kernels for 24% -> 22%
where the time goes in v2:
time: 294 us; the launch traced here: 289 us
  starting transfers between devices  117 us (40%)
  waiting for transfers between devices  69.9 us (24%)
  Pallas kernels  64.2 us (22%)
  local copies, waits for them, and re-layouts  15.2 us (5%)
  other arithmetic  15 us (5%)
  matrix products  5.3 us (2%)
    ppermute x12, starting transfers between devices, reduce_line(): right = lax.ppermute(sent[0], 'tp', rights(s))  50.4 us
    pallas_call x1, Pallas kernels, expert_rows(): pl.pallas_call(functools.partial(expert_kernel, [len(source) for source i...  34.8 us
    ppermute x12, waiting for transfers between devices, reduce_line(): right = lax.ppermute(sent[0], 'tp', rights(s))  28.3 us
    pallas_call x2, Pallas kernels, attend(): pl.pallas_call(kernel, grid_spec=pltpu.PrefetchScalarGridSpec(num_scalar_...  24.7 us
    ppermute x4, starting transfers between devices, gather_line(): lax.ppermute(right, 'tp', to_right)  18.8 us
    ppermute x9, starting transfers between devices, shift(): lax.ppermute(parts[s], 'tp', moves[s])  17.7 us
    unnamed x103, local copies, waits for them, and re-layouts  13.9 us
    ppermute x9, waiting for transfers between devices, shift(): lax.ppermute(parts[s], 'tp', moves[s])  13.5 us
  transfers between devices with their start and end apart: 48, of which 21 were waited for; matrix products, arithmetic and copies ran while one was open for 6% of the time, Pallas kernels for 22%

profile of v2, /device:TPU:0, one launch (start us, length us, event | category | flops | bytes accessed | tf_op | source)
XLA Modules:
  0.0 289.0 jit_solution(14306117647508249351)
XLA Ops:
  2.7 3.0 %collective-permute-start.22 = (bf16[128,512]{1,0:T(8,128)(2,1)}, bf16[128,512]{1,0:T(8,128)(2,1)S(1)}, u32[]{:S(2)}, u32[]{:S(2)}) collective-permute-start(bf16[128,512]{1,0:T(8,128)(2,1)} %get-tuple-element.179), channel_id=1, source_target_pairs={{0,1},{1,2},{2,3},{3,0},{4,5},{5,6},{6,7},{7,4},{8,9},{9,10},{10,1... | collective-permute-start | bytes 393224 | tf_op jit(solution)/shard_map/ppermute | solution.py:388
  12.4 4.8 %collective-permute-done.23 = bf16[128,512]{1,0:T(8,128)(2,1)S(1)} collective-permute-done((bf16[128,512]{1,0:T(8,128)(2,1)}, bf16[128,512]{1,0:T(8,128)(2,1)S(1)}, u32[]{:S(2)}, u32[]{:S(2)}) %collective-permute-start.23) | collective-permute-done | bytes 131104 | tf_op jit(solution)/shard_map/ppermute | solution.py:388
  22.0 3.3 %collective-permute-start.26 = (bf16[64,1024]{1,0:T(8,128)(2,1)}, bf16[64,1024]{1,0:T(8,128)(2,1)S(1)}, u32[]{:S(2)}, u32[]{:S(2)}) collective-permute-start(bf16[64,1024]{1,0:T(8,128)(2,1)} %get-tuple-element.185), channel_id=1, source_target_pairs={{0,1},{1,2},{2,3},{3,0},{4,5},{5,6},{6,7},{7,4},{8,9},{9,10},{10,1... | collective-permute-start | bytes 393224 | tf_op jit(solution)/shard_map/ppermute | solution.py:388
  27.8 3.2 %collective-permute-done.26.refs_2_ = bf16[64,1024]{1,0:T(8,128)(2,1)S(1)} collective-permute-done((bf16[64,1024]{1,0:T(8,128)(2,1)}, bf16[64,1024]{1,0:T(8,128)(2,1)S(1)}, u32[]{:S(2)}, u32[]{:S(2)}) %collective-permute-start.26) | collective-permute-done | bytes 131104 | tf_op jit(solution)/shard_map/ppermute | solution.py:388
  31.6 3.7 %collective-permute-done.27.refs_4_ = bf16[64,1024]{1,0:T(8,128)(2,1)S(1)} collective-permute-done((bf16[64,1024]{1,0:T(8,128)(2,1)}, bf16[64,1024]{1,0:T(8,128)(2,1)S(1)}, u32[]{:S(2)}, u32[]{:S(2)}) %collective-permute-start.27) | collective-permute-done | bytes 131104 | tf_op jit(solution)/shard_map/ppermute | solution.py:388
  50.7 12.3 %shard_map.133 = (bf16[64,3072]{1,0:T(8,128)(2,1)S(1)}, bf16[64,3072]{1,0:T(8,128)(2,1)S(1)}, bf16[64,3072]{1,0:T(8,128)(2,1)S(1)}, bf16[64,3072]{1,0:T(8,128)(2...) custom-call(s32[4]{0:T(128)S(1)} %copy-done.37, ...), custom_call_target="tpu_custom_call" | custom-call | flops 21474836480 | bytes 15728640 | tf_op jit(solution)/shard_map/pallas_call | solution.py:151
  63.0 3.9 %collective-permute-start.40 = (bf16[64,3072]{1,0:T(8,128)(2,1)S(1)}, bf16[64,3072]{1,0:T(8,128)(2,1)S(1)}, u32[]{:S(2)}, u32[]{:S(2)}) collective-permute-start(bf16[64,3072]{1,0:T(8,128)(2,1)S(1)} %get-tuple-element.221), channel_id=1, source_target_pairs={{0,1},{4,5},{8,9},{12,13},{16,17},{20,21},{24,25},{28,29}} | collective-permute-start | bytes 1179656 | tf_op jit(solution)/shard_map/ppermute | solution.py:416
  69.7 3.3 %collective-permute-done.40 = bf16[64,3072]{1,0:T(8,128)(2,1)S(1)} collective-permute-done((bf16[64,3072]{1,0:T(8,128)(2,1)S(1)}, bf16[64,3072]{1,0:T(8,128)(2,1)S(1)}, u32[]{:S(2)}, u32[]{:S(2)}) %collective-permute-start.40) | collective-permute-done | bytes 393248 | tf_op jit(solution)/shard_map/ppermute | solution.py:416
  74.0 5.1 %collective-permute-start.42 = (bf16[64,3072]{1,0:T(8,128)(2,1)}, bf16[64,3072]{1,0:T(8,128)(2,1)}, u32[]{:S(2)}, u32[]{:S(2)}) collective-permute-start(bf16[64,3072]{1,0:T(8,128)(2,1)} %get-tuple-element.324), channel_id=1, source_target_pairs={{0,1},{1,2},{4,5},{5,6},{8,9},{9,10},{12,13},{13,14},{16,17},{17,1... | collective-permute-start | bytes 1179656 | tf_op jit(solution)/shard_map/ppermute | solution.py:416
  82.4 5.1 %collective-permute-start.36 = (bf16[64,3072]{1,0:T(8,128)(2,1)}, bf16[64,3072]{1,0:T(8,128)(2,1)}, u32[]{:S(2)}, u32[]{:S(2)}) collective-permute-start(bf16[64,3072]{1,0:T(8,128)(2,1)} %get-tuple-element.322), channel_id=1, source_target_pairs={{0,1},{1,2},{4,5},{5,6},{8,9},{9,10},{12,13},{13,14},{16,17},{17,1... | collective-permute-start | bytes 1179656 | tf_op jit(solution)/shard_map/ppermute | solution.py:416
  94.2 4.6 %collective-permute-start.44 = (bf16[64,3072]{1,0:T(8,128)(2,1)S(1)}, bf16[64,3072]{1,0:T(8,128)(2,1)S(1)}, u32[]{:S(2)}, u32[]{:S(2)}) collective-permute-start(bf16[64,3072]{1,0:T(8,128)(2,1)S(1)} %add.239), channel_id=1, source_target_pairs={{0,1},{1,2},{2,3},{4,5},{5,6},{6,7},{8,9},{9,10},{10,11},{12,13},{... | collective-permute-start | bytes 1179656 | tf_op jit(solution)/shard_map/ppermute | solution.py:416
  102.2 4.7 %collective-permute-start.38 = (bf16[64,3072]{1,0:T(8,128)(2,1)S(1)}, bf16[64,3072]{1,0:T(8,128)(2,1)S(1)}, u32[]{:S(2)}, u32[]{:S(2)}) collective-permute-start(bf16[64,3072]{1,0:T(8,128)(2,1)S(1)} %add.232), channel_id=1, source_target_pairs={{0,1},{1,2},{2,3},{4,5},{5,6},{6,7},{8,9},{9,10},{10,11},{12,13},{... | collective-permute-start | bytes 1179656 | tf_op jit(solution)/shard_map/ppermute | solution.py:416
  107.1 4.6 %collective-permute-done.39 = bf16[64,3072]{1,0:T(8,128)(2,1)S(1)} collective-permute-done((bf16[64,3072]{1,0:T(8,128)(2,1)S(1)}, bf16[64,3072]{1,0:T(8,128)(2,1)S(1)}, u32[]{:S(2)}, u32[]{:S(2)}) %collective-permute-start.39) | collective-permute-done | bytes 393248 | tf_op jit(solution)/shard_map/ppermute | solution.py:417
  111.7 2.9 %collective-permute-done.38 = bf16[64,3072]{1,0:T(8,128)(2,1)S(1)} collective-permute-done((bf16[64,3072]{1,0:T(8,128)(2,1)S(1)}, bf16[64,3072]{1,0:T(8,128)(2,1)S(1)}, u32[]{:S(2)}, u32[]{:S(2)}) %collective-permute-start.38) | collective-permute-done | bytes 393248 | tf_op jit(solution)/shard_map/ppermute | solution.py:416
  115.6 4.6 %collective-permute-start.46 = (bf16[64,6144]{1,0:T(8,128)(2,1)S(1)}, bf16[64,6144]{1,0:T(8,128)(2,1)S(1)}, u32[]{:S(2)}, u32[]{:S(2)}) collective-permute-start(bf16[64,6144]{1,0:T(8,128)(2,1)S(1)} %fusion.7.refs_1_), channel_id=1, source_target_pairs={{0,1},{1,2},{2,3},{4,5},{5,6},{6,7},{8,9},{9,10},{10,11},{12,13},{... | collective-permute-start | bytes 2359304 | tf_op jit(solution)/shard_map/ppermute | solution.py:429
  121.6 12.4 %shard_map.134 = (bf16[64,3072]{1,0:T(8,128)(2,1)S(1)}, bf16[64,3072]{1,0:T(8,128)(2,1)S(1)}, bf16[64,3072]{1,0:T(8,128)(2,1)S(1)}, bf16[64,3072]{1,0:T(8,128)(2...) custom-call(s32[4]{0:T(128)S(1)} %copy-done.37, ...), custom_call_target="tpu_custom_call" | custom-call | flops 21474836480 | bytes 15728640 | tf_op jit(solution)/shard_map/pallas_call | solution.py:151
  135.2 4.7 %collective-permute-done.47 = bf16[64,6144]{1,0:T(8,128)(2,1)S(1)} collective-permute-done((bf16[64,6144]{1,0:T(8,128)(2,1)S(1)}, bf16[64,6144]{1,0:T(8,128)(2,1)S(1)}, u32[]{:S(2)}, u32[]{:S(2)}) %collective-permute-start.47) | collective-permute-done | bytes 786464 | tf_op jit(solution)/shard_map/ppermute | solution.py:430
  141.6 5.3 %collective-permute-start.48 = (bf16[64,3072]{1,0:T(8,128)(2,1)S(1)}, bf16[64,3072]{1,0:T(8,128)(2,1)}, u32[]{:S(2)}, u32[]{:S(2)}) collective-permute-start(bf16[64,3072]{1,0:T(8,128)(2,1)S(1)} %get-tuple-element.312.refs_2_), channel_id=1, source_target_pairs={{0,1},{1,2},{2,3},{4,5},{5,6},{6,7},{8,9},{9,10},{10,11},{12,13},{... | collective-permute-start | bytes 1179656 | tf_op jit(solution)/shard_map/ppermute | solution.py:451
  148.4 4.6 %collective-permute-start.50 = (bf16[64,3072]{1,0:T(8,128)(2,1)S(1)}, bf16[64,3072]{1,0:T(8,128)(2,1)S(1)}, u32[]{:S(2)}, u32[]{:S(2)}) collective-permute-start(bf16[64,3072]{1,0:T(8,128)(2,1)S(1)} %get-tuple-element.311.refs_3_), channel_id=1, source_target_pairs={{0,1},{1,2},{2,3},{4,5},{5,6},{6,7},{8,9},{9,10},{10,11},{12,13},{... | collective-permute-start | bytes 1179656 | tf_op jit(solution)/shard_map/ppermute | solution.py:451
  155.3 4.5 %collective-permute-start.52 = (bf16[64,3072]{1,0:T(8,128)(2,1)S(1)}, bf16[64,3072]{1,0:T(8,128)(2,1)S(1)}, u32[]{:S(2)}, u32[]{:S(2)}) collective-permute-start(bf16[64,3072]{1,0:T(8,128)(2,1)S(1)} %get-tuple-element.320.refs_4_), channel_id=1, source_target_pairs={{0,1},{1,2},{2,3},{4,5},{5,6},{6,7},{8,9},{9,10},{10,11},{12,13},{... | collective-permute-start | bytes 1179656 | tf_op jit(solution)/shard_map/ppermute | solution.py:451
  162.6 4.4 %collective-permute-start.54 = (bf16[64,3072]{1,0:T(8,128)(2,1)S(1)}, bf16[64,3072]{1,0:T(8,128)(2,1)S(1)}, u32[]{:S(2)}, u32[]{:S(2)}) collective-permute-start(bf16[64,3072]{1,0:T(8,128)(2,1)S(1)} %get-tuple-element.318.refs_5_), channel_id=1, source_target_pairs={{0,1},{1,2},{2,3},{4,5},{5,6},{6,7},{8,9},{9,10},{10,11},{12,13},{... | collective-permute-start | bytes 1179656 | tf_op jit(solution)/shard_map/ppermute | solution.py:451
  171.6 7.8 %collective-permute-done.54.refs_7_ = bf16[64,3072]{1,0:T(8,128)(2,1)S(1)} collective-permute-done((bf16[64,3072]{1,0:T(8,128)(2,1)S(1)}, bf16[64,3072]{1,0:T(8,128)(2,1)S(1)}, u32[]{:S(2)}, u32[]{:S(2)}) %collective-permute-start.54) | collective-permute-done | bytes 393248 | tf_op jit(solution)/shard_map/ppermute | solution.py:451
  181.1 2.9 collective-permute-start.56
  185.7 34.8 %shard_map.135 = (bf16[64,3072]{1,0:T(8,128)(2,1)S(1)}, bf16[64,3072]{1,0:T(8,128)(2,1)S(1)}, bf16[64,3072]{1,0:T(8,128)(2,1)S(1)}, bf16[64,3072]{1,0:T(8,128)(2...) custom-call(s32[1]{0:T(128)} %bitcast.6.mine.refs_0_, ...), custom_call_target="tpu_custom_call" | custom-call | flops 19327352832 | bytes 75497472 | tf_op jit(solution)/shard_map/pallas_call | solution.py:244
  221.5 4.6 %collective-permute-start.58 = (bf16[64,3072]{1,0:T(8,128)(2,1)S(1)}, bf16[64,3072]{1,0:T(8,128)(2,1)S(1)}, u32[]{:S(2)}, u32[]{:S(2)}) collective-permute-start(bf16[64,3072]{1,0:T(8,128)(2,1)S(1)} %get-tuple-element.268), channel_id=1, source_target_pairs={{0,1},{4,5},{8,9},{12,13},{16,17},{20,21},{24,25},{28,29}} | collective-permute-start | bytes 1179656 | tf_op jit(solution)/shard_map/ppermute | solution.py:416
  230.2 5.3 %collective-permute-done.58 = bf16[64,3072]{1,0:T(8,128)(2,1)S(1)} collective-permute-done((bf16[64,3072]{1,0:T(8,128)(2,1)S(1)}, bf16[64,3072]{1,0:T(8,128)(2,1)S(1)}, u32[]{:S(2)}, u32[]{:S(2)}) %collective-permute-start.58) | collective-permute-done | bytes 393248 | tf_op jit(solution)/shard_map/ppermute | solution.py:416
  235.5 8.4 %collective-permute-done.64 = bf16[64,3072]{1,0:T(8,128)(2,1)} collective-permute-done((bf16[64,3072]{1,0:T(8,128)(2,1)}, bf16[64,3072]{1,0:T(8,128)(2,1)}, u32[]{:S(2)}, u32[]{:S(2)}) %collective-permute-start.64) | collective-permute-done | bytes 393248 | tf_op jit(solution)/shard_map/ppermute | solution.py:416
  245.3 4.4 %collective-permute-start.66 = (bf16[64,3072]{1,0:T(8,128)(2,1)S(1)}, bf16[64,3072]{1,0:T(8,128)(2,1)S(1)}, u32[]{:S(2)}, u32[]{:S(2)}) collective-permute-start(bf16[64,3072]{1,0:T(8,128)(2,1)S(1)} %get-tuple-element.316), channel_id=1, source_target_pairs={{0,1},{1,2},{4,5},{5,6},{8,9},{9,10},{12,13},{13,14},{16,17},{17,1... | collective-permute-start | bytes 1179656 | tf_op jit(solution)/shard_map/ppermute | solution.py:416
  254.0 5.2 %collective-permute-done.66 = bf16[64,3072]{1,0:T(8,128)(2,1)S(1)} collective-permute-done((bf16[64,3072]{1,0:T(8,128)(2,1)S(1)}, bf16[64,3072]{1,0:T(8,128)(2,1)S(1)}, u32[]{:S(2)}, u32[]{:S(2)}) %collective-permute-start.66) | collective-permute-done | bytes 393248 | tf_op jit(solution)/shard_map/ppermute | solution.py:416
  262.8 7.1 %collective-permute-start.68 = (bf16[64,3072]{1,0:T(8,128)(2,1)S(1)}, bf16[64,3072]{1,0:T(8,128)(2,1)S(1)}, u32[]{:S(2)}, u32[]{:S(2)}) collective-permute-start(bf16[64,3072]{1,0:T(8,128)(2,1)S(1)} %add.272), channel_id=1, source_target_pairs={{0,1},{1,2},{2,3},{4,5},{5,6},{6,7},{8,9},{9,10},{10,11},{12,13},{... | collective-permute-start | bytes 1179656 | tf_op jit(solution)/shard_map/ppermute | solution.py:416
  271.4 4.9 %collective-permute-start.62 = (bf16[64,3072]{1,0:T(8,128)(2,1)S(1)}, bf16[64,3072]{1,0:T(8,128)(2,1)S(1)}, u32[]{:S(2)}, u32[]{:S(2)}) collective-permute-start(bf16[64,3072]{1,0:T(8,128)(2,1)S(1)} %add.262), channel_id=1, source_target_pairs={{0,1},{1,2},{2,3},{4,5},{5,6},{6,7},{8,9},{9,10},{10,11},{12,13},{... | collective-permute-start | bytes 1179656 | tf_op jit(solution)/shard_map/ppermute | solution.py:416
  280.3 2.7 collective-permute-done.63
  (216 shorter events, 93.6 us)
Async XLA Ops:
  17.2 19.4 %collective-permute-start.25 = (bf16[512,512]{1,0:T(8,128)(2,1)S(1)}, bf16[512,512]{1,0:T(8,128)(2,1)S(1)}, u32[]{:S(2)}, u32[]{:S(2)}) collective-permute-start(bf16[512,512]{1,0:T(8,128)(2,1)S(1)} %constant_dynamic-update-slice_fusion.refs_7_), channel_id=1, source_target_pairs={{0,8},{4,12},{8,0},{12,4},{1,9},{5,13},{9,1},{13,5},{2,10},{6,14},... | collective-permute-start | bytes 1572872 | tf_op jit(solution)/shard_map/ppermute | solution.py:494
  27.8 14.7 %collective-permute-start.29 = (bf16[512,512]{1,0:T(8,128)(2,1)S(1)}, bf16[512,512]{1,0:T(8,128)(2,1)S(1)}, u32[]{:S(2)}, u32[]{:S(2)}) collective-permute-start(bf16[512,512]{1,0:T(8,128)(2,1)S(1)} %constant_dynamic-update-slice_fusion.refs_7_), channel_id=1, source_target_pairs={{0,4},{4,0},{8,12},{12,8},{1,5},{5,1},{9,13},{13,9},{2,6},{6,2},{1... | collective-permute-start | bytes 1572872 | tf_op jit(solution)/shard_map/ppermute | solution.py:494
  37.4 25.6 %collective-permute-start.31 = (bf16[64,1024]{1,0:T(8,128)(2,1)}, bf16[64,1024]{1,0:T(8,128)(2,1)}, u32[]{:S(2)}, u32[]{:S(2)}) collective-permute-start(bf16[64,1024]{1,0:T(8,128)(2,1)} %get-tuple-element.203), channel_id=1, source_target_pairs={{0,1},{1,2},{2,3},{3,0},{4,5},{5,6},{6,7},{7,4},{8,9},{9,10},{10,1... | collective-permute-start | bytes 393224 | tf_op jit(solution)/shard_map/ppermute | solution.py:388
  40.0 23.0 %collective-permute-start.32 = (bf16[64,1024]{1,0:T(8,128)(2,1)}, bf16[64,1024]{1,0:T(8,128)(2,1)}, u32[]{:S(2)}, u32[]{:S(2)}) collective-permute-start(bf16[64,1024]{1,0:T(8,128)(2,1)} %get-tuple-element.204), channel_id=1, source_target_pairs={{0,2},{1,3},{2,0},{3,1},{4,6},{5,7},{6,4},{7,5},{8,10},{9,11},{10,... | collective-permute-start | bytes 393224 | tf_op jit(solution)/shard_map/ppermute | solution.py:388
  42.4 20.6 %collective-permute-start.33 = (bf16[64,1024]{1,0:T(8,128)(2,1)}, bf16[64,1024]{1,0:T(8,128)(2,1)}, u32[]{:S(2)}, u32[]{:S(2)}) collective-permute-start(bf16[64,1024]{1,0:T(8,128)(2,1)} %get-tuple-element.205), channel_id=1, source_target_pairs={{0,3},{1,0},{2,1},{3,2},{4,7},{5,4},{6,5},{7,6},{8,11},{9,8},{10,9... | collective-permute-start | bytes 393224 | tf_op jit(solution)/shard_map/ppermute | solution.py:388
  67.7 13.8 %collective-permute-start.34 = (bf16[64,3072]{1,0:T(8,128)(2,1)S(1)}, bf16[64,3072]{1,0:T(8,128)(2,1)S(1)}, u32[]{:S(2)}, u32[]{:S(2)}) collective-permute-start(bf16[64,3072]{1,0:T(8,128)(2,1)S(1)} %get-tuple-element.206), channel_id=1, source_target_pairs={{0,1},{4,5},{8,9},{12,13},{16,17},{20,21},{24,25},{28,29}} | collective-permute-start | bytes 1179656 | tf_op jit(solution)/shard_map/ppermute | solution.py:416
  69.0 12.4 %collective-permute-start.35 = (bf16[64,3072]{1,0:T(8,128)(2,1)S(1)}, bf16[64,3072]{1,0:T(8,128)(2,1)S(1)}, u32[]{:S(2)}, u32[]{:S(2)}) collective-permute-start(bf16[64,3072]{1,0:T(8,128)(2,1)S(1)} %get-tuple-element.207), channel_id=1, source_target_pairs={{3,2},{7,6},{11,10},{15,14},{19,18},{23,22},{27,26},{31,30}} | collective-permute-start | bytes 1179656 | tf_op jit(solution)/shard_map/ppermute | solution.py:417
  74.0 16.4 %collective-permute-start.42 = (bf16[64,3072]{1,0:T(8,128)(2,1)}, bf16[64,3072]{1,0:T(8,128)(2,1)}, u32[]{:S(2)}, u32[]{:S(2)}) collective-permute-start(bf16[64,3072]{1,0:T(8,128)(2,1)} %get-tuple-element.324), channel_id=1, source_target_pairs={{0,1},{1,2},{4,5},{5,6},{8,9},{9,10},{12,13},{13,14},{16,17},{17,1... | collective-permute-start | bytes 1179656 | tf_op jit(solution)/shard_map/ppermute | solution.py:416
  82.4 16.3 %collective-permute-start.36 = (bf16[64,3072]{1,0:T(8,128)(2,1)}, bf16[64,3072]{1,0:T(8,128)(2,1)}, u32[]{:S(2)}, u32[]{:S(2)}) collective-permute-start(bf16[64,3072]{1,0:T(8,128)(2,1)} %get-tuple-element.322), channel_id=1, source_target_pairs={{0,1},{1,2},{4,5},{5,6},{8,9},{9,10},{12,13},{13,14},{16,17},{17,1... | collective-permute-start | bytes 1179656 | tf_op jit(solution)/shard_map/ppermute | solution.py:416
  91.8 15.3 %collective-permute-start.45 = (bf16[64,3072]{1,0:T(8,128)(2,1)S(1)}, bf16[64,3072]{1,0:T(8,128)(2,1)S(1)}, u32[]{:S(2)}, u32[]{:S(2)}) collective-permute-start(bf16[64,3072]{1,0:T(8,128)(2,1)S(1)} %add.240), channel_id=1, source_target_pairs={{1,0},{2,1},{3,2},{5,4},{6,5},{7,6},{9,8},{10,9},{11,10},{13,12},{... | collective-permute-start | bytes 1179656 | tf_op jit(solution)/shard_map/ppermute | solution.py:417
  94.2 12.9 %collective-permute-start.44 = (bf16[64,3072]{1,0:T(8,128)(2,1)S(1)}, bf16[64,3072]{1,0:T(8,128)(2,1)S(1)}, u32[]{:S(2)}, u32[]{:S(2)}) collective-permute-start(bf16[64,3072]{1,0:T(8,128)(2,1)S(1)} %add.239), channel_id=1, source_target_pairs={{0,1},{1,2},{2,3},{4,5},{5,6},{6,7},{8,9},{9,10},{10,11},{12,13},{... | collective-permute-start | bytes 1179656 | tf_op jit(solution)/shard_map/ppermute | solution.py:416
  102.2 12.4 %collective-permute-start.38 = (bf16[64,3072]{1,0:T(8,128)(2,1)S(1)}, bf16[64,3072]{1,0:T(8,128)(2,1)S(1)}, u32[]{:S(2)}, u32[]{:S(2)}) collective-permute-start(bf16[64,3072]{1,0:T(8,128)(2,1)S(1)} %add.232), channel_id=1, source_target_pairs={{0,1},{1,2},{2,3},{4,5},{5,6},{6,7},{8,9},{9,10},{10,11},{12,13},{... | collective-permute-start | bytes 1179656 | tf_op jit(solution)/shard_map/ppermute | solution.py:416
  115.6 19.6 %collective-permute-start.46 = (bf16[64,6144]{1,0:T(8,128)(2,1)S(1)}, bf16[64,6144]{1,0:T(8,128)(2,1)S(1)}, u32[]{:S(2)}, u32[]{:S(2)}) collective-permute-start(bf16[64,6144]{1,0:T(8,128)(2,1)S(1)} %fusion.7.refs_1_), channel_id=1, source_target_pairs={{0,1},{1,2},{2,3},{4,5},{5,6},{6,7},{8,9},{9,10},{10,11},{12,13},{... | collective-permute-start | bytes 2359304 | tf_op jit(solution)/shard_map/ppermute | solution.py:429
  120.2 19.7 %collective-permute-start.47 = (bf16[64,6144]{1,0:T(8,128)(2,1)S(1)}, bf16[64,6144]{1,0:T(8,128)(2,1)S(1)}, u32[]{:S(2)}, u32[]{:S(2)}) collective-permute-start(bf16[64,6144]{1,0:T(8,128)(2,1)S(1)} %fusion.7.refs_1_), channel_id=1, source_target_pairs={{1,0},{2,1},{3,2},{5,4},{6,5},{7,6},{9,8},{10,9},{11,10},{13,12},{... | collective-permute-start | bytes 2359304 | tf_op jit(solution)/shard_map/ppermute | solution.py:430
  140.0 12.9 %collective-permute-start.49 = (bf16[64,3072]{1,0:T(8,128)(2,1)S(1)}, bf16[64,3072]{1,0:T(8,128)(2,1)}, u32[]{:S(2)}, u32[]{:S(2)}) collective-permute-start(bf16[64,3072]{1,0:T(8,128)(2,1)S(1)} %get-tuple-element.310.refs_8_), channel_id=1, source_target_pairs={{1,0},{2,1},{3,2},{5,4},{6,5},{7,6},{9,8},{10,9},{11,10},{13,12},{... | collective-permute-start | bytes 1179656 | tf_op jit(solution)/shard_map/ppermute | solution.py:451
  147.0 14.1 %collective-permute-start.51 = (bf16[64,3072]{1,0:T(8,128)(2,1)S(1)}, bf16[64,3072]{1,0:T(8,128)(2,1)S(1)}, u32[]{:S(2)}, u32[]{:S(2)}) collective-permute-start(bf16[64,3072]{1,0:T(8,128)(2,1)S(1)} %get-tuple-element.309.refs_9_), channel_id=1, source_target_pairs={{1,0},{2,1},{3,2},{5,4},{6,5},{7,6},{9,8},{10,9},{11,10},{13,12},{... | collective-permute-start | bytes 1179656 | tf_op jit(solution)/shard_map/ppermute | solution.py:451
  148.4 14.1 %collective-permute-start.50 = (bf16[64,3072]{1,0:T(8,128)(2,1)S(1)}, bf16[64,3072]{1,0:T(8,128)(2,1)S(1)}, u32[]{:S(2)}, u32[]{:S(2)}) collective-permute-start(bf16[64,3072]{1,0:T(8,128)(2,1)S(1)} %get-tuple-element.311.refs_3_), channel_id=1, source_target_pairs={{0,1},{1,2},{2,3},{4,5},{5,6},{6,7},{8,9},{9,10},{10,11},{12,13},{... | collective-permute-start | bytes 1179656 | tf_op jit(solution)/shard_map/ppermute | solution.py:451
  155.3 15.6 %collective-permute-start.52 = (bf16[64,3072]{1,0:T(8,128)(2,1)S(1)}, bf16[64,3072]{1,0:T(8,128)(2,1)S(1)}, u32[]{:S(2)}, u32[]{:S(2)}) collective-permute-start(bf16[64,3072]{1,0:T(8,128)(2,1)S(1)} %get-tuple-element.320.refs_4_), channel_id=1, source_target_pairs={{0,1},{1,2},{2,3},{4,5},{5,6},{6,7},{8,9},{9,10},{10,11},{12,13},{... | collective-permute-start | bytes 1179656 | tf_op jit(solution)/shard_map/ppermute | solution.py:451
  162.6 16.8 %collective-permute-start.54 = (bf16[64,3072]{1,0:T(8,128)(2,1)S(1)}, bf16[64,3072]{1,0:T(8,128)(2,1)S(1)}, u32[]{:S(2)}, u32[]{:S(2)}) collective-permute-start(bf16[64,3072]{1,0:T(8,128)(2,1)S(1)} %get-tuple-element.318.refs_5_), channel_id=1, source_target_pairs={{0,1},{1,2},{2,3},{4,5},{5,6},{6,7},{8,9},{9,10},{10,11},{12,13},{... | collective-permute-start | bytes 1179656 | tf_op jit(solution)/shard_map/ppermute | solution.py:451
  167.0 13.9 %collective-permute-start.55 = (bf16[64,3072]{1,0:T(8,128)(2,1)S(1)}, bf16[64,3072]{1,0:T(8,128)(2,1)S(1)}, u32[]{:S(2)}, u32[]{:S(2)}) collective-permute-start(bf16[64,3072]{1,0:T(8,128)(2,1)S(1)} %get-tuple-element.317.refs_11_), channel_id=1, source_target_pairs={{1,0},{2,1},{3,2},{5,4},{6,5},{7,6},{9,8},{10,9},{11,10},{13,12},{... | collective-permute-start | bytes 1179656 | tf_op jit(solution)/shard_map/ppermute | solution.py:451
  181.1 39.4 %collective-permute-start.56 = (bf16[64,6144]{1,0:T(8,128)(2,1)S(1)}, bf16[64,6144]{1,0:T(8,128)(2,1)S(1)}, u32[]{:S(2)}, u32[]{:S(2)}) collective-permute-start(bf16[64,6144]{1,0:T(8,128)(2,1)S(1)} %pad_maximum_fusion.2), channel_id=1, source_target_pairs={{0,1},{1,2},{2,3},{4,5},{5,6},{6,7},{8,9},{9,10},{10,11},{12,13},{... | collective-permute-start | bytes 2359304 | tf_op jit(solution)/shard_map/ppermute | solution.py:460
  184.2 36.2 %collective-permute-start.57 = (bf16[64,6144]{1,0:T(8,128)(2,1)S(1)}, bf16[64,6144]{1,0:T(8,128)(2,1)S(1)}, u32[]{:S(2)}, u32[]{:S(2)}) collective-permute-start(bf16[64,6144]{1,0:T(8,128)(2,1)S(1)} %pad_maximum_fusion.3), channel_id=1, source_target_pairs={{1,0},{2,1},{3,2},{5,4},{6,5},{7,6},{9,8},{10,9},{11,10},{13,12},{... | collective-permute-start | bytes 2359304 | tf_op jit(solution)/shard_map/ppermute | solution.py:461
  221.5 14.0 %collective-permute-start.58 = (bf16[64,3072]{1,0:T(8,128)(2,1)S(1)}, bf16[64,3072]{1,0:T(8,128)(2,1)S(1)}, u32[]{:S(2)}, u32[]{:S(2)}) collective-permute-start(bf16[64,3072]{1,0:T(8,128)(2,1)S(1)} %get-tuple-element.268), channel_id=1, source_target_pairs={{0,1},{4,5},{8,9},{12,13},{16,17},{20,21},{24,25},{28,29}} | collective-permute-start | bytes 1179656 | tf_op jit(solution)/shard_map/ppermute | solution.py:416
  226.7 17.2 %collective-permute-start.64 = (bf16[64,3072]{1,0:T(8,128)(2,1)}, bf16[64,3072]{1,0:T(8,128)(2,1)}, u32[]{:S(2)}, u32[]{:S(2)}) collective-permute-start(bf16[64,3072]{1,0:T(8,128)(2,1)} %get-tuple-element.279), channel_id=1, source_target_pairs={{0,1},{4,5},{8,9},{12,13},{16,17},{20,21},{24,25},{28,29}} | collective-permute-start | bytes 1179656 | tf_op jit(solution)/shard_map/ppermute | solution.py:416
  228.8 15.2 %collective-permute-start.65 = (bf16[64,3072]{1,0:T(8,128)(2,1)}, bf16[64,3072]{1,0:T(8,128)(2,1)}, u32[]{:S(2)}, u32[]{:S(2)}) collective-permute-start(bf16[64,3072]{1,0:T(8,128)(2,1)} %get-tuple-element.277), channel_id=1, source_target_pairs={{3,2},{7,6},{11,10},{15,14},{19,18},{23,22},{27,26},{31,30}} | collective-permute-start | bytes 1179656 | tf_op jit(solution)/shard_map/ppermute | solution.py:417
  245.3 13.9 %collective-permute-start.66 = (bf16[64,3072]{1,0:T(8,128)(2,1)S(1)}, bf16[64,3072]{1,0:T(8,128)(2,1)S(1)}, u32[]{:S(2)}, u32[]{:S(2)}) collective-permute-start(bf16[64,3072]{1,0:T(8,128)(2,1)S(1)} %get-tuple-element.316), channel_id=1, source_target_pairs={{0,1},{1,2},{4,5},{5,6},{8,9},{9,10},{12,13},{13,14},{16,17},{17,1... | collective-permute-start | bytes 1179656 | tf_op jit(solution)/shard_map/ppermute | solution.py:416
  250.4 19.4 %collective-permute-start.60 = (bf16[64,3072]{1,0:T(8,128)(2,1)S(1)}, bf16[64,3072]{1,0:T(8,128)(2,1)S(1)}, u32[]{:S(2)}, u32[]{:S(2)}) collective-permute-start(bf16[64,3072]{1,0:T(8,128)(2,1)S(1)} %get-tuple-element.314), channel_id=1, source_target_pairs={{0,1},{1,2},{4,5},{5,6},{8,9},{9,10},{12,13},{13,14},{16,17},{17,1... | collective-permute-start | bytes 1179656 | tf_op jit(solution)/shard_map/ppermute | solution.py:416
  253.1 16.8 %collective-permute-start.61 = (bf16[64,3072]{1,0:T(8,128)(2,1)S(1)}, bf16[64,3072]{1,0:T(8,128)(2,1)S(1)}, u32[]{:S(2)}, u32[]{:S(2)}) collective-permute-start(bf16[64,3072]{1,0:T(8,128)(2,1)S(1)} %get-tuple-element.313), channel_id=1, source_target_pairs={{2,1},{3,2},{6,5},{7,6},{10,9},{11,10},{14,13},{15,14},{18,17},{19... | collective-permute-start | bytes 1179656 | tf_op jit(solution)/shard_map/ppermute | solution.py:417
  260.2 20.1 %collective-permute-start.69 = (bf16[64,3072]{1,0:T(8,128)(2,1)S(1)}, bf16[64,3072]{1,0:T(8,128)(2,1)S(1)}, u32[]{:S(2)}, u32[]{:S(2)}) collective-permute-start(bf16[64,3072]{1,0:T(8,128)(2,1)S(1)} %add.273), channel_id=1, source_target_pairs={{1,0},{2,1},{3,2},{5,4},{6,5},{7,6},{9,8},{10,9},{11,10},{13,12},{... | collective-permute-start | bytes 1179656 | tf_op jit(solution)/shard_map/ppermute | solution.py:417
  262.8 17.5 %collective-permute-start.68 = (bf16[64,3072]{1,0:T(8,128)(2,1)S(1)}, bf16[64,3072]{1,0:T(8,128)(2,1)S(1)}, u32[]{:S(2)}, u32[]{:S(2)}) collective-permute-start(bf16[64,3072]{1,0:T(8,128)(2,1)S(1)} %add.272), channel_id=1, source_target_pairs={{0,1},{1,2},{2,3},{4,5},{5,6},{6,7},{8,9},{9,10},{10,11},{12,13},{... | collective-permute-start | bytes 1179656 | tf_op jit(solution)/shard_map/ppermute | solution.py:416
  270.0 13.1 %collective-permute-start.63 = (bf16[64,3072]{1,0:T(8,128)(2,1)S(1)}, bf16[64,3072]{1,0:T(8,128)(2,1)S(1)}, u32[]{:S(2)}, u32[]{:S(2)}) collective-permute-start(bf16[64,3072]{1,0:T(8,128)(2,1)S(1)} %add.263), channel_id=1, source_target_pairs={{1,0},{2,1},{3,2},{5,4},{6,5},{7,6},{9,8},{10,9},{11,10},{13,12},{... | collective-permute-start | bytes 1179656 | tf_op jit(solution)/shard_map/ppermute | solution.py:417
  271.4 13.9 %collective-permute-start.62 = (bf16[64,3072]{1,0:T(8,128)(2,1)S(1)}, bf16[64,3072]{1,0:T(8,128)(2,1)S(1)}, u32[]{:S(2)}, u32[]{:S(2)}) collective-permute-start(bf16[64,3072]{1,0:T(8,128)(2,1)S(1)} %add.262), channel_id=1, source_target_pairs={{0,1},{1,2},{2,3},{4,5},{5,6},{6,7},{8,9},{9,10},{10,11},{12,13},{... | collective-permute-start | bytes 1179656 | tf_op jit(solution)/shard_map/ppermute | solution.py:416
  (66 other events, 713.5 us)

commit v3 on v2

--- a/solution.py
+++ b/solution.py
@@ -15,9 +15,8 @@
 LINE = 4
 SUM_ROWS = 16
 TILE = 256
-VMEM_SMALL = 12 * 1024 * 1024
-VMEM_HELD = 20 * 1024 * 1024
-VMEM_LARGE = 40 * 1024 * 1024
+VMEM_HELD = 21 * 1024 * 1024
+VMEM_LARGE = 28 * 1024 * 1024
 
 
 def attention_kernel(slots, together, held, pairs, sharing, block_rows, plan, *refs):
@@ -170,7 +169,7 @@
             ],
         ),
         out_shape=shapes,
-        compiler_params=pltpu.CompilerParams(vmem_limit_bytes=VMEM_LARGE),
+        compiler_params=pltpu.CompilerParams(vmem_limit_bytes=VMEM_HELD),
         cost_estimate=pl.CostEstimate(
             flops=40 * slots * half * width * count,
             bytes_accessed=2 * (2 * slots * half * width + count * 2 * pairs * HD + weight.size),
@@ -551,8 +550,6 @@
         if beside is not None:
             terms, beside = lax.optimization_barrier((terms, beside))
         sums, marks = reduce_line(terms)
-        if beside is not None:
-            beside = (beside[0], lax.optimization_barrier((beside[1], marks[0]))[0][0, 0] > half)
         if line:
             normed, _ = lax.optimization_barrier((normed, marks[0]))
         share = share_of(which, normed)
@@ -580,9 +577,9 @@
     asked[1], _ = lax.optimization_barrier((asked[1], normed))
     sources, second_sum = gather_line(normed, project(1))
     second_half = (hidden[half:].astype(jnp.float32) + second_sum).astype(jnp.bfloat16)
-    part, (second_half, crowded) = expert(0, normed, sources, (second_half, fullest))
-    part, late, crowded = lax.optimization_barrier((part, second_half, crowded))
-    late = lax.cond(crowded, late_expert, jnp.zeros_like, late)
+    part, second_half = expert(0, normed, sources, second_half)
+    part, late = lax.optimization_barrier((part, second_half))
+    late = lax.cond(fullest[0, 0] > half, late_expert, jnp.zeros_like, late)
     return (restore([first_half, second_half]), restore([part, late]))
 
 

time: 294 us -> 293 us (level)
  the two profiles are of different devices: /device:TPU:0 before, /device:TPU:26 now
where the time goes in v3:
time: 293 us; the launch traced here: 292 us
  starting transfers between devices  103 us (35%)
  waiting for transfers between devices  76 us (26%)
  Pallas kernels  70.5 us (24%)
  local copies, waits for them, and re-layouts  19.8 us (7%)
  other arithmetic  14.8 us (5%)
  matrix products  5.31 us (2%)
    ppermute x12, starting transfers between devices, reduce_line(): left = lax.ppermute(sent[1], 'tp', lefts(s))  45.1 us
    pallas_call x1, Pallas kernels, expert_rows(): pl.pallas_call(functools.partial(expert_kernel, [len(source) for source i...  34.8 us
    pallas_call x2, Pallas kernels, attend(): pl.pallas_call(kernel, grid_spec=pltpu.PrefetchScalarGridSpec(num_scalar_...  31.1 us
    ppermute x12, waiting for transfers between devices, reduce_line(): left = lax.ppermute(sent[1], 'tp', lefts(s))  25.4 us
    ppermute x9, waiting for transfers between devices, shift(): lax.ppermute(parts[s], 'tp', moves[s])  19.8 us
    ppermute x4, starting transfers between devices, gather_line(): lax.ppermute(left, 'tp', to_left)  19.2 us
    unnamed x111, local copies, waits for them, and re-layouts  18.6 us
    ppermute x4, waiting for transfers between devices, gather_line(): lax.ppermute(right, 'tp', to_right)  16 us
  transfers between devices with their start and end apart: 48, of which 24 were waited for; matrix products, arithmetic and copies ran while one was open for 6% of the time, Pallas kernels for 24%

profile of v3, /device:TPU:26, one launch (start us, length us, event | category | flops | bytes accessed | tf_op | source)
XLA Modules:
  0.0 291.5 jit_solution(8657149213305152315)
XLA Ops:
  5.9 2.7 collective-permute-done.22
  8.7 7.7 %collective-permute-done.23 = bf16[128,512]{1,0:T(8,128)(2,1)S(1)} collective-permute-done((bf16[128,512]{1,0:T(8,128)(2,1)}, bf16[128,512]{1,0:T(8,128)(2,1)S(1)}, u32[]{:S(2)}, u32[]{:S(2)}) %collective-permute-start.23) | collective-permute-done | bytes 131104 | tf_op jit(solution)/shard_map/ppermute | solution.py:387
  17.6 2.7 shard_map.132
  23.7 2.6 collective-permute-done.26.refs_2_
  26.9 6.8 %collective-permute-done.27.refs_4_ = bf16[64,1024]{1,0:T(8,128)(2,1)S(1)} collective-permute-done((bf16[64,1024]{1,0:T(8,128)(2,1)}, bf16[64,1024]{1,0:T(8,128)(2,1)S(1)}, u32[]{:S(2)}, u32[]{:S(2)}) %collective-permute-start.27) | collective-permute-done | bytes 131104 | tf_op jit(solution)/shard_map/ppermute | solution.py:387
  40.3 4.6 %copy-done.23 = bf16[1024,6144]{1,0:T(8,128)(2,1)S(1)} copy-done((bf16[1024,6144]{1,0:T(8,128)(2,1)S(1)}, bf16[1024,6144]{1,0:T(8,128)(2,1)}, u32[]{:S(2)}) %copy-start.23) | copy-done | bytes 12582936
  51.3 15.5 %shard_map.133 = (bf16[64,3072]{1,0:T(8,128)(2,1)S(1)}, bf16[64,3072]{1,0:T(8,128)(2,1)S(1)}, bf16[64,3072]{1,0:T(8,128)(2,1)S(1)}, bf16[64,3072]{1,0:T(8,128)(2...) custom-call(s32[4]{0:T(128)S(1)} %copy-done.41, ...), custom_call_target="tpu_custom_call" | custom-call | flops 21474836480 | bytes 15728640 | tf_op jit(solution)/shard_map/pallas_call | solution.py:150
  67.5 2.8 collective-permute-start.41
  72.3 6.1 %collective-permute-done.41 = bf16[64,3072]{1,0:T(8,128)(2,1)S(1)} collective-permute-done((bf16[64,3072]{1,0:T(8,128)(2,1)S(1)}, bf16[64,3072]{1,0:T(8,128)(2,1)S(1)}, u32[]{:S(2)}, u32[]{:S(2)}) %collective-permute-start.41) | collective-permute-done | bytes 393248 | tf_op jit(solution)/shard_map/ppermute | solution.py:416
  80.8 5.0 %collective-permute-start.43 = (bf16[64,3072]{1,0:T(8,128)(2,1)}, bf16[64,3072]{1,0:T(8,128)(2,1)}, u32[]{:S(2)}, u32[]{:S(2)}) collective-permute-start(bf16[64,3072]{1,0:T(8,128)(2,1)} %get-tuple-element.317), channel_id=1, source_target_pairs={{2,1},{3,2},{6,5},{7,6},{10,9},{11,10},{14,13},{15,14},{18,17},{19... | collective-permute-start | bytes 1179656 | tf_op jit(solution)/shard_map/ppermute | solution.py:416
  89.3 5.0 %collective-permute-start.37 = (bf16[64,3072]{1,0:T(8,128)(2,1)}, bf16[64,3072]{1,0:T(8,128)(2,1)}, u32[]{:S(2)}, u32[]{:S(2)}) collective-permute-start(bf16[64,3072]{1,0:T(8,128)(2,1)} %get-tuple-element.315), channel_id=1, source_target_pairs={{2,1},{3,2},{6,5},{7,6},{10,9},{11,10},{14,13},{15,14},{18,17},{19... | collective-permute-start | bytes 1179656 | tf_op jit(solution)/shard_map/ppermute | solution.py:416
  97.3 4.2 %collective-permute-start.45 = (bf16[64,3072]{1,0:T(8,128)(2,1)S(1)}, bf16[64,3072]{1,0:T(8,128)(2,1)S(1)}, u32[]{:S(2)}, u32[]{:S(2)}) collective-permute-start(bf16[64,3072]{1,0:T(8,128)(2,1)S(1)} %add.240), channel_id=1, source_target_pairs={{1,0},{2,1},{3,2},{5,4},{6,5},{7,6},{9,8},{10,9},{11,10},{13,12},{... | collective-permute-start | bytes 1179656 | tf_op jit(solution)/shard_map/ppermute | solution.py:416
  105.0 4.6 %collective-permute-start.39 = (bf16[64,3072]{1,0:T(8,128)(2,1)S(1)}, bf16[64,3072]{1,0:T(8,128)(2,1)S(1)}, u32[]{:S(2)}, u32[]{:S(2)}) collective-permute-start(bf16[64,3072]{1,0:T(8,128)(2,1)S(1)} %add.233), channel_id=1, source_target_pairs={{1,0},{2,1},{3,2},{5,4},{6,5},{7,6},{9,8},{10,9},{11,10},{13,12},{... | collective-permute-start | bytes 1179656 | tf_op jit(solution)/shard_map/ppermute | solution.py:416
  112.2 2.9 %collective-permute-done.44 = bf16[64,3072]{1,0:T(8,128)(2,1)S(1)} collective-permute-done((bf16[64,3072]{1,0:T(8,128)(2,1)S(1)}, bf16[64,3072]{1,0:T(8,128)(2,1)S(1)}, u32[]{:S(2)}, u32[]{:S(2)}) %collective-permute-start.44) | collective-permute-done | bytes 393248 | tf_op jit(solution)/shard_map/ppermute | solution.py:415
  115.1 5.5 %collective-permute-done.39 = bf16[64,3072]{1,0:T(8,128)(2,1)S(1)} collective-permute-done((bf16[64,3072]{1,0:T(8,128)(2,1)S(1)}, bf16[64,3072]{1,0:T(8,128)(2,1)S(1)}, u32[]{:S(2)}, u32[]{:S(2)}) %collective-permute-start.39) | collective-permute-done | bytes 393248 | tf_op jit(solution)/shard_map/ppermute | solution.py:416
  120.6 3.5 %collective-permute-done.38 = bf16[64,3072]{1,0:T(8,128)(2,1)S(1)} collective-permute-done((bf16[64,3072]{1,0:T(8,128)(2,1)S(1)}, bf16[64,3072]{1,0:T(8,128)(2,1)S(1)}, u32[]{:S(2)}, u32[]{:S(2)}) %collective-permute-start.38) | collective-permute-done | bytes 393248 | tf_op jit(solution)/shard_map/ppermute | solution.py:415
  126.5 4.6 %collective-permute-start.47 = (bf16[64,6144]{1,0:T(8,128)(2,1)S(1)}, bf16[64,6144]{1,0:T(8,128)(2,1)S(1)}, u32[]{:S(2)}, u32[]{:S(2)}) collective-permute-start(bf16[64,6144]{1,0:T(8,128)(2,1)S(1)} %fusion.7.refs_1_), channel_id=1, source_target_pairs={{1,0},{2,1},{3,2},{5,4},{6,5},{7,6},{9,8},{10,9},{11,10},{13,12},{... | collective-permute-start | bytes 2359304 | tf_op jit(solution)/shard_map/ppermute | solution.py:429
  131.2 15.6 %shard_map.134 = (bf16[64,3072]{1,0:T(8,128)(2,1)S(1)}, bf16[64,3072]{1,0:T(8,128)(2,1)S(1)}, bf16[64,3072]{1,0:T(8,128)(2,1)S(1)}, bf16[64,3072]{1,0:T(8,128)(2...) custom-call(s32[4]{0:T(128)S(1)} %copy-done.41, ...), custom_call_target="tpu_custom_call" | custom-call | flops 21474836480 | bytes 15728640 | tf_op jit(solution)/shard_map/pallas_call | solution.py:150
  148.5 5.3 %collective-permute-start.49 = (bf16[64,3072]{1,0:T(8,128)(2,1)S(1)}, bf16[64,3072]{1,0:T(8,128)(2,1)}, u32[]{:S(2)}, u32[]{:S(2)}) collective-permute-start(bf16[64,3072]{1,0:T(8,128)(2,1)S(1)} %get-tuple-element.304.refs_8_), channel_id=1, source_target_pairs={{1,0},{2,1},{3,2},{5,4},{6,5},{7,6},{9,8},{10,9},{11,10},{13,12},{... | collective-permute-start | bytes 1179656 | tf_op jit(solution)/shard_map/ppermute | solution.py:450
  155.3 4.7 %collective-permute-start.51 = (bf16[64,3072]{1,0:T(8,128)(2,1)S(1)}, bf16[64,3072]{1,0:T(8,128)(2,1)S(1)}, u32[]{:S(2)}, u32[]{:S(2)}) collective-permute-start(bf16[64,3072]{1,0:T(8,128)(2,1)S(1)} %get-tuple-element.303.refs_9_), channel_id=1, source_target_pairs={{1,0},{2,1},{3,2},{5,4},{6,5},{7,6},{9,8},{10,9},{11,10},{13,12},{... | collective-permute-start | bytes 1179656 | tf_op jit(solution)/shard_map/ppermute | solution.py:450
  162.4 5.6 %collective-permute-done.48 = bf16[64,3072]{1,0:T(8,128)(2,1)} collective-permute-done((bf16[64,3072]{1,0:T(8,128)(2,1)S(1)}, bf16[64,3072]{1,0:T(8,128)(2,1)}, u32[]{:S(2)}, u32[]{:S(2)}) %collective-permute-start.48) | collective-permute-done | bytes 393248 | tf_op jit(solution)/shard_map/ppermute | solution.py:450
  170.7 4.6 %collective-permute-start.53 = (bf16[64,3072]{1,0:T(8,128)(2,1)S(1)}, bf16[64,3072]{1,0:T(8,128)(2,1)S(1)}, u32[]{:S(2)}, u32[]{:S(2)}) collective-permute-start(bf16[64,3072]{1,0:T(8,128)(2,1)S(1)} %get-tuple-element.313.refs_10_), channel_id=1, source_target_pairs={{1,0},{2,1},{3,2},{5,4},{6,5},{7,6},{9,8},{10,9},{11,10},{13,12},{... | collective-permute-start | bytes 1179656 | tf_op jit(solution)/shard_map/ppermute | solution.py:450
  177.7 4.6 %collective-permute-start.55 = (bf16[64,3072]{1,0:T(8,128)(2,1)S(1)}, bf16[64,3072]{1,0:T(8,128)(2,1)S(1)}, u32[]{:S(2)}, u32[]{:S(2)}) collective-permute-start(bf16[64,3072]{1,0:T(8,128)(2,1)S(1)} %get-tuple-element.311.refs_11_), channel_id=1, source_target_pairs={{1,0},{2,1},{3,2},{5,4},{6,5},{7,6},{9,8},{10,9},{11,10},{13,12},{... | collective-permute-start | bytes 1179656 | tf_op jit(solution)/shard_map/ppermute | solution.py:450
  184.9 6.8 %collective-permute-done.54.refs_7_ = bf16[64,3072]{1,0:T(8,128)(2,1)S(1)} collective-permute-done((bf16[64,3072]{1,0:T(8,128)(2,1)S(1)}, bf16[64,3072]{1,0:T(8,128)(2,1)S(1)}, u32[]{:S(2)}, u32[]{:S(2)}) %collective-permute-start.54) | collective-permute-done | bytes 393248 | tf_op jit(solution)/shard_map/ppermute | solution.py:450
  193.5 4.7 %collective-permute-start.57 = (bf16[64,6144]{1,0:T(8,128)(2,1)S(1)}, bf16[64,6144]{1,0:T(8,128)(2,1)S(1)}, u32[]{:S(2)}, u32[]{:S(2)}) collective-permute-start(bf16[64,6144]{1,0:T(8,128)(2,1)S(1)} %pad_maximum_fusion.3), channel_id=1, source_target_pairs={{1,0},{2,1},{3,2},{5,4},{6,5},{7,6},{9,8},{10,9},{11,10},{13,12},{... | collective-permute-start | bytes 2359304 | tf_op jit(solution)/shard_map/ppermute | solution.py:460
  198.2 34.8 %shard_map.135 = (bf16[64,3072]{1,0:T(8,128)(2,1)S(1)}, bf16[64,3072]{1,0:T(8,128)(2,1)S(1)}, bf16[64,3072]{1,0:T(8,128)(2,1)S(1)}, bf16[64,3072]{1,0:T(8,128)(2...) custom-call(s32[1]{0:T(128)} %bitcast.6.mine.refs_0_, ...), custom_call_target="tpu_custom_call" | custom-call | flops 19327352832 | bytes 75497472 | tf_op jit(solution)/shard_map/pallas_call | solution.py:243
  240.6 6.0 %collective-permute-done.65 = bf16[64,3072]{1,0:T(8,128)(2,1)S(1)} collective-permute-done((bf16[64,3072]{1,0:T(8,128)(2,1)}, bf16[64,3072]{1,0:T(8,128)(2,1)S(1)}, u32[]{:S(2)}, u32[]{:S(2)}) %collective-permute-start.65) | collective-permute-done | bytes 393248 | tf_op jit(solution)/shard_map/ppermute | solution.py:416
  248.3 4.9 %collective-permute-start.67 = (bf16[64,3072]{1,0:T(8,128)(2,1)S(1)}, bf16[64,3072]{1,0:T(8,128)(2,1)S(1)}, u32[]{:S(2)}, u32[]{:S(2)}) collective-permute-start(bf16[64,3072]{1,0:T(8,128)(2,1)S(1)} %get-tuple-element.309), channel_id=1, source_target_pairs={{2,1},{3,2},{6,5},{7,6},{10,9},{11,10},{14,13},{15,14},{18,17},{19... | collective-permute-start | bytes 1179656 | tf_op jit(solution)/shard_map/ppermute | solution.py:416
  255.9 4.9 %collective-permute-start.61 = (bf16[64,3072]{1,0:T(8,128)(2,1)S(1)}, bf16[64,3072]{1,0:T(8,128)(2,1)S(1)}, u32[]{:S(2)}, u32[]{:S(2)}) collective-permute-start(bf16[64,3072]{1,0:T(8,128)(2,1)S(1)} %get-tuple-element.307), channel_id=1, source_target_pairs={{2,1},{3,2},{6,5},{7,6},{10,9},{11,10},{14,13},{15,14},{18,17},{19... | collective-permute-start | bytes 1179656 | tf_op jit(solution)/shard_map/ppermute | solution.py:416
  264.4 4.5 %collective-permute-start.69 = (bf16[64,3072]{1,0:T(8,128)(2,1)S(1)}, bf16[64,3072]{1,0:T(8,128)(2,1)S(1)}, u32[]{:S(2)}, u32[]{:S(2)}) collective-permute-start(bf16[64,3072]{1,0:T(8,128)(2,1)S(1)} %add.273), channel_id=1, source_target_pairs={{1,0},{2,1},{3,2},{5,4},{6,5},{7,6},{9,8},{10,9},{11,10},{13,12},{... | collective-permute-start | bytes 1179656 | tf_op jit(solution)/shard_map/ppermute | solution.py:416
  271.8 4.4 %collective-permute-start.63 = (bf16[64,3072]{1,0:T(8,128)(2,1)S(1)}, bf16[64,3072]{1,0:T(8,128)(2,1)S(1)}, u32[]{:S(2)}, u32[]{:S(2)}) collective-permute-start(bf16[64,3072]{1,0:T(8,128)(2,1)S(1)} %add.263), channel_id=1, source_target_pairs={{1,0},{2,1},{3,2},{5,4},{6,5},{7,6},{9,8},{10,9},{11,10},{13,12},{... | collective-permute-start | bytes 1179656 | tf_op jit(solution)/shard_map/ppermute | solution.py:416
  280.1 3.5 %collective-permute-done.68 = bf16[64,3072]{1,0:T(8,128)(2,1)S(1)} collective-permute-done((bf16[64,3072]{1,0:T(8,128)(2,1)S(1)}, bf16[64,3072]{1,0:T(8,128)(2,1)S(1)}, u32[]{:S(2)}, u32[]{:S(2)}) %collective-permute-start.68) | collective-permute-done | bytes 393248 | tf_op jit(solution)/shard_map/ppermute | solution.py:415
  (224 shorter events, 87.4 us)
Async XLA Ops:
  16.5 18.5 %collective-permute-start.25 = (bf16[512,512]{1,0:T(8,128)(2,1)S(1)}, bf16[512,512]{1,0:T(8,128)(2,1)S(1)}, u32[]{:S(2)}, u32[]{:S(2)}) collective-permute-start(bf16[512,512]{1,0:T(8,128)(2,1)S(1)} %constant_dynamic-update-slice_fusion.refs_7_), channel_id=1, source_target_pairs={{0,8},{4,12},{8,0},{12,4},{1,9},{5,13},{9,1},{13,5},{2,10},{6,14},... | collective-permute-start | bytes 1572872 | tf_op jit(solution)/shard_map/ppermute | solution.py:493
  23.7 14.8 %collective-permute-start.29 = (bf16[512,512]{1,0:T(8,128)(2,1)S(1)}, bf16[512,512]{1,0:T(8,128)(2,1)S(1)}, u32[]{:S(2)}, u32[]{:S(2)}) collective-permute-start(bf16[512,512]{1,0:T(8,128)(2,1)S(1)} %constant_dynamic-update-slice_fusion.refs_7_), channel_id=1, source_target_pairs={{0,4},{4,0},{8,12},{12,8},{1,5},{5,1},{9,13},{13,9},{2,6},{6,2},{1... | collective-permute-start | bytes 1572872 | tf_op jit(solution)/shard_map/ppermute | solution.py:493
  35.8 31.0 %collective-permute-start.31 = (bf16[64,1024]{1,0:T(8,128)(2,1)}, bf16[64,1024]{1,0:T(8,128)(2,1)}, u32[]{:S(2)}, u32[]{:S(2)}) collective-permute-start(bf16[64,1024]{1,0:T(8,128)(2,1)} %get-tuple-element.200), channel_id=1, source_target_pairs={{0,1},{1,2},{2,3},{3,0},{4,5},{5,6},{6,7},{7,4},{8,9},{9,10},{10,1... | collective-permute-start | bytes 393224 | tf_op jit(solution)/shard_map/ppermute | solution.py:387
  35.8 31.0 %collective-permute-start.32 = (bf16[64,1024]{1,0:T(8,128)(2,1)}, bf16[64,1024]{1,0:T(8,128)(2,1)}, u32[]{:S(2)}, u32[]{:S(2)}) collective-permute-start(bf16[64,1024]{1,0:T(8,128)(2,1)} %get-tuple-element.201), channel_id=1, source_target_pairs={{0,2},{1,3},{2,0},{3,1},{4,6},{5,7},{6,4},{7,5},{8,10},{9,11},{10,... | collective-permute-start | bytes 393224 | tf_op jit(solution)/shard_map/ppermute | solution.py:387
  36.4 30.4 %collective-permute-start.33 = (bf16[64,1024]{1,0:T(8,128)(2,1)}, bf16[64,1024]{1,0:T(8,128)(2,1)}, u32[]{:S(2)}, u32[]{:S(2)}) collective-permute-start(bf16[64,1024]{1,0:T(8,128)(2,1)} %get-tuple-element.202), channel_id=1, source_target_pairs={{0,3},{1,0},{2,1},{3,2},{4,7},{5,4},{6,5},{7,6},{8,11},{9,8},{10,9... | collective-permute-start | bytes 393224 | tf_op jit(solution)/shard_map/ppermute | solution.py:387
  70.3 15.5 %collective-permute-start.34 = (bf16[64,3072]{1,0:T(8,128)(2,1)S(1)}, bf16[64,3072]{1,0:T(8,128)(2,1)S(1)}, u32[]{:S(2)}, u32[]{:S(2)}) collective-permute-start(bf16[64,3072]{1,0:T(8,128)(2,1)S(1)} %get-tuple-element.203), channel_id=1, source_target_pairs={{0,1},{4,5},{8,9},{12,13},{16,17},{20,21},{24,25},{28,29}} | collective-permute-start | bytes 1179656 | tf_op jit(solution)/shard_map/ppermute | solution.py:415
  71.0 15.9 %collective-permute-start.35 = (bf16[64,3072]{1,0:T(8,128)(2,1)S(1)}, bf16[64,3072]{1,0:T(8,128)(2,1)S(1)}, u32[]{:S(2)}, u32[]{:S(2)}) collective-permute-start(bf16[64,3072]{1,0:T(8,128)(2,1)S(1)} %get-tuple-element.204), channel_id=1, source_target_pairs={{3,2},{7,6},{11,10},{15,14},{19,18},{23,22},{27,26},{31,30}} | collective-permute-start | bytes 1179656 | tf_op jit(solution)/shard_map/ppermute | solution.py:416
  79.4 16.3 %collective-permute-start.42 = (bf16[64,3072]{1,0:T(8,128)(2,1)}, bf16[64,3072]{1,0:T(8,128)(2,1)}, u32[]{:S(2)}, u32[]{:S(2)}) collective-permute-start(bf16[64,3072]{1,0:T(8,128)(2,1)} %get-tuple-element.318), channel_id=1, source_target_pairs={{0,1},{1,2},{4,5},{5,6},{8,9},{9,10},{12,13},{13,14},{16,17},{17,1... | collective-permute-start | bytes 1179656 | tf_op jit(solution)/shard_map/ppermute | solution.py:415
  80.8 14.9 %collective-permute-start.43 = (bf16[64,3072]{1,0:T(8,128)(2,1)}, bf16[64,3072]{1,0:T(8,128)(2,1)}, u32[]{:S(2)}, u32[]{:S(2)}) collective-permute-start(bf16[64,3072]{1,0:T(8,128)(2,1)} %get-tuple-element.317), channel_id=1, source_target_pairs={{2,1},{3,2},{6,5},{7,6},{10,9},{11,10},{14,13},{15,14},{18,17},{19... | collective-permute-start | bytes 1179656 | tf_op jit(solution)/shard_map/ppermute | solution.py:416
  87.9 16.1 %collective-permute-start.36 = (bf16[64,3072]{1,0:T(8,128)(2,1)}, bf16[64,3072]{1,0:T(8,128)(2,1)}, u32[]{:S(2)}, u32[]{:S(2)}) collective-permute-start(bf16[64,3072]{1,0:T(8,128)(2,1)} %get-tuple-element.316), channel_id=1, source_target_pairs={{0,1},{1,2},{4,5},{5,6},{8,9},{9,10},{12,13},{13,14},{16,17},{17,1... | collective-permute-start | bytes 1179656 | tf_op jit(solution)/shard_map/ppermute | solution.py:415
  89.3 14.7 %collective-permute-start.37 = (bf16[64,3072]{1,0:T(8,128)(2,1)}, bf16[64,3072]{1,0:T(8,128)(2,1)}, u32[]{:S(2)}, u32[]{:S(2)}) collective-permute-start(bf16[64,3072]{1,0:T(8,128)(2,1)} %get-tuple-element.315), channel_id=1, source_target_pairs={{2,1},{3,2},{6,5},{7,6},{10,9},{11,10},{14,13},{15,14},{18,17},{19... | collective-permute-start | bytes 1179656 | tf_op jit(solution)/shard_map/ppermute | solution.py:416
  97.3 14.9 %collective-permute-start.45 = (bf16[64,3072]{1,0:T(8,128)(2,1)S(1)}, bf16[64,3072]{1,0:T(8,128)(2,1)S(1)}, u32[]{:S(2)}, u32[]{:S(2)}) collective-permute-start(bf16[64,3072]{1,0:T(8,128)(2,1)S(1)} %add.240), channel_id=1, source_target_pairs={{1,0},{2,1},{3,2},{5,4},{6,5},{7,6},{9,8},{10,9},{11,10},{13,12},{... | collective-permute-start | bytes 1179656 | tf_op jit(solution)/shard_map/ppermute | solution.py:416
  105.0 15.6 %collective-permute-start.39 = (bf16[64,3072]{1,0:T(8,128)(2,1)S(1)}, bf16[64,3072]{1,0:T(8,128)(2,1)S(1)}, u32[]{:S(2)}, u32[]{:S(2)}) collective-permute-start(bf16[64,3072]{1,0:T(8,128)(2,1)S(1)} %add.233), channel_id=1, source_target_pairs={{1,0},{2,1},{3,2},{5,4},{6,5},{7,6},{9,8},{10,9},{11,10},{13,12},{... | collective-permute-start | bytes 1179656 | tf_op jit(solution)/shard_map/ppermute | solution.py:416
  125.1 22.1 %collective-permute-start.46 = (bf16[64,6144]{1,0:T(8,128)(2,1)S(1)}, bf16[64,6144]{1,0:T(8,128)(2,1)S(1)}, u32[]{:S(2)}, u32[]{:S(2)}) collective-permute-start(bf16[64,6144]{1,0:T(8,128)(2,1)S(1)} %fusion.7.refs_1_), channel_id=1, source_target_pairs={{0,1},{1,2},{2,3},{4,5},{5,6},{6,7},{8,9},{9,10},{10,11},{12,13},{... | collective-permute-start | bytes 2359304 | tf_op jit(solution)/shard_map/ppermute | solution.py:428
  126.5 21.9 %collective-permute-start.47 = (bf16[64,6144]{1,0:T(8,128)(2,1)S(1)}, bf16[64,6144]{1,0:T(8,128)(2,1)S(1)}, u32[]{:S(2)}, u32[]{:S(2)}) collective-permute-start(bf16[64,6144]{1,0:T(8,128)(2,1)S(1)} %fusion.7.refs_1_), channel_id=1, source_target_pairs={{1,0},{2,1},{3,2},{5,4},{6,5},{7,6},{9,8},{10,9},{11,10},{13,12},{... | collective-permute-start | bytes 2359304 | tf_op jit(solution)/shard_map/ppermute | solution.py:429
  148.5 13.9 %collective-permute-start.49 = (bf16[64,3072]{1,0:T(8,128)(2,1)S(1)}, bf16[64,3072]{1,0:T(8,128)(2,1)}, u32[]{:S(2)}, u32[]{:S(2)}) collective-permute-start(bf16[64,3072]{1,0:T(8,128)(2,1)S(1)} %get-tuple-element.304.refs_8_), channel_id=1, source_target_pairs={{1,0},{2,1},{3,2},{5,4},{6,5},{7,6},{9,8},{10,9},{11,10},{13,12},{... | collective-permute-start | bytes 1179656 | tf_op jit(solution)/shard_map/ppermute | solution.py:450
  154.0 14.0 %collective-permute-start.48 = (bf16[64,3072]{1,0:T(8,128)(2,1)S(1)}, bf16[64,3072]{1,0:T(8,128)(2,1)}, u32[]{:S(2)}, u32[]{:S(2)}) collective-permute-start(bf16[64,3072]{1,0:T(8,128)(2,1)S(1)} %get-tuple-element.306.refs_2_), channel_id=1, source_target_pairs={{0,1},{1,2},{2,3},{4,5},{5,6},{6,7},{8,9},{9,10},{10,11},{12,13},{... | collective-permute-start | bytes 1179656 | tf_op jit(solution)/shard_map/ppermute | solution.py:450
  155.3 20.0 %collective-permute-start.51 = (bf16[64,3072]{1,0:T(8,128)(2,1)S(1)}, bf16[64,3072]{1,0:T(8,128)(2,1)S(1)}, u32[]{:S(2)}, u32[]{:S(2)}) collective-permute-start(bf16[64,3072]{1,0:T(8,128)(2,1)S(1)} %get-tuple-element.303.refs_9_), channel_id=1, source_target_pairs={{1,0},{2,1},{3,2},{5,4},{6,5},{7,6},{9,8},{10,9},{11,10},{13,12},{... | collective-permute-start | bytes 1179656 | tf_op jit(solution)/shard_map/ppermute | solution.py:450
  160.0 16.3 %collective-permute-start.50 = (bf16[64,3072]{1,0:T(8,128)(2,1)S(1)}, bf16[64,3072]{1,0:T(8,128)(2,1)S(1)}, u32[]{:S(2)}, u32[]{:S(2)}) collective-permute-start(bf16[64,3072]{1,0:T(8,128)(2,1)S(1)} %get-tuple-element.305.refs_3_), channel_id=1, source_target_pairs={{0,1},{1,2},{2,3},{4,5},{5,6},{6,7},{8,9},{9,10},{10,11},{12,13},{... | collective-permute-start | bytes 1179656 | tf_op jit(solution)/shard_map/ppermute | solution.py:450
  169.4 15.4 %collective-permute-start.52 = (bf16[64,3072]{1,0:T(8,128)(2,1)S(1)}, bf16[64,3072]{1,0:T(8,128)(2,1)S(1)}, u32[]{:S(2)}, u32[]{:S(2)}) collective-permute-start(bf16[64,3072]{1,0:T(8,128)(2,1)S(1)} %get-tuple-element.314.refs_4_), channel_id=1, source_target_pairs={{0,1},{1,2},{2,3},{4,5},{5,6},{6,7},{8,9},{9,10},{10,11},{12,13},{... | collective-permute-start | bytes 1179656 | tf_op jit(solution)/shard_map/ppermute | solution.py:450
  170.7 14.1 %collective-permute-start.53 = (bf16[64,3072]{1,0:T(8,128)(2,1)S(1)}, bf16[64,3072]{1,0:T(8,128)(2,1)S(1)}, u32[]{:S(2)}, u32[]{:S(2)}) collective-permute-start(bf16[64,3072]{1,0:T(8,128)(2,1)S(1)} %get-tuple-element.313.refs_10_), channel_id=1, source_target_pairs={{1,0},{2,1},{3,2},{5,4},{6,5},{7,6},{9,8},{10,9},{11,10},{13,12},{... | collective-permute-start | bytes 1179656 | tf_op jit(solution)/shard_map/ppermute | solution.py:450
  176.4 15.3 %collective-permute-start.54 = (bf16[64,3072]{1,0:T(8,128)(2,1)S(1)}, bf16[64,3072]{1,0:T(8,128)(2,1)S(1)}, u32[]{:S(2)}, u32[]{:S(2)}) collective-permute-start(bf16[64,3072]{1,0:T(8,128)(2,1)S(1)} %get-tuple-element.312.refs_5_), channel_id=1, source_target_pairs={{0,1},{1,2},{2,3},{4,5},{5,6},{6,7},{8,9},{9,10},{10,11},{12,13},{... | collective-permute-start | bytes 1179656 | tf_op jit(solution)/shard_map/ppermute | solution.py:450
  177.7 14.0 %collective-permute-start.55 = (bf16[64,3072]{1,0:T(8,128)(2,1)S(1)}, bf16[64,3072]{1,0:T(8,128)(2,1)S(1)}, u32[]{:S(2)}, u32[]{:S(2)}) collective-permute-start(bf16[64,3072]{1,0:T(8,128)(2,1)S(1)} %get-tuple-element.311.refs_11_), channel_id=1, source_target_pairs={{1,0},{2,1},{3,2},{5,4},{6,5},{7,6},{9,8},{10,9},{11,10},{13,12},{... | collective-permute-start | bytes 1179656 | tf_op jit(solution)/shard_map/ppermute | solution.py:450
  191.9 41.1 %collective-permute-start.56 = (bf16[64,6144]{1,0:T(8,128)(2,1)S(1)}, bf16[64,6144]{1,0:T(8,128)(2,1)S(1)}, u32[]{:S(2)}, u32[]{:S(2)}) collective-permute-start(bf16[64,6144]{1,0:T(8,128)(2,1)S(1)} %pad_maximum_fusion.2), channel_id=1, source_target_pairs={{0,1},{1,2},{2,3},{4,5},{5,6},{6,7},{8,9},{9,10},{10,11},{12,13},{... | collective-permute-start | bytes 2359304 | tf_op jit(solution)/shard_map/ppermute | solution.py:459
  193.5 39.5 %collective-permute-start.57 = (bf16[64,6144]{1,0:T(8,128)(2,1)S(1)}, bf16[64,6144]{1,0:T(8,128)(2,1)S(1)}, u32[]{:S(2)}, u32[]{:S(2)}) collective-permute-start(bf16[64,6144]{1,0:T(8,128)(2,1)S(1)} %pad_maximum_fusion.3), channel_id=1, source_target_pairs={{1,0},{2,1},{3,2},{5,4},{6,5},{7,6},{9,8},{10,9},{11,10},{13,12},{... | collective-permute-start | bytes 2359304 | tf_op jit(solution)/shard_map/ppermute | solution.py:460
  238.6 14.7 %collective-permute-start.58 = (bf16[64,3072]{1,0:T(8,128)(2,1)S(1)}, bf16[64,3072]{1,0:T(8,128)(2,1)S(1)}, u32[]{:S(2)}, u32[]{:S(2)}) collective-permute-start(bf16[64,3072]{1,0:T(8,128)(2,1)S(1)} %get-tuple-element.264), channel_id=1, source_target_pairs={{0,1},{4,5},{8,9},{12,13},{16,17},{20,21},{24,25},{28,29}} | collective-permute-start | bytes 1179656 | tf_op jit(solution)/shard_map/ppermute | solution.py:415
  239.2 15.7 %collective-permute-start.59 = (bf16[64,3072]{1,0:T(8,128)(2,1)}, bf16[64,3072]{1,0:T(8,128)(2,1)S(1)}, u32[]{:S(2)}, u32[]{:S(2)}) collective-permute-start(bf16[64,3072]{1,0:T(8,128)(2,1)} %copy-done.7), channel_id=1, source_target_pairs={{3,2},{7,6},{11,10},{15,14},{19,18},{23,22},{27,26},{31,30}} | collective-permute-start | bytes 1179656 | tf_op jit(solution)/shard_map/ppermute | solution.py:416
  248.3 15.0 %collective-permute-start.67 = (bf16[64,3072]{1,0:T(8,128)(2,1)S(1)}, bf16[64,3072]{1,0:T(8,128)(2,1)S(1)}, u32[]{:S(2)}, u32[]{:S(2)}) collective-permute-start(bf16[64,3072]{1,0:T(8,128)(2,1)S(1)} %get-tuple-element.309), channel_id=1, source_target_pairs={{2,1},{3,2},{6,5},{7,6},{10,9},{11,10},{14,13},{15,14},{18,17},{19... | collective-permute-start | bytes 1179656 | tf_op jit(solution)/shard_map/ppermute | solution.py:416
  255.0 16.3 %collective-permute-start.60 = (bf16[64,3072]{1,0:T(8,128)(2,1)S(1)}, bf16[64,3072]{1,0:T(8,128)(2,1)S(1)}, u32[]{:S(2)}, u32[]{:S(2)}) collective-permute-start(bf16[64,3072]{1,0:T(8,128)(2,1)S(1)} %get-tuple-element.308), channel_id=1, source_target_pairs={{0,1},{1,2},{4,5},{5,6},{8,9},{9,10},{12,13},{13,14},{16,17},{17,1... | collective-permute-start | bytes 1179656 | tf_op jit(solution)/shard_map/ppermute | solution.py:415
  255.9 15.8 %collective-permute-start.61 = (bf16[64,3072]{1,0:T(8,128)(2,1)S(1)}, bf16[64,3072]{1,0:T(8,128)(2,1)S(1)}, u32[]{:S(2)}, u32[]{:S(2)}) collective-permute-start(bf16[64,3072]{1,0:T(8,128)(2,1)S(1)} %get-tuple-element.307), channel_id=1, source_target_pairs={{2,1},{3,2},{6,5},{7,6},{10,9},{11,10},{14,13},{15,14},{18,17},{19... | collective-permute-start | bytes 1179656 | tf_op jit(solution)/shard_map/ppermute | solution.py:416
  264.4 15.7 %collective-permute-start.69 = (bf16[64,3072]{1,0:T(8,128)(2,1)S(1)}, bf16[64,3072]{1,0:T(8,128)(2,1)S(1)}, u32[]{:S(2)}, u32[]{:S(2)}) collective-permute-start(bf16[64,3072]{1,0:T(8,128)(2,1)S(1)} %add.273), channel_id=1, source_target_pairs={{1,0},{2,1},{3,2},{5,4},{6,5},{7,6},{9,8},{10,9},{11,10},{13,12},{... | collective-permute-start | bytes 1179656 | tf_op jit(solution)/shard_map/ppermute | solution.py:416
  271.8 14.0 %collective-permute-start.63 = (bf16[64,3072]{1,0:T(8,128)(2,1)S(1)}, bf16[64,3072]{1,0:T(8,128)(2,1)S(1)}, u32[]{:S(2)}, u32[]{:S(2)}) collective-permute-start(bf16[64,3072]{1,0:T(8,128)(2,1)S(1)} %add.263), channel_id=1, source_target_pairs={{1,0},{2,1},{3,2},{5,4},{6,5},{7,6},{9,8},{10,9},{11,10},{13,12},{... | collective-permute-start | bytes 1179656 | tf_op jit(solution)/shard_map/ppermute | solution.py:416
  (70 other events, 835.3 us)

commit v4 on v3

--- a/solution.py
+++ b/solution.py
@@ -22,22 +22,36 @@
 def attention_kernel(slots, together, held, pairs, sharing, block_rows, plan, *refs):
     pieces, grouped = plan
     (order, mine), refs = refs[:2], refs[2:]
-    query_refs, refs = refs[:slots], refs[slots:]
+    sent_queries, refs = refs[:slots], refs[slots:]
     place_ref, refs = refs[0], refs[1:]
-    pair_refs, weight, refs = refs[: len(held)], refs[len(held)], refs[len(held) + 1 :]
+    sent_pairs, weight, refs = refs[: len(held)], refs[len(held)], refs[len(held) + 1 :]
     outs, refs = refs[: pieces * (slots if grouped else 1)], refs[pieces * (slots if grouped else 1) :]
-    query_ref, key_ref, value_ref, top_ref, total_ref, head_ref, weight_ref, arrived = refs
+    query_refs, pair_refs, refs = refs[:slots], refs[slots : slots + len(held)], refs[slots + len(held) :]
+    query_ref, key_ref, value_ref, top_ref, total_ref, head_ref, weight_ref, arrived, here = refs
     half = query_refs[0].shape[0]
     step = pl.program_id(0)
     me = mine[0]
     my_block = order[me]
     blocks = [(ref, index, offset) for ref, group in zip(pair_refs, held) for index, offset in enumerate(group)]
     weight_copy = pltpu.make_async_copy(weight, weight_ref, arrived)
+    moves = [
+        pltpu.make_async_copy(source, target, here.at[i])
+        for i, (source, target) in enumerate(
+            list(zip(sent_pairs, pair_refs)) + list(zip(sent_queries, query_refs))
+        )
+    ]
 
     @pl.when(step == 0)
     def _():
+        for move in moves:
+            move.start()
+        value_ref[:, :, HD:, :] = jnp.ones((len(blocks), pairs, SUM_ROWS, block_rows), jnp.bfloat16)
+
+    @pl.when(step == 0)
+    def _():
+        for move in moves:
+            move.wait()
         weight_copy.start()
-        value_ref[:, :, HD:, :] = jnp.ones((len(blocks), pairs, SUM_ROWS, block_rows), jnp.bfloat16)
 
     for at, (ref, index, offset) in enumerate(blocks):
 
@@ -152,12 +166,14 @@
         grid_spec=pltpu.PrefetchScalarGridSpec(
             num_scalar_prefetch=2,
             grid=(slots // together,),
-            in_specs=[pl.BlockSpec((half, width), lambda s, *_: (0, 0))] * slots
+            in_specs=[pl.BlockSpec(memory_space=pl.ANY)] * slots
             + [pl.BlockSpec((together, 1, half), lambda s, *_: (s, 0, 0))]
-            + [pl.BlockSpec(pair.shape, lambda s, *_: (0, 0)) for pair in pair_list]
-            + [pl.BlockSpec(memory_space=pl.ANY)],
+            + [pl.BlockSpec(memory_space=pl.ANY)] * len(pair_list)
+            + [pl.BlockSpec(memory_space=pltpu.HBM)],
             out_specs=[pl.BlockSpec(shape.shape, lambda s, *_: (0, 0)) for shape in shapes],
-            scratch_shapes=[
+            scratch_shapes=[pltpu.VMEM((half, width), jnp.bfloat16)] * slots
+            + [pltpu.VMEM(pair.shape, pair.dtype) for pair in pair_list]
+            + [
                 pltpu.VMEM((pairs, tall, HD), jnp.bfloat16),
                 pltpu.VMEM((blocks, pairs, block_rows, HD), jnp.bfloat16),
                 pltpu.VMEM((blocks, pairs, HD + SUM_ROWS, block_rows), jnp.bfloat16),
@@ -166,6 +182,7 @@
                 pltpu.VMEM((slots * half, width), jnp.bfloat16),
                 pltpu.VMEM(weight.shape, weight.dtype),
                 pltpu.SemaphoreType.DMA,
+                pltpu.SemaphoreType.DMA((slots + len(pair_list),)),
             ],
         ),
         out_shape=shapes,
@@ -175,7 +192,7 @@
             bytes_accessed=2 * (2 * slots * half * width + count * 2 * pairs * HD + weight.size),
             transcendentals=slots * half * width // HD * count,
         ),
-    )(order, mine, *queries, places, *pair_list, weight)
+    )(order, mine, *queries, places, *pair_list, pltpu.with_memory_space_constraint(weight, pltpu.HBM))
     return by_piece(outs, slots, pieces, grouped)
 
 
@@ -303,7 +320,7 @@
     count = seen[:, rows - 1 : rows]
     row_ids = lax.broadcasted_iota(jnp.int32, seen.shape, 1)
     slot = jnp.where(picked > 0, seen - 1, count + row_ids - seen)
-    count_ref[...] = jnp.broadcast_to(jnp.max(count, axis=0, keepdims=True), count_ref.shape).astype(jnp.float32)
+    count_ref[0] = jnp.max(jnp.where(count > half, 1, 0))
     ids = row_ids.astype(jnp.bfloat16)
     for s in range(shards):
         shard = lax.rem(me - s + shards, shards)
@@ -331,7 +348,7 @@
     packed = (rows // halves, width // shards)
     shapes = [jax.ShapeDtypeStruct(packed, jnp.bfloat16)] * (halves * shards)
     shapes += [jax.ShapeDtypeStruct((shards, 1, rows // halves), jnp.int32)] * halves
-    shapes += [jax.ShapeDtypeStruct((rows, rows), jnp.bfloat16), jax.ShapeDtypeStruct((8, 128), jnp.float32)]
+    shapes += [jax.ShapeDtypeStruct((rows, rows), jnp.bfloat16), jax.ShapeDtypeStruct((1,), jnp.int32)]
 
     def whole(shape):
         return pl.BlockSpec(shape, lambda k, *_: (0,) * len(shape))
@@ -342,7 +359,7 @@
             num_scalar_prefetch=1,
             grid=(1,),
             in_specs=[whole(picked.shape), whole(queries.shape)],
-            out_specs=[whole(shape.shape) for shape in shapes],
+            out_specs=[whole(shape.shape) for shape in shapes[:-1]] + [pl.BlockSpec(memory_space=pltpu.SMEM)],
         ),
         out_shape=shapes,
     )(mine, picked, queries)
@@ -466,7 +483,7 @@
         sent_pairs = pack_pairs(me[None], keys, values, shards)
         own_pairs = jnp.concatenate(shift(sent_pairs), axis=0)
         picked, _ = lax.optimization_barrier((picked.astype(jnp.int32), sent_pairs))
-        packed, places, order, fullest = pack_queries(me[None], picked, queries, slots, halves)
+        packed, places, order, crowded = pack_queries(me[None], picked, queries, slots, halves)
         asked = [shift(packed[0])]
     else:
 
@@ -579,7 +596,7 @@
     second_half = (hidden[half:].astype(jnp.float32) + second_sum).astype(jnp.bfloat16)
     part, second_half = expert(0, normed, sources, second_half)
     part, late = lax.optimization_barrier((part, second_half))
-    late = lax.cond(fullest[0, 0] > half, late_expert, jnp.zeros_like, late)
+    late = lax.cond(crowded[0] > 0, late_expert, jnp.zeros_like, late)
     return (restore([first_half, second_half]), restore([part, late]))
 
 

time: 293 us -> 285 us (0.973)
  the two profiles are of different devices: /device:TPU:26 before, /device:TPU:0 now
where the time goes in v4:
time: 285 us
  starting transfers between devices  118 us (41%)
  waiting for transfers between devices  65 us (23%)
  Pallas kernels  64.6 us (23%)
  other arithmetic  14.7 us (5%)
  local copies, waits for them, and re-layouts  14 us (5%)
  matrix products  5.29 us (2%)
    ppermute x12, starting transfers between devices, reduce_line(): right = lax.ppermute(sent[0], 'tp', rights(s))  51.3 us
    pallas_call x1, Pallas kernels, expert_rows(): pl.pallas_call(functools.partial(expert_kernel, [len(source) for source i...  34.8 us
    pallas_call x2, Pallas kernels, attend(): pl.pallas_call(kernel, grid_spec=pltpu.PrefetchScalarGridSpec(num_scalar_...  25.1 us
    ppermute x12, waiting for transfers between devices, reduce_line(): right = lax.ppermute(sent[0], 'tp', rights(s))  22.9 us
    ppermute x4, starting transfers between devices, gather_line(): lax.ppermute(right, 'tp', to_right)  18.8 us
    ppermute x9, starting transfers between devices, shift(): lax.ppermute(parts[s], 'tp', moves[s])  17.7 us
    unnamed x107, local copies, waits for them, and re-layouts  14 us
    ppermute x9, waiting for transfers between devices, shift(): lax.ppermute(parts[s], 'tp', moves[s])  13.4 us
  transfers between devices with their start and end apart: 48, of which 23 were waited for; matrix products, arithmetic and copies ran while one was open for 6% of the time, Pallas kernels for 22%

profile of v4, /device:TPU:0, one launch (start us, length us, event | category | flops | bytes accessed | tf_op | source)
XLA Modules:
  0.0 284.5 jit_solution(6548041571926801232)
XLA Ops:
  2.7 3.0 %collective-permute-start.22 = (bf16[128,512]{1,0:T(8,128)(2,1)}, bf16[128,512]{1,0:T(8,128)(2,1)S(1)}, u32[]{:S(2)}, u32[]{:S(2)}) collective-permute-start(bf16[128,512]{1,0:T(8,128)(2,1)} %get-tuple-element.176), channel_id=1, source_target_pairs={{0,1},{1,2},{2,3},{3,0},{4,5},{5,6},{6,7},{7,4},{8,9},{9,10},{10,1... | collective-permute-start | bytes 393224 | tf_op jit(solution)/shard_map/ppermute | solution.py:404
  12.4 4.8 %collective-permute-done.23 = bf16[128,512]{1,0:T(8,128)(2,1)S(1)} collective-permute-done((bf16[128,512]{1,0:T(8,128)(2,1)}, bf16[128,512]{1,0:T(8,128)(2,1)S(1)}, u32[]{:S(2)}, u32[]{:S(2)}) %collective-permute-start.23) | collective-permute-done | bytes 131104 | tf_op jit(solution)/shard_map/ppermute | solution.py:404
  22.1 3.3 %collective-permute-start.26 = (bf16[64,1024]{1,0:T(8,128)(2,1)}, bf16[64,1024]{1,0:T(8,128)(2,1)S(1)}, u32[]{:S(2)}, u32[]{:S(2)}) collective-permute-start(bf16[64,1024]{1,0:T(8,128)(2,1)} %get-tuple-element.182), channel_id=1, source_target_pairs={{0,1},{1,2},{2,3},{3,0},{4,5},{5,6},{6,7},{7,4},{8,9},{9,10},{10,1... | collective-permute-start | bytes 393224 | tf_op jit(solution)/shard_map/ppermute | solution.py:404
  27.8 3.2 %collective-permute-done.26.refs_2_ = bf16[64,1024]{1,0:T(8,128)(2,1)S(1)} collective-permute-done((bf16[64,1024]{1,0:T(8,128)(2,1)}, bf16[64,1024]{1,0:T(8,128)(2,1)S(1)}, u32[]{:S(2)}, u32[]{:S(2)}) %collective-permute-start.26) | collective-permute-done | bytes 131104 | tf_op jit(solution)/shard_map/ppermute | solution.py:404
  31.7 3.6 %collective-permute-done.27.refs_4_ = bf16[64,1024]{1,0:T(8,128)(2,1)S(1)} collective-permute-done((bf16[64,1024]{1,0:T(8,128)(2,1)}, bf16[64,1024]{1,0:T(8,128)(2,1)S(1)}, u32[]{:S(2)}, u32[]{:S(2)}) %collective-permute-start.27) | collective-permute-done | bytes 131104 | tf_op jit(solution)/shard_map/ppermute | solution.py:404
  50.7 12.5 %shard_map.133 = (bf16[64,3072]{1,0:T(8,128)(2,1)S(1)}, bf16[64,3072]{1,0:T(8,128)(2,1)S(1)}, bf16[64,3072]{1,0:T(8,128)(2,1)S(1)}, bf16[64,3072]{1,0:T(8,128)(2...) custom-call(s32[4]{0:T(128)S(1)} %copy-done.39, ...), custom_call_target="tpu_custom_call" | custom-call | flops 21474836480 | bytes 15728640 | tf_op jit(solution)/shard_map/pallas_call | solution.py:164
  63.3 3.9 %collective-permute-start.40 = (bf16[64,3072]{1,0:T(8,128)(2,1)S(1)}, bf16[64,3072]{1,0:T(8,128)(2,1)S(1)}, u32[]{:S(2)}, u32[]{:S(2)}) collective-permute-start(bf16[64,3072]{1,0:T(8,128)(2,1)S(1)} %get-tuple-element.218), channel_id=1, source_target_pairs={{0,1},{4,5},{8,9},{12,13},{16,17},{20,21},{24,25},{28,29}} | collective-permute-start | bytes 1179656 | tf_op jit(solution)/shard_map/ppermute | solution.py:432
  69.9 5.7 %collective-permute-done.40 = bf16[64,3072]{1,0:T(8,128)(2,1)S(1)} collective-permute-done((bf16[64,3072]{1,0:T(8,128)(2,1)S(1)}, bf16[64,3072]{1,0:T(8,128)(2,1)S(1)}, u32[]{:S(2)}, u32[]{:S(2)}) %collective-permute-start.40) | collective-permute-done | bytes 393248 | tf_op jit(solution)/shard_map/ppermute | solution.py:432
  76.6 5.1 %collective-permute-start.42 = (bf16[64,3072]{1,0:T(8,128)(2,1)}, bf16[64,3072]{1,0:T(8,128)(2,1)}, u32[]{:S(2)}, u32[]{:S(2)}) collective-permute-start(bf16[64,3072]{1,0:T(8,128)(2,1)} %get-tuple-element.318), channel_id=1, source_target_pairs={{0,1},{1,2},{4,5},{5,6},{8,9},{9,10},{12,13},{13,14},{16,17},{17,1... | collective-permute-start | bytes 1179656 | tf_op jit(solution)/shard_map/ppermute | solution.py:432
  85.1 5.1 %collective-permute-start.36 = (bf16[64,3072]{1,0:T(8,128)(2,1)}, bf16[64,3072]{1,0:T(8,128)(2,1)}, u32[]{:S(2)}, u32[]{:S(2)}) collective-permute-start(bf16[64,3072]{1,0:T(8,128)(2,1)} %get-tuple-element.316), channel_id=1, source_target_pairs={{0,1},{1,2},{4,5},{5,6},{8,9},{9,10},{12,13},{13,14},{16,17},{17,1... | collective-permute-start | bytes 1179656 | tf_op jit(solution)/shard_map/ppermute | solution.py:432
  96.8 4.6 %collective-permute-start.44 = (bf16[64,3072]{1,0:T(8,128)(2,1)S(1)}, bf16[64,3072]{1,0:T(8,128)(2,1)S(1)}, u32[]{:S(2)}, u32[]{:S(2)}) collective-permute-start(bf16[64,3072]{1,0:T(8,128)(2,1)S(1)} %add.239), channel_id=1, source_target_pairs={{0,1},{1,2},{2,3},{4,5},{5,6},{6,7},{8,9},{9,10},{10,11},{12,13},{... | collective-permute-start | bytes 1179656 | tf_op jit(solution)/shard_map/ppermute | solution.py:432
  104.9 4.7 %collective-permute-start.38 = (bf16[64,3072]{1,0:T(8,128)(2,1)S(1)}, bf16[64,3072]{1,0:T(8,128)(2,1)S(1)}, u32[]{:S(2)}, u32[]{:S(2)}) collective-permute-start(bf16[64,3072]{1,0:T(8,128)(2,1)S(1)} %add.232), channel_id=1, source_target_pairs={{0,1},{1,2},{2,3},{4,5},{5,6},{6,7},{8,9},{9,10},{10,11},{12,13},{... | collective-permute-start | bytes 1179656 | tf_op jit(solution)/shard_map/ppermute | solution.py:432
  109.9 5.5 %collective-permute-done.39 = bf16[64,3072]{1,0:T(8,128)(2,1)S(1)} collective-permute-done((bf16[64,3072]{1,0:T(8,128)(2,1)S(1)}, bf16[64,3072]{1,0:T(8,128)(2,1)S(1)}, u32[]{:S(2)}, u32[]{:S(2)}) %collective-permute-start.39) | collective-permute-done | bytes 393248 | tf_op jit(solution)/shard_map/ppermute | solution.py:433
  115.4 2.9 %collective-permute-done.38 = bf16[64,3072]{1,0:T(8,128)(2,1)S(1)} collective-permute-done((bf16[64,3072]{1,0:T(8,128)(2,1)S(1)}, bf16[64,3072]{1,0:T(8,128)(2,1)S(1)}, u32[]{:S(2)}, u32[]{:S(2)}) %collective-permute-start.38) | collective-permute-done | bytes 393248 | tf_op jit(solution)/shard_map/ppermute | solution.py:432
  119.3 4.6 %collective-permute-start.46 = (bf16[64,6144]{1,0:T(8,128)(2,1)S(1)}, bf16[64,6144]{1,0:T(8,128)(2,1)S(1)}, u32[]{:S(2)}, u32[]{:S(2)}) collective-permute-start(bf16[64,6144]{1,0:T(8,128)(2,1)S(1)} %fusion.7.refs_1_), channel_id=1, source_target_pairs={{0,1},{1,2},{2,3},{4,5},{5,6},{6,7},{8,9},{9,10},{10,11},{12,13},{... | collective-permute-start | bytes 2359304 | tf_op jit(solution)/shard_map/ppermute | solution.py:445
  125.4 12.6 %shard_map.134 = (bf16[64,3072]{1,0:T(8,128)(2,1)S(1)}, bf16[64,3072]{1,0:T(8,128)(2,1)S(1)}, bf16[64,3072]{1,0:T(8,128)(2,1)S(1)}, bf16[64,3072]{1,0:T(8,128)(2...) custom-call(s32[4]{0:T(128)S(1)} %copy-done.39, ...), custom_call_target="tpu_custom_call" | custom-call | flops 21474836480 | bytes 15728640 | tf_op jit(solution)/shard_map/pallas_call | solution.py:164
  138.1 3.6 %collective-permute-done.46 = bf16[64,6144]{1,0:T(8,128)(2,1)S(1)} collective-permute-done((bf16[64,6144]{1,0:T(8,128)(2,1)S(1)}, bf16[64,6144]{1,0:T(8,128)(2,1)S(1)}, u32[]{:S(2)}, u32[]{:S(2)}) %collective-permute-start.46) | collective-permute-done | bytes 786464 | tf_op jit(solution)/shard_map/ppermute | solution.py:445
  141.6 4.2 %collective-permute-done.47 = bf16[64,6144]{1,0:T(8,128)(2,1)S(1)} collective-permute-done((bf16[64,6144]{1,0:T(8,128)(2,1)S(1)}, bf16[64,6144]{1,0:T(8,128)(2,1)S(1)}, u32[]{:S(2)}, u32[]{:S(2)}) %collective-permute-start.47) | collective-permute-done | bytes 786464 | tf_op jit(solution)/shard_map/ppermute | solution.py:446
  147.3 5.3 %collective-permute-start.48 = (bf16[64,3072]{1,0:T(8,128)(2,1)S(1)}, bf16[64,3072]{1,0:T(8,128)(2,1)}, u32[]{:S(2)}, u32[]{:S(2)}) collective-permute-start(bf16[64,3072]{1,0:T(8,128)(2,1)S(1)} %get-tuple-element.306.refs_2_), channel_id=1, source_target_pairs={{0,1},{1,2},{2,3},{4,5},{5,6},{6,7},{8,9},{9,10},{10,11},{12,13},{... | collective-permute-start | bytes 1179656 | tf_op jit(solution)/shard_map/ppermute | solution.py:467
  154.1 4.6 %collective-permute-start.50 = (bf16[64,3072]{1,0:T(8,128)(2,1)S(1)}, bf16[64,3072]{1,0:T(8,128)(2,1)S(1)}, u32[]{:S(2)}, u32[]{:S(2)}) collective-permute-start(bf16[64,3072]{1,0:T(8,128)(2,1)S(1)} %get-tuple-element.305.refs_3_), channel_id=1, source_target_pairs={{0,1},{1,2},{2,3},{4,5},{5,6},{6,7},{8,9},{9,10},{10,11},{12,13},{... | collective-permute-start | bytes 1179656 | tf_op jit(solution)/shard_map/ppermute | solution.py:467
  162.8 4.5 %collective-permute-start.52 = (bf16[64,3072]{1,0:T(8,128)(2,1)S(1)}, bf16[64,3072]{1,0:T(8,128)(2,1)S(1)}, u32[]{:S(2)}, u32[]{:S(2)}) collective-permute-start(bf16[64,3072]{1,0:T(8,128)(2,1)S(1)} %get-tuple-element.314.refs_4_), channel_id=1, source_target_pairs={{0,1},{1,2},{2,3},{4,5},{5,6},{6,7},{8,9},{9,10},{10,11},{12,13},{... | collective-permute-start | bytes 1179656 | tf_op jit(solution)/shard_map/ppermute | solution.py:467
  169.9 4.4 %collective-permute-start.54 = (bf16[64,3072]{1,0:T(8,128)(2,1)S(1)}, bf16[64,3072]{1,0:T(8,128)(2,1)S(1)}, u32[]{:S(2)}, u32[]{:S(2)}) collective-permute-start(bf16[64,3072]{1,0:T(8,128)(2,1)S(1)} %get-tuple-element.312.refs_5_), channel_id=1, source_target_pairs={{0,1},{1,2},{2,3},{4,5},{5,6},{6,7},{8,9},{9,10},{10,11},{12,13},{... | collective-permute-start | bytes 1179656 | tf_op jit(solution)/shard_map/ppermute | solution.py:467
  178.6 6.7 %collective-permute-done.54.refs_7_ = bf16[64,3072]{1,0:T(8,128)(2,1)S(1)} collective-permute-done((bf16[64,3072]{1,0:T(8,128)(2,1)S(1)}, bf16[64,3072]{1,0:T(8,128)(2,1)S(1)}, u32[]{:S(2)}, u32[]{:S(2)}) %collective-permute-start.54) | collective-permute-done | bytes 393248 | tf_op jit(solution)/shard_map/ppermute | solution.py:467
  185.7 4.1 %collective-permute-start.56 = (bf16[64,6144]{1,0:T(8,128)(2,1)S(1)}, bf16[64,6144]{1,0:T(8,128)(2,1)S(1)}, u32[]{:S(2)}, u32[]{:S(2)}) collective-permute-start(bf16[64,6144]{1,0:T(8,128)(2,1)S(1)} %pad_maximum_fusion.2), channel_id=1, source_target_pairs={{0,1},{1,2},{2,3},{4,5},{5,6},{6,7},{8,9},{9,10},{10,11},{12,13},{... | collective-permute-start | bytes 2359304 | tf_op jit(solution)/shard_map/ppermute | solution.py:476
  191.6 34.8 %shard_map.135 = (bf16[64,3072]{1,0:T(8,128)(2,1)S(1)}, bf16[64,3072]{1,0:T(8,128)(2,1)S(1)}, bf16[64,3072]{1,0:T(8,128)(2,1)S(1)}, bf16[64,3072]{1,0:T(8,128)(2...) custom-call(s32[1]{0:T(128)} %bitcast.6.mine.refs_0_, ...), custom_call_target="tpu_custom_call" | custom-call | flops 19327352832 | bytes 75497472 | tf_op jit(solution)/shard_map/pallas_call | solution.py:260
  227.4 4.6 %collective-permute-start.64 = (bf16[64,3072]{1,0:T(8,128)(2,1)}, bf16[64,3072]{1,0:T(8,128)(2,1)S(1)}, u32[]{:S(2)}, u32[]{:S(2)}) collective-permute-start(bf16[64,3072]{1,0:T(8,128)(2,1)} %get-tuple-element.275), channel_id=1, source_target_pairs={{0,1},{4,5},{8,9},{12,13},{16,17},{20,21},{24,25},{28,29}} | collective-permute-start | bytes 1179656 | tf_op jit(solution)/shard_map/ppermute | solution.py:432
  235.3 6.5 %collective-permute-done.64 = bf16[64,3072]{1,0:T(8,128)(2,1)S(1)} collective-permute-done((bf16[64,3072]{1,0:T(8,128)(2,1)}, bf16[64,3072]{1,0:T(8,128)(2,1)S(1)}, u32[]{:S(2)}, u32[]{:S(2)}) %collective-permute-start.64) | collective-permute-done | bytes 393248 | tf_op jit(solution)/shard_map/ppermute | solution.py:432
  242.9 4.3 %collective-permute-start.66 = (bf16[64,3072]{1,0:T(8,128)(2,1)S(1)}, bf16[64,3072]{1,0:T(8,128)(2,1)S(1)}, u32[]{:S(2)}, u32[]{:S(2)}) collective-permute-start(bf16[64,3072]{1,0:T(8,128)(2,1)S(1)} %get-tuple-element.310), channel_id=1, source_target_pairs={{0,1},{1,2},{4,5},{5,6},{8,9},{9,10},{12,13},{13,14},{16,17},{17,1... | collective-permute-start | bytes 1179656 | tf_op jit(solution)/shard_map/ppermute | solution.py:432
  250.2 4.5 %collective-permute-start.60 = (bf16[64,3072]{1,0:T(8,128)(2,1)S(1)}, bf16[64,3072]{1,0:T(8,128)(2,1)S(1)}, u32[]{:S(2)}, u32[]{:S(2)}) collective-permute-start(bf16[64,3072]{1,0:T(8,128)(2,1)S(1)} %get-tuple-element.308), channel_id=1, source_target_pairs={{0,1},{1,2},{4,5},{5,6},{8,9},{9,10},{12,13},{13,14},{16,17},{17,1... | collective-permute-start | bytes 1179656 | tf_op jit(solution)/shard_map/ppermute | solution.py:432
  255.6 2.9 %collective-permute-done.66 = bf16[64,3072]{1,0:T(8,128)(2,1)S(1)} collective-permute-done((bf16[64,3072]{1,0:T(8,128)(2,1)S(1)}, bf16[64,3072]{1,0:T(8,128)(2,1)S(1)}, u32[]{:S(2)}, u32[]{:S(2)}) %collective-permute-start.66) | collective-permute-done | bytes 393248 | tf_op jit(solution)/shard_map/ppermute | solution.py:432
  262.2 6.9 %collective-permute-start.68 = (bf16[64,3072]{1,0:T(8,128)(2,1)S(1)}, bf16[64,3072]{1,0:T(8,128)(2,1)S(1)}, u32[]{:S(2)}, u32[]{:S(2)}) collective-permute-start(bf16[64,3072]{1,0:T(8,128)(2,1)S(1)} %add.272), channel_id=1, source_target_pairs={{0,1},{1,2},{2,3},{4,5},{5,6},{6,7},{8,9},{9,10},{10,11},{12,13},{... | collective-permute-start | bytes 1179656 | tf_op jit(solution)/shard_map/ppermute | solution.py:432
  270.7 4.9 %collective-permute-start.62 = (bf16[64,3072]{1,0:T(8,128)(2,1)S(1)}, bf16[64,3072]{1,0:T(8,128)(2,1)S(1)}, u32[]{:S(2)}, u32[]{:S(2)}) collective-permute-start(bf16[64,3072]{1,0:T(8,128)(2,1)S(1)} %add.262), channel_id=1, source_target_pairs={{0,1},{1,2},{2,3},{4,5},{5,6},{6,7},{8,9},{9,10},{10,11},{12,13},{... | collective-permute-start | bytes 1179656 | tf_op jit(solution)/shard_map/ppermute | solution.py:432
  (219 shorter events, 90.3 us)
Async XLA Ops:
  17.2 19.5 %collective-permute-start.25 = (bf16[512,512]{1,0:T(8,128)(2,1)S(1)}, bf16[512,512]{1,0:T(8,128)(2,1)S(1)}, u32[]{:S(2)}, u32[]{:S(2)}) collective-permute-start(bf16[512,512]{1,0:T(8,128)(2,1)S(1)} %constant_dynamic-update-slice_fusion.refs_7_), channel_id=1, source_target_pairs={{0,8},{4,12},{8,0},{12,4},{1,9},{5,13},{9,1},{13,5},{2,10},{6,14},... | collective-permute-start | bytes 1572872 | tf_op jit(solution)/shard_map/ppermute | solution.py:510
  27.8 14.7 %collective-permute-start.29 = (bf16[512,512]{1,0:T(8,128)(2,1)S(1)}, bf16[512,512]{1,0:T(8,128)(2,1)S(1)}, u32[]{:S(2)}, u32[]{:S(2)}) collective-permute-start(bf16[512,512]{1,0:T(8,128)(2,1)S(1)} %constant_dynamic-update-slice_fusion.refs_7_), channel_id=1, source_target_pairs={{0,4},{4,0},{8,12},{12,8},{1,5},{5,1},{9,13},{13,9},{2,6},{6,2},{1... | collective-permute-start | bytes 1572872 | tf_op jit(solution)/shard_map/ppermute | solution.py:510
  37.5 25.8 %collective-permute-start.31 = (bf16[64,1024]{1,0:T(8,128)(2,1)}, bf16[64,1024]{1,0:T(8,128)(2,1)}, u32[]{:S(2)}, u32[]{:S(2)}) collective-permute-start(bf16[64,1024]{1,0:T(8,128)(2,1)} %get-tuple-element.200), channel_id=1, source_target_pairs={{0,1},{1,2},{2,3},{3,0},{4,5},{5,6},{6,7},{7,4},{8,9},{9,10},{10,1... | collective-permute-start | bytes 393224 | tf_op jit(solution)/shard_map/ppermute | solution.py:404
  40.1 23.2 %collective-permute-start.32 = (bf16[64,1024]{1,0:T(8,128)(2,1)}, bf16[64,1024]{1,0:T(8,128)(2,1)}, u32[]{:S(2)}, u32[]{:S(2)}) collective-permute-start(bf16[64,1024]{1,0:T(8,128)(2,1)} %get-tuple-element.201), channel_id=1, source_target_pairs={{0,2},{1,3},{2,0},{3,1},{4,6},{5,7},{6,4},{7,5},{8,10},{9,11},{10,... | collective-permute-start | bytes 393224 | tf_op jit(solution)/shard_map/ppermute | solution.py:404
  42.4 20.8 %collective-permute-start.33 = (bf16[64,1024]{1,0:T(8,128)(2,1)}, bf16[64,1024]{1,0:T(8,128)(2,1)}, u32[]{:S(2)}, u32[]{:S(2)}) collective-permute-start(bf16[64,1024]{1,0:T(8,128)(2,1)} %get-tuple-element.202), channel_id=1, source_target_pairs={{0,3},{1,0},{2,1},{3,2},{4,7},{5,4},{6,5},{7,6},{8,11},{9,8},{10,9... | collective-permute-start | bytes 393224 | tf_op jit(solution)/shard_map/ppermute | solution.py:404
  63.3 12.4 %collective-permute-start.40 = (bf16[64,3072]{1,0:T(8,128)(2,1)S(1)}, bf16[64,3072]{1,0:T(8,128)(2,1)S(1)}, u32[]{:S(2)}, u32[]{:S(2)}) collective-permute-start(bf16[64,3072]{1,0:T(8,128)(2,1)S(1)} %get-tuple-element.218), channel_id=1, source_target_pairs={{0,1},{4,5},{8,9},{12,13},{16,17},{20,21},{24,25},{28,29}} | collective-permute-start | bytes 1179656 | tf_op jit(solution)/shard_map/ppermute | solution.py:432
  67.9 16.2 %collective-permute-start.34 = (bf16[64,3072]{1,0:T(8,128)(2,1)S(1)}, bf16[64,3072]{1,0:T(8,128)(2,1)S(1)}, u32[]{:S(2)}, u32[]{:S(2)}) collective-permute-start(bf16[64,3072]{1,0:T(8,128)(2,1)S(1)} %get-tuple-element.203), channel_id=1, source_target_pairs={{0,1},{4,5},{8,9},{12,13},{16,17},{20,21},{24,25},{28,29}} | collective-permute-start | bytes 1179656 | tf_op jit(solution)/shard_map/ppermute | solution.py:432
  69.2 14.9 %collective-permute-start.35 = (bf16[64,3072]{1,0:T(8,128)(2,1)S(1)}, bf16[64,3072]{1,0:T(8,128)(2,1)S(1)}, u32[]{:S(2)}, u32[]{:S(2)}) collective-permute-start(bf16[64,3072]{1,0:T(8,128)(2,1)S(1)} %get-tuple-element.204), channel_id=1, source_target_pairs={{3,2},{7,6},{11,10},{15,14},{19,18},{23,22},{27,26},{31,30}} | collective-permute-start | bytes 1179656 | tf_op jit(solution)/shard_map/ppermute | solution.py:433
  76.6 16.4 %collective-permute-start.42 = (bf16[64,3072]{1,0:T(8,128)(2,1)}, bf16[64,3072]{1,0:T(8,128)(2,1)}, u32[]{:S(2)}, u32[]{:S(2)}) collective-permute-start(bf16[64,3072]{1,0:T(8,128)(2,1)} %get-tuple-element.318), channel_id=1, source_target_pairs={{0,1},{1,2},{4,5},{5,6},{8,9},{9,10},{12,13},{13,14},{16,17},{17,1... | collective-permute-start | bytes 1179656 | tf_op jit(solution)/shard_map/ppermute | solution.py:432
  85.1 16.3 %collective-permute-start.36 = (bf16[64,3072]{1,0:T(8,128)(2,1)}, bf16[64,3072]{1,0:T(8,128)(2,1)}, u32[]{:S(2)}, u32[]{:S(2)}) collective-permute-start(bf16[64,3072]{1,0:T(8,128)(2,1)} %get-tuple-element.316), channel_id=1, source_target_pairs={{0,1},{1,2},{4,5},{5,6},{8,9},{9,10},{12,13},{13,14},{16,17},{17,1... | collective-permute-start | bytes 1179656 | tf_op jit(solution)/shard_map/ppermute | solution.py:432
  94.4 15.3 %collective-permute-start.45 = (bf16[64,3072]{1,0:T(8,128)(2,1)S(1)}, bf16[64,3072]{1,0:T(8,128)(2,1)S(1)}, u32[]{:S(2)}, u32[]{:S(2)}) collective-permute-start(bf16[64,3072]{1,0:T(8,128)(2,1)S(1)} %add.240), channel_id=1, source_target_pairs={{1,0},{2,1},{3,2},{5,4},{6,5},{7,6},{9,8},{10,9},{11,10},{13,12},{... | collective-permute-start | bytes 1179656 | tf_op jit(solution)/shard_map/ppermute | solution.py:433
  96.8 13.1 %collective-permute-start.44 = (bf16[64,3072]{1,0:T(8,128)(2,1)S(1)}, bf16[64,3072]{1,0:T(8,128)(2,1)S(1)}, u32[]{:S(2)}, u32[]{:S(2)}) collective-permute-start(bf16[64,3072]{1,0:T(8,128)(2,1)S(1)} %add.239), channel_id=1, source_target_pairs={{0,1},{1,2},{2,3},{4,5},{5,6},{6,7},{8,9},{9,10},{10,11},{12,13},{... | collective-permute-start | bytes 1179656 | tf_op jit(solution)/shard_map/ppermute | solution.py:432
  102.5 12.9 %collective-permute-start.39 = (bf16[64,3072]{1,0:T(8,128)(2,1)S(1)}, bf16[64,3072]{1,0:T(8,128)(2,1)S(1)}, u32[]{:S(2)}, u32[]{:S(2)}) collective-permute-start(bf16[64,3072]{1,0:T(8,128)(2,1)S(1)} %add.233), channel_id=1, source_target_pairs={{1,0},{2,1},{3,2},{5,4},{6,5},{7,6},{9,8},{10,9},{11,10},{13,12},{... | collective-permute-start | bytes 1179656 | tf_op jit(solution)/shard_map/ppermute | solution.py:433
  104.9 13.3 %collective-permute-start.38 = (bf16[64,3072]{1,0:T(8,128)(2,1)S(1)}, bf16[64,3072]{1,0:T(8,128)(2,1)S(1)}, u32[]{:S(2)}, u32[]{:S(2)}) collective-permute-start(bf16[64,3072]{1,0:T(8,128)(2,1)S(1)} %add.232), channel_id=1, source_target_pairs={{0,1},{1,2},{2,3},{4,5},{5,6},{6,7},{8,9},{9,10},{10,11},{12,13},{... | collective-permute-start | bytes 1179656 | tf_op jit(solution)/shard_map/ppermute | solution.py:432
  119.3 22.3 %collective-permute-start.46 = (bf16[64,6144]{1,0:T(8,128)(2,1)S(1)}, bf16[64,6144]{1,0:T(8,128)(2,1)S(1)}, u32[]{:S(2)}, u32[]{:S(2)}) collective-permute-start(bf16[64,6144]{1,0:T(8,128)(2,1)S(1)} %fusion.7.refs_1_), channel_id=1, source_target_pairs={{0,1},{1,2},{2,3},{4,5},{5,6},{6,7},{8,9},{9,10},{10,11},{12,13},{... | collective-permute-start | bytes 2359304 | tf_op jit(solution)/shard_map/ppermute | solution.py:445
  123.9 21.9 %collective-permute-start.47 = (bf16[64,6144]{1,0:T(8,128)(2,1)S(1)}, bf16[64,6144]{1,0:T(8,128)(2,1)S(1)}, u32[]{:S(2)}, u32[]{:S(2)}) collective-permute-start(bf16[64,6144]{1,0:T(8,128)(2,1)S(1)} %fusion.7.refs_1_), channel_id=1, source_target_pairs={{1,0},{2,1},{3,2},{5,4},{6,5},{7,6},{9,8},{10,9},{11,10},{13,12},{... | collective-permute-start | bytes 2359304 | tf_op jit(solution)/shard_map/ppermute | solution.py:446
  145.9 14.0 %collective-permute-start.49 = (bf16[64,3072]{1,0:T(8,128)(2,1)S(1)}, bf16[64,3072]{1,0:T(8,128)(2,1)}, u32[]{:S(2)}, u32[]{:S(2)}) collective-permute-start(bf16[64,3072]{1,0:T(8,128)(2,1)S(1)} %get-tuple-element.304.refs_8_), channel_id=1, source_target_pairs={{1,0},{2,1},{3,2},{5,4},{6,5},{7,6},{9,8},{10,9},{11,10},{13,12},{... | collective-permute-start | bytes 1179656 | tf_op jit(solution)/shard_map/ppermute | solution.py:467
  147.3 14.1 %collective-permute-start.48 = (bf16[64,3072]{1,0:T(8,128)(2,1)S(1)}, bf16[64,3072]{1,0:T(8,128)(2,1)}, u32[]{:S(2)}, u32[]{:S(2)}) collective-permute-start(bf16[64,3072]{1,0:T(8,128)(2,1)S(1)} %get-tuple-element.306.refs_2_), channel_id=1, source_target_pairs={{0,1},{1,2},{2,3},{4,5},{5,6},{6,7},{8,9},{9,10},{10,11},{12,13},{... | collective-permute-start | bytes 1179656 | tf_op jit(solution)/shard_map/ppermute | solution.py:467
  152.7 16.0 %collective-permute-start.51 = (bf16[64,3072]{1,0:T(8,128)(2,1)S(1)}, bf16[64,3072]{1,0:T(8,128)(2,1)S(1)}, u32[]{:S(2)}, u32[]{:S(2)}) collective-permute-start(bf16[64,3072]{1,0:T(8,128)(2,1)S(1)} %get-tuple-element.303.refs_9_), channel_id=1, source_target_pairs={{1,0},{2,1},{3,2},{5,4},{6,5},{7,6},{9,8},{10,9},{11,10},{13,12},{... | collective-permute-start | bytes 1179656 | tf_op jit(solution)/shard_map/ppermute | solution.py:467
  154.1 15.8 %collective-permute-start.50 = (bf16[64,3072]{1,0:T(8,128)(2,1)S(1)}, bf16[64,3072]{1,0:T(8,128)(2,1)S(1)}, u32[]{:S(2)}, u32[]{:S(2)}) collective-permute-start(bf16[64,3072]{1,0:T(8,128)(2,1)S(1)} %get-tuple-element.305.refs_3_), channel_id=1, source_target_pairs={{0,1},{1,2},{2,3},{4,5},{5,6},{6,7},{8,9},{9,10},{10,11},{12,13},{... | collective-permute-start | bytes 1179656 | tf_op jit(solution)/shard_map/ppermute | solution.py:467
  162.8 15.5 %collective-permute-start.52 = (bf16[64,3072]{1,0:T(8,128)(2,1)S(1)}, bf16[64,3072]{1,0:T(8,128)(2,1)S(1)}, u32[]{:S(2)}, u32[]{:S(2)}) collective-permute-start(bf16[64,3072]{1,0:T(8,128)(2,1)S(1)} %get-tuple-element.314.refs_4_), channel_id=1, source_target_pairs={{0,1},{1,2},{2,3},{4,5},{5,6},{6,7},{8,9},{9,10},{10,11},{12,13},{... | collective-permute-start | bytes 1179656 | tf_op jit(solution)/shard_map/ppermute | solution.py:467
  169.9 15.3 %collective-permute-start.54 = (bf16[64,3072]{1,0:T(8,128)(2,1)S(1)}, bf16[64,3072]{1,0:T(8,128)(2,1)S(1)}, u32[]{:S(2)}, u32[]{:S(2)}) collective-permute-start(bf16[64,3072]{1,0:T(8,128)(2,1)S(1)} %get-tuple-element.312.refs_5_), channel_id=1, source_target_pairs={{0,1},{1,2},{2,3},{4,5},{5,6},{6,7},{8,9},{9,10},{10,11},{12,13},{... | collective-permute-start | bytes 1179656 | tf_op jit(solution)/shard_map/ppermute | solution.py:467
  185.7 40.7 %collective-permute-start.56 = (bf16[64,6144]{1,0:T(8,128)(2,1)S(1)}, bf16[64,6144]{1,0:T(8,128)(2,1)S(1)}, u32[]{:S(2)}, u32[]{:S(2)}) collective-permute-start(bf16[64,6144]{1,0:T(8,128)(2,1)S(1)} %pad_maximum_fusion.2), channel_id=1, source_target_pairs={{0,1},{1,2},{2,3},{4,5},{5,6},{6,7},{8,9},{9,10},{10,11},{12,13},{... | collective-permute-start | bytes 2359304 | tf_op jit(solution)/shard_map/ppermute | solution.py:476
  190.2 36.2 %collective-permute-start.57 = (bf16[64,6144]{1,0:T(8,128)(2,1)S(1)}, bf16[64,6144]{1,0:T(8,128)(2,1)S(1)}, u32[]{:S(2)}, u32[]{:S(2)}) collective-permute-start(bf16[64,6144]{1,0:T(8,128)(2,1)S(1)} %pad_maximum_fusion.3), channel_id=1, source_target_pairs={{1,0},{2,1},{3,2},{5,4},{6,5},{7,6},{9,8},{10,9},{11,10},{13,12},{... | collective-permute-start | bytes 2359304 | tf_op jit(solution)/shard_map/ppermute | solution.py:477
  227.4 14.4 %collective-permute-start.64 = (bf16[64,3072]{1,0:T(8,128)(2,1)}, bf16[64,3072]{1,0:T(8,128)(2,1)S(1)}, u32[]{:S(2)}, u32[]{:S(2)}) collective-permute-start(bf16[64,3072]{1,0:T(8,128)(2,1)} %get-tuple-element.275), channel_id=1, source_target_pairs={{0,1},{4,5},{8,9},{12,13},{16,17},{20,21},{24,25},{28,29}} | collective-permute-start | bytes 1179656 | tf_op jit(solution)/shard_map/ppermute | solution.py:432
  233.3 16.8 %collective-permute-start.58 = (bf16[64,3072]{1,0:T(8,128)(2,1)S(1)}, bf16[64,3072]{1,0:T(8,128)(2,1)S(1)}, u32[]{:S(2)}, u32[]{:S(2)}) collective-permute-start(bf16[64,3072]{1,0:T(8,128)(2,1)S(1)} %get-tuple-element.264), channel_id=1, source_target_pairs={{0,1},{4,5},{8,9},{12,13},{16,17},{20,21},{24,25},{28,29}} | collective-permute-start | bytes 1179656 | tf_op jit(solution)/shard_map/ppermute | solution.py:432
  234.6 15.5 %collective-permute-start.59 = (bf16[64,3072]{1,0:T(8,128)(2,1)}, bf16[64,3072]{1,0:T(8,128)(2,1)S(1)}, u32[]{:S(2)}, u32[]{:S(2)}) collective-permute-start(bf16[64,3072]{1,0:T(8,128)(2,1)} %copy-done.7), channel_id=1, source_target_pairs={{3,2},{7,6},{11,10},{15,14},{19,18},{23,22},{27,26},{31,30}} | collective-permute-start | bytes 1179656 | tf_op jit(solution)/shard_map/ppermute | solution.py:433
  242.9 15.7 %collective-permute-start.66 = (bf16[64,3072]{1,0:T(8,128)(2,1)S(1)}, bf16[64,3072]{1,0:T(8,128)(2,1)S(1)}, u32[]{:S(2)}, u32[]{:S(2)}) collective-permute-start(bf16[64,3072]{1,0:T(8,128)(2,1)S(1)} %get-tuple-element.310), channel_id=1, source_target_pairs={{0,1},{1,2},{4,5},{5,6},{8,9},{9,10},{12,13},{13,14},{16,17},{17,1... | collective-permute-start | bytes 1179656 | tf_op jit(solution)/shard_map/ppermute | solution.py:432
  250.2 18.9 %collective-permute-start.60 = (bf16[64,3072]{1,0:T(8,128)(2,1)S(1)}, bf16[64,3072]{1,0:T(8,128)(2,1)S(1)}, u32[]{:S(2)}, u32[]{:S(2)}) collective-permute-start(bf16[64,3072]{1,0:T(8,128)(2,1)S(1)} %get-tuple-element.308), channel_id=1, source_target_pairs={{0,1},{1,2},{4,5},{5,6},{8,9},{9,10},{12,13},{13,14},{16,17},{17,1... | collective-permute-start | bytes 1179656 | tf_op jit(solution)/shard_map/ppermute | solution.py:432
  254.8 14.4 %collective-permute-start.61 = (bf16[64,3072]{1,0:T(8,128)(2,1)S(1)}, bf16[64,3072]{1,0:T(8,128)(2,1)S(1)}, u32[]{:S(2)}, u32[]{:S(2)}) collective-permute-start(bf16[64,3072]{1,0:T(8,128)(2,1)S(1)} %get-tuple-element.307), channel_id=1, source_target_pairs={{2,1},{3,2},{6,5},{7,6},{10,9},{11,10},{14,13},{15,14},{18,17},{19... | collective-permute-start | bytes 1179656 | tf_op jit(solution)/shard_map/ppermute | solution.py:433
  259.7 18.0 %collective-permute-start.69 = (bf16[64,3072]{1,0:T(8,128)(2,1)S(1)}, bf16[64,3072]{1,0:T(8,128)(2,1)S(1)}, u32[]{:S(2)}, u32[]{:S(2)}) collective-permute-start(bf16[64,3072]{1,0:T(8,128)(2,1)S(1)} %add.273), channel_id=1, source_target_pairs={{1,0},{2,1},{3,2},{5,4},{6,5},{7,6},{9,8},{10,9},{11,10},{13,12},{... | collective-permute-start | bytes 1179656 | tf_op jit(solution)/shard_map/ppermute | solution.py:433
  262.2 15.5 %collective-permute-start.68 = (bf16[64,3072]{1,0:T(8,128)(2,1)S(1)}, bf16[64,3072]{1,0:T(8,128)(2,1)S(1)}, u32[]{:S(2)}, u32[]{:S(2)}) collective-permute-start(bf16[64,3072]{1,0:T(8,128)(2,1)S(1)} %add.272), channel_id=1, source_target_pairs={{0,1},{1,2},{2,3},{4,5},{5,6},{6,7},{8,9},{9,10},{10,11},{12,13},{... | collective-permute-start | bytes 1179656 | tf_op jit(solution)/shard_map/ppermute | solution.py:432
  (68 other events, 751.6 us)

commit v5 on v4

--- a/solution.py
+++ b/solution.py
@@ -150,6 +150,10 @@
     return [[out[s * (out.shape[0] // slots) : (s + 1) * (out.shape[0] // slots)] for s in range(slots)] for out in outs]
 
 
+def in_hbm(arrays):
+    return [pltpu.with_memory_space_constraint(array, pltpu.HBM) for array in arrays]
+
+
 def attend(order, mine, queries, places, pair_list, held, pairs, sharing, block_rows, weight, pieces, grouped):
     slots = len(queries)
     half, width = queries[0].shape
@@ -166,10 +170,9 @@
         grid_spec=pltpu.PrefetchScalarGridSpec(
             num_scalar_prefetch=2,
             grid=(slots // together,),
-            in_specs=[pl.BlockSpec(memory_space=pl.ANY)] * slots
+            in_specs=[pl.BlockSpec(memory_space=pltpu.HBM)] * slots
             + [pl.BlockSpec((together, 1, half), lambda s, *_: (s, 0, 0))]
-            + [pl.BlockSpec(memory_space=pl.ANY)] * len(pair_list)
-            + [pl.BlockSpec(memory_space=pltpu.HBM)],
+            + [pl.BlockSpec(memory_space=pltpu.HBM)] * (len(pair_list) + 1),
             out_specs=[pl.BlockSpec(shape.shape, lambda s, *_: (0, 0)) for shape in shapes],
             scratch_shapes=[pltpu.VMEM((half, width), jnp.bfloat16)] * slots
             + [pltpu.VMEM(pair.shape, pair.dtype) for pair in pair_list]
@@ -192,7 +195,7 @@
             bytes_accessed=2 * (2 * slots * half * width + count * 2 * pairs * HD + weight.size),
             transcendentals=slots * half * width // HD * count,
         ),
-    )(order, mine, *queries, places, *pair_list, pltpu.with_memory_space_constraint(weight, pltpu.HBM))
+    )(order, mine, *in_hbm(queries), places, *in_hbm(pair_list), *in_hbm([weight]))
     return by_piece(outs, slots, pieces, grouped)
 
 
@@ -563,7 +566,7 @@
         return share + jnp.where(named[:, 1] == 0, 1.0 / (1.0 + jnp.exp(first - second)), 0.0)
 
     def expert(which, normed, sources, beside=None):
-        terms = expert_rows(me[None], sources, gate_weight, up_weight, down_weight, shards, pieces, line)
+        terms = expert_rows(me[None], sources, gate_weight, up_weight, down_weight, shards, pieces, False)
         if beside is not None:
             terms, beside = lax.optimization_barrier((terms, beside))
         sums, marks = reduce_line(terms)

time: 285 us -> 278 us (0.975)
  local copies, waits for them, and re-layouts: 14 us -> 6.25 us
    unnamed x107 -> x77, local copies, waits for them, and re-layouts: 14 us -> 4.87 us
  transfers between devices with their start and end apart: 48 -> 48, of which waited for: 23 -> 23; matrix products, arithmetic and copies ran while one was open for 6% -> 6% of each run, Pallas kernels for 22% -> 23%
where the time goes in v5:
time: 278 us; the launch traced here: 277 us
  starting transfers between devices  120 us (43%)
  waiting for transfers between devices  64.8 us (23%)
  Pallas kernels  64.6 us (23%)
  other arithmetic  13.9 us (5%)
  local copies, waits for them, and re-layouts  6.25 us (2%)
  matrix products  5.3 us (2%)
    ppermute x12, starting transfers between devices, reduce_line(): right = lax.ppermute(sent[0], 'tp', rights(s))  51.9 us
    pallas_call x1, Pallas kernels, expert_rows(): pl.pallas_call(functools.partial(expert_kernel, [len(source) for source i...  33.9 us
    pallas_call x2, Pallas kernels, attend(): pl.pallas_call(kernel, grid_spec=pltpu.PrefetchScalarGridSpec(num_scalar_...  26 us
    ppermute x12, waiting for transfers between devices, reduce_line(): right = lax.ppermute(sent[0], 'tp', rights(s))  22.8 us
    ppermute x4, starting transfers between devices, gather_line(): lax.ppermute(right, 'tp', to_right)  18.8 us
    ppermute x9, starting transfers between devices, shift(): lax.ppermute(parts[s], 'tp', moves[s])  18.5 us
    ppermute x9, waiting for transfers between devices, shift(): lax.ppermute(parts[s], 'tp', moves[s])  14.1 us
    ppermute x12, starting transfers between devices, reduce_line(): left = lax.ppermute(sent[1], 'tp', lefts(s))  13 us
  transfers between devices with their start and end apart: 48, of which 23 were waited for; matrix products, arithmetic and copies ran while one was open for 6% of the time, Pallas kernels for 23%

profile of v5, /device:TPU:0, one launch (start us, length us, event | category | flops | bytes accessed | tf_op | source)
XLA Modules:
  0.0 277.1 jit_solution(10376908976753899527)
XLA Ops:
  2.7 3.0 %collective-permute-start.22 = (bf16[128,512]{1,0:T(8,128)(2,1)}, bf16[128,512]{1,0:T(8,128)(2,1)S(1)}, u32[]{:S(2)}, u32[]{:S(2)}) collective-permute-start(bf16[128,512]{1,0:T(8,128)(2,1)} %get-tuple-element.164), channel_id=1, source_target_pairs={{0,1},{1,2},{2,3},{3,0},{4,5},{5,6},{6,7},{7,4},{8,9},{9,10},{10,1... | collective-permute-start | bytes 393224 | tf_op jit(solution)/shard_map/ppermute | solution.py:407
  12.4 4.8 %collective-permute-done.23 = bf16[128,512]{1,0:T(8,128)(2,1)S(1)} collective-permute-done((bf16[128,512]{1,0:T(8,128)(2,1)}, bf16[128,512]{1,0:T(8,128)(2,1)S(1)}, u32[]{:S(2)}, u32[]{:S(2)}) %collective-permute-start.23) | collective-permute-done | bytes 131104 | tf_op jit(solution)/shard_map/ppermute | solution.py:407
  22.1 3.3 %collective-permute-start.26 = (bf16[64,1024]{1,0:T(8,128)(2,1)}, bf16[64,1024]{1,0:T(8,128)(2,1)S(1)}, u32[]{:S(2)}, u32[]{:S(2)}) collective-permute-start(bf16[64,1024]{1,0:T(8,128)(2,1)} %get-tuple-element.170), channel_id=1, source_target_pairs={{0,1},{1,2},{2,3},{3,0},{4,5},{5,6},{6,7},{7,4},{8,9},{9,10},{10,1... | collective-permute-start | bytes 393224 | tf_op jit(solution)/shard_map/ppermute | solution.py:407
  27.8 3.2 %collective-permute-done.26.refs_2_ = bf16[64,1024]{1,0:T(8,128)(2,1)S(1)} collective-permute-done((bf16[64,1024]{1,0:T(8,128)(2,1)}, bf16[64,1024]{1,0:T(8,128)(2,1)S(1)}, u32[]{:S(2)}, u32[]{:S(2)}) %collective-permute-start.26) | collective-permute-done | bytes 131104 | tf_op jit(solution)/shard_map/ppermute | solution.py:407
  31.0 4.3 %collective-permute-done.27.refs_4_ = bf16[64,1024]{1,0:T(8,128)(2,1)S(1)} collective-permute-done((bf16[64,1024]{1,0:T(8,128)(2,1)}, bf16[64,1024]{1,0:T(8,128)(2,1)S(1)}, u32[]{:S(2)}, u32[]{:S(2)}) %collective-permute-start.27) | collective-permute-done | bytes 131104 | tf_op jit(solution)/shard_map/ppermute | solution.py:407
  35.4 3.3 %collective-permute-start.31 = (bf16[64,1024]{1,0:T(8,128)(2,1)}, bf16[64,1024]{1,0:T(8,128)(2,1)}, u32[]{:S(2)}, u32[]{:S(2)}) collective-permute-start(bf16[64,1024]{1,0:T(8,128)(2,1)} %get-tuple-element.188), channel_id=1, source_target_pairs={{0,1},{1,2},{2,3},{3,0},{4,5},{5,6},{6,7},{7,4},{8,9},{9,10},{10,1... | collective-permute-start | bytes 393224 | tf_op jit(solution)/shard_map/ppermute | solution.py:407
  42.8 13.0 %shard_map.133 = (bf16[64,3072]{1,0:T(8,128)(2,1)S(1)}, bf16[64,3072]{1,0:T(8,128)(2,1)S(1)}, bf16[64,3072]{1,0:T(8,128)(2,1)S(1)}, bf16[64,3072]{1,0:T(8,128)(2...) custom-call(s32[4]{0:T(128)S(1)} %copy-done.15, ...), custom_call_target="tpu_custom_call" | custom-call | flops 21474836480 | bytes 15728640 | tf_op jit(solution)/shard_map/pallas_call | solution.py:168
  55.8 3.2 %collective-permute-start.40 = (bf16[64,3072]{1,0:T(8,128)(2,1)S(1)}, bf16[64,3072]{1,0:T(8,128)(2,1)S(1)}, u32[]{:S(2)}, u32[]{:S(2)}) collective-permute-start(bf16[64,3072]{1,0:T(8,128)(2,1)S(1)} %get-tuple-element.206), channel_id=1, source_target_pairs={{0,1},{4,5},{8,9},{12,13},{16,17},{20,21},{24,25},{28,29}} | collective-permute-start | bytes 1179656 | tf_op jit(solution)/shard_map/ppermute | solution.py:435
  61.7 5.8 %collective-permute-done.40 = bf16[64,3072]{1,0:T(8,128)(2,1)S(1)} collective-permute-done((bf16[64,3072]{1,0:T(8,128)(2,1)S(1)}, bf16[64,3072]{1,0:T(8,128)(2,1)S(1)}, u32[]{:S(2)}, u32[]{:S(2)}) %collective-permute-start.40) | collective-permute-done | bytes 393248 | tf_op jit(solution)/shard_map/ppermute | solution.py:435
  68.5 5.1 %collective-permute-start.42 = (bf16[64,3072]{1,0:T(8,128)(2,1)}, bf16[64,3072]{1,0:T(8,128)(2,1)}, u32[]{:S(2)}, u32[]{:S(2)}) collective-permute-start(bf16[64,3072]{1,0:T(8,128)(2,1)} %get-tuple-element.316), channel_id=1, source_target_pairs={{0,1},{1,2},{4,5},{5,6},{8,9},{9,10},{12,13},{13,14},{16,17},{17,1... | collective-permute-start | bytes 1179656 | tf_op jit(solution)/shard_map/ppermute | solution.py:435
  76.9 5.1 %collective-permute-start.36 = (bf16[64,3072]{1,0:T(8,128)(2,1)}, bf16[64,3072]{1,0:T(8,128)(2,1)}, u32[]{:S(2)}, u32[]{:S(2)}) collective-permute-start(bf16[64,3072]{1,0:T(8,128)(2,1)} %get-tuple-element.314), channel_id=1, source_target_pairs={{0,1},{1,2},{4,5},{5,6},{8,9},{9,10},{12,13},{13,14},{16,17},{17,1... | collective-permute-start | bytes 1179656 | tf_op jit(solution)/shard_map/ppermute | solution.py:435
  88.7 4.6 %collective-permute-start.44 = (bf16[64,3072]{1,0:T(8,128)(2,1)S(1)}, bf16[64,3072]{1,0:T(8,128)(2,1)S(1)}, u32[]{:S(2)}, u32[]{:S(2)}) collective-permute-start(bf16[64,3072]{1,0:T(8,128)(2,1)S(1)} %add.239), channel_id=1, source_target_pairs={{0,1},{1,2},{2,3},{4,5},{5,6},{6,7},{8,9},{9,10},{10,11},{12,13},{... | collective-permute-start | bytes 1179656 | tf_op jit(solution)/shard_map/ppermute | solution.py:435
  96.8 4.7 %collective-permute-start.38 = (bf16[64,3072]{1,0:T(8,128)(2,1)S(1)}, bf16[64,3072]{1,0:T(8,128)(2,1)S(1)}, u32[]{:S(2)}, u32[]{:S(2)}) collective-permute-start(bf16[64,3072]{1,0:T(8,128)(2,1)S(1)} %add.232), channel_id=1, source_target_pairs={{0,1},{1,2},{2,3},{4,5},{5,6},{6,7},{8,9},{9,10},{10,11},{12,13},{... | collective-permute-start | bytes 1179656 | tf_op jit(solution)/shard_map/ppermute | solution.py:435
  102.0 5.5 %collective-permute-done.39 = bf16[64,3072]{1,0:T(8,128)(2,1)S(1)} collective-permute-done((bf16[64,3072]{1,0:T(8,128)(2,1)S(1)}, bf16[64,3072]{1,0:T(8,128)(2,1)S(1)}, u32[]{:S(2)}, u32[]{:S(2)}) %collective-permute-start.39) | collective-permute-done | bytes 393248 | tf_op jit(solution)/shard_map/ppermute | solution.py:436
  111.4 4.4 %collective-permute-start.46 = (bf16[64,6144]{1,0:T(8,128)(2,1)S(1)}, bf16[64,6144]{1,0:T(8,128)(2,1)S(1)}, u32[]{:S(2)}, u32[]{:S(2)}) collective-permute-start(bf16[64,6144]{1,0:T(8,128)(2,1)S(1)} %fusion.7.refs_1_), channel_id=1, source_target_pairs={{0,1},{1,2},{2,3},{4,5},{5,6},{6,7},{8,9},{9,10},{10,11},{12,13},{... | collective-permute-start | bytes 2359304 | tf_op jit(solution)/shard_map/ppermute | solution.py:448
  117.2 13.0 %shard_map.134 = (bf16[64,3072]{1,0:T(8,128)(2,1)S(1)}, bf16[64,3072]{1,0:T(8,128)(2,1)S(1)}, bf16[64,3072]{1,0:T(8,128)(2,1)S(1)}, bf16[64,3072]{1,0:T(8,128)(2...) custom-call(s32[4]{0:T(128)S(1)} %copy-done.15, ...), custom_call_target="tpu_custom_call" | custom-call | flops 21474836480 | bytes 15728640 | tf_op jit(solution)/shard_map/pallas_call | solution.py:168
  130.3 3.1 %collective-permute-done.46 = bf16[64,6144]{1,0:T(8,128)(2,1)S(1)} collective-permute-done((bf16[64,6144]{1,0:T(8,128)(2,1)S(1)}, bf16[64,6144]{1,0:T(8,128)(2,1)S(1)}, u32[]{:S(2)}, u32[]{:S(2)}) %collective-permute-start.46) | collective-permute-done | bytes 786464 | tf_op jit(solution)/shard_map/ppermute | solution.py:448
  133.4 4.2 %collective-permute-done.47 = bf16[64,6144]{1,0:T(8,128)(2,1)S(1)} collective-permute-done((bf16[64,6144]{1,0:T(8,128)(2,1)S(1)}, bf16[64,6144]{1,0:T(8,128)(2,1)S(1)}, u32[]{:S(2)}, u32[]{:S(2)}) %collective-permute-start.47) | collective-permute-done | bytes 786464 | tf_op jit(solution)/shard_map/ppermute | solution.py:449
  139.1 5.3 %collective-permute-start.48 = (bf16[64,3072]{1,0:T(8,128)(2,1)S(1)}, bf16[64,3072]{1,0:T(8,128)(2,1)}, u32[]{:S(2)}, u32[]{:S(2)}) collective-permute-start(bf16[64,3072]{1,0:T(8,128)(2,1)S(1)} %get-tuple-element.304.refs_2_), channel_id=1, source_target_pairs={{0,1},{1,2},{2,3},{4,5},{5,6},{6,7},{8,9},{9,10},{10,11},{12,13},{... | collective-permute-start | bytes 1179656 | tf_op jit(solution)/shard_map/ppermute | solution.py:470
  145.8 4.6 %collective-permute-start.50 = (bf16[64,3072]{1,0:T(8,128)(2,1)S(1)}, bf16[64,3072]{1,0:T(8,128)(2,1)S(1)}, u32[]{:S(2)}, u32[]{:S(2)}) collective-permute-start(bf16[64,3072]{1,0:T(8,128)(2,1)S(1)} %get-tuple-element.303.refs_3_), channel_id=1, source_target_pairs={{0,1},{1,2},{2,3},{4,5},{5,6},{6,7},{8,9},{9,10},{10,11},{12,13},{... | collective-permute-start | bytes 1179656 | tf_op jit(solution)/shard_map/ppermute | solution.py:470
  154.5 4.5 %collective-permute-start.52 = (bf16[64,3072]{1,0:T(8,128)(2,1)S(1)}, bf16[64,3072]{1,0:T(8,128)(2,1)S(1)}, u32[]{:S(2)}, u32[]{:S(2)}) collective-permute-start(bf16[64,3072]{1,0:T(8,128)(2,1)S(1)} %get-tuple-element.312.refs_4_), channel_id=1, source_target_pairs={{0,1},{1,2},{2,3},{4,5},{5,6},{6,7},{8,9},{9,10},{10,11},{12,13},{... | collective-permute-start | bytes 1179656 | tf_op jit(solution)/shard_map/ppermute | solution.py:470
  161.7 4.4 %collective-permute-start.54 = (bf16[64,3072]{1,0:T(8,128)(2,1)S(1)}, bf16[64,3072]{1,0:T(8,128)(2,1)S(1)}, u32[]{:S(2)}, u32[]{:S(2)}) collective-permute-start(bf16[64,3072]{1,0:T(8,128)(2,1)S(1)} %get-tuple-element.310.refs_5_), channel_id=1, source_target_pairs={{0,1},{1,2},{2,3},{4,5},{5,6},{6,7},{8,9},{9,10},{10,11},{12,13},{... | collective-permute-start | bytes 1179656 | tf_op jit(solution)/shard_map/ppermute | solution.py:470
  170.7 6.0 %collective-permute-done.54.refs_7_ = bf16[64,3072]{1,0:T(8,128)(2,1)S(1)} collective-permute-done((bf16[64,3072]{1,0:T(8,128)(2,1)S(1)}, bf16[64,3072]{1,0:T(8,128)(2,1)S(1)}, u32[]{:S(2)}, u32[]{:S(2)}) %collective-permute-start.54) | collective-permute-done | bytes 393248 | tf_op jit(solution)/shard_map/ppermute | solution.py:470
  177.3 3.9 %collective-permute-start.56 = (bf16[64,6144]{1,0:T(8,128)(2,1)S(1)}, bf16[64,6144]{1,0:T(8,128)(2,1)S(1)}, u32[]{:S(2)}, u32[]{:S(2)}) collective-permute-start(bf16[64,6144]{1,0:T(8,128)(2,1)S(1)} %pad_maximum_fusion.2), channel_id=1, source_target_pairs={{0,1},{1,2},{2,3},{4,5},{5,6},{6,7},{8,9},{9,10},{10,11},{12,13},{... | collective-permute-start | bytes 2359304 | tf_op jit(solution)/shard_map/ppermute | solution.py:479
  182.8 33.9 %shard_map.135 = (bf16[256,3072]{1,0:T(8,128)(2,1)S(1)}, bf16[256,3072]{1,0:T(8,128)(2,1)S(1)}) custom-call(s32[1]{0:T(128)} %bitcast.6.mine.refs_0_, bf16[64,6144]{1,0:T(8,128)(2,1)S(1)} %fusion.7.refs_1_, bf16[64,3072]{1,0:T(8,128)(2,1)S(1)} %get-tuple-element.304.refs_2_, bf16[64,3072]{1,0:T(8,128)(2,1)S(1)} %get-tuple-element.303.refs_3_, ...), custom_call_target="tpu_custom_call" | custom-call | flops 19327352832 | bytes 75497472 | tf_op jit(solution)/shard_map/pallas_call | solution.py:263
  219.5 4.7 %collective-permute-start.64 = (bf16[64,3072]{1,0:T(8,128)(2,1)}, bf16[64,3072]{1,0:T(8,128)(2,1)S(1)}, u32[]{:S(2)}, u32[]{:S(2)}) collective-permute-start(bf16[64,3072]{1,0:T(8,128)(2,1)} %get-tuple-element.257), channel_id=1, source_target_pairs={{0,1},{4,5},{8,9},{12,13},{16,17},{20,21},{24,25},{28,29}} | collective-permute-start | bytes 1179656 | tf_op jit(solution)/shard_map/ppermute | solution.py:435
  228.2 5.8 %collective-permute-done.64 = bf16[64,3072]{1,0:T(8,128)(2,1)S(1)} collective-permute-done((bf16[64,3072]{1,0:T(8,128)(2,1)}, bf16[64,3072]{1,0:T(8,128)(2,1)S(1)}, u32[]{:S(2)}, u32[]{:S(2)}) %collective-permute-start.64) | collective-permute-done | bytes 393248 | tf_op jit(solution)/shard_map/ppermute | solution.py:435
  235.2 4.3 %collective-permute-start.66 = (bf16[64,3072]{1,0:T(8,128)(2,1)S(1)}, bf16[64,3072]{1,0:T(8,128)(2,1)S(1)}, u32[]{:S(2)}, u32[]{:S(2)}) collective-permute-start(bf16[64,3072]{1,0:T(8,128)(2,1)S(1)} %get-tuple-element.308), channel_id=1, source_target_pairs={{0,1},{1,2},{4,5},{5,6},{8,9},{9,10},{12,13},{13,14},{16,17},{17,1... | collective-permute-start | bytes 1179656 | tf_op jit(solution)/shard_map/ppermute | solution.py:435
  242.4 4.4 %collective-permute-start.60 = (bf16[64,3072]{1,0:T(8,128)(2,1)S(1)}, bf16[64,3072]{1,0:T(8,128)(2,1)S(1)}, u32[]{:S(2)}, u32[]{:S(2)}) collective-permute-start(bf16[64,3072]{1,0:T(8,128)(2,1)S(1)} %get-tuple-element.306), channel_id=1, source_target_pairs={{0,1},{1,2},{4,5},{5,6},{8,9},{9,10},{12,13},{13,14},{16,17},{17,1... | collective-permute-start | bytes 1179656 | tf_op jit(solution)/shard_map/ppermute | solution.py:435
  247.7 3.1 %collective-permute-done.66 = bf16[64,3072]{1,0:T(8,128)(2,1)S(1)} collective-permute-done((bf16[64,3072]{1,0:T(8,128)(2,1)S(1)}, bf16[64,3072]{1,0:T(8,128)(2,1)S(1)}, u32[]{:S(2)}, u32[]{:S(2)}) %collective-permute-start.66) | collective-permute-done | bytes 393248 | tf_op jit(solution)/shard_map/ppermute | solution.py:435
  253.4 7.3 %collective-permute-start.68 = (bf16[64,3072]{1,0:T(8,128)(2,1)S(1)}, bf16[64,3072]{1,0:T(8,128)(2,1)S(1)}, u32[]{:S(2)}, u32[]{:S(2)}) collective-permute-start(bf16[64,3072]{1,0:T(8,128)(2,1)S(1)} %add.272), channel_id=1, source_target_pairs={{0,1},{1,2},{2,3},{4,5},{5,6},{6,7},{8,9},{9,10},{10,11},{12,13},{... | collective-permute-start | bytes 1179656 | tf_op jit(solution)/shard_map/ppermute | solution.py:435
  262.3 5.9 %collective-permute-start.62 = (bf16[64,3072]{1,0:T(8,128)(2,1)S(1)}, bf16[64,3072]{1,0:T(8,128)(2,1)S(1)}, u32[]{:S(2)}, u32[]{:S(2)}) collective-permute-start(bf16[64,3072]{1,0:T(8,128)(2,1)S(1)} %add.262), channel_id=1, source_target_pairs={{0,1},{1,2},{2,3},{4,5},{5,6},{6,7},{8,9},{9,10},{10,11},{12,13},{... | collective-permute-start | bytes 1179656 | tf_op jit(solution)/shard_map/ppermute | solution.py:435
  (190 shorter events, 83.2 us)
Async XLA Ops:
  17.2 18.1 %collective-permute-start.25 = (bf16[512,512]{1,0:T(8,128)(2,1)S(1)}, bf16[512,512]{1,0:T(8,128)(2,1)S(1)}, u32[]{:S(2)}, u32[]{:S(2)}) collective-permute-start(bf16[512,512]{1,0:T(8,128)(2,1)S(1)} %constant_dynamic-update-slice_fusion.refs_7_), channel_id=1, source_target_pairs={{0,8},{4,12},{8,0},{12,4},{1,9},{5,13},{9,1},{13,5},{2,10},{6,14},... | collective-permute-start | bytes 1572872 | tf_op jit(solution)/shard_map/ppermute | solution.py:513
  27.8 13.5 %collective-permute-start.29 = (bf16[512,512]{1,0:T(8,128)(2,1)S(1)}, bf16[512,512]{1,0:T(8,128)(2,1)S(1)}, u32[]{:S(2)}, u32[]{:S(2)}) collective-permute-start(bf16[512,512]{1,0:T(8,128)(2,1)S(1)} %constant_dynamic-update-slice_fusion.refs_7_), channel_id=1, source_target_pairs={{0,4},{4,0},{8,12},{12,8},{1,5},{5,1},{9,13},{13,9},{2,6},{6,2},{1... | collective-permute-start | bytes 1572872 | tf_op jit(solution)/shard_map/ppermute | solution.py:513
  35.4 20.3 %collective-permute-start.31 = (bf16[64,1024]{1,0:T(8,128)(2,1)}, bf16[64,1024]{1,0:T(8,128)(2,1)}, u32[]{:S(2)}, u32[]{:S(2)}) collective-permute-start(bf16[64,1024]{1,0:T(8,128)(2,1)} %get-tuple-element.188), channel_id=1, source_target_pairs={{0,1},{1,2},{2,3},{3,0},{4,5},{5,6},{6,7},{7,4},{8,9},{9,10},{10,1... | collective-permute-start | bytes 393224 | tf_op jit(solution)/shard_map/ppermute | solution.py:407
  38.7 17.0 %collective-permute-start.32 = (bf16[64,1024]{1,0:T(8,128)(2,1)}, bf16[64,1024]{1,0:T(8,128)(2,1)}, u32[]{:S(2)}, u32[]{:S(2)}) collective-permute-start(bf16[64,1024]{1,0:T(8,128)(2,1)} %get-tuple-element.189), channel_id=1, source_target_pairs={{0,2},{1,3},{2,0},{3,1},{4,6},{5,7},{6,4},{7,5},{8,10},{9,11},{10,... | collective-permute-start | bytes 393224 | tf_op jit(solution)/shard_map/ppermute | solution.py:407
  40.5 15.3 %collective-permute-start.33 = (bf16[64,1024]{1,0:T(8,128)(2,1)}, bf16[64,1024]{1,0:T(8,128)(2,1)}, u32[]{:S(2)}, u32[]{:S(2)}) collective-permute-start(bf16[64,1024]{1,0:T(8,128)(2,1)} %get-tuple-element.190), channel_id=1, source_target_pairs={{0,3},{1,0},{2,1},{3,2},{4,7},{5,4},{6,5},{7,6},{8,11},{9,8},{10,9... | collective-permute-start | bytes 393224 | tf_op jit(solution)/shard_map/ppermute | solution.py:407
  55.8 11.8 %collective-permute-start.40 = (bf16[64,3072]{1,0:T(8,128)(2,1)S(1)}, bf16[64,3072]{1,0:T(8,128)(2,1)S(1)}, u32[]{:S(2)}, u32[]{:S(2)}) collective-permute-start(bf16[64,3072]{1,0:T(8,128)(2,1)S(1)} %get-tuple-element.206), channel_id=1, source_target_pairs={{0,1},{4,5},{8,9},{12,13},{16,17},{20,21},{24,25},{28,29}} | collective-permute-start | bytes 1179656 | tf_op jit(solution)/shard_map/ppermute | solution.py:435
  59.7 16.3 %collective-permute-start.34 = (bf16[64,3072]{1,0:T(8,128)(2,1)S(1)}, bf16[64,3072]{1,0:T(8,128)(2,1)S(1)}, u32[]{:S(2)}, u32[]{:S(2)}) collective-permute-start(bf16[64,3072]{1,0:T(8,128)(2,1)S(1)} %get-tuple-element.191), channel_id=1, source_target_pairs={{0,1},{4,5},{8,9},{12,13},{16,17},{20,21},{24,25},{28,29}} | collective-permute-start | bytes 1179656 | tf_op jit(solution)/shard_map/ppermute | solution.py:435
  61.0 14.9 %collective-permute-start.35 = (bf16[64,3072]{1,0:T(8,128)(2,1)S(1)}, bf16[64,3072]{1,0:T(8,128)(2,1)S(1)}, u32[]{:S(2)}, u32[]{:S(2)}) collective-permute-start(bf16[64,3072]{1,0:T(8,128)(2,1)S(1)} %get-tuple-element.192), channel_id=1, source_target_pairs={{3,2},{7,6},{11,10},{15,14},{19,18},{23,22},{27,26},{31,30}} | collective-permute-start | bytes 1179656 | tf_op jit(solution)/shard_map/ppermute | solution.py:436
  68.5 16.4 %collective-permute-start.42 = (bf16[64,3072]{1,0:T(8,128)(2,1)}, bf16[64,3072]{1,0:T(8,128)(2,1)}, u32[]{:S(2)}, u32[]{:S(2)}) collective-permute-start(bf16[64,3072]{1,0:T(8,128)(2,1)} %get-tuple-element.316), channel_id=1, source_target_pairs={{0,1},{1,2},{4,5},{5,6},{8,9},{9,10},{12,13},{13,14},{16,17},{17,1... | collective-permute-start | bytes 1179656 | tf_op jit(solution)/shard_map/ppermute | solution.py:435
  76.9 16.4 %collective-permute-start.36 = (bf16[64,3072]{1,0:T(8,128)(2,1)}, bf16[64,3072]{1,0:T(8,128)(2,1)}, u32[]{:S(2)}, u32[]{:S(2)}) collective-permute-start(bf16[64,3072]{1,0:T(8,128)(2,1)} %get-tuple-element.314), channel_id=1, source_target_pairs={{0,1},{1,2},{4,5},{5,6},{8,9},{9,10},{12,13},{13,14},{16,17},{17,1... | collective-permute-start | bytes 1179656 | tf_op jit(solution)/shard_map/ppermute | solution.py:435
  86.3 15.3 %collective-permute-start.45 = (bf16[64,3072]{1,0:T(8,128)(2,1)S(1)}, bf16[64,3072]{1,0:T(8,128)(2,1)S(1)}, u32[]{:S(2)}, u32[]{:S(2)}) collective-permute-start(bf16[64,3072]{1,0:T(8,128)(2,1)S(1)} %add.240), channel_id=1, source_target_pairs={{1,0},{2,1},{3,2},{5,4},{6,5},{7,6},{9,8},{10,9},{11,10},{13,12},{... | collective-permute-start | bytes 1179656 | tf_op jit(solution)/shard_map/ppermute | solution.py:436
  88.7 13.3 %collective-permute-start.44 = (bf16[64,3072]{1,0:T(8,128)(2,1)S(1)}, bf16[64,3072]{1,0:T(8,128)(2,1)S(1)}, u32[]{:S(2)}, u32[]{:S(2)}) collective-permute-start(bf16[64,3072]{1,0:T(8,128)(2,1)S(1)} %add.239), channel_id=1, source_target_pairs={{0,1},{1,2},{2,3},{4,5},{5,6},{6,7},{8,9},{9,10},{10,11},{12,13},{... | collective-permute-start | bytes 1179656 | tf_op jit(solution)/shard_map/ppermute | solution.py:435
  94.4 13.1 %collective-permute-start.39 = (bf16[64,3072]{1,0:T(8,128)(2,1)S(1)}, bf16[64,3072]{1,0:T(8,128)(2,1)S(1)}, u32[]{:S(2)}, u32[]{:S(2)}) collective-permute-start(bf16[64,3072]{1,0:T(8,128)(2,1)S(1)} %add.233), channel_id=1, source_target_pairs={{1,0},{2,1},{3,2},{5,4},{6,5},{7,6},{9,8},{10,9},{11,10},{13,12},{... | collective-permute-start | bytes 1179656 | tf_op jit(solution)/shard_map/ppermute | solution.py:436
  96.8 13.6 %collective-permute-start.38 = (bf16[64,3072]{1,0:T(8,128)(2,1)S(1)}, bf16[64,3072]{1,0:T(8,128)(2,1)S(1)}, u32[]{:S(2)}, u32[]{:S(2)}) collective-permute-start(bf16[64,3072]{1,0:T(8,128)(2,1)S(1)} %add.232), channel_id=1, source_target_pairs={{0,1},{1,2},{2,3},{4,5},{5,6},{6,7},{8,9},{9,10},{10,11},{12,13},{... | collective-permute-start | bytes 1179656 | tf_op jit(solution)/shard_map/ppermute | solution.py:435
  111.4 21.9 %collective-permute-start.46 = (bf16[64,6144]{1,0:T(8,128)(2,1)S(1)}, bf16[64,6144]{1,0:T(8,128)(2,1)S(1)}, u32[]{:S(2)}, u32[]{:S(2)}) collective-permute-start(bf16[64,6144]{1,0:T(8,128)(2,1)S(1)} %fusion.7.refs_1_), channel_id=1, source_target_pairs={{0,1},{1,2},{2,3},{4,5},{5,6},{6,7},{8,9},{9,10},{10,11},{12,13},{... | collective-permute-start | bytes 2359304 | tf_op jit(solution)/shard_map/ppermute | solution.py:448
  115.9 21.7 %collective-permute-start.47 = (bf16[64,6144]{1,0:T(8,128)(2,1)S(1)}, bf16[64,6144]{1,0:T(8,128)(2,1)S(1)}, u32[]{:S(2)}, u32[]{:S(2)}) collective-permute-start(bf16[64,6144]{1,0:T(8,128)(2,1)S(1)} %fusion.7.refs_1_), channel_id=1, source_target_pairs={{1,0},{2,1},{3,2},{5,4},{6,5},{7,6},{9,8},{10,9},{11,10},{13,12},{... | collective-permute-start | bytes 2359304 | tf_op jit(solution)/shard_map/ppermute | solution.py:449
  137.6 14.0 %collective-permute-start.49 = (bf16[64,3072]{1,0:T(8,128)(2,1)S(1)}, bf16[64,3072]{1,0:T(8,128)(2,1)}, u32[]{:S(2)}, u32[]{:S(2)}) collective-permute-start(bf16[64,3072]{1,0:T(8,128)(2,1)S(1)} %get-tuple-element.302.refs_8_), channel_id=1, source_target_pairs={{1,0},{2,1},{3,2},{5,4},{6,5},{7,6},{9,8},{10,9},{11,10},{13,12},{... | collective-permute-start | bytes 1179656 | tf_op jit(solution)/shard_map/ppermute | solution.py:470
  139.1 14.1 %collective-permute-start.48 = (bf16[64,3072]{1,0:T(8,128)(2,1)S(1)}, bf16[64,3072]{1,0:T(8,128)(2,1)}, u32[]{:S(2)}, u32[]{:S(2)}) collective-permute-start(bf16[64,3072]{1,0:T(8,128)(2,1)S(1)} %get-tuple-element.304.refs_2_), channel_id=1, source_target_pairs={{0,1},{1,2},{2,3},{4,5},{5,6},{6,7},{8,9},{9,10},{10,11},{12,13},{... | collective-permute-start | bytes 1179656 | tf_op jit(solution)/shard_map/ppermute | solution.py:470
  144.4 16.0 %collective-permute-start.51 = (bf16[64,3072]{1,0:T(8,128)(2,1)S(1)}, bf16[64,3072]{1,0:T(8,128)(2,1)S(1)}, u32[]{:S(2)}, u32[]{:S(2)}) collective-permute-start(bf16[64,3072]{1,0:T(8,128)(2,1)S(1)} %get-tuple-element.301.refs_9_), channel_id=1, source_target_pairs={{1,0},{2,1},{3,2},{5,4},{6,5},{7,6},{9,8},{10,9},{11,10},{13,12},{... | collective-permute-start | bytes 1179656 | tf_op jit(solution)/shard_map/ppermute | solution.py:470
  145.8 15.8 %collective-permute-start.50 = (bf16[64,3072]{1,0:T(8,128)(2,1)S(1)}, bf16[64,3072]{1,0:T(8,128)(2,1)S(1)}, u32[]{:S(2)}, u32[]{:S(2)}) collective-permute-start(bf16[64,3072]{1,0:T(8,128)(2,1)S(1)} %get-tuple-element.303.refs_3_), channel_id=1, source_target_pairs={{0,1},{1,2},{2,3},{4,5},{5,6},{6,7},{8,9},{9,10},{10,11},{12,13},{... | collective-permute-start | bytes 1179656 | tf_op jit(solution)/shard_map/ppermute | solution.py:470
  154.5 15.5 %collective-permute-start.52 = (bf16[64,3072]{1,0:T(8,128)(2,1)S(1)}, bf16[64,3072]{1,0:T(8,128)(2,1)S(1)}, u32[]{:S(2)}, u32[]{:S(2)}) collective-permute-start(bf16[64,3072]{1,0:T(8,128)(2,1)S(1)} %get-tuple-element.312.refs_4_), channel_id=1, source_target_pairs={{0,1},{1,2},{2,3},{4,5},{5,6},{6,7},{8,9},{9,10},{10,11},{12,13},{... | collective-permute-start | bytes 1179656 | tf_op jit(solution)/shard_map/ppermute | solution.py:470
  161.7 15.0 %collective-permute-start.54 = (bf16[64,3072]{1,0:T(8,128)(2,1)S(1)}, bf16[64,3072]{1,0:T(8,128)(2,1)S(1)}, u32[]{:S(2)}, u32[]{:S(2)}) collective-permute-start(bf16[64,3072]{1,0:T(8,128)(2,1)S(1)} %get-tuple-element.310.refs_5_), channel_id=1, source_target_pairs={{0,1},{1,2},{2,3},{4,5},{5,6},{6,7},{8,9},{9,10},{10,11},{12,13},{... | collective-permute-start | bytes 1179656 | tf_op jit(solution)/shard_map/ppermute | solution.py:470
  177.3 40.7 %collective-permute-start.56 = (bf16[64,6144]{1,0:T(8,128)(2,1)S(1)}, bf16[64,6144]{1,0:T(8,128)(2,1)S(1)}, u32[]{:S(2)}, u32[]{:S(2)}) collective-permute-start(bf16[64,6144]{1,0:T(8,128)(2,1)S(1)} %pad_maximum_fusion.2), channel_id=1, source_target_pairs={{0,1},{1,2},{2,3},{4,5},{5,6},{6,7},{8,9},{9,10},{10,11},{12,13},{... | collective-permute-start | bytes 2359304 | tf_op jit(solution)/shard_map/ppermute | solution.py:479
  181.5 36.5 %collective-permute-start.57 = (bf16[64,6144]{1,0:T(8,128)(2,1)S(1)}, bf16[64,6144]{1,0:T(8,128)(2,1)S(1)}, u32[]{:S(2)}, u32[]{:S(2)}) collective-permute-start(bf16[64,6144]{1,0:T(8,128)(2,1)S(1)} %pad_maximum_fusion.3), channel_id=1, source_target_pairs={{1,0},{2,1},{3,2},{5,4},{6,5},{7,6},{9,8},{10,9},{11,10},{13,12},{... | collective-permute-start | bytes 2359304 | tf_op jit(solution)/shard_map/ppermute | solution.py:480
  219.5 14.6 %collective-permute-start.64 = (bf16[64,3072]{1,0:T(8,128)(2,1)}, bf16[64,3072]{1,0:T(8,128)(2,1)S(1)}, u32[]{:S(2)}, u32[]{:S(2)}) collective-permute-start(bf16[64,3072]{1,0:T(8,128)(2,1)} %get-tuple-element.257), channel_id=1, source_target_pairs={{0,1},{4,5},{8,9},{12,13},{16,17},{20,21},{24,25},{28,29}} | collective-permute-start | bytes 1179656 | tf_op jit(solution)/shard_map/ppermute | solution.py:435
  226.2 16.1 %collective-permute-start.58 = (bf16[64,3072]{1,0:T(8,128)(2,1)S(1)}, bf16[64,3072]{1,0:T(8,128)(2,1)S(1)}, u32[]{:S(2)}, u32[]{:S(2)}) collective-permute-start(bf16[64,3072]{1,0:T(8,128)(2,1)S(1)} %get-tuple-element.246), channel_id=1, source_target_pairs={{0,1},{4,5},{8,9},{12,13},{16,17},{20,21},{24,25},{28,29}} | collective-permute-start | bytes 1179656 | tf_op jit(solution)/shard_map/ppermute | solution.py:435
  227.5 14.8 %collective-permute-start.59 = (bf16[64,3072]{1,0:T(8,128)(2,1)S(1)}, bf16[64,3072]{1,0:T(8,128)(2,1)S(1)}, u32[]{:S(2)}, u32[]{:S(2)}) collective-permute-start(bf16[64,3072]{1,0:T(8,128)(2,1)S(1)} %get-tuple-element.244), channel_id=1, source_target_pairs={{3,2},{7,6},{11,10},{15,14},{19,18},{23,22},{27,26},{31,30}} | collective-permute-start | bytes 1179656 | tf_op jit(solution)/shard_map/ppermute | solution.py:436
  235.2 15.6 %collective-permute-start.66 = (bf16[64,3072]{1,0:T(8,128)(2,1)S(1)}, bf16[64,3072]{1,0:T(8,128)(2,1)S(1)}, u32[]{:S(2)}, u32[]{:S(2)}) collective-permute-start(bf16[64,3072]{1,0:T(8,128)(2,1)S(1)} %get-tuple-element.308), channel_id=1, source_target_pairs={{0,1},{1,2},{4,5},{5,6},{8,9},{9,10},{12,13},{13,14},{16,17},{17,1... | collective-permute-start | bytes 1179656 | tf_op jit(solution)/shard_map/ppermute | solution.py:435
  242.4 18.3 %collective-permute-start.60 = (bf16[64,3072]{1,0:T(8,128)(2,1)S(1)}, bf16[64,3072]{1,0:T(8,128)(2,1)S(1)}, u32[]{:S(2)}, u32[]{:S(2)}) collective-permute-start(bf16[64,3072]{1,0:T(8,128)(2,1)S(1)} %get-tuple-element.306), channel_id=1, source_target_pairs={{0,1},{1,2},{4,5},{5,6},{8,9},{9,10},{12,13},{13,14},{16,17},{17,1... | collective-permute-start | bytes 1179656 | tf_op jit(solution)/shard_map/ppermute | solution.py:435
  246.8 13.9 %collective-permute-start.61 = (bf16[64,3072]{1,0:T(8,128)(2,1)S(1)}, bf16[64,3072]{1,0:T(8,128)(2,1)S(1)}, u32[]{:S(2)}, u32[]{:S(2)}) collective-permute-start(bf16[64,3072]{1,0:T(8,128)(2,1)S(1)} %get-tuple-element.305), channel_id=1, source_target_pairs={{2,1},{3,2},{6,5},{7,6},{10,9},{11,10},{14,13},{15,14},{18,17},{19... | collective-permute-start | bytes 1179656 | tf_op jit(solution)/shard_map/ppermute | solution.py:436
  251.9 18.4 %collective-permute-start.69 = (bf16[64,3072]{1,0:T(8,128)(2,1)S(1)}, bf16[64,3072]{1,0:T(8,128)(2,1)S(1)}, u32[]{:S(2)}, u32[]{:S(2)}) collective-permute-start(bf16[64,3072]{1,0:T(8,128)(2,1)S(1)} %add.273), channel_id=1, source_target_pairs={{1,0},{2,1},{3,2},{5,4},{6,5},{7,6},{9,8},{10,9},{11,10},{13,12},{... | collective-permute-start | bytes 1179656 | tf_op jit(solution)/shard_map/ppermute | solution.py:436
  253.4 16.9 %collective-permute-start.68 = (bf16[64,3072]{1,0:T(8,128)(2,1)S(1)}, bf16[64,3072]{1,0:T(8,128)(2,1)S(1)}, u32[]{:S(2)}, u32[]{:S(2)}) collective-permute-start(bf16[64,3072]{1,0:T(8,128)(2,1)S(1)} %add.272), channel_id=1, source_target_pairs={{0,1},{1,2},{2,3},{4,5},{5,6},{6,7},{8,9},{9,10},{10,11},{12,13},{... | collective-permute-start | bytes 1179656 | tf_op jit(solution)/shard_map/ppermute | solution.py:435
  (53 other events, 618.3 us)

commit v6 on v5

--- a/solution.py
+++ b/solution.py
@@ -476,9 +476,9 @@
         if terms is not None:
             right = jnp.concatenate([right + term[shards - 1] for (right, _), term in zip(got, terms)], axis=1)
             left = jnp.concatenate([left + term[1] for (_, left), term in zip(got, terms)], axis=1)
-            right = lax.ppermute(right, "tp", rights(shards - 1)).astype(jnp.float32)
-            left = lax.ppermute(left, "tp", lefts(shards - 1)).astype(jnp.float32)
-            total = jnp.concatenate([term[0] for term in terms], axis=1).astype(jnp.float32) + right + left
+            right = lax.ppermute(right, "tp", rights(shards - 1))
+            left = lax.ppermute(left, "tp", lefts(shards - 1))
+            total = (right, left)
         return [[source]] + from_left + from_right, total
 
     picked = ((routes[:, 0] == 0) | (routes[:, 1] == 0)).reshape(shards, rows)
@@ -541,7 +541,7 @@
             block_rows,
             out_weight,
             pieces,
-            line,
+            False,
         )
         return [[term[slots.index(s)] for s in range(shards)] for term in terms]
 
@@ -595,9 +595,12 @@
     if halves == 1:
         return (restore([first_half]), restore([expert(0, normed, gather_line(normed)[0])[0]]))
     asked[1], _ = lax.optimization_barrier((asked[1], normed))
-    sources, second_sum = gather_line(normed, project(1))
+    terms = project(1)
+    sources, arrived = gather_line(normed, terms)
+    part, (right, left) = expert(0, normed, sources, arrived)
+    own = jnp.concatenate([term[0] for term in terms], axis=1).astype(jnp.float32)
+    second_sum = own + right.astype(jnp.float32) + left.astype(jnp.float32)
     second_half = (hidden[half:].astype(jnp.float32) + second_sum).astype(jnp.bfloat16)
-    part, second_half = expert(0, normed, sources, second_half)
     part, late = lax.optimization_barrier((part, second_half))
     late = lax.cond(crowded[0] > 0, late_expert, jnp.zeros_like, late)
     return (restore([first_half, second_half]), restore([part, late]))

time: 278 us -> 280 us (level); the launches traced: 277 us -> 275 us
  starting transfers between devices: 120 us -> 109 us
  waiting for transfers between devices: 64.8 us -> 71.3 us
    ppermute x4, waiting for transfers between devices: 2.35 us -> 14.4 us  [gather_line(): lax.ppermute(left, 'tp', to_left)]
    ppermute x4, waiting for transfers between devices: 11.3 us -> 4.15 us  [gather_line(): lax.ppermute(right, 'tp', to_right)]
    ppermute x4, starting transfers between devices: 18.8 us -> 12.9 us  [gather_line(): lax.ppermute(right, 'tp', to_right)]
    ppermute x12, starting transfers between devices: 51.9 us -> 47.2 us  [reduce_line(): right = lax.ppermute(sent[0], 'tp', rights(s))]
    ppermute x12, waiting for transfers between devices: 6.94 us -> 9.99 us  [reduce_line(): left = lax.ppermute(sent[1], 'tp', lefts(s))]
  transfers between devices with their start and end apart: 48 -> 48, of which waited for: 23 -> 21; matrix products, arithmetic and copies ran while one was open for 6% -> 6% of each run, Pallas kernels for 23% -> 23%
where the time goes in v6:
time: 280 us; the launch traced here: 275 us
  starting transfers between devices  109 us (39%)
  waiting for transfers between devices  71.3 us (25%)
  Pallas kernels  66.3 us (24%)
  other arithmetic  16.6 us (6%)
  matrix products  5.3 us (2%)
  local copies, waits for them, and re-layouts  3.66 us (1%)
    ppermute x12, starting transfers between devices, reduce_line(): right = lax.ppermute(sent[0], 'tp', rights(s))  47.2 us
    pallas_call x1, Pallas kernels, expert_rows(): pl.pallas_call(functools.partial(expert_kernel, [len(source) for source i...  35.7 us
    pallas_call x2, Pallas kernels, attend(): pl.pallas_call(kernel, grid_spec=pltpu.PrefetchScalarGridSpec(num_scalar_...  25.9 us
    ppermute x12, waiting for transfers between devices, reduce_line(): right = lax.ppermute(sent[0], 'tp', rights(s))  23.3 us
    ppermute x9, starting transfers between devices, shift(): lax.ppermute(parts[s], 'tp', moves[s])  18.5 us
    ppermute x4, waiting for transfers between devices, gather_line(): lax.ppermute(left, 'tp', to_left)  14.4 us
    ppermute x9, waiting for transfers between devices, shift(): lax.ppermute(parts[s], 'tp', moves[s])  14.1 us
    ppermute x4, starting transfers between devices, gather_line(): lax.ppermute(right, 'tp', to_right)  12.9 us
  transfers between devices with their start and end apart: 48, of which 21 were waited for; matrix products, arithmetic and copies ran while one was open for 6% of the time, Pallas kernels for 23%

profile of v6, /device:TPU:0, one launch (start us, length us, event | category | flops | bytes accessed | tf_op | source)
XLA Modules:
  0.0 274.9 jit_solution(7149352281908846756)
XLA Ops:
  12.3 4.8 %collective-permute-done.23 = bf16[128,512]{1,0:T(8,128)(2,1)S(1)} collective-permute-done((bf16[128,512]{1,0:T(8,128)(2,1)}, bf16[128,512]{1,0:T(8,128)(2,1)S(1)}, u32[]{:S(2)}, u32[]{:S(2)}) %collective-permute-start.23) | collective-permute-done | bytes 131104 | tf_op jit(solution)/shard_map/ppermute | solution.py:407
  22.0 3.3 %collective-permute-start.26 = (bf16[64,1024]{1,0:T(8,128)(2,1)}, bf16[64,1024]{1,0:T(8,128)(2,1)S(1)}, u32[]{:S(2)}, u32[]{:S(2)}) collective-permute-start(bf16[64,1024]{1,0:T(8,128)(2,1)} %get-tuple-element.159), channel_id=1, source_target_pairs={{0,1},{1,2},{2,3},{3,0},{4,5},{5,6},{6,7},{7,4},{8,9},{9,10},{10,1... | collective-permute-start | bytes 393224 | tf_op jit(solution)/shard_map/ppermute | solution.py:407
  27.8 3.2 %collective-permute-done.26.refs_2_ = bf16[64,1024]{1,0:T(8,128)(2,1)S(1)} collective-permute-done((bf16[64,1024]{1,0:T(8,128)(2,1)}, bf16[64,1024]{1,0:T(8,128)(2,1)S(1)}, u32[]{:S(2)}, u32[]{:S(2)}) %collective-permute-start.26) | collective-permute-done | bytes 131104 | tf_op jit(solution)/shard_map/ppermute | solution.py:407
  31.0 4.3 %collective-permute-done.27.refs_4_ = bf16[64,1024]{1,0:T(8,128)(2,1)S(1)} collective-permute-done((bf16[64,1024]{1,0:T(8,128)(2,1)}, bf16[64,1024]{1,0:T(8,128)(2,1)S(1)}, u32[]{:S(2)}, u32[]{:S(2)}) %collective-permute-start.27) | collective-permute-done | bytes 131104 | tf_op jit(solution)/shard_map/ppermute | solution.py:407
  35.4 3.3 %collective-permute-start.31 = (bf16[64,1024]{1,0:T(8,128)(2,1)}, bf16[64,1024]{1,0:T(8,128)(2,1)}, u32[]{:S(2)}, u32[]{:S(2)}) collective-permute-start(bf16[64,1024]{1,0:T(8,128)(2,1)} %get-tuple-element.171), channel_id=1, source_target_pairs={{0,1},{1,2},{2,3},{3,0},{4,5},{5,6},{6,7},{7,4},{8,9},{9,10},{10,1... | collective-permute-start | bytes 393224 | tf_op jit(solution)/shard_map/ppermute | solution.py:407
  42.7 12.9 %shard_map.133 = (bf16[256,3072]{1,0:T(8,128)(2,1)S(1)}, bf16[256,3072]{1,0:T(8,128)(2,1)S(1)}) custom-call(s32[4]{0:T(128)S(1)} %copy-done.6, s32[2]{0:T(128)S(1)} %pad_add_fusion.refs_1_, bf16[64,1024]{1,0:T(8,128)(2,1)} %copy-done.23, bf16[64,1024]{1,0:T(8,128)(2,1)} %copy-done.25, bf16[64,1024]{1,0:T(8,128)(2,1)} %copy-done.24, ...), custom_call_target="tpu_custom_call" | custom-call | flops 21474836480 | bytes 15728640 | tf_op jit(solution)/shard_map/pallas_call | solution.py:168
  56.0 3.2 %collective-permute-start.40 = (bf16[64,3072]{1,0:T(8,128)(2,1)S(1)}, bf16[64,3072]{1,0:T(8,128)(2,1)S(1)}, u32[]{:S(2)}, u32[]{:S(2)}) collective-permute-start(bf16[64,3072]{1,0:T(8,128)(2,1)S(1)} %get-tuple-element.189), channel_id=1, source_target_pairs={{0,1},{4,5},{8,9},{12,13},{16,17},{20,21},{24,25},{28,29}} | collective-permute-start | bytes 1179656 | tf_op jit(solution)/shard_map/ppermute | solution.py:435
  61.9 3.4 %collective-permute-done.40 = bf16[64,3072]{1,0:T(8,128)(2,1)S(1)} collective-permute-done((bf16[64,3072]{1,0:T(8,128)(2,1)S(1)}, bf16[64,3072]{1,0:T(8,128)(2,1)S(1)}, u32[]{:S(2)}, u32[]{:S(2)}) %collective-permute-start.40) | collective-permute-done | bytes 393248 | tf_op jit(solution)/shard_map/ppermute | solution.py:435
  66.3 5.1 %collective-permute-start.42 = (bf16[64,3072]{1,0:T(8,128)(2,1)}, bf16[64,3072]{1,0:T(8,128)(2,1)}, u32[]{:S(2)}, u32[]{:S(2)}) collective-permute-start(bf16[64,3072]{1,0:T(8,128)(2,1)} %get-tuple-element.310), channel_id=1, source_target_pairs={{0,1},{1,2},{4,5},{5,6},{8,9},{9,10},{12,13},{13,14},{16,17},{17,1... | collective-permute-start | bytes 1179656 | tf_op jit(solution)/shard_map/ppermute | solution.py:435
  74.7 5.1 %collective-permute-start.36 = (bf16[64,3072]{1,0:T(8,128)(2,1)}, bf16[64,3072]{1,0:T(8,128)(2,1)}, u32[]{:S(2)}, u32[]{:S(2)}) collective-permute-start(bf16[64,3072]{1,0:T(8,128)(2,1)} %get-tuple-element.308), channel_id=1, source_target_pairs={{0,1},{1,2},{4,5},{5,6},{8,9},{9,10},{12,13},{13,14},{16,17},{17,1... | collective-permute-start | bytes 1179656 | tf_op jit(solution)/shard_map/ppermute | solution.py:435
  86.5 4.6 %collective-permute-start.44 = (bf16[64,3072]{1,0:T(8,128)(2,1)S(1)}, bf16[64,3072]{1,0:T(8,128)(2,1)S(1)}, u32[]{:S(2)}, u32[]{:S(2)}) collective-permute-start(bf16[64,3072]{1,0:T(8,128)(2,1)S(1)} %add.239), channel_id=1, source_target_pairs={{0,1},{1,2},{2,3},{4,5},{5,6},{6,7},{8,9},{9,10},{10,11},{12,13},{... | collective-permute-start | bytes 1179656 | tf_op jit(solution)/shard_map/ppermute | solution.py:435
  94.6 4.7 %collective-permute-start.38 = (bf16[64,3072]{1,0:T(8,128)(2,1)S(1)}, bf16[64,3072]{1,0:T(8,128)(2,1)S(1)}, u32[]{:S(2)}, u32[]{:S(2)}) collective-permute-start(bf16[64,3072]{1,0:T(8,128)(2,1)S(1)} %add.232), channel_id=1, source_target_pairs={{0,1},{1,2},{2,3},{4,5},{5,6},{6,7},{8,9},{9,10},{10,11},{12,13},{... | collective-permute-start | bytes 1179656 | tf_op jit(solution)/shard_map/ppermute | solution.py:435
  99.4 4.5 %collective-permute-done.39 = bf16[64,3072]{1,0:T(8,128)(2,1)S(1)} collective-permute-done((bf16[64,3072]{1,0:T(8,128)(2,1)S(1)}, bf16[64,3072]{1,0:T(8,128)(2,1)S(1)}, u32[]{:S(2)}, u32[]{:S(2)}) %collective-permute-start.39) | collective-permute-done | bytes 393248 | tf_op jit(solution)/shard_map/ppermute | solution.py:436
  103.9 3.1 %collective-permute-done.38 = bf16[64,3072]{1,0:T(8,128)(2,1)S(1)} collective-permute-done((bf16[64,3072]{1,0:T(8,128)(2,1)S(1)}, bf16[64,3072]{1,0:T(8,128)(2,1)S(1)}, u32[]{:S(2)}, u32[]{:S(2)}) %collective-permute-start.38) | collective-permute-done | bytes 393248 | tf_op jit(solution)/shard_map/ppermute | solution.py:435
  108.0 4.4 %collective-permute-start.46 = (bf16[64,6144]{1,0:T(8,128)(2,1)S(1)}, bf16[64,6144]{1,0:T(8,128)(2,1)S(1)}, u32[]{:S(2)}, u32[]{:S(2)}) collective-permute-start(bf16[64,6144]{1,0:T(8,128)(2,1)S(1)} %fusion.7.refs_1_), channel_id=1, source_target_pairs={{0,1},{1,2},{2,3},{4,5},{5,6},{6,7},{8,9},{9,10},{10,11},{12,13},{... | collective-permute-start | bytes 2359304 | tf_op jit(solution)/shard_map/ppermute | solution.py:448
  114.0 13.0 %shard_map.134 = (bf16[256,3072]{1,0:T(8,128)(2,1)S(1)}, bf16[256,3072]{1,0:T(8,128)(2,1)S(1)}) custom-call(s32[4]{0:T(128)S(1)} %copy-done.6, s32[2]{0:T(128)S(1)} %pad_add_fusion.refs_1_, bf16[64,1024]{1,0:T(8,128)(2,1)} %collective-permute-done.31.refs_2_, bf16[64,1024]{1,0:T(8,128)(2,1)} %collective-permute-done.33.refs_3_, ...), custom_call_target="tpu_custom_call" | custom-call | flops 21474836480 | bytes 15728640 | tf_op jit(solution)/shard_map/pallas_call | solution.py:168
  127.6 4.7 %collective-permute-done.47 = bf16[64,6144]{1,0:T(8,128)(2,1)S(1)} collective-permute-done((bf16[64,6144]{1,0:T(8,128)(2,1)S(1)}, bf16[64,6144]{1,0:T(8,128)(2,1)S(1)}, u32[]{:S(2)}, u32[]{:S(2)}) %collective-permute-start.47) | collective-permute-done | bytes 786464 | tf_op jit(solution)/shard_map/ppermute | solution.py:449
  133.2 3.4 %collective-permute-start.48 = (bf16[64,3072]{1,0:T(8,128)(2,1)S(1)}, bf16[64,3072]{1,0:T(8,128)(2,1)}, u32[]{:S(2)}, u32[]{:S(2)}) collective-permute-start(bf16[64,3072]{1,0:T(8,128)(2,1)S(1)} %get-tuple-element.290.refs_2_), channel_id=1, source_target_pairs={{0,1},{1,2},{2,3},{4,5},{5,6},{6,7},{8,9},{9,10},{10,11},{12,13},{... | collective-permute-start | bytes 1179656 | tf_op jit(solution)/shard_map/ppermute | solution.py:470
  138.0 4.6 %collective-permute-start.50 = (bf16[64,3072]{1,0:T(8,128)(2,1)S(1)}, bf16[64,3072]{1,0:T(8,128)(2,1)S(1)}, u32[]{:S(2)}, u32[]{:S(2)}) collective-permute-start(bf16[64,3072]{1,0:T(8,128)(2,1)S(1)} %get-tuple-element.291.refs_3_), channel_id=1, source_target_pairs={{0,1},{1,2},{2,3},{4,5},{5,6},{6,7},{8,9},{9,10},{10,11},{12,13},{... | collective-permute-start | bytes 1179656 | tf_op jit(solution)/shard_map/ppermute | solution.py:470
  143.8 3.4 %collective-permute-done.49 = bf16[64,3072]{1,0:T(8,128)(2,1)} collective-permute-done((bf16[64,3072]{1,0:T(8,128)(2,1)S(1)}, bf16[64,3072]{1,0:T(8,128)(2,1)}, u32[]{:S(2)}, u32[]{:S(2)}) %collective-permute-start.49) | collective-permute-done | bytes 393248 | tf_op jit(solution)/shard_map/ppermute | solution.py:470
  152.9 3.8 %collective-permute-done.51 = bf16[64,3072]{1,0:T(8,128)(2,1)S(1)} collective-permute-done((bf16[64,3072]{1,0:T(8,128)(2,1)}, bf16[64,3072]{1,0:T(8,128)(2,1)S(1)}, u32[]{:S(2)}, u32[]{:S(2)}) %collective-permute-start.51) | collective-permute-done | bytes 393248 | tf_op jit(solution)/shard_map/ppermute | solution.py:470
  164.2 4.1 %collective-permute-done.54.refs_7_ = bf16[64,3072]{1,0:T(8,128)(2,1)} collective-permute-done((bf16[64,3072]{1,0:T(8,128)(2,1)}, bf16[64,3072]{1,0:T(8,128)(2,1)}, u32[]{:S(2)}, u32[]{:S(2)}) %collective-permute-start.54) | collective-permute-done | bytes 393248 | tf_op jit(solution)/shard_map/ppermute | solution.py:470
  168.3 5.4 %collective-permute-done.55.refs_13_ = bf16[64,3072]{1,0:T(8,128)(2,1)} collective-permute-done((bf16[64,3072]{1,0:T(8,128)(2,1)}, bf16[64,3072]{1,0:T(8,128)(2,1)}, u32[]{:S(2)}, u32[]{:S(2)}) %collective-permute-start.55) | collective-permute-done | bytes 393248 | tf_op jit(solution)/shard_map/ppermute | solution.py:470
  178.1 4.6 %collective-permute-start.56 = (bf16[64,6144]{1,0:T(8,128)(2,1)S(1)}, bf16[64,6144]{1,0:T(8,128)(2,1)S(1)}, u32[]{:S(2)}, u32[]{:S(2)}) collective-permute-start(bf16[64,6144]{1,0:T(8,128)(2,1)S(1)} %pad_maximum_fusion.2), channel_id=1, source_target_pairs={{0,1},{1,2},{2,3},{4,5},{5,6},{6,7},{8,9},{9,10},{10,11},{12,13},{... | collective-permute-start | bytes 2359304 | tf_op jit(solution)/shard_map/ppermute | solution.py:479
  182.7 35.7 %shard_map.135 = (bf16[256,3072]{1,0:T(8,128)(2,1)S(1)}, bf16[256,3072]{1,0:T(8,128)(2,1)S(1)}) custom-call(s32[1]{0:T(128)} %bitcast.6.mine.refs_0_, bf16[64,6144]{1,0:T(8,128)(2,1)S(1)} %fusion.7.refs_1_, bf16[64,3072]{1,0:T(8,128)(2,1)S(1)} %get-tuple-element.290.refs_2_, bf16[64,3072]{1,0:T(8,128)(2,1)S(1)} %get-tuple-element.291.refs_3_, ...), custom_call_target="tpu_custom_call" | custom-call | flops 19327352832 | bytes 75497472 | tf_op jit(solution)/shard_map/pallas_call | solution.py:263
  223.8 6.0 %collective-permute-done.64 = bf16[64,3072]{1,0:T(8,128)(2,1)S(1)} collective-permute-done((bf16[64,3072]{1,0:T(8,128)(2,1)S(1)}, bf16[64,3072]{1,0:T(8,128)(2,1)S(1)}, u32[]{:S(2)}, u32[]{:S(2)}) %collective-permute-start.64) | collective-permute-done | bytes 393248 | tf_op jit(solution)/shard_map/ppermute | solution.py:435
  229.9 4.4 %collective-permute-start.66 = (bf16[64,3072]{1,0:T(8,128)(2,1)S(1)}, bf16[64,3072]{1,0:T(8,128)(2,1)S(1)}, u32[]{:S(2)}, u32[]{:S(2)}) collective-permute-start(bf16[64,3072]{1,0:T(8,128)(2,1)S(1)} %get-tuple-element.306), channel_id=1, source_target_pairs={{0,1},{1,2},{4,5},{5,6},{8,9},{9,10},{12,13},{13,14},{16,17},{17,1... | collective-permute-start | bytes 1179656 | tf_op jit(solution)/shard_map/ppermute | solution.py:435
  235.0 3.2 %collective-permute-done.58 = bf16[64,3072]{1,0:T(8,128)(2,1)S(1)} collective-permute-done((bf16[64,3072]{1,0:T(8,128)(2,1)S(1)}, bf16[64,3072]{1,0:T(8,128)(2,1)S(1)}, u32[]{:S(2)}, u32[]{:S(2)}) %collective-permute-start.58) | collective-permute-done | bytes 393248 | tf_op jit(solution)/shard_map/ppermute | solution.py:435
  238.3 4.4 %collective-permute-start.60 = (bf16[64,3072]{1,0:T(8,128)(2,1)S(1)}, bf16[64,3072]{1,0:T(8,128)(2,1)S(1)}, u32[]{:S(2)}, u32[]{:S(2)}) collective-permute-start(bf16[64,3072]{1,0:T(8,128)(2,1)S(1)} %get-tuple-element.304), channel_id=1, source_target_pairs={{0,1},{1,2},{4,5},{5,6},{8,9},{9,10},{12,13},{13,14},{16,17},{17,1... | collective-permute-start | bytes 1179656 | tf_op jit(solution)/shard_map/ppermute | solution.py:435
  248.3 5.0 %collective-permute-start.68 = (bf16[64,3072]{1,0:T(8,128)(2,1)S(1)}, bf16[64,3072]{1,0:T(8,128)(2,1)S(1)}, u32[]{:S(2)}, u32[]{:S(2)}) collective-permute-start(bf16[64,3072]{1,0:T(8,128)(2,1)S(1)} %add.272), channel_id=1, source_target_pairs={{0,1},{1,2},{2,3},{4,5},{5,6},{6,7},{8,9},{9,10},{10,11},{12,13},{... | collective-permute-start | bytes 1179656 | tf_op jit(solution)/shard_map/ppermute | solution.py:435
  256.6 5.6 %collective-permute-start.62 = (bf16[64,3072]{1,0:T(8,128)(2,1)S(1)}, bf16[64,3072]{1,0:T(8,128)(2,1)S(1)}, u32[]{:S(2)}, u32[]{:S(2)}) collective-permute-start(bf16[64,3072]{1,0:T(8,128)(2,1)S(1)} %add.262), channel_id=1, source_target_pairs={{0,1},{1,2},{2,3},{4,5},{5,6},{6,7},{8,9},{9,10},{10,11},{12,13},{... | collective-permute-start | bytes 1179656 | tf_op jit(solution)/shard_map/ppermute | solution.py:435
  264.4 5.5 %collective-permute-done.63 = bf16[64,3072]{1,0:T(8,128)(2,1)S(1)} collective-permute-done((bf16[64,3072]{1,0:T(8,128)(2,1)S(1)}, bf16[64,3072]{1,0:T(8,128)(2,1)S(1)}, u32[]{:S(2)}, u32[]{:S(2)}) %collective-permute-start.63) | collective-permute-done | bytes 393248 | tf_op jit(solution)/shard_map/ppermute | solution.py:436
  (167 shorter events, 85.8 us)
Async XLA Ops:
  17.2 18.1 %collective-permute-start.25 = (bf16[512,512]{1,0:T(8,128)(2,1)S(1)}, bf16[512,512]{1,0:T(8,128)(2,1)S(1)}, u32[]{:S(2)}, u32[]{:S(2)}) collective-permute-start(bf16[512,512]{1,0:T(8,128)(2,1)S(1)} %constant_dynamic-update-slice_fusion.refs_7_), channel_id=1, source_target_pairs={{0,8},{4,12},{8,0},{12,4},{1,9},{5,13},{9,1},{13,5},{2,10},{6,14},... | collective-permute-start | bytes 1572872 | tf_op jit(solution)/shard_map/ppermute | solution.py:513
  27.8 13.5 %collective-permute-start.29 = (bf16[512,512]{1,0:T(8,128)(2,1)S(1)}, bf16[512,512]{1,0:T(8,128)(2,1)S(1)}, u32[]{:S(2)}, u32[]{:S(2)}) collective-permute-start(bf16[512,512]{1,0:T(8,128)(2,1)S(1)} %constant_dynamic-update-slice_fusion.refs_7_), channel_id=1, source_target_pairs={{0,4},{4,0},{8,12},{12,8},{1,5},{5,1},{9,13},{13,9},{2,6},{6,2},{1... | collective-permute-start | bytes 1572872 | tf_op jit(solution)/shard_map/ppermute | solution.py:513
  35.4 20.5 %collective-permute-start.31 = (bf16[64,1024]{1,0:T(8,128)(2,1)}, bf16[64,1024]{1,0:T(8,128)(2,1)}, u32[]{:S(2)}, u32[]{:S(2)}) collective-permute-start(bf16[64,1024]{1,0:T(8,128)(2,1)} %get-tuple-element.171), channel_id=1, source_target_pairs={{0,1},{1,2},{2,3},{3,0},{4,5},{5,6},{6,7},{7,4},{8,9},{9,10},{10,1... | collective-permute-start | bytes 393224 | tf_op jit(solution)/shard_map/ppermute | solution.py:407
  38.7 17.2 %collective-permute-start.32 = (bf16[64,1024]{1,0:T(8,128)(2,1)}, bf16[64,1024]{1,0:T(8,128)(2,1)}, u32[]{:S(2)}, u32[]{:S(2)}) collective-permute-start(bf16[64,1024]{1,0:T(8,128)(2,1)} %get-tuple-element.172), channel_id=1, source_target_pairs={{0,2},{1,3},{2,0},{3,1},{4,6},{5,7},{6,4},{7,5},{8,10},{9,11},{10,... | collective-permute-start | bytes 393224 | tf_op jit(solution)/shard_map/ppermute | solution.py:407
  40.5 15.5 %collective-permute-start.33 = (bf16[64,1024]{1,0:T(8,128)(2,1)}, bf16[64,1024]{1,0:T(8,128)(2,1)}, u32[]{:S(2)}, u32[]{:S(2)}) collective-permute-start(bf16[64,1024]{1,0:T(8,128)(2,1)} %get-tuple-element.173), channel_id=1, source_target_pairs={{0,3},{1,0},{2,1},{3,2},{4,7},{5,4},{6,5},{7,6},{8,11},{9,8},{10,9... | collective-permute-start | bytes 393224 | tf_op jit(solution)/shard_map/ppermute | solution.py:407
  59.9 13.8 %collective-permute-start.34 = (bf16[64,3072]{1,0:T(8,128)(2,1)S(1)}, bf16[64,3072]{1,0:T(8,128)(2,1)S(1)}, u32[]{:S(2)}, u32[]{:S(2)}) collective-permute-start(bf16[64,3072]{1,0:T(8,128)(2,1)S(1)} %get-tuple-element.174), channel_id=1, source_target_pairs={{0,1},{4,5},{8,9},{12,13},{16,17},{20,21},{24,25},{28,29}} | collective-permute-start | bytes 1179656 | tf_op jit(solution)/shard_map/ppermute | solution.py:435
  61.2 12.5 %collective-permute-start.35 = (bf16[64,3072]{1,0:T(8,128)(2,1)S(1)}, bf16[64,3072]{1,0:T(8,128)(2,1)S(1)}, u32[]{:S(2)}, u32[]{:S(2)}) collective-permute-start(bf16[64,3072]{1,0:T(8,128)(2,1)S(1)} %get-tuple-element.175), channel_id=1, source_target_pairs={{3,2},{7,6},{11,10},{15,14},{19,18},{23,22},{27,26},{31,30}} | collective-permute-start | bytes 1179656 | tf_op jit(solution)/shard_map/ppermute | solution.py:436
  66.3 16.4 %collective-permute-start.42 = (bf16[64,3072]{1,0:T(8,128)(2,1)}, bf16[64,3072]{1,0:T(8,128)(2,1)}, u32[]{:S(2)}, u32[]{:S(2)}) collective-permute-start(bf16[64,3072]{1,0:T(8,128)(2,1)} %get-tuple-element.310), channel_id=1, source_target_pairs={{0,1},{1,2},{4,5},{5,6},{8,9},{9,10},{12,13},{13,14},{16,17},{17,1... | collective-permute-start | bytes 1179656 | tf_op jit(solution)/shard_map/ppermute | solution.py:435
  74.7 16.3 %collective-permute-start.36 = (bf16[64,3072]{1,0:T(8,128)(2,1)}, bf16[64,3072]{1,0:T(8,128)(2,1)}, u32[]{:S(2)}, u32[]{:S(2)}) collective-permute-start(bf16[64,3072]{1,0:T(8,128)(2,1)} %get-tuple-element.308), channel_id=1, source_target_pairs={{0,1},{1,2},{4,5},{5,6},{8,9},{9,10},{12,13},{13,14},{16,17},{17,1... | collective-permute-start | bytes 1179656 | tf_op jit(solution)/shard_map/ppermute | solution.py:435
  84.1 15.3 %collective-permute-start.45 = (bf16[64,3072]{1,0:T(8,128)(2,1)S(1)}, bf16[64,3072]{1,0:T(8,128)(2,1)S(1)}, u32[]{:S(2)}, u32[]{:S(2)}) collective-permute-start(bf16[64,3072]{1,0:T(8,128)(2,1)S(1)} %add.240), channel_id=1, source_target_pairs={{1,0},{2,1},{3,2},{5,4},{6,5},{7,6},{9,8},{10,9},{11,10},{13,12},{... | collective-permute-start | bytes 1179656 | tf_op jit(solution)/shard_map/ppermute | solution.py:436
  86.5 12.9 %collective-permute-start.44 = (bf16[64,3072]{1,0:T(8,128)(2,1)S(1)}, bf16[64,3072]{1,0:T(8,128)(2,1)S(1)}, u32[]{:S(2)}, u32[]{:S(2)}) collective-permute-start(bf16[64,3072]{1,0:T(8,128)(2,1)S(1)} %add.239), channel_id=1, source_target_pairs={{0,1},{1,2},{2,3},{4,5},{5,6},{6,7},{8,9},{9,10},{10,11},{12,13},{... | collective-permute-start | bytes 1179656 | tf_op jit(solution)/shard_map/ppermute | solution.py:435
  92.2 11.7 %collective-permute-start.39 = (bf16[64,3072]{1,0:T(8,128)(2,1)S(1)}, bf16[64,3072]{1,0:T(8,128)(2,1)S(1)}, u32[]{:S(2)}, u32[]{:S(2)}) collective-permute-start(bf16[64,3072]{1,0:T(8,128)(2,1)S(1)} %add.233), channel_id=1, source_target_pairs={{1,0},{2,1},{3,2},{5,4},{6,5},{7,6},{9,8},{10,9},{11,10},{13,12},{... | collective-permute-start | bytes 1179656 | tf_op jit(solution)/shard_map/ppermute | solution.py:436
  94.6 12.4 %collective-permute-start.38 = (bf16[64,3072]{1,0:T(8,128)(2,1)S(1)}, bf16[64,3072]{1,0:T(8,128)(2,1)S(1)}, u32[]{:S(2)}, u32[]{:S(2)}) collective-permute-start(bf16[64,3072]{1,0:T(8,128)(2,1)S(1)} %add.232), channel_id=1, source_target_pairs={{0,1},{1,2},{2,3},{4,5},{5,6},{6,7},{8,9},{9,10},{10,11},{12,13},{... | collective-permute-start | bytes 1179656 | tf_op jit(solution)/shard_map/ppermute | solution.py:435
  108.0 19.6 %collective-permute-start.46 = (bf16[64,6144]{1,0:T(8,128)(2,1)S(1)}, bf16[64,6144]{1,0:T(8,128)(2,1)S(1)}, u32[]{:S(2)}, u32[]{:S(2)}) collective-permute-start(bf16[64,6144]{1,0:T(8,128)(2,1)S(1)} %fusion.7.refs_1_), channel_id=1, source_target_pairs={{0,1},{1,2},{2,3},{4,5},{5,6},{6,7},{8,9},{9,10},{10,11},{12,13},{... | collective-permute-start | bytes 2359304 | tf_op jit(solution)/shard_map/ppermute | solution.py:448
  112.5 19.8 %collective-permute-start.47 = (bf16[64,6144]{1,0:T(8,128)(2,1)S(1)}, bf16[64,6144]{1,0:T(8,128)(2,1)S(1)}, u32[]{:S(2)}, u32[]{:S(2)}) collective-permute-start(bf16[64,6144]{1,0:T(8,128)(2,1)S(1)} %fusion.7.refs_1_), channel_id=1, source_target_pairs={{1,0},{2,1},{3,2},{5,4},{6,5},{7,6},{9,8},{10,9},{11,10},{13,12},{... | collective-permute-start | bytes 2359304 | tf_op jit(solution)/shard_map/ppermute | solution.py:449
  138.0 15.0 %collective-permute-start.50 = (bf16[64,3072]{1,0:T(8,128)(2,1)S(1)}, bf16[64,3072]{1,0:T(8,128)(2,1)S(1)}, u32[]{:S(2)}, u32[]{:S(2)}) collective-permute-start(bf16[64,3072]{1,0:T(8,128)(2,1)S(1)} %get-tuple-element.291.refs_3_), channel_id=1, source_target_pairs={{0,1},{1,2},{2,3},{4,5},{5,6},{6,7},{8,9},{9,10},{10,11},{12,13},{... | collective-permute-start | bytes 1179656 | tf_op jit(solution)/shard_map/ppermute | solution.py:470
  142.5 14.2 %collective-permute-start.51 = (bf16[64,3072]{1,0:T(8,128)(2,1)}, bf16[64,3072]{1,0:T(8,128)(2,1)S(1)}, u32[]{:S(2)}, u32[]{:S(2)}) collective-permute-start(bf16[64,3072]{1,0:T(8,128)(2,1)} %get-tuple-element.292.refs_9_), channel_id=1, source_target_pairs={{1,0},{2,1},{3,2},{5,4},{6,5},{7,6},{9,8},{10,9},{11,10},{13,12},{... | collective-permute-start | bytes 1179656 | tf_op jit(solution)/shard_map/ppermute | solution.py:470
  149.4 12.9 %collective-permute-start.52 = (bf16[64,3072]{1,0:T(8,128)(2,1)}, bf16[64,3072]{1,0:T(8,128)(2,1)}, u32[]{:S(2)}, u32[]{:S(2)}) collective-permute-start(bf16[64,3072]{1,0:T(8,128)(2,1)} %get-tuple-element.286.refs_4_), channel_id=1, source_target_pairs={{0,1},{1,2},{2,3},{4,5},{5,6},{6,7},{8,9},{9,10},{10,11},{12,13},{... | collective-permute-start | bytes 1179656 | tf_op jit(solution)/shard_map/ppermute | solution.py:470
  151.6 12.6 %collective-permute-start.53 = (bf16[64,3072]{1,0:T(8,128)(2,1)}, bf16[64,3072]{1,0:T(8,128)(2,1)}, u32[]{:S(2)}, u32[]{:S(2)}) collective-permute-start(bf16[64,3072]{1,0:T(8,128)(2,1)} %get-tuple-element.285.refs_10_), channel_id=1, source_target_pairs={{1,0},{2,1},{3,2},{5,4},{6,5},{7,6},{9,8},{10,9},{11,10},{13,12},{... | collective-permute-start | bytes 1179656 | tf_op jit(solution)/shard_map/ppermute | solution.py:470
  160.3 13.4 %collective-permute-start.55 = (bf16[64,3072]{1,0:T(8,128)(2,1)}, bf16[64,3072]{1,0:T(8,128)(2,1)}, u32[]{:S(2)}, u32[]{:S(2)}) collective-permute-start(bf16[64,3072]{1,0:T(8,128)(2,1)} %get-tuple-element.283.refs_11_), channel_id=1, source_target_pairs={{1,0},{2,1},{3,2},{5,4},{6,5},{7,6},{9,8},{10,9},{11,10},{13,12},{... | collective-permute-start | bytes 1179656 | tf_op jit(solution)/shard_map/ppermute | solution.py:470
  176.6 42.1 %collective-permute-start.57 = (bf16[64,6144]{1,0:T(8,128)(2,1)S(1)}, bf16[64,6144]{1,0:T(8,128)(2,1)S(1)}, u32[]{:S(2)}, u32[]{:S(2)}) collective-permute-start(bf16[64,6144]{1,0:T(8,128)(2,1)S(1)} %pad_maximum_fusion.3), channel_id=1, source_target_pairs={{1,0},{2,1},{3,2},{5,4},{6,5},{7,6},{9,8},{10,9},{11,10},{13,12},{... | collective-permute-start | bytes 2359304 | tf_op jit(solution)/shard_map/ppermute | solution.py:480
  178.1 40.6 %collective-permute-start.56 = (bf16[64,6144]{1,0:T(8,128)(2,1)S(1)}, bf16[64,6144]{1,0:T(8,128)(2,1)S(1)}, u32[]{:S(2)}, u32[]{:S(2)}) collective-permute-start(bf16[64,6144]{1,0:T(8,128)(2,1)S(1)} %pad_maximum_fusion.2), channel_id=1, source_target_pairs={{0,1},{1,2},{2,3},{4,5},{5,6},{6,7},{8,9},{9,10},{10,11},{12,13},{... | collective-permute-start | bytes 2359304 | tf_op jit(solution)/shard_map/ppermute | solution.py:479
  221.7 16.6 %collective-permute-start.58 = (bf16[64,3072]{1,0:T(8,128)(2,1)S(1)}, bf16[64,3072]{1,0:T(8,128)(2,1)S(1)}, u32[]{:S(2)}, u32[]{:S(2)}) collective-permute-start(bf16[64,3072]{1,0:T(8,128)(2,1)S(1)} %get-tuple-element.224), channel_id=1, source_target_pairs={{0,1},{4,5},{8,9},{12,13},{16,17},{20,21},{24,25},{28,29}} | collective-permute-start | bytes 1179656 | tf_op jit(solution)/shard_map/ppermute | solution.py:435
  223.1 15.1 %collective-permute-start.59 = (bf16[64,3072]{1,0:T(8,128)(2,1)S(1)}, bf16[64,3072]{1,0:T(8,128)(2,1)S(1)}, u32[]{:S(2)}, u32[]{:S(2)}) collective-permute-start(bf16[64,3072]{1,0:T(8,128)(2,1)S(1)} %get-tuple-element.222), channel_id=1, source_target_pairs={{3,2},{7,6},{11,10},{15,14},{19,18},{23,22},{27,26},{31,30}} | collective-permute-start | bytes 1179656 | tf_op jit(solution)/shard_map/ppermute | solution.py:436
  229.9 16.8 %collective-permute-start.66 = (bf16[64,3072]{1,0:T(8,128)(2,1)S(1)}, bf16[64,3072]{1,0:T(8,128)(2,1)S(1)}, u32[]{:S(2)}, u32[]{:S(2)}) collective-permute-start(bf16[64,3072]{1,0:T(8,128)(2,1)S(1)} %get-tuple-element.306), channel_id=1, source_target_pairs={{0,1},{1,2},{4,5},{5,6},{8,9},{9,10},{12,13},{13,14},{16,17},{17,1... | collective-permute-start | bytes 1179656 | tf_op jit(solution)/shard_map/ppermute | solution.py:435
  234.3 12.4 %collective-permute-start.67 = (bf16[64,3072]{1,0:T(8,128)(2,1)S(1)}, bf16[64,3072]{1,0:T(8,128)(2,1)S(1)}, u32[]{:S(2)}, u32[]{:S(2)}) collective-permute-start(bf16[64,3072]{1,0:T(8,128)(2,1)S(1)} %get-tuple-element.305), channel_id=1, source_target_pairs={{2,1},{3,2},{6,5},{7,6},{10,9},{11,10},{14,13},{15,14},{18,17},{19... | collective-permute-start | bytes 1179656 | tf_op jit(solution)/shard_map/ppermute | solution.py:436
  238.3 16.8 %collective-permute-start.60 = (bf16[64,3072]{1,0:T(8,128)(2,1)S(1)}, bf16[64,3072]{1,0:T(8,128)(2,1)S(1)}, u32[]{:S(2)}, u32[]{:S(2)}) collective-permute-start(bf16[64,3072]{1,0:T(8,128)(2,1)S(1)} %get-tuple-element.304), channel_id=1, source_target_pairs={{0,1},{1,2},{4,5},{5,6},{8,9},{9,10},{12,13},{13,14},{16,17},{17,1... | collective-permute-start | bytes 1179656 | tf_op jit(solution)/shard_map/ppermute | solution.py:435
  242.8 12.4 %collective-permute-start.61 = (bf16[64,3072]{1,0:T(8,128)(2,1)S(1)}, bf16[64,3072]{1,0:T(8,128)(2,1)S(1)}, u32[]{:S(2)}, u32[]{:S(2)}) collective-permute-start(bf16[64,3072]{1,0:T(8,128)(2,1)S(1)} %get-tuple-element.303), channel_id=1, source_target_pairs={{2,1},{3,2},{6,5},{7,6},{10,9},{11,10},{14,13},{15,14},{18,17},{19... | collective-permute-start | bytes 1179656 | tf_op jit(solution)/shard_map/ppermute | solution.py:436
  246.8 17.6 %collective-permute-start.69 = (bf16[64,3072]{1,0:T(8,128)(2,1)S(1)}, bf16[64,3072]{1,0:T(8,128)(2,1)S(1)}, u32[]{:S(2)}, u32[]{:S(2)}) collective-permute-start(bf16[64,3072]{1,0:T(8,128)(2,1)S(1)} %add.273), channel_id=1, source_target_pairs={{1,0},{2,1},{3,2},{5,4},{6,5},{7,6},{9,8},{10,9},{11,10},{13,12},{... | collective-permute-start | bytes 1179656 | tf_op jit(solution)/shard_map/ppermute | solution.py:436
  248.3 16.1 %collective-permute-start.68 = (bf16[64,3072]{1,0:T(8,128)(2,1)S(1)}, bf16[64,3072]{1,0:T(8,128)(2,1)S(1)}, u32[]{:S(2)}, u32[]{:S(2)}) collective-permute-start(bf16[64,3072]{1,0:T(8,128)(2,1)S(1)} %add.272), channel_id=1, source_target_pairs={{0,1},{1,2},{2,3},{4,5},{5,6},{6,7},{8,9},{9,10},{10,11},{12,13},{... | collective-permute-start | bytes 1179656 | tf_op jit(solution)/shard_map/ppermute | solution.py:435
  255.2 14.7 %collective-permute-start.63 = (bf16[64,3072]{1,0:T(8,128)(2,1)S(1)}, bf16[64,3072]{1,0:T(8,128)(2,1)S(1)}, u32[]{:S(2)}, u32[]{:S(2)}) collective-permute-start(bf16[64,3072]{1,0:T(8,128)(2,1)S(1)} %add.263), channel_id=1, source_target_pairs={{1,0},{2,1},{3,2},{5,4},{6,5},{7,6},{9,8},{10,9},{11,10},{13,12},{... | collective-permute-start | bytes 1179656 | tf_op jit(solution)/shard_map/ppermute | solution.py:436
  256.6 15.3 %collective-permute-start.62 = (bf16[64,3072]{1,0:T(8,128)(2,1)S(1)}, bf16[64,3072]{1,0:T(8,128)(2,1)S(1)}, u32[]{:S(2)}, u32[]{:S(2)}) collective-permute-start(bf16[64,3072]{1,0:T(8,128)(2,1)S(1)} %add.262), channel_id=1, source_target_pairs={{0,1},{1,2},{2,3},{4,5},{5,6},{6,7},{8,9},{9,10},{10,11},{12,13},{... | collective-permute-start | bytes 1179656 | tf_op jit(solution)/shard_map/ppermute | solution.py:435
  (42 other events, 489.8 us)

commit v7 on v6

--- a/solution.py
+++ b/solution.py
@@ -205,8 +205,8 @@
     for count in plan:
         sources.append(refs[:count])
         refs = refs[count:]
-    gate_weight, up_weight, down_weights, refs = refs[0], refs[1], refs[2:4], refs[4:]
-    outs, (chosen, acts) = refs[:-2], refs[-2:]
+    gate_weight, up_weight, down_weight, refs = refs[0], refs[1], refs[2], refs[3:]
+    outs, (chosen, acts, strips_ref, arrived) = refs[:-4], refs[-4:]
     step = pl.program_id(0)
     tile = gate_weight.shape[1]
     first = acts.shape[1] // tile
@@ -237,25 +237,36 @@
         columns = pl.ds(pl.multiple_of(step * tile, tile), tile)
         acts[:, columns] = (gate / (1.0 + jnp.exp(-gate)) * upward).astype(jnp.bfloat16)
 
+    strip = strips_ref.shape[2]
+
+    def strip_copy(n):
+        slot = lax.rem(n, 2)
+        columns = pl.ds(pl.multiple_of(n * strip, strip), strip)
+        return pltpu.make_async_copy(down_weight.at[:, columns], strips_ref.at[slot], arrived.at[slot])
+
+    @pl.when((step >= first - 1) & (step < pl.num_programs(0) - 1))
+    def _():
+        strip_copy(step - first + 1).start()
+
     @pl.when(step >= first)
     def _():
-        strip = down_weights[0].shape[1]
-        pairs = outs[0].shape[1] // (2 * strip)
-        for j, down_weight in enumerate(down_weights):
-            value = jnp.dot(acts[...], down_weight[...], preferred_element_type=jnp.float32)
-            for c in range(pieces):
-
-                @pl.when((step - first) // pairs == c)
-                def _():
-                    at = (2 * (step - first - c * pairs) + j) * strip
-                    share_out(outs[c * len(outs) // pieces :], pl.ds(pl.multiple_of(at, strip), strip), value)
+        n = step - first
+        strip_copy(n).wait()
+        value = jnp.dot(acts[...], strips_ref[lax.rem(n, 2)], preferred_element_type=jnp.float32)
+        per_piece = outs[0].shape[1] // strip
+        for c in range(pieces):
+
+            @pl.when(n // per_piece == c)
+            def _():
+                at = pl.multiple_of((n - c * per_piece) * strip, strip)
+                share_out(outs[c * len(outs) // pieces :], pl.ds(at, strip), value)
 
 
 def expert_rows(mine, sources, gate_weight, up_weight, down_weight, slots, pieces, grouped):
     flat = [piece for source in sources for piece in source]
     rows = flat[0].shape[0] * ((len(sources) + 1) // 2)
     depth, width = gate_weight.shape
-    tile, strip = min(TILE, width), 2 * TILE
+    tile, strip = min(TILE, width), 4 * TILE
     first = width // tile
     shapes = piece_shapes(rows, depth, slots, pieces, grouped)
     in_place = pl.BlockSpec(memory_space=pltpu.VMEM)
@@ -264,22 +275,22 @@
         functools.partial(expert_kernel, [len(source) for source in sources], pieces),
         grid_spec=pltpu.PrefetchScalarGridSpec(
             num_scalar_prefetch=1,
-            grid=(first + depth // (2 * strip),),
-            in_specs=[in_place] * len(flat)
-            + [weight, weight]
-            + [
-                pl.BlockSpec((width, strip), functools.partial(lambda j, n, *_: (0, 2 * jnp.maximum(n - first, 0) + j), j))
-                for j in range(2)
+            grid=(first + depth // strip,),
+            in_specs=[in_place] * len(flat) + [weight, weight, pl.BlockSpec(memory_space=pltpu.HBM)],
+            out_specs=[in_place] * len(shapes),
+            scratch_shapes=[
+                pltpu.VMEM((rows, depth), jnp.bfloat16),
+                pltpu.VMEM((rows, width), jnp.bfloat16),
+                pltpu.VMEM((2, width, strip), jnp.bfloat16),
+                pltpu.SemaphoreType.DMA((2,)),
             ],
-            out_specs=[in_place] * len(shapes),
-            scratch_shapes=[pltpu.VMEM((rows, depth), jnp.bfloat16), pltpu.VMEM((rows, width), jnp.bfloat16)],
         ),
         out_shape=shapes,
         compiler_params=pltpu.CompilerParams(vmem_limit_bytes=VMEM_LARGE),
         cost_estimate=pl.CostEstimate(
             flops=6 * rows * depth * width, bytes_accessed=6 * depth * width, transcendentals=rows * width
         ),
-    )(mine, *flat, gate_weight, up_weight, down_weight, down_weight)
+    )(mine, *flat, gate_weight, up_weight, *in_hbm([down_weight]))
     return by_piece(outs, slots, pieces, grouped)
 
 
@@ -528,7 +539,7 @@
     mine = lax.axis_index("ctx").astype(jnp.int32)[None]
     expert_ids = jnp.arange(router_weight.shape[1], dtype=jnp.int32)
 
-    def project(which):
+    def project(which, grouped=False):
         terms = attend(
             block_order,
             jnp.stack([lax.axis_index("ctx"), me]).astype(jnp.int32),
@@ -541,7 +552,7 @@
             block_rows,
             out_weight,
             pieces,
-            False,
+            grouped,
         )
         return [[term[slots.index(s)] for s in range(shards)] for term in terms]
 
@@ -595,7 +606,7 @@
     if halves == 1:
         return (restore([first_half]), restore([expert(0, normed, gather_line(normed)[0])[0]]))
     asked[1], _ = lax.optimization_barrier((asked[1], normed))
-    terms = project(1)
+    terms = project(1, line)
     sources, arrived = gather_line(normed, terms)
     part, (right, left) = expert(0, normed, sources, arrived)
     own = jnp.concatenate([term[0] for term in terms], axis=1).astype(jnp.float32)

time: 280 us -> 280 us (level)
  the two profiles are of different devices: /device:TPU:0 before, /device:TPU:20 now
where the time goes in v7:
time: 280 us
  starting transfers between devices  106 us (38%)
  Pallas kernels  74.1 us (26%)
  waiting for transfers between devices  69.7 us (25%)
  other arithmetic  16.5 us (6%)
  local copies, waits for them, and re-layouts  5.98 us (2%)
  matrix products  5.29 us (2%)
    ppermute x12, starting transfers between devices, reduce_line(): left = lax.ppermute(sent[1], 'tp', lefts(s))  36.1 us
    pallas_call x2, Pallas kernels, attend(): pl.pallas_call(kernel, grid_spec=pltpu.PrefetchScalarGridSpec(num_scalar_...  35.3 us
    pallas_call x1, Pallas kernels, expert_rows(): pl.pallas_call(functools.partial(expert_kernel, [len(source) for source i...  34.1 us
    ppermute x12, waiting for transfers between devices, reduce_line(): left = lax.ppermute(sent[1], 'tp', lefts(s))  29.4 us
    ppermute x12, starting transfers between devices, reduce_line(): right = lax.ppermute(sent[0], 'tp', rights(s))  19.2 us
    ppermute x9, waiting for transfers between devices, shift(): lax.ppermute(parts[s], 'tp', moves[s])  17.7 us
    ppermute x4, starting transfers between devices, gather_line(): lax.ppermute(right, 'tp', to_right)  17.5 us
    ppermute x9, starting transfers between devices, shift(): lax.ppermute(parts[s], 'tp', moves[s])  11.7 us
  transfers between devices with their start and end apart: 48, of which 21 were waited for; matrix products, arithmetic and copies ran while one was open for 7% of the time, Pallas kernels for 26%

profile of v7, /device:TPU:20, one launch (start us, length us, event | category | flops | bytes accessed | tf_op | source)
XLA Modules:
  0.0 280.0 jit_solution(8847052261968300689)
XLA Ops:
  6.8 8.0 %collective-permute-done.22 = bf16[128,512]{1,0:T(8,128)(2,1)S(1)} collective-permute-done((bf16[128,512]{1,0:T(8,128)(2,1)}, bf16[128,512]{1,0:T(8,128)(2,1)S(1)}, u32[]{:S(2)}, u32[]{:S(2)}) %collective-permute-start.22) | collective-permute-done | bytes 131104 | tf_op jit(solution)/shard_map/ppermute | solution.py:418
  17.6 2.7 shard_map.132
  20.4 2.6 collective-permute-start.26
  24.5 3.8 %collective-permute-done.26.refs_2_ = bf16[64,1024]{1,0:T(8,128)(2,1)S(1)} collective-permute-done((bf16[64,1024]{1,0:T(8,128)(2,1)}, bf16[64,1024]{1,0:T(8,128)(2,1)S(1)}, u32[]{:S(2)}, u32[]{:S(2)}) %collective-permute-start.26) | collective-permute-done | bytes 131104 | tf_op jit(solution)/shard_map/ppermute | solution.py:418
  28.4 3.4 %collective-permute-done.27.refs_4_ = bf16[64,1024]{1,0:T(8,128)(2,1)S(1)} collective-permute-done((bf16[64,1024]{1,0:T(8,128)(2,1)}, bf16[64,1024]{1,0:T(8,128)(2,1)S(1)}, u32[]{:S(2)}, u32[]{:S(2)}) %collective-permute-start.27) | collective-permute-done | bytes 131104 | tf_op jit(solution)/shard_map/ppermute | solution.py:418
  33.7 2.8 collective-permute-start.31
  39.5 17.6 %shard_map.133 = (bf16[256,3072]{1,0:T(8,128)(2,1)S(1)}, bf16[256,3072]{1,0:T(8,128)(2,1)S(1)}) custom-call(s32[4]{0:T(128)S(1)} %copy-done.16, s32[2]{0:T(128)S(1)} %pad_add_fusion.refs_1_, bf16[64,1024]{1,0:T(8,128)(2,1)} %copy-done.34, bf16[64,1024]{1,0:T(8,128)(2,1)} %copy-done.36, bf16[64,1024]{1,0:T(8,128)(2,1)} %copy-done.35, ...), custom_call_target="tpu_custom_call" | custom-call | flops 21474836480 | bytes 15728640 | tf_op jit(solution)/shard_map/pallas_call | solution.py:168
  61.5 10.6 %collective-permute-done.41 = bf16[64,3072]{1,0:T(8,128)(2,1)S(1)} collective-permute-done((bf16[64,3072]{1,0:T(8,128)(2,1)S(1)}, bf16[64,3072]{1,0:T(8,128)(2,1)S(1)}, u32[]{:S(2)}, u32[]{:S(2)}) %collective-permute-start.41) | collective-permute-done | bytes 393248 | tf_op jit(solution)/shard_map/ppermute | solution.py:447
  74.3 4.6 %collective-permute-start.43 = (bf16[64,3072]{1,0:T(8,128)(2,1)}, bf16[64,3072]{1,0:T(8,128)(2,1)}, u32[]{:S(2)}, u32[]{:S(2)}) collective-permute-start(bf16[64,3072]{1,0:T(8,128)(2,1)} %get-tuple-element.313), channel_id=1, source_target_pairs={{2,1},{3,2},{6,5},{7,6},{10,9},{11,10},{14,13},{15,14},{18,17},{19... | collective-permute-start | bytes 1179656 | tf_op jit(solution)/shard_map/ppermute | solution.py:447
  82.8 4.6 %collective-permute-start.37 = (bf16[64,3072]{1,0:T(8,128)(2,1)}, bf16[64,3072]{1,0:T(8,128)(2,1)}, u32[]{:S(2)}, u32[]{:S(2)}) collective-permute-start(bf16[64,3072]{1,0:T(8,128)(2,1)} %get-tuple-element.311), channel_id=1, source_target_pairs={{2,1},{3,2},{6,5},{7,6},{10,9},{11,10},{14,13},{15,14},{18,17},{19... | collective-permute-start | bytes 1179656 | tf_op jit(solution)/shard_map/ppermute | solution.py:447
  90.4 3.6 %collective-permute-start.45 = (bf16[64,3072]{1,0:T(8,128)(2,1)S(1)}, bf16[64,3072]{1,0:T(8,128)(2,1)S(1)}, u32[]{:S(2)}, u32[]{:S(2)}) collective-permute-start(bf16[64,3072]{1,0:T(8,128)(2,1)S(1)} %add.240), channel_id=1, source_target_pairs={{1,0},{2,1},{3,2},{5,4},{6,5},{7,6},{9,8},{10,9},{11,10},{13,12},{... | collective-permute-start | bytes 1179656 | tf_op jit(solution)/shard_map/ppermute | solution.py:447
  98.6 4.1 %collective-permute-start.39 = (bf16[64,3072]{1,0:T(8,128)(2,1)S(1)}, bf16[64,3072]{1,0:T(8,128)(2,1)S(1)}, u32[]{:S(2)}, u32[]{:S(2)}) collective-permute-start(bf16[64,3072]{1,0:T(8,128)(2,1)S(1)} %add.233), channel_id=1, source_target_pairs={{1,0},{2,1},{3,2},{5,4},{6,5},{7,6},{9,8},{10,9},{11,10},{13,12},{... | collective-permute-start | bytes 1179656 | tf_op jit(solution)/shard_map/ppermute | solution.py:447
  108.1 2.6 collective-permute-done.39
  110.7 3.3 %collective-permute-done.38 = bf16[64,3072]{1,0:T(8,128)(2,1)S(1)} collective-permute-done((bf16[64,3072]{1,0:T(8,128)(2,1)S(1)}, bf16[64,3072]{1,0:T(8,128)(2,1)S(1)}, u32[]{:S(2)}, u32[]{:S(2)}) %collective-permute-start.38) | collective-permute-done | bytes 393248 | tf_op jit(solution)/shard_map/ppermute | solution.py:446
  117.0 4.1 %collective-permute-start.47 = (bf16[64,6144]{1,0:T(8,128)(2,1)S(1)}, bf16[64,6144]{1,0:T(8,128)(2,1)S(1)}, u32[]{:S(2)}, u32[]{:S(2)}) collective-permute-start(bf16[64,6144]{1,0:T(8,128)(2,1)S(1)} %fusion.7.refs_1_), channel_id=1, source_target_pairs={{1,0},{2,1},{3,2},{5,4},{6,5},{7,6},{9,8},{10,9},{11,10},{13,12},{... | collective-permute-start | bytes 2359304 | tf_op jit(solution)/shard_map/ppermute | solution.py:460
  121.1 17.6 %shard_map.134 = (bf16[64,3072]{1,0:T(8,128)(2,1)S(1)}, bf16[64,3072]{1,0:T(8,128)(2,1)S(1)}, bf16[64,3072]{1,0:T(8,128)(2,1)S(1)}, bf16[64,3072]{1,0:T(8,128)(2...) custom-call(s32[4]{0:T(128)S(1)} %copy-done.16, ...), custom_call_target="tpu_custom_call" | custom-call | flops 21474836480 | bytes 15728640 | tf_op jit(solution)/shard_map/pallas_call | solution.py:168
  142.5 4.7 %collective-permute-start.48 = (bf16[64,3072]{1,0:T(8,128)(2,1)S(1)}, bf16[64,3072]{1,0:T(8,128)(2,1)S(1)}, u32[]{:S(2)}, u32[]{:S(2)}) collective-permute-start(bf16[64,3072]{1,0:T(8,128)(2,1)S(1)} %get-tuple-element.302.refs_2_), channel_id=1, source_target_pairs={{0,1},{1,2},{2,3},{4,5},{5,6},{6,7},{8,9},{9,10},{10,11},{12,13},{... | collective-permute-start | bytes 1179656 | tf_op jit(solution)/shard_map/ppermute | solution.py:481
  149.2 3.9 %collective-permute-start.50 = (bf16[64,3072]{1,0:T(8,128)(2,1)S(1)}, bf16[64,3072]{1,0:T(8,128)(2,1)S(1)}, u32[]{:S(2)}, u32[]{:S(2)}) collective-permute-start(bf16[64,3072]{1,0:T(8,128)(2,1)S(1)} %get-tuple-element.301.refs_3_), channel_id=1, source_target_pairs={{0,1},{1,2},{2,3},{4,5},{5,6},{6,7},{8,9},{9,10},{10,11},{12,13},{... | collective-permute-start | bytes 1179656 | tf_op jit(solution)/shard_map/ppermute | solution.py:481
  153.2 3.4 %collective-permute-done.48 = bf16[64,3072]{1,0:T(8,128)(2,1)S(1)} collective-permute-done((bf16[64,3072]{1,0:T(8,128)(2,1)S(1)}, bf16[64,3072]{1,0:T(8,128)(2,1)S(1)}, u32[]{:S(2)}, u32[]{:S(2)}) %collective-permute-start.48) | collective-permute-done | bytes 393248 | tf_op jit(solution)/shard_map/ppermute | solution.py:481
  158.6 4.4 %collective-permute-start.52 = (bf16[64,3072]{1,0:T(8,128)(2,1)S(1)}, bf16[64,3072]{1,0:T(8,128)(2,1)}, u32[]{:S(2)}, u32[]{:S(2)}) collective-permute-start(bf16[64,3072]{1,0:T(8,128)(2,1)S(1)} %get-tuple-element.310.refs_4_), channel_id=1, source_target_pairs={{0,1},{1,2},{2,3},{4,5},{5,6},{6,7},{8,9},{9,10},{10,11},{12,13},{... | collective-permute-start | bytes 1179656 | tf_op jit(solution)/shard_map/ppermute | solution.py:481
  165.9 4.5 %collective-permute-start.54 = (bf16[64,3072]{1,0:T(8,128)(2,1)}, bf16[64,3072]{1,0:T(8,128)(2,1)}, u32[]{:S(2)}, u32[]{:S(2)}) collective-permute-start(bf16[64,3072]{1,0:T(8,128)(2,1)} %get-tuple-element.308.refs_5_), channel_id=1, source_target_pairs={{0,1},{1,2},{2,3},{4,5},{5,6},{6,7},{8,9},{9,10},{10,11},{12,13},{... | collective-permute-start | bytes 1179656 | tf_op jit(solution)/shard_map/ppermute | solution.py:481
  176.4 8.1 %collective-permute-done.55.refs_13_ = bf16[64,3072]{1,0:T(8,128)(2,1)} collective-permute-done((bf16[64,3072]{1,0:T(8,128)(2,1)S(1)}, bf16[64,3072]{1,0:T(8,128)(2,1)}, u32[]{:S(2)}, u32[]{:S(2)}) %collective-permute-start.55) | collective-permute-done | bytes 393248 | tf_op jit(solution)/shard_map/ppermute | solution.py:481
  190.1 4.0 %collective-permute-start.56 = (bf16[64,6144]{1,0:T(8,128)(2,1)S(1)}, bf16[64,6144]{1,0:T(8,128)(2,1)S(1)}, u32[]{:S(2)}, u32[]{:S(2)}) collective-permute-start(bf16[64,6144]{1,0:T(8,128)(2,1)S(1)} %pad_maximum_fusion.2), channel_id=1, source_target_pairs={{0,1},{1,2},{2,3},{4,5},{5,6},{6,7},{8,9},{9,10},{10,11},{12,13},{... | collective-permute-start | bytes 2359304 | tf_op jit(solution)/shard_map/ppermute | solution.py:490
  194.1 34.1 %shard_map.135 = (bf16[256,3072]{1,0:T(8,128)(2,1)S(1)}, bf16[256,3072]{1,0:T(8,128)(2,1)S(1)}) custom-call(s32[1]{0:T(128)} %bitcast.6.mine.refs_0_, bf16[64,6144]{1,0:T(8,128)(2,1)S(1)} %fusion.7.refs_1_, bf16[64,3072]{1,0:T(8,128)(2,1)S(1)} %get-tuple-element.302.refs_2_, bf16[64,3072]{1,0:T(8,128)(2,1)S(1)} %get-tuple-element.301.refs_3_, ...), custom_call_target="tpu_custom_call" | custom-call | flops 19327352832 | bytes 75497472 | tf_op jit(solution)/shard_map/pallas_call | solution.py:274
  232.8 10.2 %collective-permute-done.65 = bf16[64,3072]{1,0:T(8,128)(2,1)S(1)} collective-permute-done((bf16[64,3072]{1,0:T(8,128)(2,1)S(1)}, bf16[64,3072]{1,0:T(8,128)(2,1)S(1)}, u32[]{:S(2)}, u32[]{:S(2)}) %collective-permute-start.65) | collective-permute-done | bytes 393248 | tf_op jit(solution)/shard_map/ppermute | solution.py:447
  244.4 4.6 %collective-permute-start.67 = (bf16[64,3072]{1,0:T(8,128)(2,1)S(1)}, bf16[64,3072]{1,0:T(8,128)(2,1)S(1)}, u32[]{:S(2)}, u32[]{:S(2)}) collective-permute-start(bf16[64,3072]{1,0:T(8,128)(2,1)S(1)} %get-tuple-element.305), channel_id=1, source_target_pairs={{2,1},{3,2},{6,5},{7,6},{10,9},{11,10},{14,13},{15,14},{18,17},{19... | collective-permute-start | bytes 1179656 | tf_op jit(solution)/shard_map/ppermute | solution.py:447
  248.9 2.5 collective-permute-done.59
  252.8 4.6 %collective-permute-start.61 = (bf16[64,3072]{1,0:T(8,128)(2,1)S(1)}, bf16[64,3072]{1,0:T(8,128)(2,1)S(1)}, u32[]{:S(2)}, u32[]{:S(2)}) collective-permute-start(bf16[64,3072]{1,0:T(8,128)(2,1)S(1)} %get-tuple-element.303), channel_id=1, source_target_pairs={{2,1},{3,2},{6,5},{7,6},{10,9},{11,10},{14,13},{15,14},{18,17},{19... | collective-permute-start | bytes 1179656 | tf_op jit(solution)/shard_map/ppermute | solution.py:447
  260.1 3.9 %collective-permute-start.68 = (bf16[64,3072]{1,0:T(8,128)(2,1)S(1)}, bf16[64,3072]{1,0:T(8,128)(2,1)S(1)}, u32[]{:S(2)}, u32[]{:S(2)}) collective-permute-start(bf16[64,3072]{1,0:T(8,128)(2,1)S(1)} %add.272), channel_id=1, source_target_pairs={{0,1},{1,2},{2,3},{4,5},{5,6},{6,7},{8,9},{9,10},{10,11},{12,13},{... | collective-permute-start | bytes 1179656 | tf_op jit(solution)/shard_map/ppermute | solution.py:446
  264.1 3.0 %collective-permute-start.63 = (bf16[64,3072]{1,0:T(8,128)(2,1)S(1)}, bf16[64,3072]{1,0:T(8,128)(2,1)S(1)}, u32[]{:S(2)}, u32[]{:S(2)}) collective-permute-start(bf16[64,3072]{1,0:T(8,128)(2,1)S(1)} %add.263), channel_id=1, source_target_pairs={{1,0},{2,1},{3,2},{5,4},{6,5},{7,6},{9,8},{10,9},{11,10},{13,12},{... | collective-permute-start | bytes 1179656 | tf_op jit(solution)/shard_map/ppermute | solution.py:447
  267.2 3.0 %collective-permute-start.62 = (bf16[64,3072]{1,0:T(8,128)(2,1)S(1)}, bf16[64,3072]{1,0:T(8,128)(2,1)S(1)}, u32[]{:S(2)}, u32[]{:S(2)}) collective-permute-start(bf16[64,3072]{1,0:T(8,128)(2,1)S(1)} %add.262), channel_id=1, source_target_pairs={{0,1},{1,2},{2,3},{4,5},{5,6},{6,7},{8,9},{9,10},{10,11},{12,13},{... | collective-permute-start | bytes 1179656 | tf_op jit(solution)/shard_map/ppermute | solution.py:446
  273.8 3.2 %collective-permute-done.62 = bf16[64,3072]{1,0:T(8,128)(2,1)S(1)} collective-permute-done((bf16[64,3072]{1,0:T(8,128)(2,1)S(1)}, bf16[64,3072]{1,0:T(8,128)(2,1)S(1)}, u32[]{:S(2)}, u32[]{:S(2)}) %collective-permute-start.62) | collective-permute-done | bytes 393248 | tf_op jit(solution)/shard_map/ppermute | solution.py:446
  (192 shorter events, 79.4 us)
Async XLA Ops:
  15.5 18.2 %collective-permute-start.25 = (bf16[512,512]{1,0:T(8,128)(2,1)S(1)}, bf16[512,512]{1,0:T(8,128)(2,1)S(1)}, u32[]{:S(2)}, u32[]{:S(2)}) collective-permute-start(bf16[512,512]{1,0:T(8,128)(2,1)S(1)} %constant_dynamic-update-slice_fusion.refs_7_), channel_id=1, source_target_pairs={{0,8},{4,12},{8,0},{12,4},{1,9},{5,13},{9,1},{13,5},{2,10},{6,14},... | collective-permute-start | bytes 1572872 | tf_op jit(solution)/shard_map/ppermute | solution.py:524
  24.5 13.6 %collective-permute-start.29 = (bf16[512,512]{1,0:T(8,128)(2,1)S(1)}, bf16[512,512]{1,0:T(8,128)(2,1)S(1)}, u32[]{:S(2)}, u32[]{:S(2)}) collective-permute-start(bf16[512,512]{1,0:T(8,128)(2,1)S(1)} %constant_dynamic-update-slice_fusion.refs_7_), channel_id=1, source_target_pairs={{0,4},{4,0},{8,12},{12,8},{1,5},{5,1},{9,13},{13,9},{2,6},{6,2},{1... | collective-permute-start | bytes 1572872 | tf_op jit(solution)/shard_map/ppermute | solution.py:524
  33.7 23.8 %collective-permute-start.31 = (bf16[64,1024]{1,0:T(8,128)(2,1)}, bf16[64,1024]{1,0:T(8,128)(2,1)}, u32[]{:S(2)}, u32[]{:S(2)}) collective-permute-start(bf16[64,1024]{1,0:T(8,128)(2,1)} %get-tuple-element.177), channel_id=1, source_target_pairs={{0,1},{1,2},{2,3},{3,0},{4,5},{5,6},{6,7},{7,4},{8,9},{9,10},{10,1... | collective-permute-start | bytes 393224 | tf_op jit(solution)/shard_map/ppermute | solution.py:418
  36.4 21.0 %collective-permute-start.32 = (bf16[64,1024]{1,0:T(8,128)(2,1)}, bf16[64,1024]{1,0:T(8,128)(2,1)}, u32[]{:S(2)}, u32[]{:S(2)}) collective-permute-start(bf16[64,1024]{1,0:T(8,128)(2,1)} %get-tuple-element.178), channel_id=1, source_target_pairs={{0,2},{1,3},{2,0},{3,1},{4,6},{5,7},{6,4},{7,5},{8,10},{9,11},{10,... | collective-permute-start | bytes 393224 | tf_op jit(solution)/shard_map/ppermute | solution.py:418
  37.6 19.8 %collective-permute-start.33 = (bf16[64,1024]{1,0:T(8,128)(2,1)}, bf16[64,1024]{1,0:T(8,128)(2,1)}, u32[]{:S(2)}, u32[]{:S(2)}) collective-permute-start(bf16[64,1024]{1,0:T(8,128)(2,1)} %get-tuple-element.179), channel_id=1, source_target_pairs={{0,3},{1,0},{2,1},{3,2},{4,7},{5,4},{6,5},{7,6},{8,11},{9,8},{10,9... | collective-permute-start | bytes 393224 | tf_op jit(solution)/shard_map/ppermute | solution.py:418
  58.2 13.9 %collective-permute-start.41 = (bf16[64,3072]{1,0:T(8,128)(2,1)S(1)}, bf16[64,3072]{1,0:T(8,128)(2,1)S(1)}, u32[]{:S(2)}, u32[]{:S(2)}) collective-permute-start(bf16[64,3072]{1,0:T(8,128)(2,1)S(1)} %get-tuple-element.193), channel_id=1, source_target_pairs={{3,2},{7,6},{11,10},{15,14},{19,18},{23,22},{27,26},{31,30}} | collective-permute-start | bytes 1179656 | tf_op jit(solution)/shard_map/ppermute | solution.py:447
  59.5 19.5 %collective-permute-start.34 = (bf16[64,3072]{1,0:T(8,128)(2,1)S(1)}, bf16[64,3072]{1,0:T(8,128)(2,1)S(1)}, u32[]{:S(2)}, u32[]{:S(2)}) collective-permute-start(bf16[64,3072]{1,0:T(8,128)(2,1)S(1)} %get-tuple-element.180), channel_id=1, source_target_pairs={{0,1},{4,5},{8,9},{12,13},{16,17},{20,21},{24,25},{28,29}} | collective-permute-start | bytes 1179656 | tf_op jit(solution)/shard_map/ppermute | solution.py:446
  60.2 20.4 %collective-permute-start.35 = (bf16[64,3072]{1,0:T(8,128)(2,1)S(1)}, bf16[64,3072]{1,0:T(8,128)(2,1)S(1)}, u32[]{:S(2)}, u32[]{:S(2)}) collective-permute-start(bf16[64,3072]{1,0:T(8,128)(2,1)S(1)} %get-tuple-element.181), channel_id=1, source_target_pairs={{3,2},{7,6},{11,10},{15,14},{19,18},{23,22},{27,26},{31,30}} | collective-permute-start | bytes 1179656 | tf_op jit(solution)/shard_map/ppermute | solution.py:447
  73.1 15.7 %collective-permute-start.42 = (bf16[64,3072]{1,0:T(8,128)(2,1)}, bf16[64,3072]{1,0:T(8,128)(2,1)}, u32[]{:S(2)}, u32[]{:S(2)}) collective-permute-start(bf16[64,3072]{1,0:T(8,128)(2,1)} %get-tuple-element.314), channel_id=1, source_target_pairs={{0,1},{1,2},{4,5},{5,6},{8,9},{9,10},{12,13},{13,14},{16,17},{17,1... | collective-permute-start | bytes 1179656 | tf_op jit(solution)/shard_map/ppermute | solution.py:446
  74.3 14.7 %collective-permute-start.43 = (bf16[64,3072]{1,0:T(8,128)(2,1)}, bf16[64,3072]{1,0:T(8,128)(2,1)}, u32[]{:S(2)}, u32[]{:S(2)}) collective-permute-start(bf16[64,3072]{1,0:T(8,128)(2,1)} %get-tuple-element.313), channel_id=1, source_target_pairs={{2,1},{3,2},{6,5},{7,6},{10,9},{11,10},{14,13},{15,14},{18,17},{19... | collective-permute-start | bytes 1179656 | tf_op jit(solution)/shard_map/ppermute | solution.py:447
  81.5 15.9 %collective-permute-start.36 = (bf16[64,3072]{1,0:T(8,128)(2,1)}, bf16[64,3072]{1,0:T(8,128)(2,1)}, u32[]{:S(2)}, u32[]{:S(2)}) collective-permute-start(bf16[64,3072]{1,0:T(8,128)(2,1)} %get-tuple-element.312), channel_id=1, source_target_pairs={{0,1},{1,2},{4,5},{5,6},{8,9},{9,10},{12,13},{13,14},{16,17},{17,1... | collective-permute-start | bytes 1179656 | tf_op jit(solution)/shard_map/ppermute | solution.py:446
  82.8 14.7 %collective-permute-start.37 = (bf16[64,3072]{1,0:T(8,128)(2,1)}, bf16[64,3072]{1,0:T(8,128)(2,1)}, u32[]{:S(2)}, u32[]{:S(2)}) collective-permute-start(bf16[64,3072]{1,0:T(8,128)(2,1)} %get-tuple-element.311), channel_id=1, source_target_pairs={{2,1},{3,2},{6,5},{7,6},{10,9},{11,10},{14,13},{15,14},{18,17},{19... | collective-permute-start | bytes 1179656 | tf_op jit(solution)/shard_map/ppermute | solution.py:447
  90.4 15.5 %collective-permute-start.45 = (bf16[64,3072]{1,0:T(8,128)(2,1)S(1)}, bf16[64,3072]{1,0:T(8,128)(2,1)S(1)}, u32[]{:S(2)}, u32[]{:S(2)}) collective-permute-start(bf16[64,3072]{1,0:T(8,128)(2,1)S(1)} %add.240), channel_id=1, source_target_pairs={{1,0},{2,1},{3,2},{5,4},{6,5},{7,6},{9,8},{10,9},{11,10},{13,12},{... | collective-permute-start | bytes 1179656 | tf_op jit(solution)/shard_map/ppermute | solution.py:447
  95.1 13.0 %collective-permute-start.44 = (bf16[64,3072]{1,0:T(8,128)(2,1)S(1)}, bf16[64,3072]{1,0:T(8,128)(2,1)S(1)}, u32[]{:S(2)}, u32[]{:S(2)}) collective-permute-start(bf16[64,3072]{1,0:T(8,128)(2,1)S(1)} %add.239), channel_id=1, source_target_pairs={{0,1},{1,2},{2,3},{4,5},{5,6},{6,7},{8,9},{9,10},{10,11},{12,13},{... | collective-permute-start | bytes 1179656 | tf_op jit(solution)/shard_map/ppermute | solution.py:446
  115.0 25.3 %collective-permute-start.46 = (bf16[64,6144]{1,0:T(8,128)(2,1)S(1)}, bf16[64,6144]{1,0:T(8,128)(2,1)S(1)}, u32[]{:S(2)}, u32[]{:S(2)}) collective-permute-start(bf16[64,6144]{1,0:T(8,128)(2,1)S(1)} %fusion.7.refs_1_), channel_id=1, source_target_pairs={{0,1},{1,2},{2,3},{4,5},{5,6},{6,7},{8,9},{9,10},{10,11},{12,13},{... | collective-permute-start | bytes 2359304 | tf_op jit(solution)/shard_map/ppermute | solution.py:459
  117.0 23.4 %collective-permute-start.47 = (bf16[64,6144]{1,0:T(8,128)(2,1)S(1)}, bf16[64,6144]{1,0:T(8,128)(2,1)S(1)}, u32[]{:S(2)}, u32[]{:S(2)}) collective-permute-start(bf16[64,6144]{1,0:T(8,128)(2,1)S(1)} %fusion.7.refs_1_), channel_id=1, source_target_pairs={{1,0},{2,1},{3,2},{5,4},{6,5},{7,6},{9,8},{10,9},{11,10},{13,12},{... | collective-permute-start | bytes 2359304 | tf_op jit(solution)/shard_map/ppermute | solution.py:460
  140.4 12.8 %collective-permute-start.49 = (bf16[64,3072]{1,0:T(8,128)(2,1)S(1)}, bf16[64,3072]{1,0:T(8,128)(2,1)}, u32[]{:S(2)}, u32[]{:S(2)}) collective-permute-start(bf16[64,3072]{1,0:T(8,128)(2,1)S(1)} %get-tuple-element.300.refs_8_), channel_id=1, source_target_pairs={{1,0},{2,1},{3,2},{5,4},{6,5},{7,6},{9,8},{10,9},{11,10},{13,12},{... | collective-permute-start | bytes 1179656 | tf_op jit(solution)/shard_map/ppermute | solution.py:481
  142.5 14.2 %collective-permute-start.48 = (bf16[64,3072]{1,0:T(8,128)(2,1)S(1)}, bf16[64,3072]{1,0:T(8,128)(2,1)S(1)}, u32[]{:S(2)}, u32[]{:S(2)}) collective-permute-start(bf16[64,3072]{1,0:T(8,128)(2,1)S(1)} %get-tuple-element.302.refs_2_), channel_id=1, source_target_pairs={{0,1},{1,2},{2,3},{4,5},{5,6},{6,7},{8,9},{9,10},{10,11},{12,13},{... | collective-permute-start | bytes 1179656 | tf_op jit(solution)/shard_map/ppermute | solution.py:481
  147.2 17.7 %collective-permute-start.51 = (bf16[64,3072]{1,0:T(8,128)(2,1)S(1)}, bf16[64,3072]{1,0:T(8,128)(2,1)S(1)}, u32[]{:S(2)}, u32[]{:S(2)}) collective-permute-start(bf16[64,3072]{1,0:T(8,128)(2,1)S(1)} %get-tuple-element.299.refs_9_), channel_id=1, source_target_pairs={{1,0},{2,1},{3,2},{5,4},{6,5},{7,6},{9,8},{10,9},{11,10},{13,12},{... | collective-permute-start | bytes 1179656 | tf_op jit(solution)/shard_map/ppermute | solution.py:481
  149.2 15.8 %collective-permute-start.50 = (bf16[64,3072]{1,0:T(8,128)(2,1)S(1)}, bf16[64,3072]{1,0:T(8,128)(2,1)S(1)}, u32[]{:S(2)}, u32[]{:S(2)}) collective-permute-start(bf16[64,3072]{1,0:T(8,128)(2,1)S(1)} %get-tuple-element.301.refs_3_), channel_id=1, source_target_pairs={{0,1},{1,2},{2,3},{4,5},{5,6},{6,7},{8,9},{9,10},{10,11},{12,13},{... | collective-permute-start | bytes 1179656 | tf_op jit(solution)/shard_map/ppermute | solution.py:481
  158.6 14.5 %collective-permute-start.52 = (bf16[64,3072]{1,0:T(8,128)(2,1)S(1)}, bf16[64,3072]{1,0:T(8,128)(2,1)}, u32[]{:S(2)}, u32[]{:S(2)}) collective-permute-start(bf16[64,3072]{1,0:T(8,128)(2,1)S(1)} %get-tuple-element.310.refs_4_), channel_id=1, source_target_pairs={{0,1},{1,2},{2,3},{4,5},{5,6},{6,7},{8,9},{9,10},{10,11},{12,13},{... | collective-permute-start | bytes 1179656 | tf_op jit(solution)/shard_map/ppermute | solution.py:481
  170.4 14.1 %collective-permute-start.55 = (bf16[64,3072]{1,0:T(8,128)(2,1)S(1)}, bf16[64,3072]{1,0:T(8,128)(2,1)}, u32[]{:S(2)}, u32[]{:S(2)}) collective-permute-start(bf16[64,3072]{1,0:T(8,128)(2,1)S(1)} %get-tuple-element.307.refs_11_), channel_id=1, source_target_pairs={{1,0},{2,1},{3,2},{5,4},{6,5},{7,6},{9,8},{10,9},{11,10},{13,12},{... | collective-permute-start | bytes 1179656 | tf_op jit(solution)/shard_map/ppermute | solution.py:481
  185.8 42.7 %collective-permute-start.57 = (bf16[64,6144]{1,0:T(8,128)(2,1)S(1)}, bf16[64,6144]{1,0:T(8,128)(2,1)S(1)}, u32[]{:S(2)}, u32[]{:S(2)}) collective-permute-start(bf16[64,6144]{1,0:T(8,128)(2,1)S(1)} %pad_maximum_fusion.3), channel_id=1, source_target_pairs={{1,0},{2,1},{3,2},{5,4},{6,5},{7,6},{9,8},{10,9},{11,10},{13,12},{... | collective-permute-start | bytes 2359304 | tf_op jit(solution)/shard_map/ppermute | solution.py:491
  190.1 38.4 %collective-permute-start.56 = (bf16[64,6144]{1,0:T(8,128)(2,1)S(1)}, bf16[64,6144]{1,0:T(8,128)(2,1)S(1)}, u32[]{:S(2)}, u32[]{:S(2)}) collective-permute-start(bf16[64,6144]{1,0:T(8,128)(2,1)S(1)} %pad_maximum_fusion.2), channel_id=1, source_target_pairs={{0,1},{1,2},{2,3},{4,5},{5,6},{6,7},{8,9},{9,10},{10,11},{12,13},{... | collective-permute-start | bytes 2359304 | tf_op jit(solution)/shard_map/ppermute | solution.py:490
  229.2 13.8 %collective-permute-start.65 = (bf16[64,3072]{1,0:T(8,128)(2,1)S(1)}, bf16[64,3072]{1,0:T(8,128)(2,1)S(1)}, u32[]{:S(2)}, u32[]{:S(2)}) collective-permute-start(bf16[64,3072]{1,0:T(8,128)(2,1)S(1)} %get-tuple-element.245), channel_id=1, source_target_pairs={{3,2},{7,6},{11,10},{15,14},{19,18},{23,22},{27,26},{31,30}} | collective-permute-start | bytes 1179656 | tf_op jit(solution)/shard_map/ppermute | solution.py:447
  230.6 18.3 %collective-permute-start.58 = (bf16[64,3072]{1,0:T(8,128)(2,1)S(1)}, bf16[64,3072]{1,0:T(8,128)(2,1)S(1)}, u32[]{:S(2)}, u32[]{:S(2)}) collective-permute-start(bf16[64,3072]{1,0:T(8,128)(2,1)S(1)} %get-tuple-element.236), channel_id=1, source_target_pairs={{0,1},{4,5},{8,9},{12,13},{16,17},{20,21},{24,25},{28,29}} | collective-permute-start | bytes 1179656 | tf_op jit(solution)/shard_map/ppermute | solution.py:446
  231.5 19.9 %collective-permute-start.59 = (bf16[64,3072]{1,0:T(8,128)(2,1)S(1)}, bf16[64,3072]{1,0:T(8,128)(2,1)S(1)}, u32[]{:S(2)}, u32[]{:S(2)}) collective-permute-start(bf16[64,3072]{1,0:T(8,128)(2,1)S(1)} %get-tuple-element.234), channel_id=1, source_target_pairs={{3,2},{7,6},{11,10},{15,14},{19,18},{23,22},{27,26},{31,30}} | collective-permute-start | bytes 1179656 | tf_op jit(solution)/shard_map/ppermute | solution.py:447
  243.1 14.7 %collective-permute-start.66 = (bf16[64,3072]{1,0:T(8,128)(2,1)S(1)}, bf16[64,3072]{1,0:T(8,128)(2,1)S(1)}, u32[]{:S(2)}, u32[]{:S(2)}) collective-permute-start(bf16[64,3072]{1,0:T(8,128)(2,1)S(1)} %get-tuple-element.306), channel_id=1, source_target_pairs={{0,1},{1,2},{4,5},{5,6},{8,9},{9,10},{12,13},{13,14},{16,17},{17,1... | collective-permute-start | bytes 1179656 | tf_op jit(solution)/shard_map/ppermute | solution.py:446
  244.4 13.4 %collective-permute-start.67 = (bf16[64,3072]{1,0:T(8,128)(2,1)S(1)}, bf16[64,3072]{1,0:T(8,128)(2,1)S(1)}, u32[]{:S(2)}, u32[]{:S(2)}) collective-permute-start(bf16[64,3072]{1,0:T(8,128)(2,1)S(1)} %get-tuple-element.305), channel_id=1, source_target_pairs={{2,1},{3,2},{6,5},{7,6},{10,9},{11,10},{14,13},{15,14},{18,17},{19... | collective-permute-start | bytes 1179656 | tf_op jit(solution)/shard_map/ppermute | solution.py:447
  251.5 12.5 %collective-permute-start.60 = (bf16[64,3072]{1,0:T(8,128)(2,1)S(1)}, bf16[64,3072]{1,0:T(8,128)(2,1)S(1)}, u32[]{:S(2)}, u32[]{:S(2)}) collective-permute-start(bf16[64,3072]{1,0:T(8,128)(2,1)S(1)} %get-tuple-element.304), channel_id=1, source_target_pairs={{0,1},{1,2},{4,5},{5,6},{8,9},{9,10},{12,13},{13,14},{16,17},{17,1... | collective-permute-start | bytes 1179656 | tf_op jit(solution)/shard_map/ppermute | solution.py:446
  257.9 14.5 %collective-permute-start.69 = (bf16[64,3072]{1,0:T(8,128)(2,1)S(1)}, bf16[64,3072]{1,0:T(8,128)(2,1)S(1)}, u32[]{:S(2)}, u32[]{:S(2)}) collective-permute-start(bf16[64,3072]{1,0:T(8,128)(2,1)S(1)} %add.273), channel_id=1, source_target_pairs={{1,0},{2,1},{3,2},{5,4},{6,5},{7,6},{9,8},{10,9},{11,10},{13,12},{... | collective-permute-start | bytes 1179656 | tf_op jit(solution)/shard_map/ppermute | solution.py:447
  260.1 12.3 %collective-permute-start.68 = (bf16[64,3072]{1,0:T(8,128)(2,1)S(1)}, bf16[64,3072]{1,0:T(8,128)(2,1)S(1)}, u32[]{:S(2)}, u32[]{:S(2)}) collective-permute-start(bf16[64,3072]{1,0:T(8,128)(2,1)S(1)} %add.272), channel_id=1, source_target_pairs={{0,1},{1,2},{2,3},{4,5},{5,6},{6,7},{8,9},{9,10},{10,11},{12,13},{... | collective-permute-start | bytes 1179656 | tf_op jit(solution)/shard_map/ppermute | solution.py:446
  (53 other events, 570.5 us)

commit v8 on v5

--- a/solution.py
+++ b/solution.py
@@ -427,13 +427,17 @@
         marks = []
         for s in range(1, shards):
             for c, terms in enumerate(pieces_terms):
-                if got[c] is None:
-                    sent = (terms[s], terms[shards - s])
+                if s == 1:
+                    sent = jnp.where(me == 0, terms[1], terms[shards - 1])
+                    arrived = lax.ppermute(sent, "tp", [(0, 1), (shards - 1, shards - 2)])
+                    got[c] = (arrived, arrived)
+                    continue
+                if s == 2:
+                    to_right = to_left = terms[s] + got[c][0]
                 else:
-                    arrived = got[c]
-                    sent = (terms[s] + arrived[0], terms[shards - s] + arrived[1])
-                right = lax.ppermute(sent[0], "tp", rights(s))
-                left = lax.ppermute(sent[1], "tp", lefts(s))
+                    to_right, to_left = terms[s] + got[c][0], terms[shards - s] + got[c][1]
+                right = lax.ppermute(to_right, "tp", rights(s))
+                left = lax.ppermute(to_left, "tp", lefts(s))
                 got[c] = lax.optimization_barrier((right, left))
             marks.append(got[0])
         return [

time: 278 us -> 279 us (level); the launches traced: 277 us -> 273 us
  waiting for transfers between devices: 64.8 us -> 54.2 us
  Pallas kernels: 64.6 us -> 69.2 us
    pallas_call x2, Pallas kernels: 26 us -> 30.6 us  [attend(): pl.pallas_call(kernel, grid_spec=pltpu.PrefetchScalarGridSpec(num_scalar_...]
    ppermute x1, waiting for transfers between devices: 4.16 us -> 0.91 us  [gather_line(): first_left = lax.ppermute(source, 'tp', lefts(shards - 1))]
    ppermute x1, waiting for transfers between devices: 3.1 us -> 0.01 us  [gather_line(): first_right = lax.ppermute(source, 'tp', rights(shards - 1))]
    ppermute x24 -> x20, starting transfers between devices: 65 us -> 62 us  [the longest x8 38.9 us: reduce_line(): right = lax.ppermute(to_right, 'tp', rights(s))]
    ppermute x24 -> x20, waiting for transfers between devices: 29.7 us -> 27.1 us  [the longest x4 16.9 us: reduce_line(): arrived = lax.ppermute(sent, 'tp', [(0, 1), (shards - 1, shards - 2)])]
  transfers between devices with their start and end apart: 48 -> 44, of which waited for: 23 -> 21; matrix products, arithmetic and copies ran while one was open for 6% -> 7% of each run, Pallas kernels for 23% -> 25%
where the time goes in v8:
time: 279 us; the launch traced here: 273 us
  starting transfers between devices  119 us (43%)
  Pallas kernels  69.2 us (25%)
  waiting for transfers between devices  54.2 us (19%)
  other arithmetic  16.3 us (6%)
  matrix products  6.75 us (2%)
  local copies, waits for them, and re-layouts  5.65 us (2%)
    ppermute x8, starting transfers between devices, reduce_line(): right = lax.ppermute(to_right, 'tp', rights(s))  38.9 us
    pallas_call x1, Pallas kernels, expert_rows(): pl.pallas_call(functools.partial(expert_kernel, [len(source) for source i...  33.9 us
    pallas_call x2, Pallas kernels, attend(): pl.pallas_call(kernel, grid_spec=pltpu.PrefetchScalarGridSpec(num_scalar_...  30.6 us
    ppermute x4, starting transfers between devices, gather_line(): lax.ppermute(right, 'tp', to_right)  18.8 us
    ppermute x9, starting transfers between devices, shift(): lax.ppermute(parts[s], 'tp', moves[s])  18.5 us
    ppermute x4, waiting for transfers between devices, reduce_line(): arrived = lax.ppermute(sent, 'tp', [(0, 1), (shards - 1, shards - 2)])  16.9 us
    ppermute x9, waiting for transfers between devices, shift(): lax.ppermute(parts[s], 'tp', moves[s])  14.1 us
    ppermute x4, starting transfers between devices, reduce_line(): arrived = lax.ppermute(sent, 'tp', [(0, 1), (shards - 1, shards - 2)])  13.4 us
  transfers between devices with their start and end apart: 44, of which 21 were waited for; matrix products, arithmetic and copies ran while one was open for 7% of the time, Pallas kernels for 25%

profile of v8, /device:TPU:0, one launch (start us, length us, event | category | flops | bytes accessed | tf_op | source)
XLA Modules:
  0.0 273.2 jit_solution(9194951593907634696)
XLA Ops:
  2.7 3.0 %collective-permute-start.20 = (bf16[128,512]{1,0:T(8,128)(2,1)}, bf16[128,512]{1,0:T(8,128)(2,1)S(1)}, u32[]{:S(2)}, u32[]{:S(2)}) collective-permute-start(bf16[128,512]{1,0:T(8,128)(2,1)} %get-tuple-element.152), channel_id=1, source_target_pairs={{0,1},{1,2},{2,3},{3,0},{4,5},{5,6},{6,7},{7,4},{8,9},{9,10},{10,1... | collective-permute-start | bytes 393224 | tf_op jit(solution)/shard_map/ppermute | solution.py:407
  5.7 2.6 collective-permute-start.21
  12.4 4.8 %collective-permute-done.21 = bf16[128,512]{1,0:T(8,128)(2,1)S(1)} collective-permute-done((bf16[128,512]{1,0:T(8,128)(2,1)}, bf16[128,512]{1,0:T(8,128)(2,1)S(1)}, u32[]{:S(2)}, u32[]{:S(2)}) %collective-permute-start.21) | collective-permute-done | bytes 131104 | tf_op jit(solution)/shard_map/ppermute | solution.py:407
  19.3 2.7 %shard_map.132 = (bf16[64,1024]{1,0:T(8,128)(2,1)}, bf16[64,1024]{1,0:T(8,128)(2,1)}, bf16[64,1024]{1,0:T(8,128)(2,1)}, bf16[64,1024]{1,0:T(8,128)(2,1)}, bf16[6...) custom-call(s32[1]{0:T(128)} %bitcast.6.mine.refs_0_, ...), custom_call_target="tpu_custom_call" | custom-call | tf_op jit(solution)/shard_map/pallas_call | solution.py:359
  22.1 3.3 %collective-permute-start.24 = (bf16[64,1024]{1,0:T(8,128)(2,1)}, bf16[64,1024]{1,0:T(8,128)(2,1)S(1)}, u32[]{:S(2)}, u32[]{:S(2)}) collective-permute-start(bf16[64,1024]{1,0:T(8,128)(2,1)} %get-tuple-element.158), channel_id=1, source_target_pairs={{0,1},{1,2},{2,3},{3,0},{4,5},{5,6},{6,7},{7,4},{8,9},{9,10},{10,1... | collective-permute-start | bytes 393224 | tf_op jit(solution)/shard_map/ppermute | solution.py:407
  27.8 3.2 %collective-permute-done.24.refs_2_ = bf16[64,1024]{1,0:T(8,128)(2,1)S(1)} collective-permute-done((bf16[64,1024]{1,0:T(8,128)(2,1)}, bf16[64,1024]{1,0:T(8,128)(2,1)S(1)}, u32[]{:S(2)}, u32[]{:S(2)}) %collective-permute-start.24) | collective-permute-done | bytes 131104 | tf_op jit(solution)/shard_map/ppermute | solution.py:407
  31.0 4.3 %collective-permute-done.25.refs_4_ = bf16[64,1024]{1,0:T(8,128)(2,1)S(1)} collective-permute-done((bf16[64,1024]{1,0:T(8,128)(2,1)}, bf16[64,1024]{1,0:T(8,128)(2,1)S(1)}, u32[]{:S(2)}, u32[]{:S(2)}) %collective-permute-start.25) | collective-permute-done | bytes 131104 | tf_op jit(solution)/shard_map/ppermute | solution.py:407
  35.5 3.3 %collective-permute-start.29 = (bf16[64,1024]{1,0:T(8,128)(2,1)}, bf16[64,1024]{1,0:T(8,128)(2,1)}, u32[]{:S(2)}, u32[]{:S(2)}) collective-permute-start(bf16[64,1024]{1,0:T(8,128)(2,1)} %get-tuple-element.176), channel_id=1, source_target_pairs={{0,1},{1,2},{2,3},{3,0},{4,5},{5,6},{6,7},{7,4},{8,9},{9,10},{10,1... | collective-permute-start | bytes 393224 | tf_op jit(solution)/shard_map/ppermute | solution.py:407
  42.8 15.3 %shard_map.133 = (bf16[64,3072]{1,0:T(8,128)(2,1)S(1)}, bf16[64,3072]{1,0:T(8,128)(2,1)S(1)}, bf16[64,3072]{1,0:T(8,128)(2,1)S(1)}, bf16[64,3072]{1,0:T(8,128)(2...) custom-call(s32[4]{0:T(128)S(1)} %copy-done.15, ...), custom_call_target="tpu_custom_call" | custom-call | flops 21474836480 | bytes 15728640 | tf_op jit(solution)/shard_map/pallas_call | solution.py:168
  58.2 3.2 %collective-permute-start.37 = (bf16[64,3072]{1,0:T(8,128)(2,1)S(1)}, bf16[64,3072]{1,0:T(8,128)(2,1)S(1)}, u32[]{:S(2)}, u32[]{:S(2)}) collective-permute-start(bf16[64,3072]{1,0:T(8,128)(2,1)S(1)} %broadcast_select_fusion.4), channel_id=1, source_target_pairs={{0,1},{3,2},{4,5},{7,6},{8,9},{11,10},{12,13},{15,14},{16,17},{19,... | collective-permute-start | bytes 1179656 | tf_op jit(solution)/shard_map/ppermute | solution.py:432
  62.8 8.2 %collective-permute-done.37 = bf16[64,3072]{1,0:T(8,128)(2,1)S(1)} collective-permute-done((bf16[64,3072]{1,0:T(8,128)(2,1)S(1)}, bf16[64,3072]{1,0:T(8,128)(2,1)S(1)}, u32[]{:S(2)}, u32[]{:S(2)}) %collective-permute-start.37) | collective-permute-done | bytes 393248 | tf_op jit(solution)/shard_map/ppermute | solution.py:432
  71.8 5.1 %collective-permute-start.38 = (bf16[64,3072]{1,0:T(8,128)(2,1)}, bf16[64,3072]{1,0:T(8,128)(2,1)}, u32[]{:S(2)}, u32[]{:S(2)}) collective-permute-start(bf16[64,3072]{1,0:T(8,128)(2,1)} %add.218), channel_id=1, source_target_pairs={{0,1},{1,2},{4,5},{5,6},{8,9},{9,10},{12,13},{13,14},{16,17},{17,1... | collective-permute-start | bytes 1179656 | tf_op jit(solution)/shard_map/ppermute | solution.py:439
  80.2 5.2 %collective-permute-start.33 = (bf16[64,3072]{1,0:T(8,128)(2,1)}, bf16[64,3072]{1,0:T(8,128)(2,1)}, u32[]{:S(2)}, u32[]{:S(2)}) collective-permute-start(bf16[64,3072]{1,0:T(8,128)(2,1)} %add.212), channel_id=1, source_target_pairs={{0,1},{1,2},{4,5},{5,6},{8,9},{9,10},{12,13},{13,14},{16,17},{17,1... | collective-permute-start | bytes 1179656 | tf_op jit(solution)/shard_map/ppermute | solution.py:439
  91.9 4.6 %collective-permute-start.40 = (bf16[64,3072]{1,0:T(8,128)(2,1)S(1)}, bf16[64,3072]{1,0:T(8,128)(2,1)S(1)}, u32[]{:S(2)}, u32[]{:S(2)}) collective-permute-start(bf16[64,3072]{1,0:T(8,128)(2,1)S(1)} %add.219), channel_id=1, source_target_pairs={{0,1},{1,2},{2,3},{4,5},{5,6},{6,7},{8,9},{9,10},{10,11},{12,13},{... | collective-permute-start | bytes 1179656 | tf_op jit(solution)/shard_map/ppermute | solution.py:439
  100.2 5.0 %collective-permute-start.35 = (bf16[64,3072]{1,0:T(8,128)(2,1)S(1)}, bf16[64,3072]{1,0:T(8,128)(2,1)S(1)}, u32[]{:S(2)}, u32[]{:S(2)}) collective-permute-start(bf16[64,3072]{1,0:T(8,128)(2,1)S(1)} %add.213), channel_id=1, source_target_pairs={{0,1},{1,2},{2,3},{4,5},{5,6},{6,7},{8,9},{9,10},{10,11},{12,13},{... | collective-permute-start | bytes 1179656 | tf_op jit(solution)/shard_map/ppermute | solution.py:439
  107.9 2.6 collective-permute-done.35
  111.4 4.4 %collective-permute-start.42 = (bf16[64,6144]{1,0:T(8,128)(2,1)S(1)}, bf16[64,6144]{1,0:T(8,128)(2,1)S(1)}, u32[]{:S(2)}, u32[]{:S(2)}) collective-permute-start(bf16[64,6144]{1,0:T(8,128)(2,1)S(1)} %fusion.7.refs_1_), channel_id=1, source_target_pairs={{0,1},{1,2},{2,3},{4,5},{5,6},{6,7},{8,9},{9,10},{10,11},{12,13},{... | collective-permute-start | bytes 2359304 | tf_op jit(solution)/shard_map/ppermute | solution.py:452
  117.2 15.3 %shard_map.134 = (bf16[64,3072]{1,0:T(8,128)(2,1)S(1)}, bf16[64,3072]{1,0:T(8,128)(2,1)S(1)}, bf16[64,3072]{1,0:T(8,128)(2,1)S(1)}, bf16[64,3072]{1,0:T(8,128)(2...) custom-call(s32[4]{0:T(128)S(1)} %copy-done.15, ...), custom_call_target="tpu_custom_call" | custom-call | flops 21474836480 | bytes 15728640 | tf_op jit(solution)/shard_map/pallas_call | solution.py:168
  135.0 5.3 %collective-permute-start.44 = (bf16[64,3072]{1,0:T(8,128)(2,1)S(1)}, bf16[64,3072]{1,0:T(8,128)(2,1)}, u32[]{:S(2)}, u32[]{:S(2)}) collective-permute-start(bf16[64,3072]{1,0:T(8,128)(2,1)S(1)} %get-tuple-element.276.refs_2_), channel_id=1, source_target_pairs={{0,1},{1,2},{2,3},{4,5},{5,6},{6,7},{8,9},{9,10},{10,11},{12,13},{... | collective-permute-start | bytes 1179656 | tf_op jit(solution)/shard_map/ppermute | solution.py:474
  141.9 4.6 %collective-permute-start.46 = (bf16[64,3072]{1,0:T(8,128)(2,1)S(1)}, bf16[64,3072]{1,0:T(8,128)(2,1)S(1)}, u32[]{:S(2)}, u32[]{:S(2)}) collective-permute-start(bf16[64,3072]{1,0:T(8,128)(2,1)S(1)} %get-tuple-element.275.refs_3_), channel_id=1, source_target_pairs={{0,1},{1,2},{2,3},{4,5},{5,6},{6,7},{8,9},{9,10},{10,11},{12,13},{... | collective-permute-start | bytes 1179656 | tf_op jit(solution)/shard_map/ppermute | solution.py:474
  150.4 4.5 %collective-permute-start.48 = (bf16[64,3072]{1,0:T(8,128)(2,1)S(1)}, bf16[64,3072]{1,0:T(8,128)(2,1)S(1)}, u32[]{:S(2)}, u32[]{:S(2)}) collective-permute-start(bf16[64,3072]{1,0:T(8,128)(2,1)S(1)} %get-tuple-element.280.refs_4_), channel_id=1, source_target_pairs={{0,1},{1,2},{2,3},{4,5},{5,6},{6,7},{8,9},{9,10},{10,11},{12,13},{... | collective-permute-start | bytes 1179656 | tf_op jit(solution)/shard_map/ppermute | solution.py:474
  157.6 4.4 %collective-permute-start.50 = (bf16[64,3072]{1,0:T(8,128)(2,1)S(1)}, bf16[64,3072]{1,0:T(8,128)(2,1)S(1)}, u32[]{:S(2)}, u32[]{:S(2)}) collective-permute-start(bf16[64,3072]{1,0:T(8,128)(2,1)S(1)} %get-tuple-element.278.refs_5_), channel_id=1, source_target_pairs={{0,1},{1,2},{2,3},{4,5},{5,6},{6,7},{8,9},{9,10},{10,11},{12,13},{... | collective-permute-start | bytes 1179656 | tf_op jit(solution)/shard_map/ppermute | solution.py:474
  164.8 4.7 %collective-permute-done.50.refs_7_ = bf16[64,3072]{1,0:T(8,128)(2,1)S(1)} collective-permute-done((bf16[64,3072]{1,0:T(8,128)(2,1)S(1)}, bf16[64,3072]{1,0:T(8,128)(2,1)S(1)}, u32[]{:S(2)}, u32[]{:S(2)}) %collective-permute-start.50) | collective-permute-done | bytes 393248 | tf_op jit(solution)/shard_map/ppermute | solution.py:474
  171.8 5.5 %collective-permute-start.52 = (bf16[64,6144]{1,0:T(8,128)(2,1)S(1)}, bf16[64,6144]{1,0:T(8,128)(2,1)S(1)}, u32[]{:S(2)}, u32[]{:S(2)}) collective-permute-start(bf16[64,6144]{1,0:T(8,128)(2,1)S(1)} %pad_maximum_fusion.2), channel_id=1, source_target_pairs={{0,1},{1,2},{2,3},{4,5},{5,6},{6,7},{8,9},{9,10},{10,11},{12,13},{... | collective-permute-start | bytes 2359304 | tf_op jit(solution)/shard_map/ppermute | solution.py:483
  178.9 33.9 %shard_map.135 = (bf16[256,3072]{1,0:T(8,128)(2,1)S(1)}, bf16[256,3072]{1,0:T(8,128)(2,1)S(1)}) custom-call(s32[1]{0:T(128)} %bitcast.6.mine.refs_0_, bf16[64,6144]{1,0:T(8,128)(2,1)S(1)} %fusion.7.refs_1_, bf16[64,3072]{1,0:T(8,128)(2,1)S(1)} %get-tuple-element.276.refs_2_, bf16[64,3072]{1,0:T(8,128)(2,1)S(1)} %get-tuple-element.275.refs_3_, ...), custom_call_target="tpu_custom_call" | custom-call | flops 19327352832 | bytes 75497472 | tf_op jit(solution)/shard_map/pallas_call | solution.py:263
  216.2 6.8 %collective-permute-start.59 = (bf16[64,3072]{1,0:T(8,128)(2,1)}, bf16[64,3072]{1,0:T(8,128)(2,1)}, u32[]{:S(2)}, u32[]{:S(2)}) collective-permute-start(bf16[64,3072]{1,0:T(8,128)(2,1)} %broadcast_select_fusion.2), channel_id=1, source_target_pairs={{0,1},{3,2},{4,5},{7,6},{8,9},{11,10},{12,13},{15,14},{16,17},{19,... | collective-permute-start | bytes 1179656 | tf_op jit(solution)/shard_map/ppermute | solution.py:432
  226.6 5.6 %collective-permute-done.59 = bf16[64,3072]{1,0:T(8,128)(2,1)} collective-permute-done((bf16[64,3072]{1,0:T(8,128)(2,1)}, bf16[64,3072]{1,0:T(8,128)(2,1)}, u32[]{:S(2)}, u32[]{:S(2)}) %collective-permute-start.59) | collective-permute-done | bytes 393248 | tf_op jit(solution)/shard_map/ppermute | solution.py:432
  233.4 4.4 %collective-permute-start.60 = (bf16[64,3072]{1,0:T(8,128)(2,1)S(1)}, bf16[64,3072]{1,0:T(8,128)(2,1)S(1)}, u32[]{:S(2)}, u32[]{:S(2)}) collective-permute-start(bf16[64,3072]{1,0:T(8,128)(2,1)S(1)} %add.249), channel_id=1, source_target_pairs={{0,1},{1,2},{4,5},{5,6},{8,9},{9,10},{12,13},{13,14},{16,17},{17,1... | collective-permute-start | bytes 1179656 | tf_op jit(solution)/shard_map/ppermute | solution.py:439
  241.7 4.4 %collective-permute-start.55 = (bf16[64,3072]{1,0:T(8,128)(2,1)S(1)}, bf16[64,3072]{1,0:T(8,128)(2,1)S(1)}, u32[]{:S(2)}, u32[]{:S(2)}) collective-permute-start(bf16[64,3072]{1,0:T(8,128)(2,1)S(1)} %add.240), channel_id=1, source_target_pairs={{0,1},{1,2},{4,5},{5,6},{8,9},{9,10},{12,13},{13,14},{16,17},{17,1... | collective-permute-start | bytes 1179656 | tf_op jit(solution)/shard_map/ppermute | solution.py:439
  250.6 5.5 %collective-permute-start.62 = (bf16[64,3072]{1,0:T(8,128)(2,1)S(1)}, bf16[64,3072]{1,0:T(8,128)(2,1)S(1)}, u32[]{:S(2)}, u32[]{:S(2)}) collective-permute-start(bf16[64,3072]{1,0:T(8,128)(2,1)S(1)} %add.250), channel_id=1, source_target_pairs={{0,1},{1,2},{2,3},{4,5},{5,6},{6,7},{8,9},{9,10},{10,11},{12,13},{... | collective-permute-start | bytes 1179656 | tf_op jit(solution)/shard_map/ppermute | solution.py:439
  257.7 4.7 %collective-permute-start.57 = (bf16[64,3072]{1,0:T(8,128)(2,1)S(1)}, bf16[64,3072]{1,0:T(8,128)(2,1)S(1)}, u32[]{:S(2)}, u32[]{:S(2)}) collective-permute-start(bf16[64,3072]{1,0:T(8,128)(2,1)S(1)} %add.241), channel_id=1, source_target_pairs={{0,1},{1,2},{2,3},{4,5},{5,6},{6,7},{8,9},{9,10},{10,11},{12,13},{... | collective-permute-start | bytes 1179656 | tf_op jit(solution)/shard_map/ppermute | solution.py:439
  270.0 3.2 %convolution_convert_fusion = bf16[128,6144]{1,0:T(8,128)(2,1)} fusion(bf16[128,128]{1,0:T(8,128)(2,1)} %get-tuple-element.181, bf16[64,6144]{1,0:T(8,128)(2,1)} %get-tuple-element.289, bf16[64,6144]{1,0:T(8,128)(2,1)} %pad_maximum_fusion.4), kind=kOutput, calls=%fused_computation.25 | convolution fusion | flops 205258752 | bytes 3178496 | tf_op jit(solution)/shard_map/dot_general | solution.py:528
  (188 shorter events, 78.2 us)
Async XLA Ops:
  5.7 11.4 %collective-permute-start.21 = (bf16[128,512]{1,0:T(8,128)(2,1)}, bf16[128,512]{1,0:T(8,128)(2,1)S(1)}, u32[]{:S(2)}, u32[]{:S(2)}) collective-permute-start(bf16[128,512]{1,0:T(8,128)(2,1)} %get-tuple-element.153), channel_id=1, source_target_pairs={{0,2},{1,3},{2,0},{3,1},{4,6},{5,7},{6,4},{7,5},{8,10},{9,11},{10,... | collective-permute-start | bytes 393224 | tf_op jit(solution)/shard_map/ppermute | solution.py:407
  17.2 18.2 %collective-permute-start.23 = (bf16[512,512]{1,0:T(8,128)(2,1)S(1)}, bf16[512,512]{1,0:T(8,128)(2,1)S(1)}, u32[]{:S(2)}, u32[]{:S(2)}) collective-permute-start(bf16[512,512]{1,0:T(8,128)(2,1)S(1)} %constant_dynamic-update-slice_fusion.refs_7_), channel_id=1, source_target_pairs={{0,8},{4,12},{8,0},{12,4},{1,9},{5,13},{9,1},{13,5},{2,10},{6,14},... | collective-permute-start | bytes 1572872 | tf_op jit(solution)/shard_map/ppermute | solution.py:517
  27.8 13.5 %collective-permute-start.27 = (bf16[512,512]{1,0:T(8,128)(2,1)S(1)}, bf16[512,512]{1,0:T(8,128)(2,1)S(1)}, u32[]{:S(2)}, u32[]{:S(2)}) collective-permute-start(bf16[512,512]{1,0:T(8,128)(2,1)S(1)} %constant_dynamic-update-slice_fusion.refs_7_), channel_id=1, source_target_pairs={{0,4},{4,0},{8,12},{12,8},{1,5},{5,1},{9,13},{13,9},{2,6},{6,2},{1... | collective-permute-start | bytes 1572872 | tf_op jit(solution)/shard_map/ppermute | solution.py:517
  35.5 22.6 %collective-permute-start.29 = (bf16[64,1024]{1,0:T(8,128)(2,1)}, bf16[64,1024]{1,0:T(8,128)(2,1)}, u32[]{:S(2)}, u32[]{:S(2)}) collective-permute-start(bf16[64,1024]{1,0:T(8,128)(2,1)} %get-tuple-element.176), channel_id=1, source_target_pairs={{0,1},{1,2},{2,3},{3,0},{4,5},{5,6},{6,7},{7,4},{8,9},{9,10},{10,1... | collective-permute-start | bytes 393224 | tf_op jit(solution)/shard_map/ppermute | solution.py:407
  38.8 19.3 %collective-permute-start.30 = (bf16[64,1024]{1,0:T(8,128)(2,1)}, bf16[64,1024]{1,0:T(8,128)(2,1)}, u32[]{:S(2)}, u32[]{:S(2)}) collective-permute-start(bf16[64,1024]{1,0:T(8,128)(2,1)} %get-tuple-element.177), channel_id=1, source_target_pairs={{0,2},{1,3},{2,0},{3,1},{4,6},{5,7},{6,4},{7,5},{8,10},{9,11},{10,... | collective-permute-start | bytes 393224 | tf_op jit(solution)/shard_map/ppermute | solution.py:407
  40.5 17.6 %collective-permute-start.31 = (bf16[64,1024]{1,0:T(8,128)(2,1)}, bf16[64,1024]{1,0:T(8,128)(2,1)}, u32[]{:S(2)}, u32[]{:S(2)}) collective-permute-start(bf16[64,1024]{1,0:T(8,128)(2,1)} %get-tuple-element.178), channel_id=1, source_target_pairs={{0,3},{1,0},{2,1},{3,2},{4,7},{5,4},{6,5},{7,6},{8,11},{9,8},{10,9... | collective-permute-start | bytes 393224 | tf_op jit(solution)/shard_map/ppermute | solution.py:407
  58.2 12.8 %collective-permute-start.37 = (bf16[64,3072]{1,0:T(8,128)(2,1)S(1)}, bf16[64,3072]{1,0:T(8,128)(2,1)S(1)}, u32[]{:S(2)}, u32[]{:S(2)}) collective-permute-start(bf16[64,3072]{1,0:T(8,128)(2,1)S(1)} %broadcast_select_fusion.4), channel_id=1, source_target_pairs={{0,1},{3,2},{4,5},{7,6},{8,9},{11,10},{12,13},{15,14},{16,17},{19,... | collective-permute-start | bytes 1179656 | tf_op jit(solution)/shard_map/ppermute | solution.py:432
  61.5 17.9 %collective-permute-start.32 = (bf16[64,3072]{1,0:T(8,128)(2,1)S(1)}, bf16[64,3072]{1,0:T(8,128)(2,1)S(1)}, u32[]{:S(2)}, u32[]{:S(2)}) collective-permute-start(bf16[64,3072]{1,0:T(8,128)(2,1)S(1)} %broadcast_select_fusion.5), channel_id=1, source_target_pairs={{0,1},{3,2},{4,5},{7,6},{8,9},{11,10},{12,13},{15,14},{16,17},{19,... | collective-permute-start | bytes 1179656 | tf_op jit(solution)/shard_map/ppermute | solution.py:432
  71.8 16.3 %collective-permute-start.38 = (bf16[64,3072]{1,0:T(8,128)(2,1)}, bf16[64,3072]{1,0:T(8,128)(2,1)}, u32[]{:S(2)}, u32[]{:S(2)}) collective-permute-start(bf16[64,3072]{1,0:T(8,128)(2,1)} %add.218), channel_id=1, source_target_pairs={{0,1},{1,2},{4,5},{5,6},{8,9},{9,10},{12,13},{13,14},{16,17},{17,1... | collective-permute-start | bytes 1179656 | tf_op jit(solution)/shard_map/ppermute | solution.py:439
  76.9 11.2 %collective-permute-start.39 = (bf16[64,3072]{1,0:T(8,128)(2,1)}, bf16[64,3072]{1,0:T(8,128)(2,1)}, u32[]{:S(2)}, u32[]{:S(2)}) collective-permute-start(bf16[64,3072]{1,0:T(8,128)(2,1)} %add.218), channel_id=1, source_target_pairs={{2,1},{3,2},{6,5},{7,6},{10,9},{11,10},{14,13},{15,14},{18,17},{19... | collective-permute-start | bytes 1179656 | tf_op jit(solution)/shard_map/ppermute | solution.py:440
  80.2 16.3 %collective-permute-start.33 = (bf16[64,3072]{1,0:T(8,128)(2,1)}, bf16[64,3072]{1,0:T(8,128)(2,1)}, u32[]{:S(2)}, u32[]{:S(2)}) collective-permute-start(bf16[64,3072]{1,0:T(8,128)(2,1)} %add.212), channel_id=1, source_target_pairs={{0,1},{1,2},{4,5},{5,6},{8,9},{9,10},{12,13},{13,14},{16,17},{17,1... | collective-permute-start | bytes 1179656 | tf_op jit(solution)/shard_map/ppermute | solution.py:439
  85.4 11.2 %collective-permute-start.34 = (bf16[64,3072]{1,0:T(8,128)(2,1)}, bf16[64,3072]{1,0:T(8,128)(2,1)}, u32[]{:S(2)}, u32[]{:S(2)}) collective-permute-start(bf16[64,3072]{1,0:T(8,128)(2,1)} %add.212), channel_id=1, source_target_pairs={{2,1},{3,2},{6,5},{7,6},{10,9},{11,10},{14,13},{15,14},{18,17},{19... | collective-permute-start | bytes 1179656 | tf_op jit(solution)/shard_map/ppermute | solution.py:440
  89.6 15.7 %collective-permute-start.41 = (bf16[64,3072]{1,0:T(8,128)(2,1)S(1)}, bf16[64,3072]{1,0:T(8,128)(2,1)S(1)}, u32[]{:S(2)}, u32[]{:S(2)}) collective-permute-start(bf16[64,3072]{1,0:T(8,128)(2,1)S(1)} %add.220), channel_id=1, source_target_pairs={{1,0},{2,1},{3,2},{5,4},{6,5},{7,6},{9,8},{10,9},{11,10},{13,12},{... | collective-permute-start | bytes 1179656 | tf_op jit(solution)/shard_map/ppermute | solution.py:440
  91.9 13.9 %collective-permute-start.40 = (bf16[64,3072]{1,0:T(8,128)(2,1)S(1)}, bf16[64,3072]{1,0:T(8,128)(2,1)S(1)}, u32[]{:S(2)}, u32[]{:S(2)}) collective-permute-start(bf16[64,3072]{1,0:T(8,128)(2,1)S(1)} %add.219), channel_id=1, source_target_pairs={{0,1},{1,2},{2,3},{4,5},{5,6},{6,7},{8,9},{9,10},{10,11},{12,13},{... | collective-permute-start | bytes 1179656 | tf_op jit(solution)/shard_map/ppermute | solution.py:439
  100.2 10.2 %collective-permute-start.35 = (bf16[64,3072]{1,0:T(8,128)(2,1)S(1)}, bf16[64,3072]{1,0:T(8,128)(2,1)S(1)}, u32[]{:S(2)}, u32[]{:S(2)}) collective-permute-start(bf16[64,3072]{1,0:T(8,128)(2,1)S(1)} %add.213), channel_id=1, source_target_pairs={{0,1},{1,2},{2,3},{4,5},{5,6},{6,7},{8,9},{9,10},{10,11},{12,13},{... | collective-permute-start | bytes 1179656 | tf_op jit(solution)/shard_map/ppermute | solution.py:439
  111.4 21.1 %collective-permute-start.42 = (bf16[64,6144]{1,0:T(8,128)(2,1)S(1)}, bf16[64,6144]{1,0:T(8,128)(2,1)S(1)}, u32[]{:S(2)}, u32[]{:S(2)}) collective-permute-start(bf16[64,6144]{1,0:T(8,128)(2,1)S(1)} %fusion.7.refs_1_), channel_id=1, source_target_pairs={{0,1},{1,2},{2,3},{4,5},{5,6},{6,7},{8,9},{9,10},{10,11},{12,13},{... | collective-permute-start | bytes 2359304 | tf_op jit(solution)/shard_map/ppermute | solution.py:452
  115.9 17.6 %collective-permute-start.43 = (bf16[64,6144]{1,0:T(8,128)(2,1)S(1)}, bf16[64,6144]{1,0:T(8,128)(2,1)S(1)}, u32[]{:S(2)}, u32[]{:S(2)}) collective-permute-start(bf16[64,6144]{1,0:T(8,128)(2,1)S(1)} %fusion.7.refs_1_), channel_id=1, source_target_pairs={{1,0},{2,1},{3,2},{5,4},{6,5},{7,6},{9,8},{10,9},{11,10},{13,12},{... | collective-permute-start | bytes 2359304 | tf_op jit(solution)/shard_map/ppermute | solution.py:453
  133.6 13.2 %collective-permute-start.45 = (bf16[64,3072]{1,0:T(8,128)(2,1)S(1)}, bf16[64,3072]{1,0:T(8,128)(2,1)}, u32[]{:S(2)}, u32[]{:S(2)}) collective-permute-start(bf16[64,3072]{1,0:T(8,128)(2,1)S(1)} %get-tuple-element.274.refs_8_), channel_id=1, source_target_pairs={{1,0},{2,1},{3,2},{5,4},{6,5},{7,6},{9,8},{10,9},{11,10},{13,12},{... | collective-permute-start | bytes 1179656 | tf_op jit(solution)/shard_map/ppermute | solution.py:474
  135.0 14.1 %collective-permute-start.44 = (bf16[64,3072]{1,0:T(8,128)(2,1)S(1)}, bf16[64,3072]{1,0:T(8,128)(2,1)}, u32[]{:S(2)}, u32[]{:S(2)}) collective-permute-start(bf16[64,3072]{1,0:T(8,128)(2,1)S(1)} %get-tuple-element.276.refs_2_), channel_id=1, source_target_pairs={{0,1},{1,2},{2,3},{4,5},{5,6},{6,7},{8,9},{9,10},{10,11},{12,13},{... | collective-permute-start | bytes 1179656 | tf_op jit(solution)/shard_map/ppermute | solution.py:474
  140.3 15.9 %collective-permute-start.47 = (bf16[64,3072]{1,0:T(8,128)(2,1)S(1)}, bf16[64,3072]{1,0:T(8,128)(2,1)S(1)}, u32[]{:S(2)}, u32[]{:S(2)}) collective-permute-start(bf16[64,3072]{1,0:T(8,128)(2,1)S(1)} %get-tuple-element.273.refs_9_), channel_id=1, source_target_pairs={{1,0},{2,1},{3,2},{5,4},{6,5},{7,6},{9,8},{10,9},{11,10},{13,12},{... | collective-permute-start | bytes 1179656 | tf_op jit(solution)/shard_map/ppermute | solution.py:474
  141.9 15.6 %collective-permute-start.46 = (bf16[64,3072]{1,0:T(8,128)(2,1)S(1)}, bf16[64,3072]{1,0:T(8,128)(2,1)S(1)}, u32[]{:S(2)}, u32[]{:S(2)}) collective-permute-start(bf16[64,3072]{1,0:T(8,128)(2,1)S(1)} %get-tuple-element.275.refs_3_), channel_id=1, source_target_pairs={{0,1},{1,2},{2,3},{4,5},{5,6},{6,7},{8,9},{9,10},{10,11},{12,13},{... | collective-permute-start | bytes 1179656 | tf_op jit(solution)/shard_map/ppermute | solution.py:474
  150.4 14.3 %collective-permute-start.48 = (bf16[64,3072]{1,0:T(8,128)(2,1)S(1)}, bf16[64,3072]{1,0:T(8,128)(2,1)S(1)}, u32[]{:S(2)}, u32[]{:S(2)}) collective-permute-start(bf16[64,3072]{1,0:T(8,128)(2,1)S(1)} %get-tuple-element.280.refs_4_), channel_id=1, source_target_pairs={{0,1},{1,2},{2,3},{4,5},{5,6},{6,7},{8,9},{9,10},{10,11},{12,13},{... | collective-permute-start | bytes 1179656 | tf_op jit(solution)/shard_map/ppermute | solution.py:474
  157.6 12.0 %collective-permute-start.50 = (bf16[64,3072]{1,0:T(8,128)(2,1)S(1)}, bf16[64,3072]{1,0:T(8,128)(2,1)S(1)}, u32[]{:S(2)}, u32[]{:S(2)}) collective-permute-start(bf16[64,3072]{1,0:T(8,128)(2,1)S(1)} %get-tuple-element.278.refs_5_), channel_id=1, source_target_pairs={{0,1},{1,2},{2,3},{4,5},{5,6},{6,7},{8,9},{9,10},{10,11},{12,13},{... | collective-permute-start | bytes 1179656 | tf_op jit(solution)/shard_map/ppermute | solution.py:474
  171.8 42.3 %collective-permute-start.52 = (bf16[64,6144]{1,0:T(8,128)(2,1)S(1)}, bf16[64,6144]{1,0:T(8,128)(2,1)S(1)}, u32[]{:S(2)}, u32[]{:S(2)}) collective-permute-start(bf16[64,6144]{1,0:T(8,128)(2,1)S(1)} %pad_maximum_fusion.2), channel_id=1, source_target_pairs={{0,1},{1,2},{2,3},{4,5},{5,6},{6,7},{8,9},{9,10},{10,11},{12,13},{... | collective-permute-start | bytes 2359304 | tf_op jit(solution)/shard_map/ppermute | solution.py:483
  177.6 36.5 %collective-permute-start.53 = (bf16[64,6144]{1,0:T(8,128)(2,1)S(1)}, bf16[64,6144]{1,0:T(8,128)(2,1)S(1)}, u32[]{:S(2)}, u32[]{:S(2)}) collective-permute-start(bf16[64,6144]{1,0:T(8,128)(2,1)S(1)} %pad_maximum_fusion.3), channel_id=1, source_target_pairs={{1,0},{2,1},{3,2},{5,4},{6,5},{7,6},{9,8},{10,9},{11,10},{13,12},{... | collective-permute-start | bytes 2359304 | tf_op jit(solution)/shard_map/ppermute | solution.py:484
  216.2 15.9 %collective-permute-start.59 = (bf16[64,3072]{1,0:T(8,128)(2,1)}, bf16[64,3072]{1,0:T(8,128)(2,1)}, u32[]{:S(2)}, u32[]{:S(2)}) collective-permute-start(bf16[64,3072]{1,0:T(8,128)(2,1)} %broadcast_select_fusion.2), channel_id=1, source_target_pairs={{0,1},{3,2},{4,5},{7,6},{8,9},{11,10},{12,13},{15,14},{16,17},{19,... | collective-permute-start | bytes 1179656 | tf_op jit(solution)/shard_map/ppermute | solution.py:432
  223.8 16.8 %collective-permute-start.54 = (bf16[64,3072]{1,0:T(8,128)(2,1)}, bf16[64,3072]{1,0:T(8,128)(2,1)}, u32[]{:S(2)}, u32[]{:S(2)}) collective-permute-start(bf16[64,3072]{1,0:T(8,128)(2,1)} %broadcast_select_fusion.3), channel_id=1, source_target_pairs={{0,1},{3,2},{4,5},{7,6},{8,9},{11,10},{12,13},{15,14},{16,17},{19,... | collective-permute-start | bytes 1179656 | tf_op jit(solution)/shard_map/ppermute | solution.py:432
  233.4 15.5 %collective-permute-start.60 = (bf16[64,3072]{1,0:T(8,128)(2,1)S(1)}, bf16[64,3072]{1,0:T(8,128)(2,1)S(1)}, u32[]{:S(2)}, u32[]{:S(2)}) collective-permute-start(bf16[64,3072]{1,0:T(8,128)(2,1)S(1)} %add.249), channel_id=1, source_target_pairs={{0,1},{1,2},{4,5},{5,6},{8,9},{9,10},{12,13},{13,14},{16,17},{17,1... | collective-permute-start | bytes 1179656 | tf_op jit(solution)/shard_map/ppermute | solution.py:439
  237.8 11.1 %collective-permute-start.61 = (bf16[64,3072]{1,0:T(8,128)(2,1)S(1)}, bf16[64,3072]{1,0:T(8,128)(2,1)S(1)}, u32[]{:S(2)}, u32[]{:S(2)}) collective-permute-start(bf16[64,3072]{1,0:T(8,128)(2,1)S(1)} %add.249), channel_id=1, source_target_pairs={{2,1},{3,2},{6,5},{7,6},{10,9},{11,10},{14,13},{15,14},{18,17},{19... | collective-permute-start | bytes 1179656 | tf_op jit(solution)/shard_map/ppermute | solution.py:440
  241.7 14.4 %collective-permute-start.55 = (bf16[64,3072]{1,0:T(8,128)(2,1)S(1)}, bf16[64,3072]{1,0:T(8,128)(2,1)S(1)}, u32[]{:S(2)}, u32[]{:S(2)}) collective-permute-start(bf16[64,3072]{1,0:T(8,128)(2,1)S(1)} %add.240), channel_id=1, source_target_pairs={{0,1},{1,2},{4,5},{5,6},{8,9},{9,10},{12,13},{13,14},{16,17},{17,1... | collective-permute-start | bytes 1179656 | tf_op jit(solution)/shard_map/ppermute | solution.py:439
  249.0 15.5 %collective-permute-start.63 = (bf16[64,3072]{1,0:T(8,128)(2,1)S(1)}, bf16[64,3072]{1,0:T(8,128)(2,1)S(1)}, u32[]{:S(2)}, u32[]{:S(2)}) collective-permute-start(bf16[64,3072]{1,0:T(8,128)(2,1)S(1)} %add.251), channel_id=1, source_target_pairs={{1,0},{2,1},{3,2},{5,4},{6,5},{7,6},{9,8},{10,9},{11,10},{13,12},{... | collective-permute-start | bytes 1179656 | tf_op jit(solution)/shard_map/ppermute | solution.py:440
  250.6 13.9 %collective-permute-start.62 = (bf16[64,3072]{1,0:T(8,128)(2,1)S(1)}, bf16[64,3072]{1,0:T(8,128)(2,1)S(1)}, u32[]{:S(2)}, u32[]{:S(2)}) collective-permute-start(bf16[64,3072]{1,0:T(8,128)(2,1)S(1)} %add.250), channel_id=1, source_target_pairs={{0,1},{1,2},{2,3},{4,5},{5,6},{6,7},{8,9},{9,10},{10,11},{12,13},{... | collective-permute-start | bytes 1179656 | tf_op jit(solution)/shard_map/ppermute | solution.py:439
  (50 other events, 565.8 us)

commit v9 on v8

--- a/solution.py
+++ b/solution.py
@@ -417,7 +417,7 @@
     def lefts(count):
         return [(i, i - 1) for i in range(shards - count, shards)]
 
-    def reduce_line(pieces_terms):
+    def reduce_line(pieces_terms, merged=False):
         if not line:
             by_shard = [jnp.take(jnp.stack(terms), shard_of, axis=0).reshape(-1, terms[0].shape[1]) for terms in pieces_terms]
             return [
@@ -427,12 +427,14 @@
         marks = []
         for s in range(1, shards):
             for c, terms in enumerate(pieces_terms):
-                if s == 1:
+                if s == 1 and merged:
                     sent = jnp.where(me == 0, terms[1], terms[shards - 1])
                     arrived = lax.ppermute(sent, "tp", [(0, 1), (shards - 1, shards - 2)])
                     got[c] = (arrived, arrived)
                     continue
-                if s == 2:
+                if s == 1:
+                    to_right, to_left = terms[s], terms[shards - s]
+                elif s == 2 and merged:
                     to_right = to_left = terms[s] + got[c][0]
                 else:
                     to_right, to_left = terms[s] + got[c][0], terms[shards - s] + got[c][1]
@@ -588,7 +590,7 @@
     if halves > 1:
         asked.append(shift(packed[1]))
         terms, asked[1] = lax.optimization_barrier((terms, asked[1]))
-    totals, marks = reduce_line(terms)
+    totals, marks = reduce_line(terms, True)
     if line:
         hidden_in, order, _ = lax.optimization_barrier((hidden_in, order, marks[0]))
     hidden = reorder(hidden_in)

time: 279 us -> 278 us (level)
  the two profiles are of different devices: /device:TPU:0 before, /device:TPU:22 now
where the time goes in v9:
time: 278 us; the launch traced here: 275 us
  starting transfers between devices  103 us (37%)
  Pallas kernels  73.9 us (27%)
  waiting for transfers between devices  70.5 us (25%)
  other arithmetic  13.5 us (5%)
  local copies, waits for them, and re-layouts  6.23 us (2%)
  matrix products  5.24 us (2%)
    pallas_call x2, Pallas kernels, attend(): pl.pallas_call(kernel, grid_spec=pltpu.PrefetchScalarGridSpec(num_scalar_...  35.3 us
    pallas_call x1, Pallas kernels, expert_rows(): pl.pallas_call(functools.partial(expert_kernel, [len(source) for source i...  33.9 us
    ppermute x10, starting transfers between devices, reduce_line(): left = lax.ppermute(to_left, 'tp', lefts(s))  32.7 us
    ppermute x10, starting transfers between devices, reduce_line(): right = lax.ppermute(to_right, 'tp', rights(s))  18.7 us
    ppermute x9, waiting for transfers between devices, shift(): lax.ppermute(parts[s], 'tp', moves[s])  17.7 us
    ppermute x10, waiting for transfers between devices, reduce_line(): left = lax.ppermute(to_left, 'tp', lefts(s))  17.6 us
    ppermute x4, starting transfers between devices, gather_line(): lax.ppermute(right, 'tp', to_right)  17.4 us
    ppermute x2, waiting for transfers between devices, reduce_line(): arrived = lax.ppermute(sent, 'tp', [(0, 1), (shards - 1, shards - 2)])  13 us
  transfers between devices with their start and end apart: 46, of which 22 were waited for; matrix products, arithmetic and copies ran while one was open for 6% of the time, Pallas kernels for 26%

profile of v9, /device:TPU:22, one launch (start us, length us, event | category | flops | bytes accessed | tf_op | source)
XLA Modules:
  0.0 275.1 jit_solution(2663841682929405054)
XLA Ops:
  6.8 8.0 %collective-permute-done.22 = bf16[128,512]{1,0:T(8,128)(2,1)S(1)} collective-permute-done((bf16[128,512]{1,0:T(8,128)(2,1)}, bf16[128,512]{1,0:T(8,128)(2,1)S(1)}, u32[]{:S(2)}, u32[]{:S(2)}) %collective-permute-start.22) | collective-permute-done | bytes 131104 | tf_op jit(solution)/shard_map/ppermute | solution.py:407
  16.7 2.7 shard_map.132
  19.4 2.6 collective-permute-start.26
  23.6 3.8 %collective-permute-done.26.refs_2_ = bf16[64,1024]{1,0:T(8,128)(2,1)S(1)} collective-permute-done((bf16[64,1024]{1,0:T(8,128)(2,1)}, bf16[64,1024]{1,0:T(8,128)(2,1)S(1)}, u32[]{:S(2)}, u32[]{:S(2)}) %collective-permute-start.26) | collective-permute-done | bytes 131104 | tf_op jit(solution)/shard_map/ppermute | solution.py:407
  27.4 3.4 %collective-permute-done.27.refs_4_ = bf16[64,1024]{1,0:T(8,128)(2,1)S(1)} collective-permute-done((bf16[64,1024]{1,0:T(8,128)(2,1)}, bf16[64,1024]{1,0:T(8,128)(2,1)S(1)}, u32[]{:S(2)}, u32[]{:S(2)}) %collective-permute-start.27) | collective-permute-done | bytes 131104 | tf_op jit(solution)/shard_map/ppermute | solution.py:407
  32.7 2.8 %collective-permute-start.31 = (bf16[64,1024]{1,0:T(8,128)(2,1)}, bf16[64,1024]{1,0:T(8,128)(2,1)}, u32[]{:S(2)}, u32[]{:S(2)}) collective-permute-start(bf16[64,1024]{1,0:T(8,128)(2,1)} %get-tuple-element.184), channel_id=1, source_target_pairs={{0,1},{1,2},{2,3},{3,0},{4,5},{5,6},{6,7},{7,4},{8,9},{9,10},{10,1... | collective-permute-start | bytes 393224 | tf_op jit(solution)/shard_map/ppermute | solution.py:407
  38.6 17.6 %shard_map.133 = (bf16[64,3072]{1,0:T(8,128)(2,1)S(1)}, bf16[64,3072]{1,0:T(8,128)(2,1)S(1)}, bf16[64,3072]{1,0:T(8,128)(2,1)S(1)}, bf16[64,3072]{1,0:T(8,128)(2...) custom-call(s32[4]{0:T(128)S(1)} %copy-done.15, ...), custom_call_target="tpu_custom_call" | custom-call | flops 21474836480 | bytes 15728640 | tf_op jit(solution)/shard_map/pallas_call | solution.py:168
  59.0 11.3 %collective-permute-done.39 = bf16[64,3072]{1,0:T(8,128)(2,1)S(1)} collective-permute-done((bf16[64,3072]{1,0:T(8,128)(2,1)S(1)}, bf16[64,3072]{1,0:T(8,128)(2,1)S(1)}, u32[]{:S(2)}, u32[]{:S(2)}) %collective-permute-start.39) | collective-permute-done | bytes 393248 | tf_op jit(solution)/shard_map/ppermute | solution.py:432
  72.4 4.6 %collective-permute-start.41 = (bf16[64,3072]{1,0:T(8,128)(2,1)}, bf16[64,3072]{1,0:T(8,128)(2,1)}, u32[]{:S(2)}, u32[]{:S(2)}) collective-permute-start(bf16[64,3072]{1,0:T(8,128)(2,1)} %add.230), channel_id=1, source_target_pairs={{2,1},{3,2},{6,5},{7,6},{10,9},{11,10},{14,13},{15,14},{18,17},{19... | collective-permute-start | bytes 1179656 | tf_op jit(solution)/shard_map/ppermute | solution.py:442
  80.8 4.6 %collective-permute-start.36 = (bf16[64,3072]{1,0:T(8,128)(2,1)}, bf16[64,3072]{1,0:T(8,128)(2,1)}, u32[]{:S(2)}, u32[]{:S(2)}) collective-permute-start(bf16[64,3072]{1,0:T(8,128)(2,1)} %add.224), channel_id=1, source_target_pairs={{2,1},{3,2},{6,5},{7,6},{10,9},{11,10},{14,13},{15,14},{18,17},{19... | collective-permute-start | bytes 1179656 | tf_op jit(solution)/shard_map/ppermute | solution.py:442
  88.4 3.8 %collective-permute-start.43 = (bf16[64,3072]{1,0:T(8,128)(2,1)S(1)}, bf16[64,3072]{1,0:T(8,128)(2,1)S(1)}, u32[]{:S(2)}, u32[]{:S(2)}) collective-permute-start(bf16[64,3072]{1,0:T(8,128)(2,1)S(1)} %add.232), channel_id=1, source_target_pairs={{1,0},{2,1},{3,2},{5,4},{6,5},{7,6},{9,8},{10,9},{11,10},{13,12},{... | collective-permute-start | bytes 1179656 | tf_op jit(solution)/shard_map/ppermute | solution.py:442
  96.7 4.1 %collective-permute-start.38 = (bf16[64,3072]{1,0:T(8,128)(2,1)S(1)}, bf16[64,3072]{1,0:T(8,128)(2,1)S(1)}, u32[]{:S(2)}, u32[]{:S(2)}) collective-permute-start(bf16[64,3072]{1,0:T(8,128)(2,1)S(1)} %add.226), channel_id=1, source_target_pairs={{1,0},{2,1},{3,2},{5,4},{6,5},{7,6},{9,8},{10,9},{11,10},{13,12},{... | collective-permute-start | bytes 1179656 | tf_op jit(solution)/shard_map/ppermute | solution.py:442
  104.0 3.1 %collective-permute-done.42 = bf16[64,3072]{1,0:T(8,128)(2,1)S(1)} collective-permute-done((bf16[64,3072]{1,0:T(8,128)(2,1)S(1)}, bf16[64,3072]{1,0:T(8,128)(2,1)S(1)}, u32[]{:S(2)}, u32[]{:S(2)}) %collective-permute-start.42) | collective-permute-done | bytes 393248 | tf_op jit(solution)/shard_map/ppermute | solution.py:441
  108.8 2.8 %collective-permute-done.37 = bf16[64,3072]{1,0:T(8,128)(2,1)S(1)} collective-permute-done((bf16[64,3072]{1,0:T(8,128)(2,1)S(1)}, bf16[64,3072]{1,0:T(8,128)(2,1)S(1)}, u32[]{:S(2)}, u32[]{:S(2)}) %collective-permute-start.37) | collective-permute-done | bytes 393248 | tf_op jit(solution)/shard_map/ppermute | solution.py:441
  114.6 3.9 %collective-permute-start.45 = (bf16[64,6144]{1,0:T(8,128)(2,1)S(1)}, bf16[64,6144]{1,0:T(8,128)(2,1)S(1)}, u32[]{:S(2)}, u32[]{:S(2)}) collective-permute-start(bf16[64,6144]{1,0:T(8,128)(2,1)S(1)} %fusion.7.refs_1_), channel_id=1, source_target_pairs={{1,0},{2,1},{3,2},{5,4},{6,5},{7,6},{9,8},{10,9},{11,10},{13,12},{... | collective-permute-start | bytes 2359304 | tf_op jit(solution)/shard_map/ppermute | solution.py:455
  118.5 17.6 %shard_map.134 = (bf16[64,3072]{1,0:T(8,128)(2,1)S(1)}, bf16[64,3072]{1,0:T(8,128)(2,1)S(1)}, bf16[64,3072]{1,0:T(8,128)(2,1)S(1)}, bf16[64,3072]{1,0:T(8,128)(2...) custom-call(s32[4]{0:T(128)S(1)} %copy-done.15, ...), custom_call_target="tpu_custom_call" | custom-call | flops 21474836480 | bytes 15728640 | tf_op jit(solution)/shard_map/pallas_call | solution.py:168
  138.5 4.6 %collective-permute-start.46 = (bf16[64,3072]{1,0:T(8,128)(2,1)S(1)}, bf16[64,3072]{1,0:T(8,128)(2,1)}, u32[]{:S(2)}, u32[]{:S(2)}) collective-permute-start(bf16[64,3072]{1,0:T(8,128)(2,1)S(1)} %get-tuple-element.296.refs_2_), channel_id=1, source_target_pairs={{0,1},{1,2},{2,3},{4,5},{5,6},{6,7},{8,9},{9,10},{10,11},{12,13},{... | collective-permute-start | bytes 1179656 | tf_op jit(solution)/shard_map/ppermute | solution.py:476
  143.1 2.2 collective-permute-start.49
  145.3 3.9 %collective-permute-start.48 = (bf16[64,3072]{1,0:T(8,128)(2,1)S(1)}, bf16[64,3072]{1,0:T(8,128)(2,1)S(1)}, u32[]{:S(2)}, u32[]{:S(2)}) collective-permute-start(bf16[64,3072]{1,0:T(8,128)(2,1)S(1)} %get-tuple-element.295.refs_3_), channel_id=1, source_target_pairs={{0,1},{1,2},{2,3},{4,5},{5,6},{6,7},{8,9},{9,10},{10,11},{12,13},{... | collective-permute-start | bytes 1179656 | tf_op jit(solution)/shard_map/ppermute | solution.py:476
  149.3 3.3 %collective-permute-done.46 = bf16[64,3072]{1,0:T(8,128)(2,1)} collective-permute-done((bf16[64,3072]{1,0:T(8,128)(2,1)S(1)}, bf16[64,3072]{1,0:T(8,128)(2,1)}, u32[]{:S(2)}, u32[]{:S(2)}) %collective-permute-start.46) | collective-permute-done | bytes 393248 | tf_op jit(solution)/shard_map/ppermute | solution.py:476
  154.0 4.5 %collective-permute-start.50 = (bf16[64,3072]{1,0:T(8,128)(2,1)S(1)}, bf16[64,3072]{1,0:T(8,128)(2,1)S(1)}, u32[]{:S(2)}, u32[]{:S(2)}) collective-permute-start(bf16[64,3072]{1,0:T(8,128)(2,1)S(1)} %get-tuple-element.304.refs_4_), channel_id=1, source_target_pairs={{0,1},{1,2},{2,3},{4,5},{5,6},{6,7},{8,9},{9,10},{10,11},{12,13},{... | collective-permute-start | bytes 1179656 | tf_op jit(solution)/shard_map/ppermute | solution.py:476
  161.1 4.4 %collective-permute-start.52 = (bf16[64,3072]{1,0:T(8,128)(2,1)S(1)}, bf16[64,3072]{1,0:T(8,128)(2,1)S(1)}, u32[]{:S(2)}, u32[]{:S(2)}) collective-permute-start(bf16[64,3072]{1,0:T(8,128)(2,1)S(1)} %get-tuple-element.302.refs_5_), channel_id=1, source_target_pairs={{0,1},{1,2},{2,3},{4,5},{5,6},{6,7},{8,9},{9,10},{10,11},{12,13},{... | collective-permute-start | bytes 1179656 | tf_op jit(solution)/shard_map/ppermute | solution.py:476
  168.3 5.0 %collective-permute-done.52.refs_7_ = bf16[64,3072]{1,0:T(8,128)(2,1)S(1)} collective-permute-done((bf16[64,3072]{1,0:T(8,128)(2,1)S(1)}, bf16[64,3072]{1,0:T(8,128)(2,1)S(1)}, u32[]{:S(2)}, u32[]{:S(2)}) %collective-permute-start.52) | collective-permute-done | bytes 393248 | tf_op jit(solution)/shard_map/ppermute | solution.py:476
  173.3 4.4 %collective-permute-done.53.refs_13_ = bf16[64,3072]{1,0:T(8,128)(2,1)S(1)} collective-permute-done((bf16[64,3072]{1,0:T(8,128)(2,1)S(1)}, bf16[64,3072]{1,0:T(8,128)(2,1)S(1)}, u32[]{:S(2)}, u32[]{:S(2)}) %collective-permute-start.53) | collective-permute-done | bytes 393248 | tf_op jit(solution)/shard_map/ppermute | solution.py:476
  180.0 3.9 %collective-permute-start.55 = (bf16[64,6144]{1,0:T(8,128)(2,1)S(1)}, bf16[64,6144]{1,0:T(8,128)(2,1)S(1)}, u32[]{:S(2)}, u32[]{:S(2)}) collective-permute-start(bf16[64,6144]{1,0:T(8,128)(2,1)S(1)} %pad_maximum_fusion.3), channel_id=1, source_target_pairs={{1,0},{2,1},{3,2},{5,4},{6,5},{7,6},{9,8},{10,9},{11,10},{13,12},{... | collective-permute-start | bytes 2359304 | tf_op jit(solution)/shard_map/ppermute | solution.py:486
  184.0 33.9 %shard_map.135 = (bf16[256,3072]{1,0:T(8,128)(2,1)S(1)}, bf16[256,3072]{1,0:T(8,128)(2,1)S(1)}) custom-call(s32[1]{0:T(128)} %bitcast.6.mine.refs_0_, bf16[64,6144]{1,0:T(8,128)(2,1)S(1)} %fusion.7.refs_1_, bf16[64,3072]{1,0:T(8,128)(2,1)S(1)} %get-tuple-element.296.refs_2_, bf16[64,3072]{1,0:T(8,128)(2,1)S(1)} %get-tuple-element.295.refs_3_, ...), custom_call_target="tpu_custom_call" | custom-call | flops 19327352832 | bytes 75497472 | tf_op jit(solution)/shard_map/pallas_call | solution.py:263
  225.4 10.1 %collective-permute-done.63 = bf16[64,3072]{1,0:T(8,128)(2,1)} collective-permute-done((bf16[64,3072]{1,0:T(8,128)(2,1)S(1)}, bf16[64,3072]{1,0:T(8,128)(2,1)}, u32[]{:S(2)}, u32[]{:S(2)}) %collective-permute-start.63) | collective-permute-done | bytes 393248 | tf_op jit(solution)/shard_map/ppermute | solution.py:442
  238.0 4.6 %collective-permute-start.65 = (bf16[64,3072]{1,0:T(8,128)(2,1)S(1)}, bf16[64,3072]{1,0:T(8,128)(2,1)S(1)}, u32[]{:S(2)}, u32[]{:S(2)}) collective-permute-start(bf16[64,3072]{1,0:T(8,128)(2,1)S(1)} %get-tuple-element.299), channel_id=1, source_target_pairs={{2,1},{3,2},{6,5},{7,6},{10,9},{11,10},{14,13},{15,14},{18,17},{19... | collective-permute-start | bytes 1179656 | tf_op jit(solution)/shard_map/ppermute | solution.py:442
  245.2 4.6 %collective-permute-start.59 = (bf16[64,3072]{1,0:T(8,128)(2,1)S(1)}, bf16[64,3072]{1,0:T(8,128)(2,1)S(1)}, u32[]{:S(2)}, u32[]{:S(2)}) collective-permute-start(bf16[64,3072]{1,0:T(8,128)(2,1)S(1)} %get-tuple-element.297), channel_id=1, source_target_pairs={{2,1},{3,2},{6,5},{7,6},{10,9},{11,10},{14,13},{15,14},{18,17},{19... | collective-permute-start | bytes 1179656 | tf_op jit(solution)/shard_map/ppermute | solution.py:442
  249.9 2.3 collective-permute-done.65
  255.5 3.9 %collective-permute-start.66 = (bf16[64,3072]{1,0:T(8,128)(2,1)S(1)}, bf16[64,3072]{1,0:T(8,128)(2,1)S(1)}, u32[]{:S(2)}, u32[]{:S(2)}) collective-permute-start(bf16[64,3072]{1,0:T(8,128)(2,1)S(1)} %add.264), channel_id=1, source_target_pairs={{0,1},{1,2},{2,3},{4,5},{5,6},{6,7},{8,9},{9,10},{10,11},{12,13},{... | collective-permute-start | bytes 1179656 | tf_op jit(solution)/shard_map/ppermute | solution.py:441
  261.7 4.1 %collective-permute-start.60 = (bf16[64,3072]{1,0:T(8,128)(2,1)S(1)}, bf16[64,3072]{1,0:T(8,128)(2,1)S(1)}, u32[]{:S(2)}, u32[]{:S(2)}) collective-permute-start(bf16[64,3072]{1,0:T(8,128)(2,1)S(1)} %add.254), channel_id=1, source_target_pairs={{0,1},{1,2},{2,3},{4,5},{5,6},{6,7},{8,9},{9,10},{10,11},{12,13},{... | collective-permute-start | bytes 1179656 | tf_op jit(solution)/shard_map/ppermute | solution.py:441
  (188 shorter events, 76.3 us)
Async XLA Ops:
  2.7 12.2 %collective-permute-start.22 = (bf16[128,512]{1,0:T(8,128)(2,1)}, bf16[128,512]{1,0:T(8,128)(2,1)S(1)}, u32[]{:S(2)}, u32[]{:S(2)}) collective-permute-start(bf16[128,512]{1,0:T(8,128)(2,1)} %get-tuple-element.160), channel_id=1, source_target_pairs={{0,1},{1,2},{2,3},{3,0},{4,5},{5,6},{6,7},{7,4},{8,9},{9,10},{10,1... | collective-permute-start | bytes 393224 | tf_op jit(solution)/shard_map/ppermute | solution.py:407
  15.5 17.2 %collective-permute-start.25 = (bf16[512,512]{1,0:T(8,128)(2,1)S(1)}, bf16[512,512]{1,0:T(8,128)(2,1)S(1)}, u32[]{:S(2)}, u32[]{:S(2)}) collective-permute-start(bf16[512,512]{1,0:T(8,128)(2,1)S(1)} %constant_dynamic-update-slice_fusion.refs_7_), channel_id=1, source_target_pairs={{0,8},{4,12},{8,0},{12,4},{1,9},{5,13},{9,1},{13,5},{2,10},{6,14},... | collective-permute-start | bytes 1572872 | tf_op jit(solution)/shard_map/ppermute | solution.py:519
  23.6 13.5 %collective-permute-start.29 = (bf16[512,512]{1,0:T(8,128)(2,1)S(1)}, bf16[512,512]{1,0:T(8,128)(2,1)S(1)}, u32[]{:S(2)}, u32[]{:S(2)}) collective-permute-start(bf16[512,512]{1,0:T(8,128)(2,1)S(1)} %constant_dynamic-update-slice_fusion.refs_7_), channel_id=1, source_target_pairs={{0,4},{4,0},{8,12},{12,8},{1,5},{5,1},{9,13},{13,9},{2,6},{6,2},{1... | collective-permute-start | bytes 1572872 | tf_op jit(solution)/shard_map/ppermute | solution.py:519
  32.7 23.5 %collective-permute-start.31 = (bf16[64,1024]{1,0:T(8,128)(2,1)}, bf16[64,1024]{1,0:T(8,128)(2,1)}, u32[]{:S(2)}, u32[]{:S(2)}) collective-permute-start(bf16[64,1024]{1,0:T(8,128)(2,1)} %get-tuple-element.184), channel_id=1, source_target_pairs={{0,1},{1,2},{2,3},{3,0},{4,5},{5,6},{6,7},{7,4},{8,9},{9,10},{10,1... | collective-permute-start | bytes 393224 | tf_op jit(solution)/shard_map/ppermute | solution.py:407
  35.5 20.8 %collective-permute-start.32 = (bf16[64,1024]{1,0:T(8,128)(2,1)}, bf16[64,1024]{1,0:T(8,128)(2,1)}, u32[]{:S(2)}, u32[]{:S(2)}) collective-permute-start(bf16[64,1024]{1,0:T(8,128)(2,1)} %get-tuple-element.185), channel_id=1, source_target_pairs={{0,2},{1,3},{2,0},{3,1},{4,6},{5,7},{6,4},{7,5},{8,10},{9,11},{10,... | collective-permute-start | bytes 393224 | tf_op jit(solution)/shard_map/ppermute | solution.py:407
  36.7 19.6 %collective-permute-start.33 = (bf16[64,1024]{1,0:T(8,128)(2,1)}, bf16[64,1024]{1,0:T(8,128)(2,1)}, u32[]{:S(2)}, u32[]{:S(2)}) collective-permute-start(bf16[64,1024]{1,0:T(8,128)(2,1)} %get-tuple-element.186), channel_id=1, source_target_pairs={{0,3},{1,0},{2,1},{3,2},{4,7},{5,4},{6,5},{7,6},{8,11},{9,8},{10,9... | collective-permute-start | bytes 393224 | tf_op jit(solution)/shard_map/ppermute | solution.py:407
  56.3 13.9 %collective-permute-start.39 = (bf16[64,3072]{1,0:T(8,128)(2,1)S(1)}, bf16[64,3072]{1,0:T(8,128)(2,1)S(1)}, u32[]{:S(2)}, u32[]{:S(2)}) collective-permute-start(bf16[64,3072]{1,0:T(8,128)(2,1)S(1)} %broadcast_select_fusion), channel_id=1, source_target_pairs={{0,1},{3,2},{4,5},{7,6},{8,9},{11,10},{12,13},{15,14},{16,17},{19,... | collective-permute-start | bytes 1179656 | tf_op jit(solution)/shard_map/ppermute | solution.py:432
  57.7 21.0 %collective-permute-start.34 = (bf16[64,3072]{1,0:T(8,128)(2,1)S(1)}, bf16[64,3072]{1,0:T(8,128)(2,1)S(1)}, u32[]{:S(2)}, u32[]{:S(2)}) collective-permute-start(bf16[64,3072]{1,0:T(8,128)(2,1)S(1)} %broadcast_select_fusion.1), channel_id=1, source_target_pairs={{0,1},{3,2},{4,5},{7,6},{8,9},{11,10},{12,13},{15,14},{16,17},{19,... | collective-permute-start | bytes 1179656 | tf_op jit(solution)/shard_map/ppermute | solution.py:432
  71.1 15.6 %collective-permute-start.40 = (bf16[64,3072]{1,0:T(8,128)(2,1)}, bf16[64,3072]{1,0:T(8,128)(2,1)}, u32[]{:S(2)}, u32[]{:S(2)}) collective-permute-start(bf16[64,3072]{1,0:T(8,128)(2,1)} %add.230), channel_id=1, source_target_pairs={{0,1},{1,2},{4,5},{5,6},{8,9},{9,10},{12,13},{13,14},{16,17},{17,1... | collective-permute-start | bytes 1179656 | tf_op jit(solution)/shard_map/ppermute | solution.py:441
  72.4 14.8 %collective-permute-start.41 = (bf16[64,3072]{1,0:T(8,128)(2,1)}, bf16[64,3072]{1,0:T(8,128)(2,1)}, u32[]{:S(2)}, u32[]{:S(2)}) collective-permute-start(bf16[64,3072]{1,0:T(8,128)(2,1)} %add.230), channel_id=1, source_target_pairs={{2,1},{3,2},{6,5},{7,6},{10,9},{11,10},{14,13},{15,14},{18,17},{19... | collective-permute-start | bytes 1179656 | tf_op jit(solution)/shard_map/ppermute | solution.py:442
  79.5 15.8 %collective-permute-start.35 = (bf16[64,3072]{1,0:T(8,128)(2,1)}, bf16[64,3072]{1,0:T(8,128)(2,1)}, u32[]{:S(2)}, u32[]{:S(2)}) collective-permute-start(bf16[64,3072]{1,0:T(8,128)(2,1)} %add.224), channel_id=1, source_target_pairs={{0,1},{1,2},{4,5},{5,6},{8,9},{9,10},{12,13},{13,14},{16,17},{17,1... | collective-permute-start | bytes 1179656 | tf_op jit(solution)/shard_map/ppermute | solution.py:441
  80.8 14.8 %collective-permute-start.36 = (bf16[64,3072]{1,0:T(8,128)(2,1)}, bf16[64,3072]{1,0:T(8,128)(2,1)}, u32[]{:S(2)}, u32[]{:S(2)}) collective-permute-start(bf16[64,3072]{1,0:T(8,128)(2,1)} %add.224), channel_id=1, source_target_pairs={{2,1},{3,2},{6,5},{7,6},{10,9},{11,10},{14,13},{15,14},{18,17},{19... | collective-permute-start | bytes 1179656 | tf_op jit(solution)/shard_map/ppermute | solution.py:442
  88.4 15.7 %collective-permute-start.43 = (bf16[64,3072]{1,0:T(8,128)(2,1)S(1)}, bf16[64,3072]{1,0:T(8,128)(2,1)S(1)}, u32[]{:S(2)}, u32[]{:S(2)}) collective-permute-start(bf16[64,3072]{1,0:T(8,128)(2,1)S(1)} %add.232), channel_id=1, source_target_pairs={{1,0},{2,1},{3,2},{5,4},{6,5},{7,6},{9,8},{10,9},{11,10},{13,12},{... | collective-permute-start | bytes 1179656 | tf_op jit(solution)/shard_map/ppermute | solution.py:442
  93.2 13.9 %collective-permute-start.42 = (bf16[64,3072]{1,0:T(8,128)(2,1)S(1)}, bf16[64,3072]{1,0:T(8,128)(2,1)S(1)}, u32[]{:S(2)}, u32[]{:S(2)}) collective-permute-start(bf16[64,3072]{1,0:T(8,128)(2,1)S(1)} %add.231), channel_id=1, source_target_pairs={{0,1},{1,2},{2,3},{4,5},{5,6},{6,7},{8,9},{9,10},{10,11},{12,13},{... | collective-permute-start | bytes 1179656 | tf_op jit(solution)/shard_map/ppermute | solution.py:441
  112.6 23.6 %collective-permute-start.44 = (bf16[64,6144]{1,0:T(8,128)(2,1)S(1)}, bf16[64,6144]{1,0:T(8,128)(2,1)S(1)}, u32[]{:S(2)}, u32[]{:S(2)}) collective-permute-start(bf16[64,6144]{1,0:T(8,128)(2,1)S(1)} %fusion.7.refs_1_), channel_id=1, source_target_pairs={{0,1},{1,2},{2,3},{4,5},{5,6},{6,7},{8,9},{9,10},{10,11},{12,13},{... | collective-permute-start | bytes 2359304 | tf_op jit(solution)/shard_map/ppermute | solution.py:454
  114.6 21.7 %collective-permute-start.45 = (bf16[64,6144]{1,0:T(8,128)(2,1)S(1)}, bf16[64,6144]{1,0:T(8,128)(2,1)S(1)}, u32[]{:S(2)}, u32[]{:S(2)}) collective-permute-start(bf16[64,6144]{1,0:T(8,128)(2,1)S(1)} %fusion.7.refs_1_), channel_id=1, source_target_pairs={{1,0},{2,1},{3,2},{5,4},{6,5},{7,6},{9,8},{10,9},{11,10},{13,12},{... | collective-permute-start | bytes 2359304 | tf_op jit(solution)/shard_map/ppermute | solution.py:455
  136.3 12.9 %collective-permute-start.47 = (bf16[64,3072]{1,0:T(8,128)(2,1)S(1)}, bf16[64,3072]{1,0:T(8,128)(2,1)}, u32[]{:S(2)}, u32[]{:S(2)}) collective-permute-start(bf16[64,3072]{1,0:T(8,128)(2,1)S(1)} %get-tuple-element.294.refs_8_), channel_id=1, source_target_pairs={{1,0},{2,1},{3,2},{5,4},{6,5},{7,6},{9,8},{10,9},{11,10},{13,12},{... | collective-permute-start | bytes 1179656 | tf_op jit(solution)/shard_map/ppermute | solution.py:476
  138.5 14.2 %collective-permute-start.46 = (bf16[64,3072]{1,0:T(8,128)(2,1)S(1)}, bf16[64,3072]{1,0:T(8,128)(2,1)}, u32[]{:S(2)}, u32[]{:S(2)}) collective-permute-start(bf16[64,3072]{1,0:T(8,128)(2,1)S(1)} %get-tuple-element.296.refs_2_), channel_id=1, source_target_pairs={{0,1},{1,2},{2,3},{4,5},{5,6},{6,7},{8,9},{9,10},{10,11},{12,13},{... | collective-permute-start | bytes 1179656 | tf_op jit(solution)/shard_map/ppermute | solution.py:476
  143.1 17.3 %collective-permute-start.49 = (bf16[64,3072]{1,0:T(8,128)(2,1)S(1)}, bf16[64,3072]{1,0:T(8,128)(2,1)S(1)}, u32[]{:S(2)}, u32[]{:S(2)}) collective-permute-start(bf16[64,3072]{1,0:T(8,128)(2,1)S(1)} %get-tuple-element.293.refs_9_), channel_id=1, source_target_pairs={{1,0},{2,1},{3,2},{5,4},{6,5},{7,6},{9,8},{10,9},{11,10},{13,12},{... | collective-permute-start | bytes 1179656 | tf_op jit(solution)/shard_map/ppermute | solution.py:476
  145.3 15.7 %collective-permute-start.48 = (bf16[64,3072]{1,0:T(8,128)(2,1)S(1)}, bf16[64,3072]{1,0:T(8,128)(2,1)S(1)}, u32[]{:S(2)}, u32[]{:S(2)}) collective-permute-start(bf16[64,3072]{1,0:T(8,128)(2,1)S(1)} %get-tuple-element.295.refs_3_), channel_id=1, source_target_pairs={{0,1},{1,2},{2,3},{4,5},{5,6},{6,7},{8,9},{9,10},{10,11},{12,13},{... | collective-permute-start | bytes 1179656 | tf_op jit(solution)/shard_map/ppermute | solution.py:476
  154.0 13.5 %collective-permute-start.50 = (bf16[64,3072]{1,0:T(8,128)(2,1)S(1)}, bf16[64,3072]{1,0:T(8,128)(2,1)S(1)}, u32[]{:S(2)}, u32[]{:S(2)}) collective-permute-start(bf16[64,3072]{1,0:T(8,128)(2,1)S(1)} %get-tuple-element.304.refs_4_), channel_id=1, source_target_pairs={{0,1},{1,2},{2,3},{4,5},{5,6},{6,7},{8,9},{9,10},{10,11},{12,13},{... | collective-permute-start | bytes 1179656 | tf_op jit(solution)/shard_map/ppermute | solution.py:476
  177.8 41.3 %collective-permute-start.54 = (bf16[64,6144]{1,0:T(8,128)(2,1)S(1)}, bf16[64,6144]{1,0:T(8,128)(2,1)S(1)}, u32[]{:S(2)}, u32[]{:S(2)}) collective-permute-start(bf16[64,6144]{1,0:T(8,128)(2,1)S(1)} %pad_maximum_fusion.2), channel_id=1, source_target_pairs={{0,1},{1,2},{2,3},{4,5},{5,6},{6,7},{8,9},{9,10},{10,11},{12,13},{... | collective-permute-start | bytes 2359304 | tf_op jit(solution)/shard_map/ppermute | solution.py:485
  180.0 39.2 %collective-permute-start.55 = (bf16[64,6144]{1,0:T(8,128)(2,1)S(1)}, bf16[64,6144]{1,0:T(8,128)(2,1)S(1)}, u32[]{:S(2)}, u32[]{:S(2)}) collective-permute-start(bf16[64,6144]{1,0:T(8,128)(2,1)S(1)} %pad_maximum_fusion.3), channel_id=1, source_target_pairs={{1,0},{2,1},{3,2},{5,4},{6,5},{7,6},{9,8},{10,9},{11,10},{13,12},{... | collective-permute-start | bytes 2359304 | tf_op jit(solution)/shard_map/ppermute | solution.py:486
  221.5 14.1 %collective-permute-start.63 = (bf16[64,3072]{1,0:T(8,128)(2,1)S(1)}, bf16[64,3072]{1,0:T(8,128)(2,1)}, u32[]{:S(2)}, u32[]{:S(2)}) collective-permute-start(bf16[64,3072]{1,0:T(8,128)(2,1)S(1)} %get-tuple-element.247), channel_id=1, source_target_pairs={{3,2},{7,6},{11,10},{15,14},{19,18},{23,22},{27,26},{31,30}} | collective-permute-start | bytes 1179656 | tf_op jit(solution)/shard_map/ppermute | solution.py:442
  223.4 19.2 %collective-permute-start.56 = (bf16[64,3072]{1,0:T(8,128)(2,1)S(1)}, bf16[64,3072]{1,0:T(8,128)(2,1)S(1)}, u32[]{:S(2)}, u32[]{:S(2)}) collective-permute-start(bf16[64,3072]{1,0:T(8,128)(2,1)S(1)} %get-tuple-element.238), channel_id=1, source_target_pairs={{0,1},{4,5},{8,9},{12,13},{16,17},{20,21},{24,25},{28,29}} | collective-permute-start | bytes 1179656 | tf_op jit(solution)/shard_map/ppermute | solution.py:441
  224.1 19.7 %collective-permute-start.57 = (bf16[64,3072]{1,0:T(8,128)(2,1)S(1)}, bf16[64,3072]{1,0:T(8,128)(2,1)S(1)}, u32[]{:S(2)}, u32[]{:S(2)}) collective-permute-start(bf16[64,3072]{1,0:T(8,128)(2,1)S(1)} %get-tuple-element.236), channel_id=1, source_target_pairs={{3,2},{7,6},{11,10},{15,14},{19,18},{23,22},{27,26},{31,30}} | collective-permute-start | bytes 1179656 | tf_op jit(solution)/shard_map/ppermute | solution.py:442
  236.7 13.2 %collective-permute-start.64 = (bf16[64,3072]{1,0:T(8,128)(2,1)S(1)}, bf16[64,3072]{1,0:T(8,128)(2,1)S(1)}, u32[]{:S(2)}, u32[]{:S(2)}) collective-permute-start(bf16[64,3072]{1,0:T(8,128)(2,1)S(1)} %get-tuple-element.300), channel_id=1, source_target_pairs={{0,1},{1,2},{4,5},{5,6},{8,9},{9,10},{12,13},{13,14},{16,17},{17,1... | collective-permute-start | bytes 1179656 | tf_op jit(solution)/shard_map/ppermute | solution.py:441
  238.0 14.3 %collective-permute-start.65 = (bf16[64,3072]{1,0:T(8,128)(2,1)S(1)}, bf16[64,3072]{1,0:T(8,128)(2,1)S(1)}, u32[]{:S(2)}, u32[]{:S(2)}) collective-permute-start(bf16[64,3072]{1,0:T(8,128)(2,1)S(1)} %get-tuple-element.299), channel_id=1, source_target_pairs={{2,1},{3,2},{6,5},{7,6},{10,9},{11,10},{14,13},{15,14},{18,17},{19... | collective-permute-start | bytes 1179656 | tf_op jit(solution)/shard_map/ppermute | solution.py:442
  243.9 15.6 %collective-permute-start.58 = (bf16[64,3072]{1,0:T(8,128)(2,1)S(1)}, bf16[64,3072]{1,0:T(8,128)(2,1)S(1)}, u32[]{:S(2)}, u32[]{:S(2)}) collective-permute-start(bf16[64,3072]{1,0:T(8,128)(2,1)S(1)} %get-tuple-element.298), channel_id=1, source_target_pairs={{0,1},{1,2},{4,5},{5,6},{8,9},{9,10},{12,13},{13,14},{16,17},{17,1... | collective-permute-start | bytes 1179656 | tf_op jit(solution)/shard_map/ppermute | solution.py:441
  245.2 14.3 %collective-permute-start.59 = (bf16[64,3072]{1,0:T(8,128)(2,1)S(1)}, bf16[64,3072]{1,0:T(8,128)(2,1)S(1)}, u32[]{:S(2)}, u32[]{:S(2)}) collective-permute-start(bf16[64,3072]{1,0:T(8,128)(2,1)S(1)} %get-tuple-element.297), channel_id=1, source_target_pairs={{2,1},{3,2},{6,5},{7,6},{10,9},{11,10},{14,13},{15,14},{18,17},{19... | collective-permute-start | bytes 1179656 | tf_op jit(solution)/shard_map/ppermute | solution.py:442
  253.4 14.5 %collective-permute-start.67 = (bf16[64,3072]{1,0:T(8,128)(2,1)S(1)}, bf16[64,3072]{1,0:T(8,128)(2,1)S(1)}, u32[]{:S(2)}, u32[]{:S(2)}) collective-permute-start(bf16[64,3072]{1,0:T(8,128)(2,1)S(1)} %add.265), channel_id=1, source_target_pairs={{1,0},{2,1},{3,2},{5,4},{6,5},{7,6},{9,8},{10,9},{11,10},{13,12},{... | collective-permute-start | bytes 1179656 | tf_op jit(solution)/shard_map/ppermute | solution.py:442
  255.5 12.4 %collective-permute-start.66 = (bf16[64,3072]{1,0:T(8,128)(2,1)S(1)}, bf16[64,3072]{1,0:T(8,128)(2,1)S(1)}, u32[]{:S(2)}, u32[]{:S(2)}) collective-permute-start(bf16[64,3072]{1,0:T(8,128)(2,1)S(1)} %add.264), channel_id=1, source_target_pairs={{0,1},{1,2},{2,3},{4,5},{5,6},{6,7},{8,9},{9,10},{10,11},{12,13},{... | collective-permute-start | bytes 1179656 | tf_op jit(solution)/shard_map/ppermute | solution.py:441
  (51 other events, 546.0 us)

commit v10 on v9

--- a/solution.py
+++ b/solution.py
@@ -417,7 +417,7 @@
     def lefts(count):
         return [(i, i - 1) for i in range(shards - count, shards)]
 
-    def reduce_line(pieces_terms, merged=False):
+    def reduce_line(pieces_terms, merged=False, beside=None):
         if not line:
             by_shard = [jnp.take(jnp.stack(terms), shard_of, axis=0).reshape(-1, terms[0].shape[1]) for terms in pieces_terms]
             return [
@@ -442,6 +442,9 @@
                 left = lax.ppermute(to_left, "tp", lefts(s))
                 got[c] = lax.optimization_barrier((right, left))
             marks.append(got[0])
+            if s == 1 and beside is not None:
+                got[0], beside = lax.optimization_barrier((got[0], beside))
+        marks.append(beside)
         return [
             terms[0].astype(jnp.float32) + right.astype(jnp.float32) + left.astype(jnp.float32)
             for terms, (right, left) in zip(pieces_terms, got)
@@ -590,10 +593,12 @@
     if halves > 1:
         asked.append(shift(packed[1]))
         terms, asked[1] = lax.optimization_barrier((terms, asked[1]))
-    totals, marks = reduce_line(terms, True)
     if line:
-        hidden_in, order, _ = lax.optimization_barrier((hidden_in, order, marks[0]))
+        hidden_in, order, terms = lax.optimization_barrier((hidden_in, order, terms))
     hidden = reorder(hidden_in)
+    totals, marks = reduce_line(terms, True, hidden if line else None)
+    if line:
+        hidden = marks[-1]
     my_routes = lax.dynamic_slice_in_dim(routes, me * rows, rows, 0).astype(jnp.bfloat16)
     my_routes = reorder(my_routes).astype(jnp.int32)
     first_half = finish(0, totals)
@@ -602,8 +607,8 @@
         return (restore([first_half]), restore([expert(0, normed, gather_line(normed)[0])[0]]))
     asked[1], _ = lax.optimization_barrier((asked[1], normed))
     sources, second_sum = gather_line(normed, project(1))
+    part, second_sum = expert(0, normed, sources, second_sum)
     second_half = (hidden[half:].astype(jnp.float32) + second_sum).astype(jnp.bfloat16)
-    part, second_half = expert(0, normed, sources, second_half)
     part, late = lax.optimization_barrier((part, second_half))
     late = lax.cond(crowded[0] > 0, late_expert, jnp.zeros_like, late)
     return (restore([first_half, second_half]), restore([part, late]))

time: 278 us -> 282 us (1.014)
  the two profiles are of different devices: /device:TPU:22 before, /device:TPU:0 now
where the time goes in v10:
time: 282 us; the launch traced here: 277 us
  starting transfers between devices  115 us (41%)
  Pallas kernels  75.3 us (27%)
  waiting for transfers between devices  57.5 us (20%)
  other arithmetic  14.4 us (5%)
  local copies, waits for them, and re-layouts  6.55 us (2%)
  matrix products  5.64 us (2%)
    ppermute x10, starting transfers between devices, reduce_line(): right = lax.ppermute(to_right, 'tp', rights(s))  45.2 us
    pallas_call x1, Pallas kernels, expert_rows(): pl.pallas_call(functools.partial(expert_kernel, [len(source) for source i...  35.3 us
    pallas_call x2, Pallas kernels, attend(): pl.pallas_call(kernel, grid_spec=pltpu.PrefetchScalarGridSpec(num_scalar_...  35.3 us
    ppermute x4, starting transfers between devices, gather_line(): lax.ppermute(right, 'tp', to_right)  20.1 us
    ppermute x9, starting transfers between devices, shift(): lax.ppermute(parts[s], 'tp', moves[s])  18.5 us
    ppermute x10, waiting for transfers between devices, reduce_line(): right = lax.ppermute(to_right, 'tp', rights(s))  16.6 us
    ppermute x9, waiting for transfers between devices, shift(): lax.ppermute(parts[s], 'tp', moves[s])  14.1 us
    ppermute x10, starting transfers between devices, reduce_line(): left = lax.ppermute(to_left, 'tp', lefts(s))  11.1 us
  transfers between devices with their start and end apart: 46, of which 18 were waited for; matrix products, arithmetic and copies ran while one was open for 6% of the time, Pallas kernels for 26%

profile of v10, /device:TPU:0, one launch (start us, length us, event | category | flops | bytes accessed | tf_op | source)
XLA Modules:
  0.0 276.9 jit_solution(15728378431857558262)
XLA Ops:
  2.7 3.0 %collective-permute-start.22 = (bf16[128,512]{1,0:T(8,128)(2,1)}, bf16[128,512]{1,0:T(8,128)(2,1)S(1)}, u32[]{:S(2)}, u32[]{:S(2)}) collective-permute-start(bf16[128,512]{1,0:T(8,128)(2,1)} %get-tuple-element.170), channel_id=1, source_target_pairs={{0,1},{1,2},{2,3},{3,0},{4,5},{5,6},{6,7},{7,4},{8,9},{9,10},{10,1... | collective-permute-start | bytes 393224 | tf_op jit(solution)/shard_map/ppermute | solution.py:407
  5.7 2.6 collective-permute-start.23
  12.4 4.8 %collective-permute-done.23 = bf16[128,512]{1,0:T(8,128)(2,1)S(1)} collective-permute-done((bf16[128,512]{1,0:T(8,128)(2,1)}, bf16[128,512]{1,0:T(8,128)(2,1)S(1)}, u32[]{:S(2)}, u32[]{:S(2)}) %collective-permute-start.23) | collective-permute-done | bytes 131104 | tf_op jit(solution)/shard_map/ppermute | solution.py:407
  19.3 2.7 shard_map.132
  22.1 3.3 %collective-permute-start.26 = (bf16[64,1024]{1,0:T(8,128)(2,1)}, bf16[64,1024]{1,0:T(8,128)(2,1)S(1)}, u32[]{:S(2)}, u32[]{:S(2)}) collective-permute-start(bf16[64,1024]{1,0:T(8,128)(2,1)} %get-tuple-element.176), channel_id=1, source_target_pairs={{0,1},{1,2},{2,3},{3,0},{4,5},{5,6},{6,7},{7,4},{8,9},{9,10},{10,1... | collective-permute-start | bytes 393224 | tf_op jit(solution)/shard_map/ppermute | solution.py:407
  27.8 3.2 %collective-permute-done.26.refs_2_ = bf16[64,1024]{1,0:T(8,128)(2,1)S(1)} collective-permute-done((bf16[64,1024]{1,0:T(8,128)(2,1)}, bf16[64,1024]{1,0:T(8,128)(2,1)S(1)}, u32[]{:S(2)}, u32[]{:S(2)}) %collective-permute-start.26) | collective-permute-done | bytes 131104 | tf_op jit(solution)/shard_map/ppermute | solution.py:407
  31.0 4.3 %collective-permute-done.27.refs_4_ = bf16[64,1024]{1,0:T(8,128)(2,1)S(1)} collective-permute-done((bf16[64,1024]{1,0:T(8,128)(2,1)}, bf16[64,1024]{1,0:T(8,128)(2,1)S(1)}, u32[]{:S(2)}, u32[]{:S(2)}) %collective-permute-start.27) | collective-permute-done | bytes 131104 | tf_op jit(solution)/shard_map/ppermute | solution.py:407
  35.4 3.3 %collective-permute-start.31 = (bf16[64,1024]{1,0:T(8,128)(2,1)}, bf16[64,1024]{1,0:T(8,128)(2,1)}, u32[]{:S(2)}, u32[]{:S(2)}) collective-permute-start(bf16[64,1024]{1,0:T(8,128)(2,1)} %get-tuple-element.194), channel_id=1, source_target_pairs={{0,1},{1,2},{2,3},{3,0},{4,5},{5,6},{6,7},{7,4},{8,9},{9,10},{10,1... | collective-permute-start | bytes 393224 | tf_op jit(solution)/shard_map/ppermute | solution.py:407
  42.8 17.6 %shard_map.133 = (bf16[64,3072]{1,0:T(8,128)(2,1)S(1)}, bf16[64,3072]{1,0:T(8,128)(2,1)S(1)}, bf16[64,3072]{1,0:T(8,128)(2,1)S(1)}, bf16[64,3072]{1,0:T(8,128)(2...) custom-call(s32[4]{0:T(128)S(1)} %copy-done.18, ...), custom_call_target="tpu_custom_call" | custom-call | flops 21474836480 | bytes 15728640 | tf_op jit(solution)/shard_map/pallas_call | solution.py:168
  60.5 3.2 %collective-permute-start.39 = (bf16[64,3072]{1,0:T(8,128)(2,1)S(1)}, bf16[64,3072]{1,0:T(8,128)(2,1)S(1)}, u32[]{:S(2)}, u32[]{:S(2)}) collective-permute-start(bf16[64,3072]{1,0:T(8,128)(2,1)S(1)} %broadcast_select_fusion), channel_id=1, source_target_pairs={{0,1},{3,2},{4,5},{7,6},{8,9},{11,10},{12,13},{15,14},{16,17},{19,... | collective-permute-start | bytes 1179656 | tf_op jit(solution)/shard_map/ppermute | solution.py:432
  65.1 8.2 %collective-permute-done.39 = bf16[64,3072]{1,0:T(8,128)(2,1)S(1)} collective-permute-done((bf16[64,3072]{1,0:T(8,128)(2,1)S(1)}, bf16[64,3072]{1,0:T(8,128)(2,1)S(1)}, u32[]{:S(2)}, u32[]{:S(2)}) %collective-permute-start.39) | collective-permute-done | bytes 393248 | tf_op jit(solution)/shard_map/ppermute | solution.py:432
  74.1 5.1 %collective-permute-start.40 = (bf16[64,3072]{1,0:T(8,128)(2,1)}, bf16[64,3072]{1,0:T(8,128)(2,1)}, u32[]{:S(2)}, u32[]{:S(2)}) collective-permute-start(bf16[64,3072]{1,0:T(8,128)(2,1)} %add.230), channel_id=1, source_target_pairs={{0,1},{1,2},{4,5},{5,6},{8,9},{9,10},{12,13},{13,14},{16,17},{17,1... | collective-permute-start | bytes 1179656 | tf_op jit(solution)/shard_map/ppermute | solution.py:441
  82.5 3.7 %collective-permute-start.35 = (bf16[64,3072]{1,0:T(8,128)(2,1)S(1)}, bf16[64,3072]{1,0:T(8,128)(2,1)S(1)}, u32[]{:S(2)}, u32[]{:S(2)}) collective-permute-start(bf16[64,3072]{1,0:T(8,128)(2,1)S(1)} %add.224), channel_id=1, source_target_pairs={{0,1},{1,2},{4,5},{5,6},{8,9},{9,10},{12,13},{13,14},{16,17},{17,1... | collective-permute-start | bytes 1179656 | tf_op jit(solution)/shard_map/ppermute | solution.py:441
  93.3 5.1 %collective-permute-start.42 = (bf16[64,3072]{1,0:T(8,128)(2,1)S(1)}, bf16[64,3072]{1,0:T(8,128)(2,1)S(1)}, u32[]{:S(2)}, u32[]{:S(2)}) collective-permute-start(bf16[64,3072]{1,0:T(8,128)(2,1)S(1)} %add.231), channel_id=1, source_target_pairs={{0,1},{1,2},{2,3},{4,5},{5,6},{6,7},{8,9},{9,10},{10,11},{12,13},{... | collective-permute-start | bytes 1179656 | tf_op jit(solution)/shard_map/ppermute | solution.py:441
  101.1 4.6 %collective-permute-start.37 = (bf16[64,3072]{1,0:T(8,128)(2,1)S(1)}, bf16[64,3072]{1,0:T(8,128)(2,1)S(1)}, u32[]{:S(2)}, u32[]{:S(2)}) collective-permute-start(bf16[64,3072]{1,0:T(8,128)(2,1)S(1)} %add.225), channel_id=1, source_target_pairs={{0,1},{1,2},{2,3},{4,5},{5,6},{6,7},{8,9},{9,10},{10,11},{12,13},{... | collective-permute-start | bytes 1179656 | tf_op jit(solution)/shard_map/ppermute | solution.py:441
  105.9 3.5 %collective-permute-done.38 = bf16[64,3072]{1,0:T(8,128)(2,1)S(1)} collective-permute-done((bf16[64,3072]{1,0:T(8,128)(2,1)S(1)}, bf16[64,3072]{1,0:T(8,128)(2,1)S(1)}, u32[]{:S(2)}, u32[]{:S(2)}) %collective-permute-start.38) | collective-permute-done | bytes 393248 | tf_op jit(solution)/shard_map/ppermute | solution.py:442
  109.4 5.7 %collective-permute-done.37 = bf16[64,3072]{1,0:T(8,128)(2,1)S(1)} collective-permute-done((bf16[64,3072]{1,0:T(8,128)(2,1)S(1)}, bf16[64,3072]{1,0:T(8,128)(2,1)S(1)}, u32[]{:S(2)}, u32[]{:S(2)}) %collective-permute-start.37) | collective-permute-done | bytes 393248 | tf_op jit(solution)/shard_map/ppermute | solution.py:441
  116.1 4.4 %collective-permute-start.44 = (bf16[64,6144]{1,0:T(8,128)(2,1)S(1)}, bf16[64,6144]{1,0:T(8,128)(2,1)S(1)}, u32[]{:S(2)}, u32[]{:S(2)}) collective-permute-start(bf16[64,6144]{1,0:T(8,128)(2,1)S(1)} %fusion.7.refs_1_), channel_id=1, source_target_pairs={{0,1},{1,2},{2,3},{4,5},{5,6},{6,7},{8,9},{9,10},{10,11},{12,13},{... | collective-permute-start | bytes 2359304 | tf_op jit(solution)/shard_map/ppermute | solution.py:457
  121.9 17.6 %shard_map.134 = (bf16[64,3072]{1,0:T(8,128)(2,1)S(1)}, bf16[64,3072]{1,0:T(8,128)(2,1)S(1)}, bf16[64,3072]{1,0:T(8,128)(2,1)S(1)}, bf16[64,3072]{1,0:T(8,128)(2...) custom-call(s32[4]{0:T(128)S(1)} %copy-done.18, ...), custom_call_target="tpu_custom_call" | custom-call | flops 21474836480 | bytes 15728640 | tf_op jit(solution)/shard_map/pallas_call | solution.py:168
  143.8 5.1 %collective-permute-start.46 = (bf16[64,3072]{1,0:T(8,128)(2,1)S(1)}, bf16[64,3072]{1,0:T(8,128)(2,1)S(1)}, u32[]{:S(2)}, u32[]{:S(2)}) collective-permute-start(bf16[64,3072]{1,0:T(8,128)(2,1)S(1)} %get-tuple-element.316.refs_2_), channel_id=1, source_target_pairs={{0,1},{1,2},{2,3},{4,5},{5,6},{6,7},{8,9},{9,10},{10,11},{12,13},{... | collective-permute-start | bytes 1179656 | tf_op jit(solution)/shard_map/ppermute | solution.py:479
  150.3 4.6 %collective-permute-start.48 = (bf16[64,3072]{1,0:T(8,128)(2,1)S(1)}, bf16[64,3072]{1,0:T(8,128)(2,1)S(1)}, u32[]{:S(2)}, u32[]{:S(2)}) collective-permute-start(bf16[64,3072]{1,0:T(8,128)(2,1)S(1)} %get-tuple-element.315.refs_3_), channel_id=1, source_target_pairs={{0,1},{1,2},{2,3},{4,5},{5,6},{6,7},{8,9},{9,10},{10,11},{12,13},{... | collective-permute-start | bytes 1179656 | tf_op jit(solution)/shard_map/ppermute | solution.py:479
  158.4 5.1 %collective-permute-start.50 = (bf16[64,3072]{1,0:T(8,128)(2,1)S(1)}, bf16[64,3072]{1,0:T(8,128)(2,1)}, u32[]{:S(2)}, u32[]{:S(2)}) collective-permute-start(bf16[64,3072]{1,0:T(8,128)(2,1)S(1)} %get-tuple-element.324.refs_4_), channel_id=1, source_target_pairs={{0,1},{1,2},{2,3},{4,5},{5,6},{6,7},{8,9},{9,10},{10,11},{12,13},{... | collective-permute-start | bytes 1179656 | tf_op jit(solution)/shard_map/ppermute | solution.py:479
  165.6 5.3 %collective-permute-start.52 = (bf16[64,3072]{1,0:T(8,128)(2,1)}, bf16[64,3072]{1,0:T(8,128)(2,1)}, u32[]{:S(2)}, u32[]{:S(2)}) collective-permute-start(bf16[64,3072]{1,0:T(8,128)(2,1)} %get-tuple-element.322.refs_5_), channel_id=1, source_target_pairs={{0,1},{1,2},{2,3},{4,5},{5,6},{6,7},{8,9},{9,10},{10,11},{12,13},{... | collective-permute-start | bytes 1179656 | tf_op jit(solution)/shard_map/ppermute | solution.py:479
  176.0 4.0 %collective-permute-done.52.refs_7_ = bf16[64,3072]{1,0:T(8,128)(2,1)} collective-permute-done((bf16[64,3072]{1,0:T(8,128)(2,1)}, bf16[64,3072]{1,0:T(8,128)(2,1)}, u32[]{:S(2)}, u32[]{:S(2)}) %collective-permute-start.52) | collective-permute-done | bytes 393248 | tf_op jit(solution)/shard_map/ppermute | solution.py:479
  180.1 4.9 %collective-permute-done.53.refs_13_ = bf16[64,3072]{1,0:T(8,128)(2,1)} collective-permute-done((bf16[64,3072]{1,0:T(8,128)(2,1)S(1)}, bf16[64,3072]{1,0:T(8,128)(2,1)}, u32[]{:S(2)}, u32[]{:S(2)}) %collective-permute-start.53) | collective-permute-done | bytes 393248 | tf_op jit(solution)/shard_map/ppermute | solution.py:479
  191.7 35.3 %shard_map.135 = (bf16[256,3072]{1,0:T(8,128)(2,1)S(1)}, bf16[256,3072]{1,0:T(8,128)(2,1)S(1)}) custom-call(s32[1]{0:T(128)} %bitcast.6.mine.refs_0_, bf16[64,6144]{1,0:T(8,128)(2,1)S(1)} %fusion.7.refs_1_, bf16[64,3072]{1,0:T(8,128)(2,1)S(1)} %get-tuple-element.316.refs_2_, bf16[64,3072]{1,0:T(8,128)(2,1)S(1)} %get-tuple-element.315.refs_3_, ...), custom_call_target="tpu_custom_call" | custom-call | flops 19327352832 | bytes 75497472 | tf_op jit(solution)/shard_map/pallas_call | solution.py:263
  228.4 4.6 %collective-permute-start.62 = (bf16[64,3072]{1,0:T(8,128)(2,1)S(1)}, bf16[64,3072]{1,0:T(8,128)(2,1)S(1)}, u32[]{:S(2)}, u32[]{:S(2)}) collective-permute-start(bf16[64,3072]{1,0:T(8,128)(2,1)S(1)} %get-tuple-element.269), channel_id=1, source_target_pairs={{0,1},{4,5},{8,9},{12,13},{16,17},{20,21},{24,25},{28,29}} | collective-permute-start | bytes 1179656 | tf_op jit(solution)/shard_map/ppermute | solution.py:441
  235.9 6.5 %collective-permute-done.62 = bf16[64,3072]{1,0:T(8,128)(2,1)S(1)} collective-permute-done((bf16[64,3072]{1,0:T(8,128)(2,1)S(1)}, bf16[64,3072]{1,0:T(8,128)(2,1)S(1)}, u32[]{:S(2)}, u32[]{:S(2)}) %collective-permute-start.62) | collective-permute-done | bytes 393248 | tf_op jit(solution)/shard_map/ppermute | solution.py:441
  242.6 4.4 %collective-permute-start.64 = (bf16[64,3072]{1,0:T(8,128)(2,1)S(1)}, bf16[64,3072]{1,0:T(8,128)(2,1)S(1)}, u32[]{:S(2)}, u32[]{:S(2)}) collective-permute-start(bf16[64,3072]{1,0:T(8,128)(2,1)S(1)} %get-tuple-element.320), channel_id=1, source_target_pairs={{0,1},{1,2},{4,5},{5,6},{8,9},{9,10},{12,13},{13,14},{16,17},{17,1... | collective-permute-start | bytes 1179656 | tf_op jit(solution)/shard_map/ppermute | solution.py:441
  248.4 4.4 %collective-permute-start.58 = (bf16[64,3072]{1,0:T(8,128)(2,1)S(1)}, bf16[64,3072]{1,0:T(8,128)(2,1)S(1)}, u32[]{:S(2)}, u32[]{:S(2)}) collective-permute-start(bf16[64,3072]{1,0:T(8,128)(2,1)S(1)} %get-tuple-element.318), channel_id=1, source_target_pairs={{0,1},{1,2},{4,5},{5,6},{8,9},{9,10},{12,13},{13,14},{16,17},{17,1... | collective-permute-start | bytes 1179656 | tf_op jit(solution)/shard_map/ppermute | solution.py:441
  255.3 7.2 %collective-permute-start.66 = (bf16[64,3072]{1,0:T(8,128)(2,1)S(1)}, bf16[64,3072]{1,0:T(8,128)(2,1)S(1)}, u32[]{:S(2)}, u32[]{:S(2)}) collective-permute-start(bf16[64,3072]{1,0:T(8,128)(2,1)S(1)} %add.264), channel_id=1, source_target_pairs={{0,1},{1,2},{2,3},{4,5},{5,6},{6,7},{8,9},{9,10},{10,11},{12,13},{... | collective-permute-start | bytes 1179656 | tf_op jit(solution)/shard_map/ppermute | solution.py:441
  264.0 4.7 %collective-permute-start.60 = (bf16[64,3072]{1,0:T(8,128)(2,1)S(1)}, bf16[64,3072]{1,0:T(8,128)(2,1)S(1)}, u32[]{:S(2)}, u32[]{:S(2)}) collective-permute-start(bf16[64,3072]{1,0:T(8,128)(2,1)S(1)} %add.254), channel_id=1, source_target_pairs={{0,1},{1,2},{2,3},{4,5},{5,6},{6,7},{8,9},{9,10},{10,11},{12,13},{... | collective-permute-start | bytes 1179656 | tf_op jit(solution)/shard_map/ppermute | solution.py:441
  (191 shorter events, 72.5 us)
Async XLA Ops:
  5.7 11.4 %collective-permute-start.23 = (bf16[128,512]{1,0:T(8,128)(2,1)}, bf16[128,512]{1,0:T(8,128)(2,1)S(1)}, u32[]{:S(2)}, u32[]{:S(2)}) collective-permute-start(bf16[128,512]{1,0:T(8,128)(2,1)} %get-tuple-element.171), channel_id=1, source_target_pairs={{0,2},{1,3},{2,0},{3,1},{4,6},{5,7},{6,4},{7,5},{8,10},{9,11},{10,... | collective-permute-start | bytes 393224 | tf_op jit(solution)/shard_map/ppermute | solution.py:407
  17.2 18.1 %collective-permute-start.25 = (bf16[512,512]{1,0:T(8,128)(2,1)S(1)}, bf16[512,512]{1,0:T(8,128)(2,1)S(1)}, u32[]{:S(2)}, u32[]{:S(2)}) collective-permute-start(bf16[512,512]{1,0:T(8,128)(2,1)S(1)} %constant_dynamic-update-slice_fusion.refs_7_), channel_id=1, source_target_pairs={{0,8},{4,12},{8,0},{12,4},{1,9},{5,13},{9,1},{13,5},{2,10},{6,14},... | collective-permute-start | bytes 1572872 | tf_op jit(solution)/shard_map/ppermute | solution.py:522
  27.8 13.5 %collective-permute-start.29 = (bf16[512,512]{1,0:T(8,128)(2,1)S(1)}, bf16[512,512]{1,0:T(8,128)(2,1)S(1)}, u32[]{:S(2)}, u32[]{:S(2)}) collective-permute-start(bf16[512,512]{1,0:T(8,128)(2,1)S(1)} %constant_dynamic-update-slice_fusion.refs_7_), channel_id=1, source_target_pairs={{0,4},{4,0},{8,12},{12,8},{1,5},{5,1},{9,13},{13,9},{2,6},{6,2},{1... | collective-permute-start | bytes 1572872 | tf_op jit(solution)/shard_map/ppermute | solution.py:522
  35.4 25.0 %collective-permute-start.31 = (bf16[64,1024]{1,0:T(8,128)(2,1)}, bf16[64,1024]{1,0:T(8,128)(2,1)}, u32[]{:S(2)}, u32[]{:S(2)}) collective-permute-start(bf16[64,1024]{1,0:T(8,128)(2,1)} %get-tuple-element.194), channel_id=1, source_target_pairs={{0,1},{1,2},{2,3},{3,0},{4,5},{5,6},{6,7},{7,4},{8,9},{9,10},{10,1... | collective-permute-start | bytes 393224 | tf_op jit(solution)/shard_map/ppermute | solution.py:407
  38.7 21.7 %collective-permute-start.32 = (bf16[64,1024]{1,0:T(8,128)(2,1)}, bf16[64,1024]{1,0:T(8,128)(2,1)}, u32[]{:S(2)}, u32[]{:S(2)}) collective-permute-start(bf16[64,1024]{1,0:T(8,128)(2,1)} %get-tuple-element.195), channel_id=1, source_target_pairs={{0,2},{1,3},{2,0},{3,1},{4,6},{5,7},{6,4},{7,5},{8,10},{9,11},{10,... | collective-permute-start | bytes 393224 | tf_op jit(solution)/shard_map/ppermute | solution.py:407
  40.5 19.9 %collective-permute-start.33 = (bf16[64,1024]{1,0:T(8,128)(2,1)}, bf16[64,1024]{1,0:T(8,128)(2,1)}, u32[]{:S(2)}, u32[]{:S(2)}) collective-permute-start(bf16[64,1024]{1,0:T(8,128)(2,1)} %get-tuple-element.196), channel_id=1, source_target_pairs={{0,3},{1,0},{2,1},{3,2},{4,7},{5,4},{6,5},{7,6},{8,11},{9,8},{10,9... | collective-permute-start | bytes 393224 | tf_op jit(solution)/shard_map/ppermute | solution.py:407
  60.5 12.8 %collective-permute-start.39 = (bf16[64,3072]{1,0:T(8,128)(2,1)S(1)}, bf16[64,3072]{1,0:T(8,128)(2,1)S(1)}, u32[]{:S(2)}, u32[]{:S(2)}) collective-permute-start(bf16[64,3072]{1,0:T(8,128)(2,1)S(1)} %broadcast_select_fusion), channel_id=1, source_target_pairs={{0,1},{3,2},{4,5},{7,6},{8,9},{11,10},{12,13},{15,14},{16,17},{19,... | collective-permute-start | bytes 1179656 | tf_op jit(solution)/shard_map/ppermute | solution.py:432
  63.8 18.6 %collective-permute-start.34 = (bf16[64,3072]{1,0:T(8,128)(2,1)S(1)}, bf16[64,3072]{1,0:T(8,128)(2,1)S(1)}, u32[]{:S(2)}, u32[]{:S(2)}) collective-permute-start(bf16[64,3072]{1,0:T(8,128)(2,1)S(1)} %broadcast_select_fusion.1), channel_id=1, source_target_pairs={{0,1},{3,2},{4,5},{7,6},{8,9},{11,10},{12,13},{15,14},{16,17},{19,... | collective-permute-start | bytes 1179656 | tf_op jit(solution)/shard_map/ppermute | solution.py:432
  74.1 15.6 %collective-permute-start.40 = (bf16[64,3072]{1,0:T(8,128)(2,1)}, bf16[64,3072]{1,0:T(8,128)(2,1)}, u32[]{:S(2)}, u32[]{:S(2)}) collective-permute-start(bf16[64,3072]{1,0:T(8,128)(2,1)} %add.230), channel_id=1, source_target_pairs={{0,1},{1,2},{4,5},{5,6},{8,9},{9,10},{12,13},{13,14},{16,17},{17,1... | collective-permute-start | bytes 1179656 | tf_op jit(solution)/shard_map/ppermute | solution.py:441
  82.5 16.0 %collective-permute-start.35 = (bf16[64,3072]{1,0:T(8,128)(2,1)S(1)}, bf16[64,3072]{1,0:T(8,128)(2,1)S(1)}, u32[]{:S(2)}, u32[]{:S(2)}) collective-permute-start(bf16[64,3072]{1,0:T(8,128)(2,1)S(1)} %add.224), channel_id=1, source_target_pairs={{0,1},{1,2},{4,5},{5,6},{8,9},{9,10},{12,13},{13,14},{16,17},{17,1... | collective-permute-start | bytes 1179656 | tf_op jit(solution)/shard_map/ppermute | solution.py:441
  86.2 12.3 %collective-permute-start.36 = (bf16[64,3072]{1,0:T(8,128)(2,1)S(1)}, bf16[64,3072]{1,0:T(8,128)(2,1)}, u32[]{:S(2)}, u32[]{:S(2)}) collective-permute-start(bf16[64,3072]{1,0:T(8,128)(2,1)S(1)} %add.224), channel_id=1, source_target_pairs={{2,1},{3,2},{6,5},{7,6},{10,9},{11,10},{14,13},{15,14},{18,17},{19... | collective-permute-start | bytes 1179656 | tf_op jit(solution)/shard_map/ppermute | solution.py:442
  90.8 15.0 %collective-permute-start.43 = (bf16[64,3072]{1,0:T(8,128)(2,1)S(1)}, bf16[64,3072]{1,0:T(8,128)(2,1)S(1)}, u32[]{:S(2)}, u32[]{:S(2)}) collective-permute-start(bf16[64,3072]{1,0:T(8,128)(2,1)S(1)} %add.232), channel_id=1, source_target_pairs={{1,0},{2,1},{3,2},{5,4},{6,5},{7,6},{9,8},{10,9},{11,10},{13,12},{... | collective-permute-start | bytes 1179656 | tf_op jit(solution)/shard_map/ppermute | solution.py:442
  93.3 12.5 %collective-permute-start.42 = (bf16[64,3072]{1,0:T(8,128)(2,1)S(1)}, bf16[64,3072]{1,0:T(8,128)(2,1)S(1)}, u32[]{:S(2)}, u32[]{:S(2)}) collective-permute-start(bf16[64,3072]{1,0:T(8,128)(2,1)S(1)} %add.231), channel_id=1, source_target_pairs={{0,1},{1,2},{2,3},{4,5},{5,6},{6,7},{8,9},{9,10},{10,11},{12,13},{... | collective-permute-start | bytes 1179656 | tf_op jit(solution)/shard_map/ppermute | solution.py:441
  101.1 14.0 %collective-permute-start.37 = (bf16[64,3072]{1,0:T(8,128)(2,1)S(1)}, bf16[64,3072]{1,0:T(8,128)(2,1)S(1)}, u32[]{:S(2)}, u32[]{:S(2)}) collective-permute-start(bf16[64,3072]{1,0:T(8,128)(2,1)S(1)} %add.225), channel_id=1, source_target_pairs={{0,1},{1,2},{2,3},{4,5},{5,6},{6,7},{8,9},{9,10},{10,11},{12,13},{... | collective-permute-start | bytes 1179656 | tf_op jit(solution)/shard_map/ppermute | solution.py:441
  116.1 25.0 %collective-permute-start.44 = (bf16[64,6144]{1,0:T(8,128)(2,1)S(1)}, bf16[64,6144]{1,0:T(8,128)(2,1)S(1)}, u32[]{:S(2)}, u32[]{:S(2)}) collective-permute-start(bf16[64,6144]{1,0:T(8,128)(2,1)S(1)} %fusion.7.refs_1_), channel_id=1, source_target_pairs={{0,1},{1,2},{2,3},{4,5},{5,6},{6,7},{8,9},{9,10},{10,11},{12,13},{... | collective-permute-start | bytes 2359304 | tf_op jit(solution)/shard_map/ppermute | solution.py:457
  120.6 21.7 %collective-permute-start.45 = (bf16[64,6144]{1,0:T(8,128)(2,1)S(1)}, bf16[64,6144]{1,0:T(8,128)(2,1)S(1)}, u32[]{:S(2)}, u32[]{:S(2)}) collective-permute-start(bf16[64,6144]{1,0:T(8,128)(2,1)S(1)} %fusion.7.refs_1_), channel_id=1, source_target_pairs={{1,0},{2,1},{3,2},{5,4},{6,5},{7,6},{9,8},{10,9},{11,10},{13,12},{... | collective-permute-start | bytes 2359304 | tf_op jit(solution)/shard_map/ppermute | solution.py:458
  142.3 13.5 %collective-permute-start.47 = (bf16[64,3072]{1,0:T(8,128)(2,1)S(1)}, bf16[64,3072]{1,0:T(8,128)(2,1)}, u32[]{:S(2)}, u32[]{:S(2)}) collective-permute-start(bf16[64,3072]{1,0:T(8,128)(2,1)S(1)} %get-tuple-element.314.refs_8_), channel_id=1, source_target_pairs={{1,0},{2,1},{3,2},{5,4},{6,5},{7,6},{9,8},{10,9},{11,10},{13,12},{... | collective-permute-start | bytes 1179656 | tf_op jit(solution)/shard_map/ppermute | solution.py:479
  143.8 12.7 %collective-permute-start.46 = (bf16[64,3072]{1,0:T(8,128)(2,1)S(1)}, bf16[64,3072]{1,0:T(8,128)(2,1)S(1)}, u32[]{:S(2)}, u32[]{:S(2)}) collective-permute-start(bf16[64,3072]{1,0:T(8,128)(2,1)S(1)} %get-tuple-element.316.refs_2_), channel_id=1, source_target_pairs={{0,1},{1,2},{2,3},{4,5},{5,6},{6,7},{8,9},{9,10},{10,11},{12,13},{... | collective-permute-start | bytes 1179656 | tf_op jit(solution)/shard_map/ppermute | solution.py:479
  148.9 15.9 %collective-permute-start.49 = (bf16[64,3072]{1,0:T(8,128)(2,1)S(1)}, bf16[64,3072]{1,0:T(8,128)(2,1)S(1)}, u32[]{:S(2)}, u32[]{:S(2)}) collective-permute-start(bf16[64,3072]{1,0:T(8,128)(2,1)S(1)} %get-tuple-element.313.refs_9_), channel_id=1, source_target_pairs={{1,0},{2,1},{3,2},{5,4},{6,5},{7,6},{9,8},{10,9},{11,10},{13,12},{... | collective-permute-start | bytes 1179656 | tf_op jit(solution)/shard_map/ppermute | solution.py:479
  150.3 14.5 %collective-permute-start.48 = (bf16[64,3072]{1,0:T(8,128)(2,1)S(1)}, bf16[64,3072]{1,0:T(8,128)(2,1)S(1)}, u32[]{:S(2)}, u32[]{:S(2)}) collective-permute-start(bf16[64,3072]{1,0:T(8,128)(2,1)S(1)} %get-tuple-element.315.refs_3_), channel_id=1, source_target_pairs={{0,1},{1,2},{2,3},{4,5},{5,6},{6,7},{8,9},{9,10},{10,11},{12,13},{... | collective-permute-start | bytes 1179656 | tf_op jit(solution)/shard_map/ppermute | solution.py:479
  158.4 14.5 %collective-permute-start.50 = (bf16[64,3072]{1,0:T(8,128)(2,1)S(1)}, bf16[64,3072]{1,0:T(8,128)(2,1)}, u32[]{:S(2)}, u32[]{:S(2)}) collective-permute-start(bf16[64,3072]{1,0:T(8,128)(2,1)S(1)} %get-tuple-element.324.refs_4_), channel_id=1, source_target_pairs={{0,1},{1,2},{2,3},{4,5},{5,6},{6,7},{8,9},{9,10},{10,11},{12,13},{... | collective-permute-start | bytes 1179656 | tf_op jit(solution)/shard_map/ppermute | solution.py:479
  163.5 11.3 %collective-permute-start.51 = (bf16[64,3072]{1,0:T(8,128)(2,1)S(1)}, bf16[64,3072]{1,0:T(8,128)(2,1)}, u32[]{:S(2)}, u32[]{:S(2)}) collective-permute-start(bf16[64,3072]{1,0:T(8,128)(2,1)S(1)} %get-tuple-element.323.refs_10_), channel_id=1, source_target_pairs={{1,0},{2,1},{3,2},{5,4},{6,5},{7,6},{9,8},{10,9},{11,10},{13,12},{... | collective-permute-start | bytes 1179656 | tf_op jit(solution)/shard_map/ppermute | solution.py:479
  165.6 14.4 %collective-permute-start.52 = (bf16[64,3072]{1,0:T(8,128)(2,1)}, bf16[64,3072]{1,0:T(8,128)(2,1)}, u32[]{:S(2)}, u32[]{:S(2)}) collective-permute-start(bf16[64,3072]{1,0:T(8,128)(2,1)} %get-tuple-element.322.refs_5_), channel_id=1, source_target_pairs={{0,1},{1,2},{2,3},{4,5},{5,6},{6,7},{8,9},{9,10},{10,11},{12,13},{... | collective-permute-start | bytes 1179656 | tf_op jit(solution)/shard_map/ppermute | solution.py:479
  170.9 14.0 %collective-permute-start.53 = (bf16[64,3072]{1,0:T(8,128)(2,1)S(1)}, bf16[64,3072]{1,0:T(8,128)(2,1)}, u32[]{:S(2)}, u32[]{:S(2)}) collective-permute-start(bf16[64,3072]{1,0:T(8,128)(2,1)S(1)} %get-tuple-element.321.refs_11_), channel_id=1, source_target_pairs={{1,0},{2,1},{3,2},{5,4},{6,5},{7,6},{9,8},{10,9},{11,10},{13,12},{... | collective-permute-start | bytes 1179656 | tf_op jit(solution)/shard_map/ppermute | solution.py:479
  186.3 41.1 %collective-permute-start.54 = (bf16[64,6144]{1,0:T(8,128)(2,1)S(1)}, bf16[64,6144]{1,0:T(8,128)(2,1)S(1)}, u32[]{:S(2)}, u32[]{:S(2)}) collective-permute-start(bf16[64,6144]{1,0:T(8,128)(2,1)S(1)} %pad_maximum_fusion.2), channel_id=1, source_target_pairs={{0,1},{1,2},{2,3},{4,5},{5,6},{6,7},{8,9},{9,10},{10,11},{12,13},{... | collective-permute-start | bytes 2359304 | tf_op jit(solution)/shard_map/ppermute | solution.py:488
  190.4 37.0 %collective-permute-start.55 = (bf16[64,6144]{1,0:T(8,128)(2,1)S(1)}, bf16[64,6144]{1,0:T(8,128)(2,1)S(1)}, u32[]{:S(2)}, u32[]{:S(2)}) collective-permute-start(bf16[64,6144]{1,0:T(8,128)(2,1)S(1)} %pad_maximum_fusion.3), channel_id=1, source_target_pairs={{1,0},{2,1},{3,2},{5,4},{6,5},{7,6},{9,8},{10,9},{11,10},{13,12},{... | collective-permute-start | bytes 2359304 | tf_op jit(solution)/shard_map/ppermute | solution.py:489
  228.4 14.1 %collective-permute-start.62 = (bf16[64,3072]{1,0:T(8,128)(2,1)S(1)}, bf16[64,3072]{1,0:T(8,128)(2,1)S(1)}, u32[]{:S(2)}, u32[]{:S(2)}) collective-permute-start(bf16[64,3072]{1,0:T(8,128)(2,1)S(1)} %get-tuple-element.269), channel_id=1, source_target_pairs={{0,1},{4,5},{8,9},{12,13},{16,17},{20,21},{24,25},{28,29}} | collective-permute-start | bytes 1179656 | tf_op jit(solution)/shard_map/ppermute | solution.py:441
  233.8 14.5 %collective-permute-start.56 = (bf16[64,3072]{1,0:T(8,128)(2,1)S(1)}, bf16[64,3072]{1,0:T(8,128)(2,1)S(1)}, u32[]{:S(2)}, u32[]{:S(2)}) collective-permute-start(bf16[64,3072]{1,0:T(8,128)(2,1)S(1)} %get-tuple-element.258), channel_id=1, source_target_pairs={{0,1},{4,5},{8,9},{12,13},{16,17},{20,21},{24,25},{28,29}} | collective-permute-start | bytes 1179656 | tf_op jit(solution)/shard_map/ppermute | solution.py:441
  235.3 13.0 %collective-permute-start.57 = (bf16[64,3072]{1,0:T(8,128)(2,1)S(1)}, bf16[64,3072]{1,0:T(8,128)(2,1)S(1)}, u32[]{:S(2)}, u32[]{:S(2)}) collective-permute-start(bf16[64,3072]{1,0:T(8,128)(2,1)S(1)} %get-tuple-element.256), channel_id=1, source_target_pairs={{3,2},{7,6},{11,10},{15,14},{19,18},{23,22},{27,26},{31,30}} | collective-permute-start | bytes 1179656 | tf_op jit(solution)/shard_map/ppermute | solution.py:442
  248.4 14.1 %collective-permute-start.58 = (bf16[64,3072]{1,0:T(8,128)(2,1)S(1)}, bf16[64,3072]{1,0:T(8,128)(2,1)S(1)}, u32[]{:S(2)}, u32[]{:S(2)}) collective-permute-start(bf16[64,3072]{1,0:T(8,128)(2,1)S(1)} %get-tuple-element.318), channel_id=1, source_target_pairs={{0,1},{1,2},{4,5},{5,6},{8,9},{9,10},{12,13},{13,14},{16,17},{17,1... | collective-permute-start | bytes 1179656 | tf_op jit(solution)/shard_map/ppermute | solution.py:441
  253.8 17.1 %collective-permute-start.67 = (bf16[64,3072]{1,0:T(8,128)(2,1)S(1)}, bf16[64,3072]{1,0:T(8,128)(2,1)S(1)}, u32[]{:S(2)}, u32[]{:S(2)}) collective-permute-start(bf16[64,3072]{1,0:T(8,128)(2,1)S(1)} %add.265), channel_id=1, source_target_pairs={{1,0},{2,1},{3,2},{5,4},{6,5},{7,6},{9,8},{10,9},{11,10},{13,12},{... | collective-permute-start | bytes 1179656 | tf_op jit(solution)/shard_map/ppermute | solution.py:442
  255.3 15.5 %collective-permute-start.66 = (bf16[64,3072]{1,0:T(8,128)(2,1)S(1)}, bf16[64,3072]{1,0:T(8,128)(2,1)S(1)}, u32[]{:S(2)}, u32[]{:S(2)}) collective-permute-start(bf16[64,3072]{1,0:T(8,128)(2,1)S(1)} %add.264), channel_id=1, source_target_pairs={{0,1},{1,2},{2,3},{4,5},{5,6},{6,7},{8,9},{9,10},{10,11},{12,13},{... | collective-permute-start | bytes 1179656 | tf_op jit(solution)/shard_map/ppermute | solution.py:441
  (52 other events, 546.0 us)

commit v11 on v10

--- a/solution.py
+++ b/solution.py
@@ -607,8 +607,8 @@
         return (restore([first_half]), restore([expert(0, normed, gather_line(normed)[0])[0]]))
     asked[1], _ = lax.optimization_barrier((asked[1], normed))
     sources, second_sum = gather_line(normed, project(1))
-    part, second_sum = expert(0, normed, sources, second_sum)
     second_half = (hidden[half:].astype(jnp.float32) + second_sum).astype(jnp.bfloat16)
+    part, second_half = expert(0, normed, sources, second_half)
     part, late = lax.optimization_barrier((part, second_half))
     late = lax.cond(crowded[0] > 0, late_expert, jnp.zeros_like, late)
     return (restore([first_half, second_half]), restore([part, late]))

time: 282 us -> 279 us (0.989)
  waiting for transfers between devices: 57.5 us -> 61.4 us
where the time goes in v11:
time: 279 us; the launch traced here: 275 us
  starting transfers between devices  114 us (41%)
  Pallas kernels  73.9 us (26%)
  waiting for transfers between devices  61.4 us (22%)
  other arithmetic  11.7 us (4%)
  local copies, waits for them, and re-layouts  6.24 us (2%)
  matrix products  5.63 us (2%)
    ppermute x10, starting transfers between devices, reduce_line(): right = lax.ppermute(to_right, 'tp', rights(s))  43.6 us
    pallas_call x2, Pallas kernels, attend(): pl.pallas_call(kernel, grid_spec=pltpu.PrefetchScalarGridSpec(num_scalar_...  35.3 us
    pallas_call x1, Pallas kernels, expert_rows(): pl.pallas_call(functools.partial(expert_kernel, [len(source) for source i...  33.9 us
    ppermute x9, starting transfers between devices, shift(): lax.ppermute(parts[s], 'tp', moves[s])  18.5 us
    ppermute x4, starting transfers between devices, gather_line(): lax.ppermute(right, 'tp', to_right)  18.2 us
    ppermute x10, waiting for transfers between devices, reduce_line(): right = lax.ppermute(to_right, 'tp', rights(s))  16 us
    ppermute x9, waiting for transfers between devices, shift(): lax.ppermute(parts[s], 'tp', moves[s])  14.1 us
    ppermute x10, starting transfers between devices, reduce_line(): left = lax.ppermute(to_left, 'tp', lefts(s))  11.9 us
  transfers between devices with their start and end apart: 46, of which 18 were waited for; matrix products, arithmetic and copies ran while one was open for 6% of the time, Pallas kernels for 26%

profile of v11, /device:TPU:0, one launch (start us, length us, event | category | flops | bytes accessed | tf_op | source)
XLA Modules:
  0.0 274.9 jit_solution(4768082372362240372)
XLA Ops:
  2.7 3.0 %collective-permute-start.22 = (bf16[128,512]{1,0:T(8,128)(2,1)}, bf16[128,512]{1,0:T(8,128)(2,1)S(1)}, u32[]{:S(2)}, u32[]{:S(2)}) collective-permute-start(bf16[128,512]{1,0:T(8,128)(2,1)} %get-tuple-element.170), channel_id=1, source_target_pairs={{0,1},{1,2},{2,3},{3,0},{4,5},{5,6},{6,7},{7,4},{8,9},{9,10},{10,1... | collective-permute-start | bytes 393224 | tf_op jit(solution)/shard_map/ppermute | solution.py:407
  12.4 4.8 %collective-permute-done.23 = bf16[128,512]{1,0:T(8,128)(2,1)S(1)} collective-permute-done((bf16[128,512]{1,0:T(8,128)(2,1)}, bf16[128,512]{1,0:T(8,128)(2,1)S(1)}, u32[]{:S(2)}, u32[]{:S(2)}) %collective-permute-start.23) | collective-permute-done | bytes 131104 | tf_op jit(solution)/shard_map/ppermute | solution.py:407
  22.1 3.3 %collective-permute-start.26 = (bf16[64,1024]{1,0:T(8,128)(2,1)}, bf16[64,1024]{1,0:T(8,128)(2,1)S(1)}, u32[]{:S(2)}, u32[]{:S(2)}) collective-permute-start(bf16[64,1024]{1,0:T(8,128)(2,1)} %get-tuple-element.176), channel_id=1, source_target_pairs={{0,1},{1,2},{2,3},{3,0},{4,5},{5,6},{6,7},{7,4},{8,9},{9,10},{10,1... | collective-permute-start | bytes 393224 | tf_op jit(solution)/shard_map/ppermute | solution.py:407
  27.8 3.2 %collective-permute-done.26.refs_2_ = bf16[64,1024]{1,0:T(8,128)(2,1)S(1)} collective-permute-done((bf16[64,1024]{1,0:T(8,128)(2,1)}, bf16[64,1024]{1,0:T(8,128)(2,1)S(1)}, u32[]{:S(2)}, u32[]{:S(2)}) %collective-permute-start.26) | collective-permute-done | bytes 131104 | tf_op jit(solution)/shard_map/ppermute | solution.py:407
  31.0 4.3 %collective-permute-done.27.refs_4_ = bf16[64,1024]{1,0:T(8,128)(2,1)S(1)} collective-permute-done((bf16[64,1024]{1,0:T(8,128)(2,1)}, bf16[64,1024]{1,0:T(8,128)(2,1)S(1)}, u32[]{:S(2)}, u32[]{:S(2)}) %collective-permute-start.27) | collective-permute-done | bytes 131104 | tf_op jit(solution)/shard_map/ppermute | solution.py:407
  35.4 3.3 %collective-permute-start.31 = (bf16[64,1024]{1,0:T(8,128)(2,1)}, bf16[64,1024]{1,0:T(8,128)(2,1)}, u32[]{:S(2)}, u32[]{:S(2)}) collective-permute-start(bf16[64,1024]{1,0:T(8,128)(2,1)} %get-tuple-element.194), channel_id=1, source_target_pairs={{0,1},{1,2},{2,3},{3,0},{4,5},{5,6},{6,7},{7,4},{8,9},{9,10},{10,1... | collective-permute-start | bytes 393224 | tf_op jit(solution)/shard_map/ppermute | solution.py:407
  42.7 17.6 %shard_map.133 = (bf16[64,3072]{1,0:T(8,128)(2,1)S(1)}, bf16[64,3072]{1,0:T(8,128)(2,1)S(1)}, bf16[64,3072]{1,0:T(8,128)(2,1)S(1)}, bf16[64,3072]{1,0:T(8,128)(2...) custom-call(s32[4]{0:T(128)S(1)} %copy-done.15, ...), custom_call_target="tpu_custom_call" | custom-call | flops 21474836480 | bytes 15728640 | tf_op jit(solution)/shard_map/pallas_call | solution.py:168
  60.5 3.2 %collective-permute-start.39 = (bf16[64,3072]{1,0:T(8,128)(2,1)S(1)}, bf16[64,3072]{1,0:T(8,128)(2,1)S(1)}, u32[]{:S(2)}, u32[]{:S(2)}) collective-permute-start(bf16[64,3072]{1,0:T(8,128)(2,1)S(1)} %broadcast_select_fusion), channel_id=1, source_target_pairs={{0,1},{3,2},{4,5},{7,6},{8,9},{11,10},{12,13},{15,14},{16,17},{19,... | collective-permute-start | bytes 1179656 | tf_op jit(solution)/shard_map/ppermute | solution.py:432
  65.1 8.2 %collective-permute-done.39 = bf16[64,3072]{1,0:T(8,128)(2,1)S(1)} collective-permute-done((bf16[64,3072]{1,0:T(8,128)(2,1)S(1)}, bf16[64,3072]{1,0:T(8,128)(2,1)S(1)}, u32[]{:S(2)}, u32[]{:S(2)}) %collective-permute-start.39) | collective-permute-done | bytes 393248 | tf_op jit(solution)/shard_map/ppermute | solution.py:432
  74.1 5.1 %collective-permute-start.40 = (bf16[64,3072]{1,0:T(8,128)(2,1)}, bf16[64,3072]{1,0:T(8,128)(2,1)}, u32[]{:S(2)}, u32[]{:S(2)}) collective-permute-start(bf16[64,3072]{1,0:T(8,128)(2,1)} %add.230), channel_id=1, source_target_pairs={{0,1},{1,2},{4,5},{5,6},{8,9},{9,10},{12,13},{13,14},{16,17},{17,1... | collective-permute-start | bytes 1179656 | tf_op jit(solution)/shard_map/ppermute | solution.py:441
  82.5 3.7 %collective-permute-start.35 = (bf16[64,3072]{1,0:T(8,128)(2,1)S(1)}, bf16[64,3072]{1,0:T(8,128)(2,1)S(1)}, u32[]{:S(2)}, u32[]{:S(2)}) collective-permute-start(bf16[64,3072]{1,0:T(8,128)(2,1)S(1)} %add.224), channel_id=1, source_target_pairs={{0,1},{1,2},{4,5},{5,6},{8,9},{9,10},{12,13},{13,14},{16,17},{17,1... | collective-permute-start | bytes 1179656 | tf_op jit(solution)/shard_map/ppermute | solution.py:441
  93.4 5.1 %collective-permute-start.42 = (bf16[64,3072]{1,0:T(8,128)(2,1)S(1)}, bf16[64,3072]{1,0:T(8,128)(2,1)S(1)}, u32[]{:S(2)}, u32[]{:S(2)}) collective-permute-start(bf16[64,3072]{1,0:T(8,128)(2,1)S(1)} %add.231), channel_id=1, source_target_pairs={{0,1},{1,2},{2,3},{4,5},{5,6},{6,7},{8,9},{9,10},{10,11},{12,13},{... | collective-permute-start | bytes 1179656 | tf_op jit(solution)/shard_map/ppermute | solution.py:441
  101.1 4.6 %collective-permute-start.37 = (bf16[64,3072]{1,0:T(8,128)(2,1)S(1)}, bf16[64,3072]{1,0:T(8,128)(2,1)S(1)}, u32[]{:S(2)}, u32[]{:S(2)}) collective-permute-start(bf16[64,3072]{1,0:T(8,128)(2,1)S(1)} %add.225), channel_id=1, source_target_pairs={{0,1},{1,2},{2,3},{4,5},{5,6},{6,7},{8,9},{9,10},{10,11},{12,13},{... | collective-permute-start | bytes 1179656 | tf_op jit(solution)/shard_map/ppermute | solution.py:441
  105.9 3.5 %collective-permute-done.38 = bf16[64,3072]{1,0:T(8,128)(2,1)S(1)} collective-permute-done((bf16[64,3072]{1,0:T(8,128)(2,1)S(1)}, bf16[64,3072]{1,0:T(8,128)(2,1)S(1)}, u32[]{:S(2)}, u32[]{:S(2)}) %collective-permute-start.38) | collective-permute-done | bytes 393248 | tf_op jit(solution)/shard_map/ppermute | solution.py:442
  109.4 5.7 %collective-permute-done.37 = bf16[64,3072]{1,0:T(8,128)(2,1)S(1)} collective-permute-done((bf16[64,3072]{1,0:T(8,128)(2,1)S(1)}, bf16[64,3072]{1,0:T(8,128)(2,1)S(1)}, u32[]{:S(2)}, u32[]{:S(2)}) %collective-permute-start.37) | collective-permute-done | bytes 393248 | tf_op jit(solution)/shard_map/ppermute | solution.py:441
  116.1 4.4 %collective-permute-start.44 = (bf16[64,6144]{1,0:T(8,128)(2,1)S(1)}, bf16[64,6144]{1,0:T(8,128)(2,1)S(1)}, u32[]{:S(2)}, u32[]{:S(2)}) collective-permute-start(bf16[64,6144]{1,0:T(8,128)(2,1)S(1)} %fusion.7.refs_1_), channel_id=1, source_target_pairs={{0,1},{1,2},{2,3},{4,5},{5,6},{6,7},{8,9},{9,10},{10,11},{12,13},{... | collective-permute-start | bytes 2359304 | tf_op jit(solution)/shard_map/ppermute | solution.py:457
  121.9 17.6 %shard_map.134 = (bf16[64,3072]{1,0:T(8,128)(2,1)S(1)}, bf16[64,3072]{1,0:T(8,128)(2,1)S(1)}, bf16[64,3072]{1,0:T(8,128)(2,1)S(1)}, bf16[64,3072]{1,0:T(8,128)(2...) custom-call(s32[4]{0:T(128)S(1)} %copy-done.15, ...), custom_call_target="tpu_custom_call" | custom-call | flops 21474836480 | bytes 15728640 | tf_op jit(solution)/shard_map/pallas_call | solution.py:168
  143.6 5.3 %collective-permute-start.46 = (bf16[64,3072]{1,0:T(8,128)(2,1)S(1)}, bf16[64,3072]{1,0:T(8,128)(2,1)}, u32[]{:S(2)}, u32[]{:S(2)}) collective-permute-start(bf16[64,3072]{1,0:T(8,128)(2,1)S(1)} %get-tuple-element.316.refs_2_), channel_id=1, source_target_pairs={{0,1},{1,2},{2,3},{4,5},{5,6},{6,7},{8,9},{9,10},{10,11},{12,13},{... | collective-permute-start | bytes 1179656 | tf_op jit(solution)/shard_map/ppermute | solution.py:479
  150.6 4.6 %collective-permute-start.48 = (bf16[64,3072]{1,0:T(8,128)(2,1)S(1)}, bf16[64,3072]{1,0:T(8,128)(2,1)S(1)}, u32[]{:S(2)}, u32[]{:S(2)}) collective-permute-start(bf16[64,3072]{1,0:T(8,128)(2,1)S(1)} %get-tuple-element.315.refs_3_), channel_id=1, source_target_pairs={{0,1},{1,2},{2,3},{4,5},{5,6},{6,7},{8,9},{9,10},{10,11},{12,13},{... | collective-permute-start | bytes 1179656 | tf_op jit(solution)/shard_map/ppermute | solution.py:479
  157.5 3.7 %collective-permute-start.50 = (bf16[64,3072]{1,0:T(8,128)(2,1)S(1)}, bf16[64,3072]{1,0:T(8,128)(2,1)S(1)}, u32[]{:S(2)}, u32[]{:S(2)}) collective-permute-start(bf16[64,3072]{1,0:T(8,128)(2,1)S(1)} %get-tuple-element.324.refs_4_), channel_id=1, source_target_pairs={{0,1},{1,2},{2,3},{4,5},{5,6},{6,7},{8,9},{9,10},{10,11},{12,13},{... | collective-permute-start | bytes 1179656 | tf_op jit(solution)/shard_map/ppermute | solution.py:479
  162.6 4.6 %collective-permute-start.52 = (bf16[64,3072]{1,0:T(8,128)(2,1)S(1)}, bf16[64,3072]{1,0:T(8,128)(2,1)S(1)}, u32[]{:S(2)}, u32[]{:S(2)}) collective-permute-start(bf16[64,3072]{1,0:T(8,128)(2,1)S(1)} %get-tuple-element.322.refs_5_), channel_id=1, source_target_pairs={{0,1},{1,2},{2,3},{4,5},{5,6},{6,7},{8,9},{9,10},{10,11},{12,13},{... | collective-permute-start | bytes 1179656 | tf_op jit(solution)/shard_map/ppermute | solution.py:479
  170.4 4.4 %collective-permute-done.51.refs_12_ = bf16[64,3072]{1,0:T(8,128)(2,1)S(1)} collective-permute-done((bf16[64,3072]{1,0:T(8,128)(2,1)S(1)}, bf16[64,3072]{1,0:T(8,128)(2,1)S(1)}, u32[]{:S(2)}, u32[]{:S(2)}) %collective-permute-start.51) | collective-permute-done | bytes 393248 | tf_op jit(solution)/shard_map/ppermute | solution.py:479
  174.9 3.9 %collective-permute-done.52.refs_7_ = bf16[64,3072]{1,0:T(8,128)(2,1)S(1)} collective-permute-done((bf16[64,3072]{1,0:T(8,128)(2,1)S(1)}, bf16[64,3072]{1,0:T(8,128)(2,1)S(1)}, u32[]{:S(2)}, u32[]{:S(2)}) %collective-permute-start.52) | collective-permute-done | bytes 393248 | tf_op jit(solution)/shard_map/ppermute | solution.py:479
  178.8 4.4 %collective-permute-done.53.refs_13_ = bf16[64,3072]{1,0:T(8,128)(2,1)S(1)} collective-permute-done((bf16[64,3072]{1,0:T(8,128)(2,1)S(1)}, bf16[64,3072]{1,0:T(8,128)(2,1)S(1)}, u32[]{:S(2)}, u32[]{:S(2)}) %collective-permute-start.53) | collective-permute-done | bytes 393248 | tf_op jit(solution)/shard_map/ppermute | solution.py:479
  183.4 2.9 %collective-permute-start.54 = (bf16[64,6144]{1,0:T(8,128)(2,1)S(1)}, bf16[64,6144]{1,0:T(8,128)(2,1)S(1)}, u32[]{:S(2)}, u32[]{:S(2)}) collective-permute-start(bf16[64,6144]{1,0:T(8,128)(2,1)S(1)} %pad_maximum_fusion.2), channel_id=1, source_target_pairs={{0,1},{1,2},{2,3},{4,5},{5,6},{6,7},{8,9},{9,10},{10,11},{12,13},{... | collective-permute-start | bytes 2359304 | tf_op jit(solution)/shard_map/ppermute | solution.py:488
  187.8 33.9 %shard_map.135 = (bf16[256,3072]{1,0:T(8,128)(2,1)S(1)}, bf16[256,3072]{1,0:T(8,128)(2,1)S(1)}) custom-call(s32[1]{0:T(128)} %bitcast.6.mine.refs_0_, bf16[64,6144]{1,0:T(8,128)(2,1)S(1)} %fusion.7.refs_1_, bf16[64,3072]{1,0:T(8,128)(2,1)S(1)} %get-tuple-element.316.refs_2_, bf16[64,3072]{1,0:T(8,128)(2,1)S(1)} %get-tuple-element.315.refs_3_, ...), custom_call_target="tpu_custom_call" | custom-call | flops 19327352832 | bytes 75497472 | tf_op jit(solution)/shard_map/pallas_call | solution.py:263
  224.5 4.7 %collective-permute-start.62 = (bf16[64,3072]{1,0:T(8,128)(2,1)}, bf16[64,3072]{1,0:T(8,128)(2,1)S(1)}, u32[]{:S(2)}, u32[]{:S(2)}) collective-permute-start(bf16[64,3072]{1,0:T(8,128)(2,1)} %get-tuple-element.269), channel_id=1, source_target_pairs={{0,1},{4,5},{8,9},{12,13},{16,17},{20,21},{24,25},{28,29}} | collective-permute-start | bytes 1179656 | tf_op jit(solution)/shard_map/ppermute | solution.py:441
  233.3 5.7 %collective-permute-done.62 = bf16[64,3072]{1,0:T(8,128)(2,1)S(1)} collective-permute-done((bf16[64,3072]{1,0:T(8,128)(2,1)}, bf16[64,3072]{1,0:T(8,128)(2,1)S(1)}, u32[]{:S(2)}, u32[]{:S(2)}) %collective-permute-start.62) | collective-permute-done | bytes 393248 | tf_op jit(solution)/shard_map/ppermute | solution.py:441
  240.2 4.3 %collective-permute-start.64 = (bf16[64,3072]{1,0:T(8,128)(2,1)S(1)}, bf16[64,3072]{1,0:T(8,128)(2,1)S(1)}, u32[]{:S(2)}, u32[]{:S(2)}) collective-permute-start(bf16[64,3072]{1,0:T(8,128)(2,1)S(1)} %get-tuple-element.320), channel_id=1, source_target_pairs={{0,1},{1,2},{4,5},{5,6},{8,9},{9,10},{12,13},{13,14},{16,17},{17,1... | collective-permute-start | bytes 1179656 | tf_op jit(solution)/shard_map/ppermute | solution.py:441
  246.1 4.4 %collective-permute-start.58 = (bf16[64,3072]{1,0:T(8,128)(2,1)S(1)}, bf16[64,3072]{1,0:T(8,128)(2,1)S(1)}, u32[]{:S(2)}, u32[]{:S(2)}) collective-permute-start(bf16[64,3072]{1,0:T(8,128)(2,1)S(1)} %get-tuple-element.318), channel_id=1, source_target_pairs={{0,1},{1,2},{4,5},{5,6},{8,9},{9,10},{12,13},{13,14},{16,17},{17,1... | collective-permute-start | bytes 1179656 | tf_op jit(solution)/shard_map/ppermute | solution.py:441
  254.1 5.6 %collective-permute-start.66 = (bf16[64,3072]{1,0:T(8,128)(2,1)S(1)}, bf16[64,3072]{1,0:T(8,128)(2,1)S(1)}, u32[]{:S(2)}, u32[]{:S(2)}) collective-permute-start(bf16[64,3072]{1,0:T(8,128)(2,1)S(1)} %add.264), channel_id=1, source_target_pairs={{0,1},{1,2},{2,3},{4,5},{5,6},{6,7},{8,9},{9,10},{10,11},{12,13},{... | collective-permute-start | bytes 1179656 | tf_op jit(solution)/shard_map/ppermute | solution.py:441
  261.2 4.7 %collective-permute-start.60 = (bf16[64,3072]{1,0:T(8,128)(2,1)S(1)}, bf16[64,3072]{1,0:T(8,128)(2,1)S(1)}, u32[]{:S(2)}, u32[]{:S(2)}) collective-permute-start(bf16[64,3072]{1,0:T(8,128)(2,1)S(1)} %add.254), channel_id=1, source_target_pairs={{0,1},{1,2},{2,3},{4,5},{5,6},{6,7},{8,9},{9,10},{10,11},{12,13},{... | collective-permute-start | bytes 1179656 | tf_op jit(solution)/shard_map/ppermute | solution.py:441
  (190 shorter events, 74.7 us)
Async XLA Ops:
  5.7 11.4 %collective-permute-start.23 = (bf16[128,512]{1,0:T(8,128)(2,1)}, bf16[128,512]{1,0:T(8,128)(2,1)S(1)}, u32[]{:S(2)}, u32[]{:S(2)}) collective-permute-start(bf16[128,512]{1,0:T(8,128)(2,1)} %get-tuple-element.171), channel_id=1, source_target_pairs={{0,2},{1,3},{2,0},{3,1},{4,6},{5,7},{6,4},{7,5},{8,10},{9,11},{10,... | collective-permute-start | bytes 393224 | tf_op jit(solution)/shard_map/ppermute | solution.py:407
  17.2 18.1 %collective-permute-start.25 = (bf16[512,512]{1,0:T(8,128)(2,1)S(1)}, bf16[512,512]{1,0:T(8,128)(2,1)S(1)}, u32[]{:S(2)}, u32[]{:S(2)}) collective-permute-start(bf16[512,512]{1,0:T(8,128)(2,1)S(1)} %constant_dynamic-update-slice_fusion.refs_7_), channel_id=1, source_target_pairs={{0,8},{4,12},{8,0},{12,4},{1,9},{5,13},{9,1},{13,5},{2,10},{6,14},... | collective-permute-start | bytes 1572872 | tf_op jit(solution)/shard_map/ppermute | solution.py:522
  27.8 13.5 %collective-permute-start.29 = (bf16[512,512]{1,0:T(8,128)(2,1)S(1)}, bf16[512,512]{1,0:T(8,128)(2,1)S(1)}, u32[]{:S(2)}, u32[]{:S(2)}) collective-permute-start(bf16[512,512]{1,0:T(8,128)(2,1)S(1)} %constant_dynamic-update-slice_fusion.refs_7_), channel_id=1, source_target_pairs={{0,4},{4,0},{8,12},{12,8},{1,5},{5,1},{9,13},{13,9},{2,6},{6,2},{1... | collective-permute-start | bytes 1572872 | tf_op jit(solution)/shard_map/ppermute | solution.py:522
  35.4 25.0 %collective-permute-start.31 = (bf16[64,1024]{1,0:T(8,128)(2,1)}, bf16[64,1024]{1,0:T(8,128)(2,1)}, u32[]{:S(2)}, u32[]{:S(2)}) collective-permute-start(bf16[64,1024]{1,0:T(8,128)(2,1)} %get-tuple-element.194), channel_id=1, source_target_pairs={{0,1},{1,2},{2,3},{3,0},{4,5},{5,6},{6,7},{7,4},{8,9},{9,10},{10,1... | collective-permute-start | bytes 393224 | tf_op jit(solution)/shard_map/ppermute | solution.py:407
  38.7 21.7 %collective-permute-start.32 = (bf16[64,1024]{1,0:T(8,128)(2,1)}, bf16[64,1024]{1,0:T(8,128)(2,1)}, u32[]{:S(2)}, u32[]{:S(2)}) collective-permute-start(bf16[64,1024]{1,0:T(8,128)(2,1)} %get-tuple-element.195), channel_id=1, source_target_pairs={{0,2},{1,3},{2,0},{3,1},{4,6},{5,7},{6,4},{7,5},{8,10},{9,11},{10,... | collective-permute-start | bytes 393224 | tf_op jit(solution)/shard_map/ppermute | solution.py:407
  40.5 19.9 %collective-permute-start.33 = (bf16[64,1024]{1,0:T(8,128)(2,1)}, bf16[64,1024]{1,0:T(8,128)(2,1)}, u32[]{:S(2)}, u32[]{:S(2)}) collective-permute-start(bf16[64,1024]{1,0:T(8,128)(2,1)} %get-tuple-element.196), channel_id=1, source_target_pairs={{0,3},{1,0},{2,1},{3,2},{4,7},{5,4},{6,5},{7,6},{8,11},{9,8},{10,9... | collective-permute-start | bytes 393224 | tf_op jit(solution)/shard_map/ppermute | solution.py:407
  60.5 12.8 %collective-permute-start.39 = (bf16[64,3072]{1,0:T(8,128)(2,1)S(1)}, bf16[64,3072]{1,0:T(8,128)(2,1)S(1)}, u32[]{:S(2)}, u32[]{:S(2)}) collective-permute-start(bf16[64,3072]{1,0:T(8,128)(2,1)S(1)} %broadcast_select_fusion), channel_id=1, source_target_pairs={{0,1},{3,2},{4,5},{7,6},{8,9},{11,10},{12,13},{15,14},{16,17},{19,... | collective-permute-start | bytes 1179656 | tf_op jit(solution)/shard_map/ppermute | solution.py:432
  63.8 18.6 %collective-permute-start.34 = (bf16[64,3072]{1,0:T(8,128)(2,1)S(1)}, bf16[64,3072]{1,0:T(8,128)(2,1)S(1)}, u32[]{:S(2)}, u32[]{:S(2)}) collective-permute-start(bf16[64,3072]{1,0:T(8,128)(2,1)S(1)} %broadcast_select_fusion.1), channel_id=1, source_target_pairs={{0,1},{3,2},{4,5},{7,6},{8,9},{11,10},{12,13},{15,14},{16,17},{19,... | collective-permute-start | bytes 1179656 | tf_op jit(solution)/shard_map/ppermute | solution.py:432
  74.1 15.6 %collective-permute-start.40 = (bf16[64,3072]{1,0:T(8,128)(2,1)}, bf16[64,3072]{1,0:T(8,128)(2,1)}, u32[]{:S(2)}, u32[]{:S(2)}) collective-permute-start(bf16[64,3072]{1,0:T(8,128)(2,1)} %add.230), channel_id=1, source_target_pairs={{0,1},{1,2},{4,5},{5,6},{8,9},{9,10},{12,13},{13,14},{16,17},{17,1... | collective-permute-start | bytes 1179656 | tf_op jit(solution)/shard_map/ppermute | solution.py:441
  82.5 16.0 %collective-permute-start.35 = (bf16[64,3072]{1,0:T(8,128)(2,1)S(1)}, bf16[64,3072]{1,0:T(8,128)(2,1)S(1)}, u32[]{:S(2)}, u32[]{:S(2)}) collective-permute-start(bf16[64,3072]{1,0:T(8,128)(2,1)S(1)} %add.224), channel_id=1, source_target_pairs={{0,1},{1,2},{4,5},{5,6},{8,9},{9,10},{12,13},{13,14},{16,17},{17,1... | collective-permute-start | bytes 1179656 | tf_op jit(solution)/shard_map/ppermute | solution.py:441
  86.2 12.3 %collective-permute-start.36 = (bf16[64,3072]{1,0:T(8,128)(2,1)S(1)}, bf16[64,3072]{1,0:T(8,128)(2,1)}, u32[]{:S(2)}, u32[]{:S(2)}) collective-permute-start(bf16[64,3072]{1,0:T(8,128)(2,1)S(1)} %add.224), channel_id=1, source_target_pairs={{2,1},{3,2},{6,5},{7,6},{10,9},{11,10},{14,13},{15,14},{18,17},{19... | collective-permute-start | bytes 1179656 | tf_op jit(solution)/shard_map/ppermute | solution.py:442
  90.8 15.0 %collective-permute-start.43 = (bf16[64,3072]{1,0:T(8,128)(2,1)S(1)}, bf16[64,3072]{1,0:T(8,128)(2,1)S(1)}, u32[]{:S(2)}, u32[]{:S(2)}) collective-permute-start(bf16[64,3072]{1,0:T(8,128)(2,1)S(1)} %add.232), channel_id=1, source_target_pairs={{1,0},{2,1},{3,2},{5,4},{6,5},{7,6},{9,8},{10,9},{11,10},{13,12},{... | collective-permute-start | bytes 1179656 | tf_op jit(solution)/shard_map/ppermute | solution.py:442
  93.4 12.5 %collective-permute-start.42 = (bf16[64,3072]{1,0:T(8,128)(2,1)S(1)}, bf16[64,3072]{1,0:T(8,128)(2,1)S(1)}, u32[]{:S(2)}, u32[]{:S(2)}) collective-permute-start(bf16[64,3072]{1,0:T(8,128)(2,1)S(1)} %add.231), channel_id=1, source_target_pairs={{0,1},{1,2},{2,3},{4,5},{5,6},{6,7},{8,9},{9,10},{10,11},{12,13},{... | collective-permute-start | bytes 1179656 | tf_op jit(solution)/shard_map/ppermute | solution.py:441
  101.1 14.0 %collective-permute-start.37 = (bf16[64,3072]{1,0:T(8,128)(2,1)S(1)}, bf16[64,3072]{1,0:T(8,128)(2,1)S(1)}, u32[]{:S(2)}, u32[]{:S(2)}) collective-permute-start(bf16[64,3072]{1,0:T(8,128)(2,1)S(1)} %add.225), channel_id=1, source_target_pairs={{0,1},{1,2},{2,3},{4,5},{5,6},{6,7},{8,9},{9,10},{10,11},{12,13},{... | collective-permute-start | bytes 1179656 | tf_op jit(solution)/shard_map/ppermute | solution.py:441
  116.1 23.5 %collective-permute-start.44 = (bf16[64,6144]{1,0:T(8,128)(2,1)S(1)}, bf16[64,6144]{1,0:T(8,128)(2,1)S(1)}, u32[]{:S(2)}, u32[]{:S(2)}) collective-permute-start(bf16[64,6144]{1,0:T(8,128)(2,1)S(1)} %fusion.7.refs_1_), channel_id=1, source_target_pairs={{0,1},{1,2},{2,3},{4,5},{5,6},{6,7},{8,9},{9,10},{10,11},{12,13},{... | collective-permute-start | bytes 2359304 | tf_op jit(solution)/shard_map/ppermute | solution.py:457
  120.6 21.5 %collective-permute-start.45 = (bf16[64,6144]{1,0:T(8,128)(2,1)S(1)}, bf16[64,6144]{1,0:T(8,128)(2,1)S(1)}, u32[]{:S(2)}, u32[]{:S(2)}) collective-permute-start(bf16[64,6144]{1,0:T(8,128)(2,1)S(1)} %fusion.7.refs_1_), channel_id=1, source_target_pairs={{1,0},{2,1},{3,2},{5,4},{6,5},{7,6},{9,8},{10,9},{11,10},{13,12},{... | collective-permute-start | bytes 2359304 | tf_op jit(solution)/shard_map/ppermute | solution.py:458
  142.2 13.9 %collective-permute-start.47 = (bf16[64,3072]{1,0:T(8,128)(2,1)S(1)}, bf16[64,3072]{1,0:T(8,128)(2,1)}, u32[]{:S(2)}, u32[]{:S(2)}) collective-permute-start(bf16[64,3072]{1,0:T(8,128)(2,1)S(1)} %get-tuple-element.314.refs_8_), channel_id=1, source_target_pairs={{1,0},{2,1},{3,2},{5,4},{6,5},{7,6},{9,8},{10,9},{11,10},{13,12},{... | collective-permute-start | bytes 1179656 | tf_op jit(solution)/shard_map/ppermute | solution.py:479
  143.6 12.5 %collective-permute-start.46 = (bf16[64,3072]{1,0:T(8,128)(2,1)S(1)}, bf16[64,3072]{1,0:T(8,128)(2,1)}, u32[]{:S(2)}, u32[]{:S(2)}) collective-permute-start(bf16[64,3072]{1,0:T(8,128)(2,1)S(1)} %get-tuple-element.316.refs_2_), channel_id=1, source_target_pairs={{0,1},{1,2},{2,3},{4,5},{5,6},{6,7},{8,9},{9,10},{10,11},{12,13},{... | collective-permute-start | bytes 1179656 | tf_op jit(solution)/shard_map/ppermute | solution.py:479
  149.0 13.5 %collective-permute-start.49 = (bf16[64,3072]{1,0:T(8,128)(2,1)S(1)}, bf16[64,3072]{1,0:T(8,128)(2,1)S(1)}, u32[]{:S(2)}, u32[]{:S(2)}) collective-permute-start(bf16[64,3072]{1,0:T(8,128)(2,1)S(1)} %get-tuple-element.313.refs_9_), channel_id=1, source_target_pairs={{1,0},{2,1},{3,2},{5,4},{6,5},{7,6},{9,8},{10,9},{11,10},{13,12},{... | collective-permute-start | bytes 1179656 | tf_op jit(solution)/shard_map/ppermute | solution.py:479
  150.6 11.9 %collective-permute-start.48 = (bf16[64,3072]{1,0:T(8,128)(2,1)S(1)}, bf16[64,3072]{1,0:T(8,128)(2,1)S(1)}, u32[]{:S(2)}, u32[]{:S(2)}) collective-permute-start(bf16[64,3072]{1,0:T(8,128)(2,1)S(1)} %get-tuple-element.315.refs_3_), channel_id=1, source_target_pairs={{0,1},{1,2},{2,3},{4,5},{5,6},{6,7},{8,9},{9,10},{10,11},{12,13},{... | collective-permute-start | bytes 1179656 | tf_op jit(solution)/shard_map/ppermute | solution.py:479
  157.5 12.9 %collective-permute-start.50 = (bf16[64,3072]{1,0:T(8,128)(2,1)S(1)}, bf16[64,3072]{1,0:T(8,128)(2,1)S(1)}, u32[]{:S(2)}, u32[]{:S(2)}) collective-permute-start(bf16[64,3072]{1,0:T(8,128)(2,1)S(1)} %get-tuple-element.324.refs_4_), channel_id=1, source_target_pairs={{0,1},{1,2},{2,3},{4,5},{5,6},{6,7},{8,9},{9,10},{10,11},{12,13},{... | collective-permute-start | bytes 1179656 | tf_op jit(solution)/shard_map/ppermute | solution.py:479
  161.2 13.6 %collective-permute-start.51 = (bf16[64,3072]{1,0:T(8,128)(2,1)S(1)}, bf16[64,3072]{1,0:T(8,128)(2,1)S(1)}, u32[]{:S(2)}, u32[]{:S(2)}) collective-permute-start(bf16[64,3072]{1,0:T(8,128)(2,1)S(1)} %get-tuple-element.323.refs_10_), channel_id=1, source_target_pairs={{1,0},{2,1},{3,2},{5,4},{6,5},{7,6},{9,8},{10,9},{11,10},{13,12},{... | collective-permute-start | bytes 1179656 | tf_op jit(solution)/shard_map/ppermute | solution.py:479
  162.6 16.2 %collective-permute-start.52 = (bf16[64,3072]{1,0:T(8,128)(2,1)S(1)}, bf16[64,3072]{1,0:T(8,128)(2,1)S(1)}, u32[]{:S(2)}, u32[]{:S(2)}) collective-permute-start(bf16[64,3072]{1,0:T(8,128)(2,1)S(1)} %get-tuple-element.322.refs_5_), channel_id=1, source_target_pairs={{0,1},{1,2},{2,3},{4,5},{5,6},{6,7},{8,9},{9,10},{10,11},{12,13},{... | collective-permute-start | bytes 1179656 | tf_op jit(solution)/shard_map/ppermute | solution.py:479
  167.2 16.0 %collective-permute-start.53 = (bf16[64,3072]{1,0:T(8,128)(2,1)S(1)}, bf16[64,3072]{1,0:T(8,128)(2,1)S(1)}, u32[]{:S(2)}, u32[]{:S(2)}) collective-permute-start(bf16[64,3072]{1,0:T(8,128)(2,1)S(1)} %get-tuple-element.321.refs_11_), channel_id=1, source_target_pairs={{1,0},{2,1},{3,2},{5,4},{6,5},{7,6},{9,8},{10,9},{11,10},{13,12},{... | collective-permute-start | bytes 1179656 | tf_op jit(solution)/shard_map/ppermute | solution.py:479
  183.4 39.7 %collective-permute-start.54 = (bf16[64,6144]{1,0:T(8,128)(2,1)S(1)}, bf16[64,6144]{1,0:T(8,128)(2,1)S(1)}, u32[]{:S(2)}, u32[]{:S(2)}) collective-permute-start(bf16[64,6144]{1,0:T(8,128)(2,1)S(1)} %pad_maximum_fusion.2), channel_id=1, source_target_pairs={{0,1},{1,2},{2,3},{4,5},{5,6},{6,7},{8,9},{9,10},{10,11},{12,13},{... | collective-permute-start | bytes 2359304 | tf_op jit(solution)/shard_map/ppermute | solution.py:488
  186.5 36.5 %collective-permute-start.55 = (bf16[64,6144]{1,0:T(8,128)(2,1)S(1)}, bf16[64,6144]{1,0:T(8,128)(2,1)S(1)}, u32[]{:S(2)}, u32[]{:S(2)}) collective-permute-start(bf16[64,6144]{1,0:T(8,128)(2,1)S(1)} %pad_maximum_fusion.3), channel_id=1, source_target_pairs={{1,0},{2,1},{3,2},{5,4},{6,5},{7,6},{9,8},{10,9},{11,10},{13,12},{... | collective-permute-start | bytes 2359304 | tf_op jit(solution)/shard_map/ppermute | solution.py:489
  224.5 14.5 %collective-permute-start.62 = (bf16[64,3072]{1,0:T(8,128)(2,1)}, bf16[64,3072]{1,0:T(8,128)(2,1)S(1)}, u32[]{:S(2)}, u32[]{:S(2)}) collective-permute-start(bf16[64,3072]{1,0:T(8,128)(2,1)} %get-tuple-element.269), channel_id=1, source_target_pairs={{0,1},{4,5},{8,9},{12,13},{16,17},{20,21},{24,25},{28,29}} | collective-permute-start | bytes 1179656 | tf_op jit(solution)/shard_map/ppermute | solution.py:441
  231.3 14.7 %collective-permute-start.56 = (bf16[64,3072]{1,0:T(8,128)(2,1)S(1)}, bf16[64,3072]{1,0:T(8,128)(2,1)S(1)}, u32[]{:S(2)}, u32[]{:S(2)}) collective-permute-start(bf16[64,3072]{1,0:T(8,128)(2,1)S(1)} %get-tuple-element.258), channel_id=1, source_target_pairs={{0,1},{4,5},{8,9},{12,13},{16,17},{20,21},{24,25},{28,29}} | collective-permute-start | bytes 1179656 | tf_op jit(solution)/shard_map/ppermute | solution.py:441
  232.6 13.4 %collective-permute-start.57 = (bf16[64,3072]{1,0:T(8,128)(2,1)S(1)}, bf16[64,3072]{1,0:T(8,128)(2,1)S(1)}, u32[]{:S(2)}, u32[]{:S(2)}) collective-permute-start(bf16[64,3072]{1,0:T(8,128)(2,1)S(1)} %get-tuple-element.256), channel_id=1, source_target_pairs={{3,2},{7,6},{11,10},{15,14},{19,18},{23,22},{27,26},{31,30}} | collective-permute-start | bytes 1179656 | tf_op jit(solution)/shard_map/ppermute | solution.py:442
  246.1 13.6 %collective-permute-start.58 = (bf16[64,3072]{1,0:T(8,128)(2,1)S(1)}, bf16[64,3072]{1,0:T(8,128)(2,1)S(1)}, u32[]{:S(2)}, u32[]{:S(2)}) collective-permute-start(bf16[64,3072]{1,0:T(8,128)(2,1)S(1)} %get-tuple-element.318), channel_id=1, source_target_pairs={{0,1},{1,2},{4,5},{5,6},{8,9},{9,10},{12,13},{13,14},{16,17},{17,1... | collective-permute-start | bytes 1179656 | tf_op jit(solution)/shard_map/ppermute | solution.py:441
  252.5 15.6 %collective-permute-start.67 = (bf16[64,3072]{1,0:T(8,128)(2,1)S(1)}, bf16[64,3072]{1,0:T(8,128)(2,1)S(1)}, u32[]{:S(2)}, u32[]{:S(2)}) collective-permute-start(bf16[64,3072]{1,0:T(8,128)(2,1)S(1)} %add.265), channel_id=1, source_target_pairs={{1,0},{2,1},{3,2},{5,4},{6,5},{7,6},{9,8},{10,9},{11,10},{13,12},{... | collective-permute-start | bytes 1179656 | tf_op jit(solution)/shard_map/ppermute | solution.py:442
  254.1 14.0 %collective-permute-start.66 = (bf16[64,3072]{1,0:T(8,128)(2,1)S(1)}, bf16[64,3072]{1,0:T(8,128)(2,1)S(1)}, u32[]{:S(2)}, u32[]{:S(2)}) collective-permute-start(bf16[64,3072]{1,0:T(8,128)(2,1)S(1)} %add.264), channel_id=1, source_target_pairs={{0,1},{1,2},{2,3},{4,5},{5,6},{6,7},{8,9},{9,10},{10,11},{12,13},{... | collective-permute-start | bytes 1179656 | tf_op jit(solution)/shard_map/ppermute | solution.py:441
  (52 other events, 571.8 us)
